TPU v7x, 512 devices: a whole 4x8x8 slice. The times are simulated.
512 devices in a mesh: ctx: 64 (over y, z_lo, core), head: 8 (over x, z_hi).
Axes of the slice: x: 4, y: 8, z: 8 (z_hi: 2, z_lo: 4; z = z_hi * 4 + z_lo), core: 2. Of those that a mesh axis runs over, the one named last changes fastest.
Arguments:
- index_query: bfloat16 [8192, 4096], P(('ctx', 'head')), may hold values from -6 to 6
- index_weight: float32 [8192, 32], P(('ctx', 'head')), may hold values from -1 to 1
- index_key: bfloat16 [8192, 128], P('ctx'), may hold values from -6 to 6
- latent_query: bfloat16 [8192, 36864], P('ctx', 'head'), may hold values from -20 to 20
- latent: bfloat16 [8192, 576], P('ctx'), may hold values from -6 to 6
- block_lists: int32 [64, 16], P('ctx'), may hold values from -1 to 63, as said below
- value_up: bfloat16 [64, 512, 128], P('head'), may hold values from -0.25 to 0.25
- out_weight: bfloat16 [8192, 3584], P('head', 'ctx'), may hold values from -0.1875 to 0.1875
Outputs:
- index_scores: float32 [8192, 8192], P(('ctx', 'head'))
- attn_out: bfloat16 [8192, 3584], P('ctx', 'head')
Inputs may be any that keep to these rules, and one draw needn't show every extreme that they name: `block_lists`: row b lists b itself first, then min(15, b) distinct blocks below b; the remaining entries are -1.
All inputs are finite; a program needn't handle non-finite values.
Results may differ from a plain program's by a relative error of at most 0.02.
Values may be sent and summed in bfloat16 or wider, within the bound.
No kernel may reach another device: no remote copies, remote signals or barrier semaphores. Data moves between devices by JAX's collectives and lax.ppermute only.
A program may use at most 64 MiB of HBM per device.

v0:
```python
import jax
import jax.numpy as jnp
from jax import lax
from jax.sharding import PartitionSpec as P

TOK_DEV = 128
KV_RANK = 512
V_DIM = 128
IDX_HEADS = 32
IDX_DIM = 128
BLOCK = 128
TOPK = 16


attention_scale = 192.0 ** (-0.5)
masked_value = -1e30


def body(
    index_query, index_weight, index_key, latent_query, latent, block_lists, value_up, out_weight
):
    ctx_count = lax.axis_size("ctx")
    head_count = lax.axis_size("head")
    ctx_pos = lax.axis_index("ctx")
    head_pos = lax.axis_index("head")
    seq_total = ctx_count * TOK_DEV
    head_rows = TOK_DEV // head_count
    first_row = ctx_pos * TOK_DEV + head_pos * head_rows
    last_row = first_row + head_rows - 1
    query_rows = index_query.reshape(head_rows * IDX_HEADS, IDX_DIM)
    row_pos = first_row + jnp.arange(head_rows, dtype=jnp.int32)

    def score_keys(key_rows, offset):
        raw_dots = lax.dot_general(
            query_rows, key_rows, (((1,), (1,)), ((), ())), preferred_element_type=jnp.float32
        )
        active = jnp.maximum(raw_dots * IDX_DIM ** (-0.5), 0.0).reshape(
            head_rows, IDX_HEADS, key_rows.shape[0]
        )
        summed = jnp.einsum("rhk,rh->rk", active, index_weight)
        key_pos = offset + jnp.arange(key_rows.shape[0], dtype=jnp.int32)
        return jnp.where(key_pos[None, :] <= row_pos[:, None], summed, jnp.zeros_like(summed))

    def score_bounded(key_rows):
        amount = key_rows.shape[0]
        sections = key_rows.reshape(amount // 512, 512, IDX_DIM)
        offsets = 512 * jnp.arange(amount // 512, dtype=jnp.int32)

        def one_section(packed):
            return score_keys(packed[0], packed[1])

        result = lax.map(one_section, (sections, offsets))
        return jnp.moveaxis(result, 0, 1).reshape(head_rows, amount)

    tile_count = TOK_DEV // BLOCK
    slice_rows = BLOCK // head_count
    lat_width = latent.shape[1]
    own_rows = lax.dynamic_slice_in_dim(
        latent.reshape(tile_count, BLOCK, lat_width), head_pos * slice_rows, slice_rows, 1
    )
    own_rows = own_rows.reshape(tile_count * slice_rows, lat_width)
    shard_rows = lax.all_gather(index_key, "ctx", axis=0, tiled=True)

    def write_in(current):
        return score_bounded(shard_rows)

    def keep_as(current):
        return current

    index_scores = lax.cond(
        jnp.int32(0) <= last_row, write_in, keep_as, jnp.zeros((head_rows, seq_total), jnp.float32)
    )
    all_rows = lax.all_gather(own_rows, "ctx", axis=0, tiled=True)
    row_pool = all_rows.reshape(seq_total // BLOCK, slice_rows, lat_width)
    safe_list = jnp.maximum(block_lists, 0)
    picked = jnp.take(row_pool, safe_list.reshape(tile_count * TOPK), axis=0).reshape(
        tile_count, TOPK, slice_rows, lat_width
    )
    chosen = lax.all_gather(picked, "head", axis=2, tiled=True)
    local_heads = value_up.shape[0]
    group_size = 512 // BLOCK
    group_count = local_heads // group_size
    queries = latent_query.reshape(tile_count, BLOCK, group_count, group_size, lat_width)
    up_groups = value_up.reshape(group_count, group_size, KV_RANK, V_DIM)
    listed = block_lists[0]
    pulled = chosen[0].reshape(TOPK * BLOCK, lat_width)
    key_pos = (safe_list[0][:, None] * BLOCK + jnp.arange(BLOCK, dtype=jnp.int32)[None, :]).reshape(
        TOPK * BLOCK
    )
    key_live = jnp.repeat(listed >= 0, BLOCK)
    query_pos = (ctx_pos * tile_count + 0) * BLOCK + jnp.arange(BLOCK, dtype=jnp.int32)
    allowed = key_live[None, :] & (key_pos[None, :] <= query_pos[:, None])
    query_groups = jnp.moveaxis(queries[0], 1, 0)

    def attend(packed):
        group_query = packed[0]
        group_up = packed[1]
        scores = (
            jnp.einsum("qhc,kc->hqk", group_query, pulled, preferred_element_type=jnp.float32)
            * attention_scale
        )
        scores = jnp.where(allowed[None], scores, masked_value)
        row_max = jnp.max(scores, axis=-1, keepdims=True)
        expo_terms = jnp.where(allowed[None], jnp.exp(scores - row_max), 0.0)
        probabilities = (expo_terms / jnp.sum(expo_terms, axis=-1, keepdims=True)).astype(
            jnp.bfloat16
        )
        latent_out = jnp.einsum(
            "hqk,kc->hqc", probabilities, pulled[:, :KV_RANK], preferred_element_type=jnp.float32
        ).astype(jnp.bfloat16)
        return jnp.einsum(
            "hqc,hcv->qhv", latent_out, group_up, preferred_element_type=jnp.float32
        ).astype(jnp.bfloat16)

    grouped = lax.map(attend, (query_groups, up_groups))
    tile_values = jnp.moveaxis(grouped, 0, 1).reshape(BLOCK, local_heads * V_DIM)
    terms = jnp.dot(
        tile_values,
        lax.all_gather(out_weight, "ctx", axis=1, tiled=True),
        preferred_element_type=jnp.float32,
    )
    summed = lax.psum_scatter(
        terms.astype(jnp.bfloat16), "head", scatter_dimension=1, tiled=True
    ).astype(jnp.float32)
    return (index_scores, summed.astype(jnp.bfloat16))


def solution(mesh):
    return jax.shard_map(
        body,
        mesh=mesh,
        in_specs=(
            P(("ctx", "head"), None),
            P(("ctx", "head"), None),
            P("ctx", None),
            P("ctx", "head"),
            P("ctx", None),
            P("ctx", None),
            P("head", None, None),
            P("head", "ctx"),
        ),
        out_specs=(P(("ctx", "head"), None), P("ctx", "head")),
        check_vma=False,
    )
```

profile of v0, /device:TPU:1, one launch (start us, length us, event | category | flops | bytes accessed | tf_op | source)
XLA Modules:
  0.0 566.3 jit_solution(9682865217719668042)
XLA Ops:
  7.2 0.8 copy-done
  8.2 0.7 copy.22
  9.0 0.7 fusion.43
  9.7 0.7 compare_and_fusion.1
  10.3 124.3 %all-gather.7.cloned.1.call-done = bf16[1024,576]{1,0:T(8,128)(2,1)} async-done(((bf16[16,576]{1,0:T(8,128)(2,1)}), bf16[1024,576]{1,0:T(8,128)(2,1)}) %all-gather.7.cloned.1.call-update) | async-done | bytes 1179664 | tf_op jit(solution)/shard_map/all_gather | solution.py:73
  134.6 1.9 gather_fusion
  136.6 0.8 bitcast_select_fusion.1
  137.5 0.7 all-gather.11.cloned.1.call-update
  138.8 0.7 bitcast_multiply_fusion
  139.4 0.7 compare_bitcast_fusion
  140.6 2.4 copy.17
  143.5 0.7 add_bitcast_fusion
  144.2 0.7 broadcast_bitcast_fusion
  144.9 79.8 %all-gather.9.cloned.1.call-done = bf16[1,16,128,576]{3,2,1,0:T(8,128)(2,1)} async-done(((bf16[1,16,16,576]{3,2,1,0:T(8,128)(2,1)}), bf16[1,16,128,576]{3,2,1,0:T(8,128)(2,1)}) %all-gather.9.cloned.1.call-update) | async-done | bytes 2359312 | tf_op jit(solution)/shard_map/all_gather | solution.py:79
  224.6 2.9 copy.19
  227.6 24.3 %while.21 = (s32[]{:T(128)}, bf16[2,128,4,128]{1,3,2,0:T(8,128)(2,1)}, bf16[2,4,512,128]{2,3,1,0:T(8,128)(2,1)S(1)}, bf16[2,128,4,576]{1,3,2,0:T(8,128)(2,1)}, b...) while((s32[]{:T(128)}, ...), condition=%wide.region_7.8_spmd.clone, body=%wide.region_4.7_spmd.clone.sunk | while | flops 2359101440 | bytes 23062704 | solution.py:115
  227.6 2.9 fusion.68
  230.8 4.6 fusion.69
  235.4 4.3 fusion.70
  239.7 2.9 fusion.68
  242.9 4.6 fusion.69
  247.5 4.4 fusion.70
  251.9 95.9 %all-gather.11.cloned.1.call-done = bf16[1024,3584]{0,1:T(8,128)(2,1)} async-done(((bf16[1024,56]{0,1:T(8,128)(2,1)}), bf16[1024,3584]{0,1:T(8,128)(2,1)}) %all-gather.11.cloned.1.call-update) | async-done | bytes 7340048 | tf_op jit(solution)/shard_map/all_gather | solution.py:119
  347.7 6.2 %convolution_convert_fusion = bf16[128,3584]{0,1:T(8,128)(2,1)} fusion(bf16[1024,3584]{0,1:T(8,128)(2,1)} %all-gather.11.cloned.1.call-done, bf16[128,1024]{0,1:T(8,128)(2,1)} %bitcast.129), kind=kOutput, calls=%fused_computation.42 | convolution fusion | flops 939982848 | bytes 8519680 | tf_op jit(solution)/shard_map/dot_general | solution.py:117
  353.9 112.5 %all-gather.5.cloned.1.call-done = bf16[8192,128]{1,0:T(8,128)(2,1)} async-done(((bf16[128,128]{1,0:T(8,128)(2,1)}), bf16[8192,128]{1,0:T(8,128)(2,1)}) %all-gather.5.cloned.1.call-update) | async-done | bytes 2097168 | tf_op jit(solution)/shard_map/all_gather | solution.py:62
  466.5 44.1 %conditional.1 = (f32[16,8192]{1,0:T(8,128)S(1)}) conditional(s32[]{:T(128)} %convert_element_type.20, () %tuple.22, (bf16[8192,128]{1,0:T(8,128)(2,1)}, bf16[16,4096]{1,0:T(8,128)(2,1)S(1)}, s32[]{:T(128)}, s32[16]{0:T(128)S(1)}, f32[16,32]{1,0:T(8,128)S(1)}) %tuple.72), branch_computations={%region_0.0_spmd, %region_1.4_spmd} | conditional | flops 68436512 | bytes 2727293 | solution.py:70
  466.6 44.0 %while.20 = (s32[]{:T(128)}, f32[16,16,512]{2,1,0:T(8,128)S(1)}, s32[16]{0:T(128)S(1)}, s32[16]{0:T(128)S(1)}, bf16[16,512,128]{2,1,0:T(8,128)(2,1)}, /*index=5*...) while((s32[]{:T(128)}, f32[16,16,512]{2,1,0:T(8,128)S(1)}, s32[16]{0:T(128)S(1)}, ...), condition=%wide.region_3.3_spmd, body=%wide.region_2.2_spmd.sunk | while | flops 68436480 | bytes 1416297 | solution.py:52
  466.6 1.2 fusion.75
  468.0 0.6 dynamic_slice.38
  469.3 1.2 fusion.75
  470.7 0.6 dynamic_slice.38
  472.1 1.2 fusion.75
  474.8 1.2 fusion.75
  477.6 1.2 fusion.75
  480.3 1.2 fusion.75
  483.1 1.2 fusion.75
  485.8 1.2 fusion.75
  488.5 1.2 fusion.75
  491.3 1.2 fusion.75
  494.0 1.2 fusion.75
  495.4 0.6 dynamic_slice.38
  496.8 1.2 fusion.75
  498.2 0.6 dynamic_slice.38
  499.5 1.2 fusion.75
  502.3 1.2 fusion.75
  505.0 1.2 fusion.75
  507.8 1.2 fusion.75
  510.6 49.2 %reduce-scatter.2.cloned.1.call-done = bf16[128,448]{0,1:T(8,128)(2,1)} async-done(((bf16[128,3584]{0,1:T(8,128)(2,1)}), bf16[128,448]{0,1:T(8,128)(2,1)}) %reduce-scatter.2.cloned.1.call-update) | async-done | bytes 114704 | tf_op jit(solution)/shard_map/reduce_scatter | solution.py:122
  (102 shorter events, 24.5 us)
Async XLA Ops:
  7.2 0.9 copy-start
  7.2 135.8 %copy-start.1 = (bf16[8,512,128]{2,1,0:T(8,128)(2,1)S(1)}, bf16[8,512,128]{2,1,0:T(8,128)(2,1)}, u32[]{:S(2)}) copy-start(bf16[8,512,128]{2,1,0:T(8,128)(2,1)} %param.20) | copy-start | bytes 3145732
  7.2 127.4 %all-gather.7.cloned.1.call-start = ((), (), s32[]{:S(2)}) async-start(), calls=%async_computation.2 | async-start | bytes 1331200 | tf_op jit(solution)/shard_map/all_gather | solution.py:73
  8.9 215.7 %all-gather.9.cloned.1.call-start = ((), (), s32[]{:S(2)}) async-start(), calls=%async_computation.3 | async-start | bytes 2949120 | tf_op jit(solution)/shard_map/all_gather | solution.py:79
  137.4 210.3 %all-gather.11.cloned.1.call-start = ((), (), s32[]{:S(2)}) async-start(), calls=%async_computation.4 | async-start | bytes 7454720 | tf_op jit(solution)/shard_map/all_gather | solution.py:119
  138.2 328.3 %all-gather.5.cloned.1.call-start = ((), (), s32[]{:S(2)}) async-start(), calls=%async_computation.1 | async-start | bytes 2129920 | tf_op jit(solution)/shard_map/all_gather | solution.py:62
  138.7 421.1 %reduce-scatter.2.cloned.1.call-start = ((), (), s32[]{:S(2)}) async-start(), calls=%async_computation.5 | async-start | bytes 1032192 | tf_op jit(solution)/shard_map/reduce_scatter | solution.py:122
  227.6 3.0 copy-start.3
  227.6 2.9 copy-start.6
  227.6 2.9 copy-start.7
  239.7 2.9 copy-start.3
  239.7 2.9 copy-start.6
  239.7 3.0 copy-start.7
  347.7 118.7 %copy-start.4 = (f32[16,32]{1,0:T(8,128)S(1)}, f32[16,32]{1,0:T(8,128)}, u32[]{:S(2)}) copy-start(f32[16,32]{1,0:T(8,128)} %param.15) | copy-start | bytes 6148
  347.7 118.7 %copy-start.5 = (bf16[16,4096]{1,0:T(8,128)(2,1)S(1)}, bf16[16,4096]{1,0:T(8,128)(2,1)}, u32[]{:S(2)}) copy-start(bf16[16,4096]{1,0:T(8,128)(2,1)} %param.14) | copy-start | bytes 393220
  510.6 49.2 %copy-start.2 = (f32[16,8192]{1,0:T(8,128)}, f32[16,8192]{1,0:T(8,128)S(1)}, u32[]{:S(2)}) copy-start(f32[16,8192]{1,0:T(8,128)S(1)} %get-tuple-element.307) | copy-start | bytes 1572868
Sparse Core Ops, SparseCore 0:
  10.8 123.8 all-gather.6
  138.4 86.1 all-gather.8
  226.8 120.9 all-gather.10
  349.7 116.6 all-gather.4
  471.4 88.3 reduce-scatter.1
where the time goes:
time: 568 us; the launch traced here: 566 us
  waiting for transfers between devices  463 us (82%)
  matrix products  42.9 us (8%)
  other arithmetic  25.5 us (4%)
  local copies, waits for them, and re-layouts  20.6 us (4%)
  between operations  13.9 us (2%)
    all_gather x1, waiting for transfers between devices, body(): all_rows = lax.all_gather(own_rows, 'ctx', axis=0, tiled=True)  124 us
    all_gather x1, waiting for transfers between devices, body(): shard_rows = lax.all_gather(index_key, 'ctx', axis=0, tiled=True)  113 us
    all_gather x1, waiting for transfers between devices, body(): lax.all_gather(out_weight, 'ctx', axis=1, tiled=True)  95.9 us
    all_gather x1, waiting for transfers between devices, body(): chosen = lax.all_gather(picked, 'head', axis=2, tiled=True)  79.8 us
    reduce_scatter x1, waiting for transfers between devices, body(): lax.psum_scatter(terms.astype(jnp.bfloat16), 'head', scatter_dimension=1,...  49.2 us
    dot_general x16, matrix products, score_keys(): lax.dot_general(query_rows, key_rows, (((1,), (1,)), ((), ())), preferred...  19.2 us
  transfers between devices with their start and end apart: 5, of which 5 were waited for; matrix products, arithmetic and copies ran while one was open for 15% of the time, Pallas kernels for 0%

commit v1 on v0

v1 whole, which is shorter than its diff:
```python
import jax
import jax.numpy as jnp
from jax import lax
from jax.experimental import pallas as pl
from jax.experimental.pallas import tpu as pltpu
from jax.sharding import Mesh
from jax.sharding import PartitionSpec as P

TOK_DEV = 128
HEADS_DEV = 8
KV_RANK = 512
LAT = 576
V_DIM = 128
IDX_HEADS = 32
IDX_DIM = 128
BLOCK = 128
TOPK = 16
NBLK = 64
COLS = 56
NY, NZ, NC, NX, NW = 8, 4, 2, 4, 2

CTX = ("y", "z", "c")
HEAD = ("x", "w")
LOG2E = 1.4426950408889634
SCORE_SCALE = 192.0 ** (-0.5) * LOG2E
MASKED = -1e30
VMEM_LIMIT = 56 * 1024 * 1024


def attend_kernel(q_ref, kv_ref, bias_ref, up_ref, out_ref, vt_ref):
    vt_ref[...] = kv_ref[:, :KV_RANK].T
    bias = bias_ref[...]
    bias2 = jnp.concatenate([bias, bias], axis=1)
    for pair in range(HEADS_DEV // 2):
        scores = lax.dot_general(
            kv_ref[...], q_ref[pair], (((1,), (1,)), ((), ())), preferred_element_type=jnp.float32
        )
        scores = scores + bias2
        row_max = jnp.max(scores, axis=0, keepdims=True)
        expo = jnp.exp2((scores - row_max) * SCORE_SCALE)
        total = jnp.sum(expo, axis=0, keepdims=True)
        lat_out = lax.dot_general(
            vt_ref[...],
            expo.astype(jnp.bfloat16),
            (((1,), (0,)), ((), ())),
            preferred_element_type=jnp.float32,
        )
        lat_out = (lat_out / total).astype(jnp.bfloat16)
        for half in range(2):
            head = 2 * pair + half
            values = lax.dot_general(
                up_ref[head],
                lat_out[:, half * BLOCK : (half + 1) * BLOCK],
                (((1,), (0,)), ((), ())),
                preferred_element_type=jnp.float32,
            )
            out_ref[head * V_DIM : (head + 1) * V_DIM, :] = values.astype(jnp.bfloat16)


def attend(queries, kv, bias, up_t):
    return pl.pallas_call(
        attend_kernel,
        out_shape=jax.ShapeDtypeStruct((HEADS_DEV * V_DIM, BLOCK), jnp.bfloat16),
        in_specs=[pl.BlockSpec(memory_space=pltpu.VMEM)] * 4,
        out_specs=pl.BlockSpec(memory_space=pltpu.VMEM),
        scratch_shapes=[pltpu.VMEM((KV_RANK, TOPK * BLOCK), jnp.bfloat16)],
        compiler_params=pltpu.CompilerParams(vmem_limit_bytes=VMEM_LIMIT),
        name="attend",
    )(queries, kv, bias, up_t)


def index_kernel(place_ref, q_ref, w_ref, own_ref, other_ref, out_ref, wb_ref):
    core = place_ref[0]
    first_row = place_ref[1]
    rows = 16
    for head in range(IDX_HEADS):
        wb_ref[head * rows : (head + 1) * rows, :] = jnp.broadcast_to(
            w_ref[:, head : head + 1] * (IDX_DIM ** (-0.5)), (rows, BLOCK)
        )
    row_pos = first_row + lax.broadcasted_iota(jnp.int32, (rows, BLOCK), 0)
    lane = lax.broadcasted_iota(jnp.int32, (rows, BLOCK), 1)

    def chunk(keys_ref, parity, step):
        keys = keys_ref[pl.ds(step * 2, 2)].reshape(2 * BLOCK, IDX_DIM)
        dots = lax.dot_general(
            q_ref[...], keys, (((1,), (1,)), ((), ())), preferred_element_type=jnp.float32
        )
        for half in range(2):
            part = dots[:, half * BLOCK : (half + 1) * BLOCK]
            active = jnp.maximum(part, 0.0) * wb_ref[...]
            summed = jnp.sum(active.reshape(IDX_HEADS, rows, BLOCK), axis=0)
            start = pl.multiple_of(((step * 2 + half) * 2 + parity) * BLOCK, BLOCK)
            out_ref[:, pl.ds(start, BLOCK)] = jnp.where(start + lane <= row_pos, summed, 0.0)

    def one(step, carry):
        chunk(own_ref, core, step)
        chunk(other_ref, 1 - core, step)
        return carry

    lax.fori_loop(0, NBLK // 4, one, 0)


def index_part(place, query, weight, own, other):
    return pl.pallas_call(
        index_kernel,
        out_shape=jax.ShapeDtypeStruct((16, NBLK * BLOCK), jnp.float32),
        in_specs=[pl.BlockSpec(memory_space=pltpu.SMEM)]
        + [pl.BlockSpec(memory_space=pltpu.VMEM)] * 4,
        out_specs=pl.BlockSpec(memory_space=pltpu.VMEM),
        scratch_shapes=[pltpu.VMEM((IDX_HEADS * 16, BLOCK), jnp.float32)],
        compiler_params=pltpu.CompilerParams(vmem_limit_bytes=VMEM_LIMIT),
        name="index_scores",
    )(place, query, weight, own, other)


def swap_core(value):
    return lax.ppermute(value, "c", [(0, 1), (1, 0)])


def spread(value, axis, count):
    wide = jnp.broadcast_to(value[None], (count,) + value.shape)
    return lax.all_to_all(wide, axis, 0, 0)


def body(
    index_query, index_weight, index_key, latent_query, latent, block_lists, value_up, out_weight
):
    y, z, core, x, w = (lax.axis_index(name) for name in ("y", "z", "c", "x", "w"))
    ctx_pos = (y * NZ + z) * NC + core
    head_pos = x * NW + w

    own = lax.dynamic_slice_in_dim(latent, x * 32, 32, 0).reshape(1, NC, 16, LAT)
    wide = jnp.broadcast_to(own, (NY * NZ, NC, 16, LAT)).reshape(NBLK, 16, LAT)
    pool = lax.all_to_all(wide, CTX, 0, 0)

    w_t = out_weight.T
    packed = jnp.concatenate([w_t, index_key.reshape(16, 1024)], axis=0)
    packed = spread(packed, "z", NZ)
    w_all = lax.all_gather(packed[:, :COLS], "y", axis=0, tiled=True)
    w_all = w_all.reshape(NY * NZ * COLS, 1024)
    keys_z = packed[:, COLS:].reshape(NZ, BLOCK, IDX_DIM)
    keys_own = lax.all_gather(keys_z, "y", axis=0, tiled=True)
    keys_other = swap_core(keys_own)

    listed = block_lists[0]
    safe = jnp.maximum(listed, 0)
    both = jnp.concatenate([safe, swap_core(safe)])
    picked = jnp.take(pool, both, axis=0, mode="clip").reshape(2, TOPK * 16, LAT)
    mine = jnp.concatenate([picked[0], swap_core(picked[1])], axis=0)
    kv = spread(mine, "x", NX).reshape(TOPK * BLOCK, LAT)

    place = jnp.arange(TOPK * BLOCK, dtype=jnp.int32)
    from_x = place // 512
    from_core = jnp.where((place // 256) % 2 == 0, core, 1 - core)
    slot = (place // 16) % TOPK
    key_pos = safe[slot] * BLOCK + from_x * 32 + from_core * 16 + place % 16
    live = listed[slot] >= 0
    query_pos = ctx_pos * BLOCK + jnp.arange(BLOCK, dtype=jnp.int32)
    allowed = live[:, None] & (key_pos[:, None] <= query_pos[None, :])
    bias = jnp.where(allowed, 0.0, MASKED).astype(jnp.float32)

    queries = jnp.moveaxis(latent_query.reshape(BLOCK, HEADS_DEV, LAT), 1, 0)
    queries = queries.reshape(HEADS_DEV // 2, 2 * BLOCK, LAT)
    up_t = jnp.swapaxes(value_up, 1, 2)
    values = attend(queries, kv, bias, up_t)

    both_values = jnp.concatenate([values, swap_core(values)], axis=1)
    terms = jnp.dot(w_all, both_values, preferred_element_type=jnp.float32).astype(jnp.bfloat16)
    terms = terms.reshape(NY, NZ * COLS, 2 * BLOCK)
    shares = lax.all_to_all(terms, HEAD, 0, 0)
    summed = jnp.sum(shares.astype(jnp.float32), axis=0).astype(jnp.bfloat16)
    kept = summed[:, :BLOCK].reshape(NZ, COLS, BLOCK)
    other = swap_core(summed[:, BLOCK:]).reshape(NZ, COLS, BLOCK)
    first = jnp.where(core == 0, kept, other)
    second = jnp.where(core == 0, other, kept)
    attn_out = jnp.stack([first, second], axis=1).reshape(NZ * NC * COLS, BLOCK).T

    idx_query = jnp.moveaxis(index_query.reshape(16, IDX_HEADS, IDX_DIM), 1, 0)
    idx_query = idx_query.reshape(IDX_HEADS * 16, IDX_DIM)
    first_row = ctx_pos * TOK_DEV + head_pos * 16
    index_scores = index_part(
        jnp.stack([core, first_row]), idx_query, index_weight, keys_own, keys_other
    )
    return index_scores, attn_out


def solution(mesh):
    fine = Mesh(mesh.devices.reshape(NY, NZ, NC, NX, NW), ("y", "z", "c", "x", "w"))
    return jax.shard_map(
        body,
        mesh=fine,
        in_specs=(
            P(CTX + HEAD, None),
            P(CTX + HEAD, None),
            P(CTX, None),
            P(CTX, HEAD),
            P(CTX, None),
            P(CTX, None),
            P(HEAD, None, None),
            P(HEAD, CTX),
        ),
        out_specs=(P(CTX + HEAD, None), P(CTX, HEAD)),
        check_vma=False,
    )
```

time: 568 us -> 216 us (0.38)
  the two profiles are of different devices: /device:TPU:1 before, /device:TPU:11 now
where the time goes in v1:
time: 216 us; the launch traced here: 215 us
  waiting for transfers between devices  56.9 us (26%)
  starting transfers between devices  49.7 us (23%)
  other arithmetic  25.5 us (12%)
  Pallas kernels  22.9 us (11%)
  blocking collectives  22.1 us (10%)
  local copies, waits for them, and re-layouts  19.2 us (9%)
  between operations  14.3 us (7%)
  matrix products  4.12 us (2%)
    all_to_all x1, waiting for transfers between devices, body(): pool = lax.all_to_all(wide, CTX, 0, 0)  41.7 us
    ppermute x5, starting transfers between devices, swap_core(): return lax.ppermute(value, 'c', [(0, 1), (1, 0)])  24.3 us
    all_to_all x1, blocking collectives, spread(): return lax.all_to_all(wide, axis, 0, 0)  22.1 us
    pallas_call x1, Pallas kernels, attend(): pl.pallas_call(attend_kernel, out_shape=jax.ShapeDtypeStruct((HEADS_DEV *...  15.4 us
    all_to_all x1, waiting for transfers between devices, body(): shares = lax.all_to_all(terms, HEAD, 0, 0)  12 us
    all_to_all x1, starting transfers between devices, body(): shares = lax.all_to_all(terms, HEAD, 0, 0)  10.7 us
    all_to_all x1, starting transfers between devices, body(): pool = lax.all_to_all(wide, CTX, 0, 0)  10.3 us
    pallas_call x1, Pallas kernels, index_part(): pl.pallas_call(index_kernel, out_shape=jax.ShapeDtypeStruct((16, NBLK * B...  7.46 us
  transfers between devices with their start and end apart: 10, of which 5 were waited for; matrix products, arithmetic and copies ran while one was open for 21% of the time, Pallas kernels for 11%

profile of v1, /device:TPU:11, one launch (start us, length us, event | category | flops | bytes accessed | tf_op | source)
XLA Modules:
  0.0 214.7 jit_solution(16873931585908403534)
XLA Ops:
  7.2 0.8 reshape.218
  8.0 0.9 pad_maximum_fusion.1
  8.9 0.1 broadcast_in_dim.44
  9.0 22.1 %all_to_all.20 = bf16[4,72,1024]{2,1,0:T(8,128)(2,1)S(1)} all-to-all(bf16[4,72,1024]{2,1,0:T(8,128)(2,1)S(1)} %broadcast_in_dim.44), channel_id=1, replica_groups=mesh['y'=8,'z'=4,'c'=2,'x'=4,'w'=2] {'z'}, dimensions={0} | all-to-all | bytes 1179648 | tf_op jit(solution)/shard_map/all_to_all | solution.py:122
  31.1 0.8 slice.96
  32.0 0.1 constant_dynamic-slice_fusion
  32.1 0.1 copy.31
  32.2 1.2 broadcast_in_dim.46
  33.4 10.3 %all-to-all-start.1 = ((bf16[64,16,576]{2,1,0:T(8,128)(2,1)}), bf16[64,16,576]{2,1,0:T(8,128)(2,1)S(1)}, u32[]{:S(2)}, u32[]{:S(2)}) async-start(bf16[64,16,576]{2,1,0:T(8,128)(2,1)} %bitcast.10), calls=%async_computation.1 | async-start | bytes 2621440 | tf_op jit(solution)/shard_map/all_to_all | solution.py:134
  43.7 2.3 %collective-permute-start.1 = (s32[16]{0:T(128)S(1)}, s32[16]{0:T(128)S(1)}, u32[]{:S(2)}, u32[]{:S(2)}) collective-permute-start(s32[16]{0:T(128)S(1)} %get-tuple-element.39), channel_id=1, source_target_pairs={{0,8},{8,0},{1,9},{9,1},{2,10},{10,2},{3,11},{11,3},{4,12},{12,4},... | collective-permute-start | bytes 200 | tf_op jit(solution)/shard_map/ppermute | solution.py:117
  46.0 0.8 collective-permute-done.1
  46.8 0.1 pad_add_fusion.1
  46.9 41.7 %all-to-all-done.1 = bf16[64,16,576]{2,1,0:T(8,128)(2,1)S(1)} async-done(((bf16[64,16,576]{2,1,0:T(8,128)(2,1)}), bf16[64,16,576]{2,1,0:T(8,128)(2,1)S(1)}, u32[]{:S(2)}, u32[]{:S(2)}) %all-to-all-start.1) | async-done | bytes 1179680 | tf_op jit(solution)/shard_map/all_to_all | solution.py:134
  88.6 0.7 gather_fusion
  89.3 0.1 fusion.19
  89.3 3.0 %collective-permute-start.2 = (bf16[256,576]{1,0:T(8,128)(2,1)S(1)}, bf16[256,576]{1,0:T(8,128)(2,1)S(1)}, u32[]{:S(2)}, u32[]{:S(2)}) collective-permute-start(bf16[256,576]{1,0:T(8,128)(2,1)S(1)} %bitcast.71), channel_id=1, source_target_pairs={{0,8},{8,0},{1,9},{9,1},{2,10},{10,2},{3,11},{11,3},{4,12},{12,4},... | collective-permute-start | bytes 884744 | tf_op jit(solution)/shard_map/ppermute | solution.py:117
  92.6 1.0 collective-permute-done.2
  93.6 0.1 pad_maximum_fusion
  93.6 0.2 copy.28
  93.9 1.6 broadcast_in_dim.48
  95.5 4.3 %all-to-all-start.2 = ((bf16[4,512,576]{1,2,0:T(8,128)(2,1)}), bf16[4,512,576]{1,2,0:T(8,128)(2,1)S(1)}, u32[]{:S(2)}, u32[]{:S(2)}) async-start(bf16[4,512,576]{1,2,0:T(8,128)(2,1)} %broadcast_in_dim.48), calls=%async_computation.2 | async-start | bytes 4718592 | tf_op jit(solution)/shard_map/all_to_all | solution.py:122
  100.0 0.2 compare_reduce_fusion.8
  100.2 0.7 fusion.20
  100.9 0.7 fusion.21
  101.6 4.4 %compare_select_fusion.4 = s32[2048,1]{0,1:T(1,128)S(1)} fusion(s32[]{:T(128)} %bitcast.41, s32[]{:T(128)} %bitcast.42, s32[]{:T(128)} %bitcast.43, s32[]{:T(128)} %bitcast.44, s32[]{:T(128)} %bitcast.45, s32[]{:T(128)} %bitcast.47, s32[]{:T(128)} %bitcast.46), kind=kLoop, calls=%fused_computation.27 | loop fusion | flops 69632 | bytes 8220 | tf_op jit(solution)/shard_map/gather | solution.py:156
  106.0 4.4 %compare_select_fusion.3 = s32[2048,1]{0,1:T(1,128)S(1)} fusion(s32[]{:T(128)} %bitcast.24, s32[]{:T(128)} %bitcast.25, s32[]{:T(128)} %bitcast.26, s32[]{:T(128)} %bitcast.27, s32[]{:T(128)} %bitcast.28, s32[]{:T(128)} %bitcast.30, s32[]{:T(128)} %bitcast.29), kind=kLoop, calls=%fused_computation.26 | loop fusion | flops 69632 | bytes 8220 | tf_op jit(solution)/shard_map/gather | solution.py:157
  110.5 5.5 %select_compare_fusion = pred[2048]{0:T(1024)(128)(4,1)S(1)} fusion(pred[2048]{0:T(1024)(128)(4,1)S(1)} %compare_reduce_fusion, pred[2048]{0:T(1024)(128)(4,1)S(1)} %compare_reduce_fusion.1, pred[2048]{0:T(1024)(128)(4,1)S(1)} %compare_reduce_fusion.2, pred[2048]{0:T(1024)(128)(4,1)S(1)} %compare_reduce_fusion.3, ...), kind=kLoop, calls=%fused_computation.61 | loop fusion | flops 20480 | bytes 28708 | tf_op jit(solution)/shard_map/ge | solution.py:157
  116.0 5.5 %fusion.7 = s32[2048]{0:T(1024)S(1)} fusion(pred[2048]{0:T(1024)(128)(4,1)S(1)} %compare_reduce_fusion, pred[2048]{0:T(1024)(128)(4,1)S(1)} %compare_reduce_fusion.1, pred[2048]{0:T(1024)(128)(4,1)S(1)} %compare_reduce_fusion.2, pred[2048]{0:T(1024)(128)(4,1)S(1)} %compare_reduce_fusion.3, pred[2048]{0:T(1024)(128)(4,1)S(1)} %compare_reduce_fusion.4, ...), kind=kLoop, calls=%fused_computation.55 | loop fusion | flops 98304 | bytes 34860 | tf_op jit(solution)/shard_map/add | solution.py:156
  121.6 0.7 reshape.219
  122.3 2.4 %copy.25 = bf16[128,4608]{0,1:T(8,128)(2,1)} copy(bf16[128,4608]{1,0:T(8,128)(2,1)} %param.11) | data formatting | bytes 2359296 | tf_op args[3]
  124.8 2.4 %copy.26 = bf16[8,128,576]{2,1,0:T(8,128)(2,1)} copy(bf16[8,128,576]{1,2,0:T(8,128)(2,1)} %bitcast.67) | data formatting | bytes 2359296 | tf_op jit(solution)/shard_map/transpose | solution.py:162
  127.2 2.3 %copy.30 = bf16[8,512,128]{1,2,0:T(8,128)(2,1)} copy(bf16[8,512,128]{2,1,0:T(8,128)(2,1)} %param.14) | data formatting | bytes 2097152 | tf_op args[6]
  129.5 2.4 %and_select_fusion.bias_ref = f32[2048,128]{1,0:T(8,128)} fusion(s32[128]{0:T(128)S(1)} %iota_add_fusion, s32[2048]{0:T(1024)S(1)} %fusion.7, pred[2048]{0:T(1024)(128)(4,1)S(1)} %select_compare_fusion), kind=kLoop, calls=%fused_computation.2 | loop fusion | flops 786432 | bytes 1059328 | tf_op jit(solution)/shard_map/jit(_where)/select_n | solution.py:160
  131.9 2.6 %copy.29 = bf16[4,512,576]{2,1,0:T(8,128)(2,1)} copy(bf16[4,512,576]{1,2,0:T(8,128)(2,1)S(1)} %all-to-all-done.2) | data formatting | bytes 4718592 | tf_op jit(solution)/shard_map/all_to_all | solution.py:122
  134.5 15.4 %attend.1 = bf16[1024,128]{1,0:T(8,128)(2,1)} custom-call(bf16[4,256,576]{2,1,0:T(8,128)(2,1)} %bitcast.66, bf16[2048,576]{1,0:T(8,128)(2,1)} %bitcast.65, f32[2048,128]{1,0:T(8,128)} %and_select_fusion.bias_ref, bf16[8,128,512]{2,1,0:T(8,128)(2,1)} %bitcast.68), custom_call_target="tpu_custom_call" | custom-call | tf_op jit(solution)/shard_map/attend/pallas_call | solution.py:61
  149.9 2.9 %collective-permute-start.3 = (bf16[1024,128]{1,0:T(8,128)(2,1)}, bf16[1024,128]{1,0:T(8,128)(2,1)S(1)}, u32[]{:S(2)}, u32[]{:S(2)}) collective-permute-start(bf16[1024,128]{1,0:T(8,128)(2,1)} %attend.1), channel_id=1, source_target_pairs={{0,8},{8,0},{1,9},{9,1},{2,10},{10,2},{3,11},{11,3},{4,12},{12,4},... | collective-permute-start | bytes 786440 | tf_op jit(solution)/shard_map/ppermute | solution.py:117
  152.8 1.4 collective-permute-done.3
  154.1 4.1 %convolution_convert_fusion = bf16[1792,256]{1,0:T(8,128)(2,1)} fusion(bf16[1792,1024]{1,0:T(8,128)(2,1)} %bitcast.79, bf16[1024,128]{1,0:T(8,128)(2,1)S(1)} %collective-permute-done.3, bf16[1024,128]{1,0:T(8,128)(2,1)} %attend.1), kind=kOutput, calls=%fused_computation.1 | convolution fusion | flops 941031424 | bytes 5111808 | tf_op jit(solution)/shard_map/dot_general | solution.py:168
  158.3 10.7 %all-to-all-start.3 = ((bf16[8,224,256]{2,1,0:T(8,128)(2,1)}), bf16[8,224,256]{2,1,0:T(8,128)(2,1)S(1)}, u32[]{:S(2)}, u32[]{:S(2)}) async-start(bf16[8,224,256]{2,1,0:T(8,128)(2,1)} %bitcast.50), calls=%async_computation.3 | async-start | bytes 1835008 | tf_op jit(solution)/shard_map/all_to_all | solution.py:170
  169.0 2.8 %collective-permute-start = (bf16[32,128,128]{2,1,0:T(8,128)(2,1)}, bf16[32,128,128]{2,1,0:T(8,128)(2,1)S(1)}, u32[]{:S(2)}, u32[]{:S(2)}) collective-permute-start(bf16[32,128,128]{2,1,0:T(8,128)(2,1)} %all-gather.3.cloned.1.call-done.own_ref), channel_id=1, source_target_pairs={{0,8},{8,0},{1,9},{9,1},{2,10},{10,2},{3,11},{11,3},{4,12},{12,4},... | collective-permute-start | bytes 3145736 | tf_op jit(solution)/shard_map/ppermute | solution.py:117
  171.9 0.7 copy_bitcast_fusion
  172.6 12.0 %all-to-all-done.3 = bf16[8,224,256]{2,1,0:T(8,128)(2,1)S(1)} async-done(((bf16[8,224,256]{2,1,0:T(8,128)(2,1)}), bf16[8,224,256]{2,1,0:T(8,128)(2,1)S(1)}, u32[]{:S(2)}, u32[]{:S(2)}) %all-to-all-start.3) | async-done | bytes 917536 | tf_op jit(solution)/shard_map/all_to_all | solution.py:170
  184.5 0.1 reduce_sum.12
  184.7 13.4 %collective-permute-start.4 = (bf16[224,128]{1,0:T(8,128)(2,1)S(1)}, bf16[224,128]{1,0:T(8,128)(2,1)S(1)}, u32[]{:S(2)}, u32[]{:S(2)}) collective-permute-start(bf16[224,128]{1,0:T(8,128)(2,1)S(1)} %slice.100), channel_id=1, source_target_pairs={{0,8},{8,0},{1,9},{9,1},{2,10},{10,2},{3,11},{11,3},{4,12},{12,4},... | collective-permute-start | bytes 172040 | tf_op jit(solution)/shard_map/ppermute | solution.py:117
  198.1 0.6 pad_add_fusion.place_ref
  198.7 1.0 copy-done.1
  199.7 7.5 %index_scores.1 = f32[16,8192]{1,0:T(8,128)} custom-call(s32[2]{0:T(128)} %pad_add_fusion.place_ref, bf16[512,128]{1,0:T(8,128)(2,1)} %bitcast.70, f32[16,32]{1,0:T(8,128)} %w_ref.1, bf16[32,128,128]{2,1,0:T(8,128)(2,1)} %all-gather.3.cloned.1.call-done.own_ref, bf16[32,128,128]{2,1,0:T(8,128)(2,1)} %copy-done.1), custom_call_target="tpu_custom_call" | custom-call | tf_op jit(solution)/shard_map/index_scores/pallas_call | solution.py:104
  207.2 0.7 pad_maximum_fusion.2
  (30 shorter events, 0.6 us)
Async XLA Ops:
  7.2 24.8 %copy-start = (bf16[128,576]{0,1:T(8,128)(2,1)S(1)}, bf16[128,576]{0,1:T(8,128)(2,1)}, u32[]{:S(2)}) copy-start(bf16[128,576]{0,1:T(8,128)(2,1)} %param.12) | copy-start | bytes 442372
  7.2 147.0 %all-gather.5.cloned.1.call-start = ((), (), s32[]{:S(2)}) async-start(), calls=%async_computation.5 | async-start | bytes 4128768 | tf_op jit(solution)/shard_map/all_gather | solution.py:139
  33.4 10.3 %copy-start.3 = (s32[1,16]{1,0:T(1,128)S(1)}, s32[1,16]{1,0:T(1,128)}, u32[]{:S(2)}) copy-start(s32[1,16]{1,0:T(1,128)} %param.13) | copy-start | bytes 196
  33.4 55.2 %all-to-all-start.1 = ((bf16[64,16,576]{2,1,0:T(8,128)(2,1)}), bf16[64,16,576]{2,1,0:T(8,128)(2,1)S(1)}, u32[]{:S(2)}, u32[]{:S(2)}) async-start(bf16[64,16,576]{2,1,0:T(8,128)(2,1)} %bitcast.10), calls=%async_computation.1 | async-start | bytes 2621440 | tf_op jit(solution)/shard_map/all_to_all | solution.py:134
  43.7 3.1 %collective-permute-start.1 = (s32[16]{0:T(128)S(1)}, s32[16]{0:T(128)S(1)}, u32[]{:S(2)}, u32[]{:S(2)}) collective-permute-start(s32[16]{0:T(128)S(1)} %get-tuple-element.39), channel_id=1, source_target_pairs={{0,8},{8,0},{1,9},{9,1},{2,10},{10,2},{3,11},{11,3},{4,12},{12,4},... | collective-permute-start | bytes 200 | tf_op jit(solution)/shard_map/ppermute | solution.py:117
  89.3 4.2 %collective-permute-start.2 = (bf16[256,576]{1,0:T(8,128)(2,1)S(1)}, bf16[256,576]{1,0:T(8,128)(2,1)S(1)}, u32[]{:S(2)}, u32[]{:S(2)}) collective-permute-start(bf16[256,576]{1,0:T(8,128)(2,1)S(1)} %bitcast.71), channel_id=1, source_target_pairs={{0,8},{8,0},{1,9},{9,1},{2,10},{10,2},{3,11},{11,3},{4,12},{12,4},... | collective-permute-start | bytes 884744 | tf_op jit(solution)/shard_map/ppermute | solution.py:117
  95.5 36.4 %all-to-all-start.2 = ((bf16[4,512,576]{1,2,0:T(8,128)(2,1)}), bf16[4,512,576]{1,2,0:T(8,128)(2,1)S(1)}, u32[]{:S(2)}, u32[]{:S(2)}) async-start(bf16[4,512,576]{1,2,0:T(8,128)(2,1)} %broadcast_in_dim.48), calls=%async_computation.2 | async-start | bytes 4718592 | tf_op jit(solution)/shard_map/all_to_all | solution.py:122
  99.8 69.3 %all-gather.3.cloned.1.call-start = ((), (), s32[]{:S(2)}) async-start(), calls=%async_computation.4 | async-start | bytes 1179648 | tf_op jit(solution)/shard_map/all_gather | solution.py:142
  149.9 4.2 %collective-permute-start.3 = (bf16[1024,128]{1,0:T(8,128)(2,1)}, bf16[1024,128]{1,0:T(8,128)(2,1)S(1)}, u32[]{:S(2)}, u32[]{:S(2)}) collective-permute-start(bf16[1024,128]{1,0:T(8,128)(2,1)} %attend.1), channel_id=1, source_target_pairs={{0,8},{8,0},{1,9},{9,1},{2,10},{10,2},{3,11},{11,3},{4,12},{12,4},... | collective-permute-start | bytes 786440 | tf_op jit(solution)/shard_map/ppermute | solution.py:117
  158.3 13.6 %copy-start.2 = (bf16[16,4096]{1,0:T(8,128)(2,1)S(1)}, bf16[16,4096]{1,0:T(8,128)(2,1)}, u32[]{:S(2)}) copy-start(bf16[16,4096]{1,0:T(8,128)(2,1)} %param.8) | copy-start | bytes 393220
  158.3 26.2 %all-to-all-start.3 = ((bf16[8,224,256]{2,1,0:T(8,128)(2,1)}), bf16[8,224,256]{2,1,0:T(8,128)(2,1)S(1)}, u32[]{:S(2)}, u32[]{:S(2)}) async-start(bf16[8,224,256]{2,1,0:T(8,128)(2,1)} %bitcast.50), calls=%async_computation.3 | async-start | bytes 1835008 | tf_op jit(solution)/shard_map/all_to_all | solution.py:170
  169.0 29.7 %collective-permute-start = (bf16[32,128,128]{2,1,0:T(8,128)(2,1)}, bf16[32,128,128]{2,1,0:T(8,128)(2,1)S(1)}, u32[]{:S(2)}, u32[]{:S(2)}) collective-permute-start(bf16[32,128,128]{2,1,0:T(8,128)(2,1)} %all-gather.3.cloned.1.call-done.own_ref), channel_id=1, source_target_pairs={{0,8},{8,0},{1,9},{9,1},{2,10},{10,2},{3,11},{11,3},{4,12},{12,4},... | collective-permute-start | bytes 3145736 | tf_op jit(solution)/shard_map/ppermute | solution.py:117
  184.7 22.5 %collective-permute-start.4 = (bf16[224,128]{1,0:T(8,128)(2,1)S(1)}, bf16[224,128]{1,0:T(8,128)(2,1)S(1)}, u32[]{:S(2)}, u32[]{:S(2)}) collective-permute-start(bf16[224,128]{1,0:T(8,128)(2,1)S(1)} %slice.100), channel_id=1, source_target_pairs={{0,8},{8,0},{1,9},{9,1},{2,10},{10,2},{3,11},{11,3},{4,12},{12,4},... | collective-permute-start | bytes 172040 | tf_op jit(solution)/shard_map/ppermute | solution.py:117
  198.7 1.0 copy-start.1
Sparse Core Ops, SparseCore 0:
  32.1 76.8 all-gather.4
  122.4 36.5 all-gather.2

commit v2 on v1

v2 whole, which is shorter than its diff:
```python
import functools

import jax
import jax.numpy as jnp
from jax import lax
from jax.experimental import pallas as pl
from jax.experimental.pallas import tpu as pltpu
from jax.sharding import Mesh
from jax.sharding import PartitionSpec as P

TOK_DEV = 128
HEADS_DEV = 8
KV_RANK = 512
LAT = 576
V_DIM = 128
IDX_HEADS = 32
IDX_DIM = 128
BLOCK = 128
TOPK = 16
NBLK = 64
COLS = 56
NY, NZ, NC, NX, NW = 8, 4, 2, 4, 2

CTX = ("y", "z", "c")
HEAD = ("x", "w")
LOG2E = 1.4426950408889634
SCORE_SCALE = 192.0 ** (-0.5) * LOG2E
MASKED = -1e30
VMEM_LIMIT = 56 * 1024 * 1024


def attend_kernel(count, first, last, *refs):
    place_ref, q_ref = refs[:2]
    kv_refs = refs[2 : 2 + count]
    refs = refs[2 + count :]
    if not first:
        max_in, total_in, sum_in = refs[:3]
        refs = refs[3:]
    if last:
        up_ref, out_ref = refs[:2]
        refs = refs[2:]
    else:
        max_out, total_out, sum_out = refs[:3]
        refs = refs[3:]
    bias_ref, vt_ref = refs
    keys = jnp.concatenate([ref[...] for ref in kv_refs], axis=0)
    n_keys = keys.shape[0]
    vt_ref[...] = keys[:, :KV_RANK].T
    row = lax.broadcasted_iota(jnp.int32, (16, BLOCK), 0)
    query = place_ref[TOPK] + lax.broadcasted_iota(jnp.int32, (16, BLOCK), 1)
    for group in range(n_keys // 16):
        part, slot = divmod(group, TOPK)
        entry = place_ref[slot]
        start = jnp.where(entry < 0, 2 * NBLK, entry) * BLOCK + place_ref[TOPK + 1 + part]
        seen = jnp.where(start + row <= query, 0.0, MASKED)
        bias_ref[group * 16 : (group + 1) * 16, :BLOCK] = seen
        bias_ref[group * 16 : (group + 1) * 16, BLOCK:] = seen
    for pair in range(HEADS_DEV // 2):
        scores = lax.dot_general(
            keys, q_ref[pair], (((1,), (1,)), ((), ())), preferred_element_type=jnp.float32
        )
        scores = scores + bias_ref[...]
        row_max = jnp.max(scores, axis=0, keepdims=True)
        if not first:
            row_max = jnp.maximum(row_max, max_in[pair])
            keep = jnp.exp2((max_in[pair] - row_max) * SCORE_SCALE)
        expo = jnp.exp2((scores - row_max) * SCORE_SCALE)
        total = jnp.sum(expo, axis=0, keepdims=True)
        lat_sum = lax.dot_general(
            vt_ref[...],
            expo.astype(jnp.bfloat16),
            (((1,), (0,)), ((), ())),
            preferred_element_type=jnp.float32,
        )
        if not first:
            total = total + total_in[pair] * keep
            lat_sum = lat_sum + sum_in[pair] * keep
        if not last:
            max_out[pair] = row_max
            total_out[pair] = total
            sum_out[pair] = lat_sum
            continue
        lat_out = (lat_sum / total).astype(jnp.bfloat16)
        for half in range(2):
            head = 2 * pair + half
            values = lax.dot_general(
                up_ref[head],
                lat_out[:, half * BLOCK : (half + 1) * BLOCK],
                (((1,), (0,)), ((), ())),
                preferred_element_type=jnp.float32,
            )
            out_ref[head * V_DIM : (head + 1) * V_DIM, :] = values.astype(jnp.bfloat16)


def attend(place, queries, parts, state, up_t):
    pairs = HEADS_DEV // 2
    n_keys = sum(part.shape[0] for part in parts)
    stat = jax.ShapeDtypeStruct((pairs, 1, 2 * BLOCK), jnp.float32)
    out = (stat, stat, jax.ShapeDtypeStruct((pairs, KV_RANK, 2 * BLOCK), jnp.float32))
    last = up_t is not None
    operands = [place, queries, *parts, *(state or ())]
    if last:
        operands.append(up_t)
        out = jax.ShapeDtypeStruct((HEADS_DEV * V_DIM, BLOCK), jnp.bfloat16)
    vmem = pl.BlockSpec(memory_space=pltpu.VMEM)
    rows = HEADS_DEV * BLOCK
    return pl.pallas_call(
        functools.partial(attend_kernel, len(parts), state is None, last),
        out_shape=out,
        in_specs=[pl.BlockSpec(memory_space=pltpu.SMEM)] + [vmem] * (len(operands) - 1),
        out_specs=vmem if last else (vmem,) * 3,
        scratch_shapes=[
            pltpu.VMEM((n_keys, 2 * BLOCK), jnp.float32),
            pltpu.VMEM((KV_RANK, n_keys), jnp.bfloat16),
        ],
        compiler_params=pltpu.CompilerParams(vmem_limit_bytes=VMEM_LIMIT),
        cost_estimate=pl.CostEstimate(
            flops=2 * rows * n_keys * (LAT + KV_RANK) * 2,
            bytes_accessed=4 * rows * KV_RANK * 2,
            transcendentals=rows * n_keys,
        ),
        name="attend",
    )(*operands)


def index_kernel(place_ref, query_ref, w_ref, own_ref, other_ref, out_ref, wb_ref, q_ref):
    core = place_ref[0]
    first_row = place_ref[1]
    rows = 16
    for head in range(IDX_HEADS):
        q_ref[head * rows : (head + 1) * rows, :] = query_ref[
            :, head * IDX_DIM : (head + 1) * IDX_DIM
        ]
        wb_ref[head * rows : (head + 1) * rows, :] = jnp.broadcast_to(
            w_ref[:, head : head + 1] * (IDX_DIM ** (-0.5)), (rows, BLOCK)
        )
    row_pos = first_row + lax.broadcasted_iota(jnp.int32, (rows, BLOCK), 0)
    lane = lax.broadcasted_iota(jnp.int32, (rows, BLOCK), 1)

    def chunk(keys_ref, parity, step):
        keys = keys_ref[pl.ds(step * 2, 2)].reshape(2 * BLOCK, IDX_DIM)
        dots = lax.dot_general(
            q_ref[...], keys, (((1,), (1,)), ((), ())), preferred_element_type=jnp.float32
        )
        for half in range(2):
            part = dots[:, half * BLOCK : (half + 1) * BLOCK]
            active = jnp.maximum(part, 0.0) * wb_ref[...]
            summed = jnp.sum(active.reshape(IDX_HEADS, rows, BLOCK), axis=0)
            start = pl.multiple_of(((step * 2 + half) * 2 + parity) * BLOCK, BLOCK)
            out_ref[:, pl.ds(start, BLOCK)] = jnp.where(start + lane <= row_pos, summed, 0.0)

    def one(step, carry):
        chunk(own_ref, core, step)
        chunk(other_ref, 1 - core, step)
        return carry

    lax.fori_loop(0, NBLK // 4, one, 0)


def index_part(place, query, weight, own, other):
    return pl.pallas_call(
        index_kernel,
        out_shape=jax.ShapeDtypeStruct((16, NBLK * BLOCK), jnp.float32),
        in_specs=[pl.BlockSpec(memory_space=pltpu.SMEM)]
        + [pl.BlockSpec(memory_space=pltpu.VMEM)] * 4,
        out_specs=pl.BlockSpec(memory_space=pltpu.VMEM),
        scratch_shapes=[
            pltpu.VMEM((IDX_HEADS * 16, BLOCK), jnp.float32),
            pltpu.VMEM((IDX_HEADS * 16, IDX_DIM), jnp.bfloat16),
        ],
        compiler_params=pltpu.CompilerParams(vmem_limit_bytes=VMEM_LIMIT),
        cost_estimate=pl.CostEstimate(
            flops=40_000_000_000, bytes_accessed=100 << 20, transcendentals=0
        ),
        name="index_scores",
    )(place, query, weight, own, other)


def prepare_kernel(lq_ref, up_ref, q_ref, up_t_ref):
    for head in range(HEADS_DEV):
        pair, half = divmod(head, 2)
        q_ref[pair, half * BLOCK : (half + 1) * BLOCK, :] = lq_ref[:, head * LAT : (head + 1) * LAT]
        up_t_ref[head] = up_ref[head].T


def prepare(latent_query, value_up):
    vmem = pl.BlockSpec(memory_space=pltpu.VMEM)
    shapes = [(HEADS_DEV // 2, 2 * BLOCK, LAT), (HEADS_DEV, V_DIM, KV_RANK)]
    return pl.pallas_call(
        prepare_kernel,
        out_shape=[jax.ShapeDtypeStruct(shape, jnp.bfloat16) for shape in shapes],
        in_specs=[vmem] * 2,
        out_specs=[vmem] * 2,
        compiler_params=pltpu.CompilerParams(vmem_limit_bytes=VMEM_LIMIT),
        cost_estimate=pl.CostEstimate(
            flops=80_000_000_000, bytes_accessed=200 << 20, transcendentals=0
        ),
        name="prepare",
    )(latent_query, value_up)


def arrange_kernel(z_ref, *refs):
    near, (w_ref, keys_ref) = refs[:NZ], refs[NZ:]
    for step in range(NZ):
        at = z_ref[0] ^ step
        w_ref[at] = near[step][16:, :]
        for block in range(8):
            keys_ref[at, block * 16 : (block + 1) * 16, :] = near[step][
                :16, block * BLOCK : (block + 1) * BLOCK
            ]


def arrange(z, near):
    vmem = pl.BlockSpec(memory_space=pltpu.VMEM)
    shapes = [(NZ, COLS, 1024), (NZ, BLOCK, IDX_DIM)]
    return pl.pallas_call(
        arrange_kernel,
        out_shape=[jax.ShapeDtypeStruct(shape, jnp.bfloat16) for shape in shapes],
        in_specs=[pl.BlockSpec(memory_space=pltpu.SMEM)] + [vmem] * NZ,
        out_specs=[vmem] * 2,
        compiler_params=pltpu.CompilerParams(vmem_limit_bytes=VMEM_LIMIT),
        name="arrange",
    )(z, *near)


def swap_core(value):
    return lax.ppermute(value, "c", [(0, 1), (1, 0)])


def spread(value, axis, count):
    wide = jnp.broadcast_to(value[None], (count,) + value.shape)
    return lax.all_to_all(wide, axis, 0, 0)


def body(
    index_query, index_weight, index_key, latent_query, latent, block_lists, value_up, out_weight
):
    y, z, core, x, w = (lax.axis_index(name) for name in ("y", "z", "c", "x", "w"))
    ctx_pos = (y * NZ + z) * NC + core
    head_pos = x * NW + w

    own = lax.dynamic_slice_in_dim(latent, x * 32, 32, 0).reshape(1, NC, 16, LAT)
    wide = jnp.broadcast_to(own, (NY * NZ, NC, 16, LAT)).reshape(NBLK, 16, LAT)

    key_rows = jnp.moveaxis(index_key.reshape(8, 16, IDX_DIM), 0, 1).reshape(16, 1024)
    packed = jnp.concatenate([key_rows, out_weight.T], axis=0)
    packed, wide = lax.optimization_barrier((packed, wide))
    near = [packed] + [
        lax.ppermute(packed, "z", [(at, at ^ step) for at in range(NZ)]) for step in range(1, NZ)
    ]
    pool = lax.all_to_all(wide, CTX, 0, 0)
    listed = block_lists[0]
    safe = jnp.maximum(listed, 0)
    both = jnp.concatenate([safe, swap_core(safe)])
    queries, up_t = prepare(latent_query, value_up)
    w_z, keys_z = arrange(z.reshape(1), near)
    w_all = lax.all_gather(w_z, "y", axis=0, tiled=True).reshape(NY * NZ * COLS, 1024)
    pool, queries, up_t, both = lax.optimization_barrier((pool, queries, up_t, both))

    picked = jnp.take(pool, both, axis=0, mode="clip").reshape(2, TOPK * 16, LAT)
    mine = jnp.concatenate([picked[0], swap_core(picked[1])], axis=0)
    up = [(at, (at + 1) % NX) for at in range(NX)]
    down = [(at, (at - 1) % NX) for at in range(NX)]
    left = lax.ppermute(mine, "x", up)
    right = lax.ppermute(mine, "x", down)

    def place(*xs):
        offsets = [((x + step) % NX) * 32 + 16 * (core ^ half) for step, half in xs]
        return jnp.concatenate([listed, jnp.stack([ctx_pos * BLOCK] + offsets)])

    places = (
        place((0, 0), (0, 1)),
        place((3, 0), (3, 1), (1, 0), (1, 1)),
        place((2, 0), (2, 1)),
    )
    state = attend(places[0], queries, [mine], None, None)
    left, right, state, keys_z = lax.optimization_barrier((left, right, state, keys_z))
    far_a = lax.ppermute(left[:256], "x", up)
    far_b = lax.ppermute(right[256:], "x", down)
    keys_own = spread(keys_z, "y", NY).reshape(NY * NZ, BLOCK, IDX_DIM)
    state = attend(places[1], queries, [left, right], state, None)
    far_a, far_b, state, keys_own = lax.optimization_barrier((far_a, far_b, state, keys_own))
    keys_other = swap_core(keys_own)
    values = attend(places[2], queries, [far_a, far_b], state, up_t)

    values, keys_other = lax.optimization_barrier((values, keys_other))

    both_values = jnp.concatenate([values, swap_core(values)], axis=1)
    terms = jnp.dot(w_all, both_values, preferred_element_type=jnp.float32).astype(jnp.bfloat16)
    terms = terms.reshape(NY, NZ * COLS, 2 * BLOCK)
    shares = lax.all_to_all(terms, HEAD, 0, 0)
    first_row = ctx_pos * TOK_DEV + head_pos * 16
    index_scores = index_part(
        jnp.stack([core, first_row]), index_query, index_weight, keys_own, keys_other
    )
    shares, index_scores = lax.optimization_barrier((shares, index_scores))
    summed = jnp.sum(shares.astype(jnp.float32), axis=0).astype(jnp.bfloat16)
    kept = summed[:, :BLOCK].reshape(NZ, COLS, BLOCK)
    other = swap_core(summed[:, BLOCK:]).reshape(NZ, COLS, BLOCK)
    first = jnp.where(core == 0, kept, other)
    second = jnp.where(core == 0, other, kept)
    attn_out = jnp.stack([first, second], axis=1).reshape(NZ * NC * COLS, BLOCK).T

    return index_scores, attn_out


def solution(mesh):
    fine = Mesh(mesh.devices.reshape(NY, NZ, NC, NX, NW), ("y", "z", "c", "x", "w"))
    return jax.shard_map(
        body,
        mesh=fine,
        in_specs=(
            P(CTX + HEAD, None),
            P(CTX + HEAD, None),
            P(CTX, None),
            P(CTX, HEAD),
            P(CTX, None),
            P(CTX, None),
            P(HEAD, None, None),
            P(HEAD, CTX),
        ),
        out_specs=(P(CTX + HEAD, None), P(CTX, HEAD)),
        check_vma=False,
    )
```

time: 216 us -> 198 us (0.917)
  the two profiles are of different devices: /device:TPU:11 before, /device:TPU:3 now
where the time goes in v2:
time: 198 us; the launch traced here: 197 us
  starting transfers between devices  73.4 us (37%)
  waiting for transfers between devices  59.2 us (30%)
  Pallas kernels  34.8 us (18%)
  between operations  14.4 us (7%)
  local copies, waits for them, and re-layouts  7.95 us (4%)
  matrix products  4.13 us (2%)
  other arithmetic  3.06 us (2%)
    all_to_all x1, waiting for transfers between devices, body(): pool = lax.all_to_all(wide, CTX, 0, 0)  28 us
    ppermute x5, starting transfers between devices, swap_core(): return lax.ppermute(value, 'c', [(0, 1), (1, 0)])  23.8 us
    pallas_call x3, Pallas kernels, attend(): pl.pallas_call(functools.partial(attend_kernel, len(parts), state is None...  21.8 us
    all_to_all x1, waiting for transfers between devices, spread(): return lax.all_to_all(wide, axis, 0, 0)  12.2 us
    all_to_all x1, starting transfers between devices, body(): pool = lax.all_to_all(wide, CTX, 0, 0)  12.2 us
    ppermute x3, starting transfers between devices, body(): lax.ppermute(packed, 'z', [(at, at ^ step) for at in range(NZ)])  11.8 us
    all_to_all x1, starting transfers between devices, body(): shares = lax.all_to_all(terms, HEAD, 0, 0)  11.2 us
    all_to_all x1, waiting for transfers between devices, body(): shares = lax.all_to_all(terms, HEAD, 0, 0)  8.4 us
  transfers between devices with their start and end apart: 16, of which 8 were waited for; matrix products, arithmetic and copies ran while one was open for 2% of the time, Pallas kernels for 18%

profile of v2, /device:TPU:3, one launch (start us, length us, event | category | flops | bytes accessed | tf_op | source)
XLA Modules:
  0.0 197.0 jit_solution(12124784227558341167)
XLA Ops:
  7.2 0.9 copy-done
  8.1 0.1 constant_dynamic-slice_fusion
  8.2 0.1 copy.21
  8.3 0.8 copy.13
  9.1 0.9 pad_maximum_fusion.1.refs_0_
  10.0 1.2 broadcast_in_dim.18
  11.2 4.1 %collective-permute-start = (bf16[72,1024]{1,0:T(8,128)(2,1)S(1)}, bf16[72,1024]{1,0:T(8,128)(2,1)S(1)}, u32[]{:S(2)}, u32[]{:S(2)}) collective-permute-start(bf16[72,1024]{1,0:T(8,128)(2,1)S(1)} %pad_maximum_fusion.1.refs_0_), channel_id=1, source_target_pairs={{0,16},{16,0},{32,48},{48,32},{1,17},{17,1},{33,49},{49,33},{2,18}... | collective-permute-start | bytes 442376 | tf_op jit(solution)/shard_map/ppermute | solution.py:249
  15.3 5.8 %collective-permute-start.1 = (bf16[72,1024]{1,0:T(8,128)(2,1)S(1)}, bf16[72,1024]{1,0:T(8,128)(2,1)S(1)}, u32[]{:S(2)}, u32[]{:S(2)}) collective-permute-start(bf16[72,1024]{1,0:T(8,128)(2,1)S(1)} %pad_maximum_fusion.1.refs_0_), channel_id=1, source_target_pairs={{0,32},{16,48},{32,0},{48,16},{1,33},{17,49},{33,1},{49,17},{2,34}... | collective-permute-start | bytes 442376 | tf_op jit(solution)/shard_map/ppermute | solution.py:249
  21.2 1.9 collective-permute-start.2
  23.1 12.2 %all-to-all-start = ((bf16[64,16,576]{2,1,0:T(8,128)(2,1)}), bf16[64,16,576]{2,1,0:T(8,128)(2,1)S(1)}, u32[]{:S(2)}, u32[]{:S(2)}) async-start(bf16[64,16,576]{2,1,0:T(8,128)(2,1)} %bitcast.5), calls=%async_computation | async-start | bytes 2621440 | tf_op jit(solution)/shard_map/all_to_all | solution.py:251
  35.3 2.4 %collective-permute-start.3 = (s32[16]{0:T(128)S(1)}, s32[16]{0:T(128)S(1)}, u32[]{:S(2)}, u32[]{:S(2)}) collective-permute-start(s32[16]{0:T(128)S(1)} %broadcast_maximum_fusion), channel_id=1, source_target_pairs={{0,8},{8,0},{1,9},{9,1},{2,10},{10,2},{3,11},{11,3},{4,12},{12,4},... | collective-permute-start | bytes 200 | tf_op jit(solution)/shard_map/ppermute | solution.py:227
  37.8 0.6 copy-done.6
  38.5 2.0 arrange.1
  40.4 3.6 %prepare.1 = (bf16[4,256,576]{2,1,0:T(8,128)(2,1)}, bf16[8,128,512]{2,1,0:T(8,128)(2,1)}) custom-call(bf16[128,4608]{1,0:T(8,128)(2,1)} %lq_ref.1, bf16[8,512,128]{2,1,0:T(8,128)(2,1)} %up_ref.1), custom_call_target="tpu_custom_call" | custom-call | flops 80000000000 | bytes 209715200 | tf_op jit(solution)/shard_map/prepare/pallas_call | solution.py:189
  44.1 28.0 %all-to-all-done = bf16[64,16,576]{2,1,0:T(8,128)(2,1)S(1)} async-done(((bf16[64,16,576]{2,1,0:T(8,128)(2,1)}), bf16[64,16,576]{2,1,0:T(8,128)(2,1)S(1)}, u32[]{:S(2)}, u32[]{:S(2)}) %all-to-all-start) | async-done | bytes 1179680 | tf_op jit(solution)/shard_map/all_to_all | solution.py:251
  72.1 0.7 gather_fusion
  72.9 4.0 %collective-permute-start.4 = (bf16[256,576]{1,0:T(8,128)(2,1)S(1)}, bf16[256,576]{1,0:T(8,128)(2,1)S(1)}, u32[]{:S(2)}, u32[]{:S(2)}) collective-permute-start(bf16[256,576]{1,0:T(8,128)(2,1)S(1)} %bitcast.37), channel_id=1, source_target_pairs={{0,8},{8,0},{1,9},{9,1},{2,10},{10,2},{3,11},{11,3},{4,12},{12,4},... | collective-permute-start | bytes 884744 | tf_op jit(solution)/shard_map/ppermute | solution.py:227
  76.9 1.2 collective-permute-done.4
  78.2 0.2 copy.15
  78.5 3.1 %collective-permute-start.5 = (bf16[512,576]{0,1:T(8,128)(2,1)S(1)}, bf16[512,576]{0,1:T(8,128)(2,1)S(1)}, u32[]{:S(2)}, u32[]{:S(2)}) collective-permute-start(bf16[512,576]{0,1:T(8,128)(2,1)S(1)} %copy.15), channel_id=1, source_target_pairs={{0,2},{2,4},{4,6},{6,0},{1,3},{3,5},{5,7},{7,1},{8,10},{10,12},{12... | collective-permute-start | bytes 1769480 | tf_op jit(solution)/shard_map/ppermute | solution.py:264
  81.6 2.2 %collective-permute-start.6 = (bf16[512,576]{0,1:T(8,128)(2,1)S(1)}, bf16[512,576]{0,1:T(8,128)(2,1)S(1)}, u32[]{:S(2)}, u32[]{:S(2)}) collective-permute-start(bf16[512,576]{0,1:T(8,128)(2,1)S(1)} %copy.15), channel_id=1, source_target_pairs={{0,6},{2,0},{4,2},{6,4},{1,7},{3,1},{5,3},{7,5},{8,14},{10,8},{12,... | collective-permute-start | bytes 1769480 | tf_op jit(solution)/shard_map/ppermute | solution.py:265
  83.8 0.6 pad_add_fusion.3
  84.4 6.1 %attend.3 = (f32[4,1,256]{2,1,0:T(1,128)}, f32[4,1,256]{2,1,0:T(1,128)}, f32[4,512,256]{2,1,0:T(8,128)}) custom-call(s32[19]{0:T(128)} %get-tuple-element.70.refs_0_, bf16[4,256,576]{2,1,0:T(8,128)(2,1)} %get-tuple-element.39.refs_1_, bf16[512,576]{1,0:T(8,128)(2,1)} %copy-done.1), custom_call_target="tpu_custom_call" | custom-call | flops 2281701376 | bytes 4194304 | tf_op jit(solution)/shard_map/attend/pallas_call | solution.py:107
  90.5 4.5 %collective-permute-done.5 = bf16[512,576]{0,1:T(8,128)(2,1)S(1)} collective-permute-done((bf16[512,576]{0,1:T(8,128)(2,1)S(1)}, bf16[512,576]{0,1:T(8,128)(2,1)S(1)}, u32[]{:S(2)}, u32[]{:S(2)}) %collective-permute-start.5) | collective-permute-done | bytes 589856 | tf_op jit(solution)/shard_map/ppermute | solution.py:264
  95.0 2.8 %collective-permute-done.6 = bf16[512,576]{0,1:T(8,128)(2,1)S(1)} collective-permute-done((bf16[512,576]{0,1:T(8,128)(2,1)S(1)}, bf16[512,576]{0,1:T(8,128)(2,1)S(1)}, u32[]{:S(2)}, u32[]{:S(2)}) %collective-permute-start.6) | collective-permute-done | bytes 589856 | tf_op jit(solution)/shard_map/ppermute | solution.py:265
  97.8 1.2 broadcast_in_dim.20
  99.0 3.8 %all-to-all-start.1 = ((bf16[8,4,128,128]{3,2,1,0:T(8,128)(2,1)}), bf16[8,4,128,128]{3,2,1,0:T(8,128)(2,1)S(1)}, u32[]{:S(2)}, u32[]{:S(2)}) async-start(bf16[8,4,128,128]{3,2,1,0:T(8,128)(2,1)} %broadcast_in_dim.20), calls=%async_computation.1 | async-start | bytes 2097152 | tf_op jit(solution)/shard_map/all_to_all | solution.py:232
  102.9 0.6 concatenate.26.refs_0_
  103.4 0.3 copy.17.refs_2_
  103.7 0.3 copy.18.refs_3_
  104.1 2.8 %collective-permute-start.7 = (bf16[256,576]{1,0:T(8,128)(2,1)S(1)}, bf16[256,576]{1,0:T(8,128)(2,1)S(1)}, u32[]{:S(2)}, u32[]{:S(2)}) collective-permute-start(bf16[256,576]{1,0:T(8,128)(2,1)S(1)} %slice.30), channel_id=1, source_target_pairs={{0,2},{2,4},{4,6},{6,0},{1,3},{3,5},{5,7},{7,1},{8,10},{10,12},{12... | collective-permute-start | bytes 884744 | tf_op jit(solution)/shard_map/ppermute | solution.py:278
  107.0 2.4 %collective-permute-start.8 = (bf16[256,576]{1,0:T(8,128)(2,1)S(1)}, bf16[256,576]{1,0:T(8,128)(2,1)}, u32[]{:S(2)}, u32[]{:S(2)}) collective-permute-start(bf16[256,576]{1,0:T(8,128)(2,1)S(1)} %slice.31), channel_id=1, source_target_pairs={{0,6},{2,0},{4,2},{6,4},{1,7},{3,1},{5,3},{7,5},{8,14},{10,8},{12,... | collective-permute-start | bytes 884744 | tf_op jit(solution)/shard_map/ppermute | solution.py:279
  109.4 9.6 %attend.4 = (f32[4,1,256]{2,1,0:T(1,128)}, f32[4,1,256]{2,1,0:T(1,128)}, f32[4,512,256]{2,1,0:T(8,128)}) custom-call(s32[21]{0:T(128)} %concatenate.26.refs_0_, bf16[4,256,576]{2,1,0:T(8,128)(2,1)} %get-tuple-element.39.refs_1_, bf16[512,576]{1,0:T(8,128)(2,1)} %copy-done.2, bf16[512,576]{1,0:T(8,128)(2,1)} %copy-done.3, ...), custom_call_target="tpu_custom_call" | custom-call | flops 4563402752 | bytes 4194304 | tf_op jit(solution)/shard_map/attend/pallas_call | solution.py:107
  119.1 0.7 copy-done.12
  119.8 12.2 %all-to-all-done.1 = bf16[8,4,128,128]{3,2,1,0:T(8,128)(2,1)S(1)} async-done(((bf16[8,4,128,128]{3,2,1,0:T(8,128)(2,1)}), bf16[8,4,128,128]{3,2,1,0:T(8,128)(2,1)S(1)}, u32[]{:S(2)}, u32[]{:S(2)}) %all-to-all-start.1) | async-done | bytes 1048608 | tf_op jit(solution)/shard_map/all_to_all | solution.py:232
  132.0 2.6 %collective-permute-start.9 = (bf16[32,128,128]{2,1,0:T(8,128)(2,1)S(1)}, bf16[32,128,128]{2,1,0:T(8,128)(2,1)S(1)}, u32[]{:S(2)}, u32[]{:S(2)}) collective-permute-start(bf16[32,128,128]{2,1,0:T(8,128)(2,1)S(1)} %bitcast.35), channel_id=1, source_target_pairs={{0,8},{8,0},{1,9},{9,1},{2,10},{10,2},{3,11},{11,3},{4,12},{12,4},... | collective-permute-start | bytes 3145736 | tf_op jit(solution)/shard_map/ppermute | solution.py:227
  134.6 6.1 %attend.5 = bf16[1024,128]{1,0:T(8,128)(2,1)} custom-call(s32[19]{0:T(128)} %get-tuple-element.71.refs_0_, bf16[4,256,576]{2,1,0:T(8,128)(2,1)} %get-tuple-element.39.refs_1_, bf16[256,576]{1,0:T(8,128)(2,1)} %copy-done.12, bf16[256,576]{1,0:T(8,128)(2,1)} %collective-permute-done.8.refs_3_, f32[4,1,256]{2,1,0:T(1,128)} %get-tuple-element.57.refs_4_, ...), custom_call_target="tpu_custom_call" | custom-call | flops 2281701376 | bytes 4194304 | tf_op jit(solution)/shard_map/attend/pallas_call | solution.py:107
  140.7 1.9 collective-permute-start.10
  142.7 0.6 pad_add_fusion.4.place_ref
  143.3 1.1 collective-permute-done.10
  144.4 4.1 %convolution_convert_fusion = bf16[1792,256]{1,0:T(8,128)(2,1)} fusion(bf16[1792,1024]{1,0:T(8,128)(2,1)} %bitcast.48, bf16[1024,128]{1,0:T(8,128)(2,1)S(1)} %collective-permute-done.10, bf16[1024,128]{1,0:T(8,128)(2,1)} %attend.5), kind=kOutput, calls=%fused_computation.1 | convolution fusion | flops 941031424 | bytes 5111808 | tf_op jit(solution)/shard_map/dot_general | solution.py:289
  148.5 11.2 %all-to-all-start.2 = ((bf16[8,224,256]{2,1,0:T(8,128)(2,1)}), bf16[8,224,256]{2,1,0:T(8,128)(2,1)S(1)}, u32[]{:S(2)}, u32[]{:S(2)}) async-start(bf16[8,224,256]{2,1,0:T(8,128)(2,1)} %bitcast.20), calls=%async_computation.2 | async-start | bytes 1835008 | tf_op jit(solution)/shard_map/all_to_all | solution.py:291
  159.7 7.5 %index_scores.1 = f32[16,8192]{1,0:T(8,128)} custom-call(s32[2]{0:T(128)} %pad_add_fusion.4.place_ref, bf16[16,4096]{1,0:T(8,128)(2,1)} %query_ref.1, f32[16,32]{1,0:T(8,128)} %w_ref.1, bf16[32,128,128]{2,1,0:T(8,128)(2,1)} %bitcast.36, bf16[32,128,128]{2,1,0:T(8,128)(2,1)} %copy-done.11), custom_call_target="tpu_custom_call" | custom-call | flops 40000000000 | bytes 104857600 | tf_op jit(solution)/shard_map/index_scores/pallas_call | solution.py:161
  167.1 8.4 %all-to-all-done.2 = bf16[8,224,256]{2,1,0:T(8,128)(2,1)S(1)} async-done(((bf16[8,224,256]{2,1,0:T(8,128)(2,1)}), bf16[8,224,256]{2,1,0:T(8,128)(2,1)S(1)}, u32[]{:S(2)}, u32[]{:S(2)}) %all-to-all-start.2) | async-done | bytes 917536 | tf_op jit(solution)/shard_map/all_to_all | solution.py:291
  175.5 0.1 reduce_sum.12
  175.7 12.9 %collective-permute-start.11 = (bf16[224,128]{1,0:T(8,128)(2,1)S(1)}, bf16[224,128]{1,0:T(8,128)(2,1)S(1)}, u32[]{:S(2)}, u32[]{:S(2)}) collective-permute-start(bf16[224,128]{1,0:T(8,128)(2,1)S(1)} %slice.33), channel_id=1, source_target_pairs={{0,8},{8,0},{1,9},{9,1},{2,10},{10,2},{3,11},{11,3},{4,12},{12,4},... | collective-permute-start | bytes 172040 | tf_op jit(solution)/shard_map/ppermute | solution.py:227
  188.6 0.9 collective-permute-done.11
  189.5 0.7 pad_maximum_fusion.2
  (43 shorter events, 0.5 us)
Async XLA Ops:
  7.2 0.9 copy-start
  10.0 13.1 %copy-start.5 = (bf16[72,1024]{1,0:T(8,128)(2,1)}, bf16[72,1024]{1,0:T(8,128)(2,1)S(1)}, u32[]{:S(2)}) copy-start(bf16[72,1024]{1,0:T(8,128)(2,1)S(1)} %pad_maximum_fusion.1.refs_0_) | copy-start | bytes 442372
  11.2 24.1 %copy-start.10 = (s32[1,16]{1,0:T(1,128)S(1)}, s32[1,16]{1,0:T(1,128)}, u32[]{:S(2)}) copy-start(s32[1,16]{1,0:T(1,128)} %param.13) | copy-start | bytes 196
  11.2 26.5 %collective-permute-start = (bf16[72,1024]{1,0:T(8,128)(2,1)S(1)}, bf16[72,1024]{1,0:T(8,128)(2,1)S(1)}, u32[]{:S(2)}, u32[]{:S(2)}) collective-permute-start(bf16[72,1024]{1,0:T(8,128)(2,1)S(1)} %pad_maximum_fusion.1.refs_0_), channel_id=1, source_target_pairs={{0,16},{16,0},{32,48},{48,32},{1,17},{17,1},{33,49},{49,33},{2,18}... | collective-permute-start | bytes 442376 | tf_op jit(solution)/shard_map/ppermute | solution.py:249
  15.3 22.4 %collective-permute-start.1 = (bf16[72,1024]{1,0:T(8,128)(2,1)S(1)}, bf16[72,1024]{1,0:T(8,128)(2,1)S(1)}, u32[]{:S(2)}, u32[]{:S(2)}) collective-permute-start(bf16[72,1024]{1,0:T(8,128)(2,1)S(1)} %pad_maximum_fusion.1.refs_0_), channel_id=1, source_target_pairs={{0,32},{16,48},{32,0},{48,16},{1,33},{17,49},{33,1},{49,17},{2,34}... | collective-permute-start | bytes 442376 | tf_op jit(solution)/shard_map/ppermute | solution.py:249
  21.2 16.6 %collective-permute-start.2 = (bf16[72,1024]{1,0:T(8,128)(2,1)S(1)}, bf16[72,1024]{1,0:T(8,128)(2,1)S(1)}, u32[]{:S(2)}, u32[]{:S(2)}) collective-permute-start(bf16[72,1024]{1,0:T(8,128)(2,1)S(1)} %pad_maximum_fusion.1.refs_0_), channel_id=1, source_target_pairs={{0,48},{16,32},{32,16},{48,0},{1,49},{17,33},{33,17},{49,1},{2,50}... | collective-permute-start | bytes 442376 | tf_op jit(solution)/shard_map/ppermute | solution.py:249
  23.1 49.0 %all-to-all-start = ((bf16[64,16,576]{2,1,0:T(8,128)(2,1)}), bf16[64,16,576]{2,1,0:T(8,128)(2,1)S(1)}, u32[]{:S(2)}, u32[]{:S(2)}) async-start(bf16[64,16,576]{2,1,0:T(8,128)(2,1)} %bitcast.5), calls=%async_computation | async-start | bytes 2621440 | tf_op jit(solution)/shard_map/all_to_all | solution.py:251
  35.2 109.1 %all-gather.2.cloned.1.call-start = ((), (), s32[]{:S(2)}) async-start(), calls=%async_computation.3 | async-start | bytes 4128768 | tf_op jit(solution)/shard_map/all_gather | solution.py:257
  35.3 8.7 %collective-permute-start.3 = (s32[16]{0:T(128)S(1)}, s32[16]{0:T(128)S(1)}, u32[]{:S(2)}, u32[]{:S(2)}) collective-permute-start(s32[16]{0:T(128)S(1)} %broadcast_maximum_fusion), channel_id=1, source_target_pairs={{0,8},{8,0},{1,9},{9,1},{2,10},{10,2},{3,11},{11,3},{4,12},{12,4},... | collective-permute-start | bytes 200 | tf_op jit(solution)/shard_map/ppermute | solution.py:227
  37.7 0.7 copy-start.6
  37.7 0.7 copy-start.7
  37.7 0.7 copy-start.8
  72.9 5.3 %collective-permute-start.4 = (bf16[256,576]{1,0:T(8,128)(2,1)S(1)}, bf16[256,576]{1,0:T(8,128)(2,1)S(1)}, u32[]{:S(2)}, u32[]{:S(2)}) collective-permute-start(bf16[256,576]{1,0:T(8,128)(2,1)S(1)} %bitcast.37), channel_id=1, source_target_pairs={{0,8},{8,0},{1,9},{9,1},{2,10},{10,2},{3,11},{11,3},{4,12},{12,4},... | collective-permute-start | bytes 884744 | tf_op jit(solution)/shard_map/ppermute | solution.py:227
  78.2 6.2 %copy-start.1 = (bf16[512,576]{1,0:T(8,128)(2,1)}, bf16[512,576]{1,0:T(8,128)(2,1)S(1)}, u32[]{:S(2)}) copy-start(bf16[512,576]{1,0:T(8,128)(2,1)S(1)} %pad_maximum_fusion.refs_2_) | copy-start | bytes 1769476
  78.5 16.5 %collective-permute-start.5 = (bf16[512,576]{0,1:T(8,128)(2,1)S(1)}, bf16[512,576]{0,1:T(8,128)(2,1)S(1)}, u32[]{:S(2)}, u32[]{:S(2)}) collective-permute-start(bf16[512,576]{0,1:T(8,128)(2,1)S(1)} %copy.15), channel_id=1, source_target_pairs={{0,2},{2,4},{4,6},{6,0},{1,3},{3,5},{5,7},{7,1},{8,10},{10,12},{12... | collective-permute-start | bytes 1769480 | tf_op jit(solution)/shard_map/ppermute | solution.py:264
  81.6 16.2 %collective-permute-start.6 = (bf16[512,576]{0,1:T(8,128)(2,1)S(1)}, bf16[512,576]{0,1:T(8,128)(2,1)S(1)}, u32[]{:S(2)}, u32[]{:S(2)}) collective-permute-start(bf16[512,576]{0,1:T(8,128)(2,1)S(1)} %copy.15), channel_id=1, source_target_pairs={{0,6},{2,0},{4,2},{6,4},{1,7},{3,1},{5,3},{7,5},{8,14},{10,8},{12,... | collective-permute-start | bytes 1769480 | tf_op jit(solution)/shard_map/ppermute | solution.py:265
  84.4 13.4 %copy-start.9 = (bf16[4,128,128]{2,1,0:T(8,128)(2,1)S(1)}, bf16[4,128,128]{2,1,0:T(8,128)(2,1)}, u32[]{:S(2)}) copy-start(bf16[4,128,128]{2,1,0:T(8,128)(2,1)} %get-tuple-element.54) | copy-start | bytes 393220
  99.0 33.0 %all-to-all-start.1 = ((bf16[8,4,128,128]{3,2,1,0:T(8,128)(2,1)}), bf16[8,4,128,128]{3,2,1,0:T(8,128)(2,1)S(1)}, u32[]{:S(2)}, u32[]{:S(2)}) async-start(bf16[8,4,128,128]{3,2,1,0:T(8,128)(2,1)} %broadcast_in_dim.20), calls=%async_computation.1 | async-start | bytes 2097152 | tf_op jit(solution)/shard_map/all_to_all | solution.py:232
  103.7 5.7 %copy-start.2 = (bf16[512,576]{1,0:T(8,128)(2,1)}, bf16[512,576]{1,0:T(8,128)(2,1)S(1)}, u32[]{:S(2)}) copy-start(bf16[512,576]{1,0:T(8,128)(2,1)S(1)} %copy.17.refs_2_) | copy-start | bytes 1769476
  104.0 5.4 %copy-start.3 = (bf16[512,576]{1,0:T(8,128)(2,1)}, bf16[512,576]{1,0:T(8,128)(2,1)S(1)}, u32[]{:S(2)}) copy-start(bf16[512,576]{1,0:T(8,128)(2,1)S(1)} %copy.18.refs_3_) | copy-start | bytes 1769476
  104.1 15.0 %collective-permute-start.7 = (bf16[256,576]{1,0:T(8,128)(2,1)S(1)}, bf16[256,576]{1,0:T(8,128)(2,1)S(1)}, u32[]{:S(2)}, u32[]{:S(2)}) collective-permute-start(bf16[256,576]{1,0:T(8,128)(2,1)S(1)} %slice.30), channel_id=1, source_target_pairs={{0,2},{2,4},{4,6},{6,0},{1,3},{3,5},{5,7},{7,1},{8,10},{10,12},{12... | collective-permute-start | bytes 884744 | tf_op jit(solution)/shard_map/ppermute | solution.py:278
  107.0 12.9 %collective-permute-start.8 = (bf16[256,576]{1,0:T(8,128)(2,1)S(1)}, bf16[256,576]{1,0:T(8,128)(2,1)}, u32[]{:S(2)}, u32[]{:S(2)}) collective-permute-start(bf16[256,576]{1,0:T(8,128)(2,1)S(1)} %slice.31), channel_id=1, source_target_pairs={{0,6},{2,0},{4,2},{6,4},{1,7},{3,1},{5,3},{7,5},{8,14},{10,8},{12,... | collective-permute-start | bytes 884744 | tf_op jit(solution)/shard_map/ppermute | solution.py:279
  119.1 0.7 copy-start.12
  132.0 8.7 %copy-start.4 = (bf16[8,4,128,128]{3,2,1,0:T(8,128)(2,1)}, bf16[8,4,128,128]{3,2,1,0:T(8,128)(2,1)S(1)}, u32[]{:S(2)}) copy-start(bf16[8,4,128,128]{3,2,1,0:T(8,128)(2,1)S(1)} %all-to-all-done.1) | copy-start | bytes 3145732
  132.0 8.7 %collective-permute-start.9 = (bf16[32,128,128]{2,1,0:T(8,128)(2,1)S(1)}, bf16[32,128,128]{2,1,0:T(8,128)(2,1)S(1)}, u32[]{:S(2)}, u32[]{:S(2)}) collective-permute-start(bf16[32,128,128]{2,1,0:T(8,128)(2,1)S(1)} %bitcast.35), channel_id=1, source_target_pairs={{0,8},{8,0},{1,9},{9,1},{2,10},{10,2},{3,11},{11,3},{4,12},{12,4},... | collective-permute-start | bytes 3145736 | tf_op jit(solution)/shard_map/ppermute | solution.py:227
  140.7 7.8 %copy-start.11 = (bf16[32,128,128]{2,1,0:T(8,128)(2,1)}, bf16[32,128,128]{2,1,0:T(8,128)(2,1)S(1)}, u32[]{:S(2)}) copy-start(bf16[32,128,128]{2,1,0:T(8,128)(2,1)S(1)} %collective-permute-done.9.other_ref) | copy-start | bytes 3145732
  140.7 3.6 %collective-permute-start.10 = (bf16[1024,128]{1,0:T(8,128)(2,1)}, bf16[1024,128]{1,0:T(8,128)(2,1)S(1)}, u32[]{:S(2)}, u32[]{:S(2)}) collective-permute-start(bf16[1024,128]{1,0:T(8,128)(2,1)} %attend.5), channel_id=1, source_target_pairs={{0,8},{8,0},{1,9},{9,1},{2,10},{10,2},{3,11},{11,3},{4,12},{12,4},... | collective-permute-start | bytes 786440 | tf_op jit(solution)/shard_map/ppermute | solution.py:227
  148.5 27.1 %all-to-all-start.2 = ((bf16[8,224,256]{2,1,0:T(8,128)(2,1)}), bf16[8,224,256]{2,1,0:T(8,128)(2,1)S(1)}, u32[]{:S(2)}, u32[]{:S(2)}) async-start(bf16[8,224,256]{2,1,0:T(8,128)(2,1)} %bitcast.20), calls=%async_computation.2 | async-start | bytes 1835008 | tf_op jit(solution)/shard_map/all_to_all | solution.py:291
  175.7 13.8 %collective-permute-start.11 = (bf16[224,128]{1,0:T(8,128)(2,1)S(1)}, bf16[224,128]{1,0:T(8,128)(2,1)S(1)}, u32[]{:S(2)}, u32[]{:S(2)}) collective-permute-start(bf16[224,128]{1,0:T(8,128)(2,1)S(1)} %slice.33), channel_id=1, source_target_pairs={{0,8},{8,0},{1,9},{9,1},{2,10},{10,2},{3,11},{11,3},{4,12},{12,4},... | collective-permute-start | bytes 172040 | tf_op jit(solution)/shard_map/ppermute | solution.py:227
Sparse Core Ops, SparseCore 0:
  40.6 61.6 all-gather.1

commit v3 on v2

--- a/solution.py
+++ b/solution.py
@@ -115,7 +115,7 @@
         ],
         compiler_params=pltpu.CompilerParams(vmem_limit_bytes=VMEM_LIMIT),
         cost_estimate=pl.CostEstimate(
-            flops=2 * rows * n_keys * (LAT + KV_RANK) * 2,
+            flops=40_000_000_000,
             bytes_accessed=4 * rows * KV_RANK * 2,
             transcendentals=rows * n_keys,
         ),
@@ -193,7 +193,7 @@
         out_specs=[vmem] * 2,
         compiler_params=pltpu.CompilerParams(vmem_limit_bytes=VMEM_LIMIT),
         cost_estimate=pl.CostEstimate(
-            flops=80_000_000_000, bytes_accessed=200 << 20, transcendentals=0
+            flops=20_000_000_000, bytes_accessed=20_000_000, transcendentals=0
         ),
         name="prepare",
     )(latent_query, value_up)
@@ -244,7 +244,6 @@
 
     key_rows = jnp.moveaxis(index_key.reshape(8, 16, IDX_DIM), 0, 1).reshape(16, 1024)
     packed = jnp.concatenate([key_rows, out_weight.T], axis=0)
-    packed, wide = lax.optimization_barrier((packed, wide))
     near = [packed] + [
         lax.ppermute(packed, "z", [(at, at ^ step) for at in range(NZ)]) for step in range(1, NZ)
     ]
@@ -255,7 +254,9 @@
     queries, up_t = prepare(latent_query, value_up)
     w_z, keys_z = arrange(z.reshape(1), near)
     w_all = lax.all_gather(w_z, "y", axis=0, tiled=True).reshape(NY * NZ * COLS, 1024)
-    pool, queries, up_t, both = lax.optimization_barrier((pool, queries, up_t, both))
+    pool, queries, up_t, both, keys_z = lax.optimization_barrier(
+        (pool, queries, up_t, both, keys_z)
+    )
 
     picked = jnp.take(pool, both, axis=0, mode="clip").reshape(2, TOPK * 16, LAT)
     mine = jnp.concatenate([picked[0], swap_core(picked[1])], axis=0)
@@ -277,22 +278,21 @@
     left, right, state, keys_z = lax.optimization_barrier((left, right, state, keys_z))
     far_a = lax.ppermute(left[:256], "x", up)
     far_b = lax.ppermute(right[256:], "x", down)
-    keys_own = spread(keys_z, "y", NY).reshape(NY * NZ, BLOCK, IDX_DIM)
+    keys_own = lax.all_gather(keys_z, "y", axis=0, tiled=True)
     state = attend(places[1], queries, [left, right], state, None)
-    far_a, far_b, state, keys_own = lax.optimization_barrier((far_a, far_b, state, keys_own))
-    keys_other = swap_core(keys_own)
+    far_a, far_b, state = lax.optimization_barrier((far_a, far_b, state))
     values = attend(places[2], queries, [far_a, far_b], state, up_t)
-
-    values, keys_other = lax.optimization_barrier((values, keys_other))
 
     both_values = jnp.concatenate([values, swap_core(values)], axis=1)
     terms = jnp.dot(w_all, both_values, preferred_element_type=jnp.float32).astype(jnp.bfloat16)
     terms = terms.reshape(NY, NZ * COLS, 2 * BLOCK)
-    shares = lax.all_to_all(terms, HEAD, 0, 0)
     first_row = ctx_pos * TOK_DEV + head_pos * 16
+    terms, keys_own = lax.optimization_barrier((terms, keys_own))
+    keys_other = swap_core(keys_own)
     index_scores = index_part(
         jnp.stack([core, first_row]), index_query, index_weight, keys_own, keys_other
     )
+    shares = lax.all_to_all(terms, HEAD, 0, 0)
     shares, index_scores = lax.optimization_barrier((shares, index_scores))
     summed = jnp.sum(shares.astype(jnp.float32), axis=0).astype(jnp.bfloat16)
     kept = summed[:, :BLOCK].reshape(NZ, COLS, BLOCK)

time: 198 us -> 216 us (1.091)
  the two profiles are of different devices: /device:TPU:3 before, /device:TPU:65 now
where the time goes in v3:
time: 216 us
  waiting for transfers between devices  90.7 us (42%)
  starting transfers between devices  62.1 us (29%)
  Pallas kernels  35 us (16%)
  between operations  14.5 us (7%)
  local copies, waits for them, and re-layouts  7.05 us (3%)
  matrix products  4.12 us (2%)
  other arithmetic  2.21 us (1%)
    ppermute x3, waiting for transfers between devices, body(): lax.ppermute(packed, 'z', [(at, at ^ step) for at in range(NZ)])  31.1 us
    all_gather x1, waiting for transfers between devices, body(): keys_own = lax.all_gather(keys_z, 'y', axis=0, tiled=True)  30.8 us
    pallas_call x3, Pallas kernels, attend(): pl.pallas_call(functools.partial(attend_kernel, len(parts), state is None...  21.9 us
    all_to_all x1, waiting for transfers between devices, body(): shares = lax.all_to_all(terms, HEAD, 0, 0)  19.7 us
    ppermute x5, starting transfers between devices, swap_core(): return lax.ppermute(value, 'c', [(0, 1), (1, 0)])  18.7 us
    all_to_all x1, starting transfers between devices, body(): pool = lax.all_to_all(wide, CTX, 0, 0)  13.2 us
    all_to_all x1, starting transfers between devices, body(): shares = lax.all_to_all(terms, HEAD, 0, 0)  8.61 us
    ppermute x3, starting transfers between devices, body(): lax.ppermute(packed, 'z', [(at, at ^ step) for at in range(NZ)])  8.37 us
  transfers between devices with their start and end apart: 16, of which 9 were waited for; matrix products, arithmetic and copies ran while one was open for 4% of the time, Pallas kernels for 16%

profile of v3, /device:TPU:65, one launch (start us, length us, event | category | flops | bytes accessed | tf_op | source)
XLA Modules:
  0.0 215.6 jit_solution(17692958449765845563)
XLA Ops:
  7.2 0.9 copy-done
  8.1 0.1 constant_dynamic-slice_fusion
  8.2 0.1 copy.21
  8.3 1.2 broadcast_in_dim.12
  9.5 13.2 %all-to-all-start = ((bf16[64,16,576]{2,1,0:T(8,128)(2,1)}), bf16[64,16,576]{2,1,0:T(8,128)(2,1)S(1)}, u32[]{:S(2)}, u32[]{:S(2)}) async-start(bf16[64,16,576]{2,1,0:T(8,128)(2,1)} %bitcast.10), calls=%async_computation | async-start | bytes 2621440 | tf_op jit(solution)/shard_map/all_to_all | solution.py:250
  22.8 2.0 collective-permute-start
  24.8 4.2 %collective-permute-start.1 = (bf16[72,1024]{1,0:T(8,128)(2,1)S(1)}, bf16[72,1024]{1,0:T(8,128)(2,1)S(1)}, u32[]{:S(2)}, u32[]{:S(2)}) collective-permute-start(bf16[72,1024]{1,0:T(8,128)(2,1)S(1)} %pad_maximum_fusion.1.refs_0_), channel_id=1, source_target_pairs={{0,32},{16,48},{32,0},{48,16},{1,33},{17,49},{33,1},{49,17},{2,34}... | collective-permute-start | bytes 442376 | tf_op jit(solution)/shard_map/ppermute | solution.py:248
  29.0 2.2 %collective-permute-start.2 = (bf16[72,1024]{1,0:T(8,128)(2,1)S(1)}, bf16[72,1024]{1,0:T(8,128)(2,1)S(1)}, u32[]{:S(2)}, u32[]{:S(2)}) collective-permute-start(bf16[72,1024]{1,0:T(8,128)(2,1)S(1)} %pad_maximum_fusion.1.refs_0_), channel_id=1, source_target_pairs={{0,48},{16,32},{32,16},{48,0},{1,49},{17,33},{33,17},{49,1},{2,50}... | collective-permute-start | bytes 442376 | tf_op jit(solution)/shard_map/ppermute | solution.py:248
  31.3 3.1 %collective-permute-start.3 = (s32[16]{0:T(128)S(1)}, s32[16]{0:T(128)S(1)}, u32[]{:S(2)}, u32[]{:S(2)}) collective-permute-start(s32[16]{0:T(128)S(1)} %broadcast_maximum_fusion), channel_id=1, source_target_pairs={{0,8},{8,0},{1,9},{9,1},{2,10},{10,2},{3,11},{11,3},{4,12},{12,4},... | collective-permute-start | bytes 200 | tf_op jit(solution)/shard_map/ppermute | solution.py:227
  34.4 4.6 %collective-permute-done.refs_1_ = bf16[72,1024]{1,0:T(8,128)(2,1)S(1)} collective-permute-done((bf16[72,1024]{1,0:T(8,128)(2,1)S(1)}, bf16[72,1024]{1,0:T(8,128)(2,1)S(1)}, u32[]{:S(2)}, u32[]{:S(2)}) %collective-permute-start) | collective-permute-done | bytes 147488 | tf_op jit(solution)/shard_map/ppermute | solution.py:248
  39.0 21.5 %collective-permute-done.1.refs_2_ = bf16[72,1024]{1,0:T(8,128)(2,1)S(1)} collective-permute-done((bf16[72,1024]{1,0:T(8,128)(2,1)S(1)}, bf16[72,1024]{1,0:T(8,128)(2,1)S(1)}, u32[]{:S(2)}, u32[]{:S(2)}) %collective-permute-start.1) | collective-permute-done | bytes 147488 | tf_op jit(solution)/shard_map/ppermute | solution.py:248
  60.5 5.0 %collective-permute-done.2.refs_3_ = bf16[72,1024]{1,0:T(8,128)(2,1)S(1)} collective-permute-done((bf16[72,1024]{1,0:T(8,128)(2,1)S(1)}, bf16[72,1024]{1,0:T(8,128)(2,1)S(1)}, u32[]{:S(2)}, u32[]{:S(2)}) %collective-permute-start.2) | collective-permute-done | bytes 147488 | tf_op jit(solution)/shard_map/ppermute | solution.py:248
  65.5 0.6 copy-done.7
  66.2 2.0 arrange.1
  68.2 3.6 %prepare.1 = (bf16[4,256,576]{2,1,0:T(8,128)(2,1)}, bf16[8,128,512]{2,1,0:T(8,128)(2,1)}) custom-call(bf16[128,4608]{1,0:T(8,128)(2,1)} %lq_ref.1, bf16[8,512,128]{2,1,0:T(8,128)(2,1)} %up_ref.1), custom_call_target="tpu_custom_call" | custom-call | flops 20000000000 | bytes 20000000 | tf_op jit(solution)/shard_map/prepare/pallas_call | solution.py:189
  71.8 0.1 pad_add_fusion.2
  71.9 0.7 gather_fusion
  72.6 2.5 %collective-permute-start.4 = (bf16[256,576]{1,0:T(8,128)(2,1)S(1)}, bf16[256,576]{1,0:T(8,128)(2,1)S(1)}, u32[]{:S(2)}, u32[]{:S(2)}) collective-permute-start(bf16[256,576]{1,0:T(8,128)(2,1)S(1)} %bitcast.34), channel_id=1, source_target_pairs={{0,8},{8,0},{1,9},{9,1},{2,10},{10,2},{3,11},{11,3},{4,12},{12,4},... | collective-permute-start | bytes 884744 | tf_op jit(solution)/shard_map/ppermute | solution.py:227
  75.2 0.6 concatenate.26.refs_0_
  75.8 0.6 pad_add_fusion.3
  76.5 0.2 copy.15
  76.8 3.1 %collective-permute-start.5 = (bf16[512,576]{0,1:T(8,128)(2,1)S(1)}, bf16[512,576]{0,1:T(8,128)(2,1)S(1)}, u32[]{:S(2)}, u32[]{:S(2)}) collective-permute-start(bf16[512,576]{0,1:T(8,128)(2,1)S(1)} %copy.15), channel_id=1, source_target_pairs={{0,2},{2,4},{4,6},{6,0},{1,3},{3,5},{5,7},{7,1},{8,10},{10,12},{12... | collective-permute-start | bytes 1769480 | tf_op jit(solution)/shard_map/ppermute | solution.py:265
  79.9 3.4 %collective-permute-start.6 = (bf16[512,576]{0,1:T(8,128)(2,1)S(1)}, bf16[512,576]{0,1:T(8,128)(2,1)S(1)}, u32[]{:S(2)}, u32[]{:S(2)}) collective-permute-start(bf16[512,576]{0,1:T(8,128)(2,1)S(1)} %copy.15), channel_id=1, source_target_pairs={{0,6},{2,0},{4,2},{6,4},{1,7},{3,1},{5,3},{7,5},{8,14},{10,8},{12,... | collective-permute-start | bytes 1769480 | tf_op jit(solution)/shard_map/ppermute | solution.py:266
  83.3 6.2 %attend.3 = (f32[4,1,256]{2,1,0:T(1,128)}, f32[4,1,256]{2,1,0:T(1,128)}, f32[4,512,256]{2,1,0:T(8,128)}) custom-call(s32[19]{0:T(128)} %get-tuple-element.66.refs_0_, bf16[4,256,576]{2,1,0:T(8,128)(2,1)} %get-tuple-element.36.refs_1_, bf16[512,576]{1,0:T(8,128)(2,1)} %copy-done.1), custom_call_target="tpu_custom_call" | custom-call | flops 40000000000 | bytes 4194304 | tf_op jit(solution)/shard_map/attend/pallas_call | solution.py:107
  89.5 5.1 %collective-permute-done.5 = bf16[512,576]{0,1:T(8,128)(2,1)S(1)} collective-permute-done((bf16[512,576]{0,1:T(8,128)(2,1)S(1)}, bf16[512,576]{0,1:T(8,128)(2,1)S(1)}, u32[]{:S(2)}, u32[]{:S(2)}) %collective-permute-start.5) | collective-permute-done | bytes 589856 | tf_op jit(solution)/shard_map/ppermute | solution.py:265
  94.6 1.6 collective-permute-done.6
  96.2 0.3 copy.17.refs_2_
  96.5 0.3 copy.18.refs_3_
  96.9 3.1 %collective-permute-start.7 = (bf16[256,576]{1,0:T(8,128)(2,1)S(1)}, bf16[256,576]{1,0:T(8,128)(2,1)S(1)}, u32[]{:S(2)}, u32[]{:S(2)}) collective-permute-start(bf16[256,576]{1,0:T(8,128)(2,1)S(1)} %slice.30), channel_id=1, source_target_pairs={{0,2},{2,4},{4,6},{6,0},{1,3},{3,5},{5,7},{7,1},{8,10},{10,12},{12... | collective-permute-start | bytes 884744 | tf_op jit(solution)/shard_map/ppermute | solution.py:279
  100.0 3.6 %collective-permute-start.8 = (bf16[256,576]{1,0:T(8,128)(2,1)S(1)}, bf16[256,576]{1,0:T(8,128)(2,1)S(1)}, u32[]{:S(2)}, u32[]{:S(2)}) collective-permute-start(bf16[256,576]{1,0:T(8,128)(2,1)S(1)} %slice.31), channel_id=1, source_target_pairs={{0,6},{2,0},{4,2},{6,4},{1,7},{3,1},{5,3},{7,5},{8,14},{10,8},{12,... | collective-permute-start | bytes 884744 | tf_op jit(solution)/shard_map/ppermute | solution.py:280
  103.7 9.7 %attend.4 = (f32[4,1,256]{2,1,0:T(1,128)}, f32[4,1,256]{2,1,0:T(1,128)}, f32[4,512,256]{2,1,0:T(8,128)}) custom-call(s32[21]{0:T(128)} %concatenate.26.refs_0_, bf16[4,256,576]{2,1,0:T(8,128)(2,1)} %get-tuple-element.36.refs_1_, bf16[512,576]{1,0:T(8,128)(2,1)} %copy-done.2, bf16[512,576]{1,0:T(8,128)(2,1)} %copy-done.3, ...), custom_call_target="tpu_custom_call" | custom-call | flops 40000000000 | bytes 4194304 | tf_op jit(solution)/shard_map/attend/pallas_call | solution.py:107
  113.4 0.7 copy-done.12
  114.1 0.1 copy-done.13
  114.2 6.1 %attend.5 = bf16[1024,128]{1,0:T(8,128)(2,1)} custom-call(s32[19]{0:T(128)} %get-tuple-element.67.refs_0_, bf16[4,256,576]{2,1,0:T(8,128)(2,1)} %get-tuple-element.36.refs_1_, bf16[256,576]{1,0:T(8,128)(2,1)} %copy-done.12, bf16[256,576]{1,0:T(8,128)(2,1)} %copy-done.13, f32[4,1,256]{2,1,0:T(1,128)} %get-tuple-element.53.refs_4_, ...), custom_call_target="tpu_custom_call" | custom-call | flops 40000000000 | bytes 4194304 | tf_op jit(solution)/shard_map/attend/pallas_call | solution.py:107
  120.3 3.8 %collective-permute-start.9 = (bf16[1024,128]{1,0:T(8,128)(2,1)}, bf16[1024,128]{1,0:T(8,128)(2,1)S(1)}, u32[]{:S(2)}, u32[]{:S(2)}) collective-permute-start(bf16[1024,128]{1,0:T(8,128)(2,1)} %attend.5), channel_id=1, source_target_pairs={{0,8},{8,0},{1,9},{9,1},{2,10},{10,2},{3,11},{11,3},{4,12},{12,4},... | collective-permute-start | bytes 786440 | tf_op jit(solution)/shard_map/ppermute | solution.py:227
  124.1 1.4 collective-permute-done.9
  125.4 4.1 %convolution_convert_fusion = bf16[1792,256]{1,0:T(8,128)(2,1)} fusion(bf16[1792,1024]{1,0:T(8,128)(2,1)} %bitcast.45, bf16[1024,128]{1,0:T(8,128)(2,1)S(1)} %collective-permute-done.9, bf16[1024,128]{1,0:T(8,128)(2,1)} %attend.5), kind=kOutput, calls=%fused_computation.1 | convolution fusion | flops 941031424 | bytes 5111808 | tf_op jit(solution)/shard_map/dot_general | solution.py:287
  129.6 30.8 %all-gather.5.cloned.1.call-done.own_ref = bf16[32,128,128]{2,1,0:T(8,128)(2,1)} async-done(((bf16[4,128,128]{2,1,0:T(8,128)(2,1)}), bf16[32,128,128]{2,1,0:T(8,128)(2,1)}) %all-gather.5.cloned.1.call-update) | async-done | bytes 1048592 | tf_op jit(solution)/shard_map/all_gather | solution.py:281
  160.4 6.5 %collective-permute-start.10 = (bf16[32,128,128]{2,1,0:T(8,128)(2,1)}, bf16[32,128,128]{2,1,0:T(8,128)(2,1)S(1)}, u32[]{:S(2)}, u32[]{:S(2)}) collective-permute-start(bf16[32,128,128]{2,1,0:T(8,128)(2,1)} %all-gather.5.cloned.1.call-done.own_ref), channel_id=1, source_target_pairs={{0,8},{8,0},{1,9},{9,1},{2,10},{10,2},{3,11},{11,3},{4,12},{12,4},... | collective-permute-start | bytes 3145736 | tf_op jit(solution)/shard_map/ppermute | solution.py:227
  166.9 0.6 pad_add_fusion.4.place_ref
  167.5 8.6 %all-to-all-start.1 = ((bf16[8,224,256]{2,1,0:T(8,128)(2,1)}), bf16[8,224,256]{2,1,0:T(8,128)(2,1)S(1)}, u32[]{:S(2)}, u32[]{:S(2)}) async-start(bf16[8,224,256]{2,1,0:T(8,128)(2,1)} %bitcast.19), calls=%async_computation.1 | async-start | bytes 1835008 | tf_op jit(solution)/shard_map/all_to_all | solution.py:295
  176.1 1.0 copy-done.11
  177.1 7.5 %index_scores.1 = f32[16,8192]{1,0:T(8,128)} custom-call(s32[2]{0:T(128)} %pad_add_fusion.4.place_ref, bf16[16,4096]{1,0:T(8,128)(2,1)} %query_ref.1, f32[16,32]{1,0:T(8,128)} %w_ref.1, bf16[32,128,128]{2,1,0:T(8,128)(2,1)} %all-gather.5.cloned.1.call-done.own_ref, bf16[32,128,128]{2,1,0:T(8,128)(2,1)} %copy-done.11), custom_call_target="tpu_custom_call" | custom-call | flops 40000000000 | bytes 104857600 | tf_op jit(solution)/shard_map/index_scores/pallas_call | solution.py:161
  184.6 19.7 %all-to-all-done.1 = bf16[8,224,256]{2,1,0:T(8,128)(2,1)S(1)} async-done(((bf16[8,224,256]{2,1,0:T(8,128)(2,1)}), bf16[8,224,256]{2,1,0:T(8,128)(2,1)S(1)}, u32[]{:S(2)}, u32[]{:S(2)}) %all-to-all-start.1) | async-done | bytes 917536 | tf_op jit(solution)/shard_map/all_to_all | solution.py:295
  204.3 0.1 reduce_sum.12
  204.4 2.7 %collective-permute-start.11 = (bf16[224,128]{1,0:T(8,128)(2,1)S(1)}, bf16[224,128]{1,0:T(8,128)(2,1)S(1)}, u32[]{:S(2)}, u32[]{:S(2)}) collective-permute-start(bf16[224,128]{1,0:T(8,128)(2,1)S(1)} %slice.33), channel_id=1, source_target_pairs={{0,8},{8,0},{1,9},{9,1},{2,10},{10,2},{3,11},{11,3},{4,12},{12,4},... | collective-permute-start | bytes 172040 | tf_op jit(solution)/shard_map/ppermute | solution.py:227
  207.2 0.9 collective-permute-done.11
  208.1 0.7 pad_maximum_fusion.2
  (45 shorter events, 0.4 us)
Async XLA Ops:
  7.2 0.9 copy-start
  9.5 13.2 %copy-start.9 = (bf16[128,128]{1,0:T(8,128)(2,1)S(1)}, bf16[128,128]{1,0:T(8,128)(2,1)}, u32[]{:S(2)}) copy-start(bf16[128,128]{1,0:T(8,128)(2,1)} %param.10) | copy-start | bytes 98308
  9.5 13.3 %copy-start.8 = (bf16[1024,56]{0,1:T(8,128)(2,1)S(1)}, bf16[1024,56]{0,1:T(8,128)(2,1)}, u32[]{:S(2)}) copy-start(bf16[1024,56]{0,1:T(8,128)(2,1)} %param.15) | copy-start | bytes 344068
  9.5 21.7 %copy-start.10 = (s32[1,16]{1,0:T(1,128)S(1)}, s32[1,16]{1,0:T(1,128)}, u32[]{:S(2)}) copy-start(s32[1,16]{1,0:T(1,128)} %param.13) | copy-start | bytes 196
  9.5 62.4 %all-to-all-start = ((bf16[64,16,576]{2,1,0:T(8,128)(2,1)}), bf16[64,16,576]{2,1,0:T(8,128)(2,1)S(1)}, u32[]{:S(2)}, u32[]{:S(2)}) async-start(bf16[64,16,576]{2,1,0:T(8,128)(2,1)} %bitcast.10), calls=%async_computation | async-start | bytes 2621440 | tf_op jit(solution)/shard_map/all_to_all | solution.py:250
  22.7 102.7 %all-gather.3.cloned.1.call-start = ((), (), s32[]{:S(2)}) async-start(), calls=%async_computation.2 | async-start | bytes 4128768 | tf_op jit(solution)/shard_map/all_gather | solution.py:256
  22.8 42.7 %copy-start.4 = (bf16[72,1024]{1,0:T(8,128)(2,1)}, bf16[72,1024]{1,0:T(8,128)(2,1)S(1)}, u32[]{:S(2)}) copy-start(bf16[72,1024]{1,0:T(8,128)(2,1)S(1)} %pad_maximum_fusion.1.refs_0_) | copy-start | bytes 442372
  22.8 16.1 %collective-permute-start = (bf16[72,1024]{1,0:T(8,128)(2,1)S(1)}, bf16[72,1024]{1,0:T(8,128)(2,1)S(1)}, u32[]{:S(2)}, u32[]{:S(2)}) collective-permute-start(bf16[72,1024]{1,0:T(8,128)(2,1)S(1)} %pad_maximum_fusion.1.refs_0_), channel_id=1, source_target_pairs={{0,16},{16,0},{32,48},{48,32},{1,17},{17,1},{33,49},{49,33},{2,18}... | collective-permute-start | bytes 442376 | tf_op jit(solution)/shard_map/ppermute | solution.py:248
  24.8 35.6 %collective-permute-start.1 = (bf16[72,1024]{1,0:T(8,128)(2,1)S(1)}, bf16[72,1024]{1,0:T(8,128)(2,1)S(1)}, u32[]{:S(2)}, u32[]{:S(2)}) collective-permute-start(bf16[72,1024]{1,0:T(8,128)(2,1)S(1)} %pad_maximum_fusion.1.refs_0_), channel_id=1, source_target_pairs={{0,32},{16,48},{32,0},{48,16},{1,33},{17,49},{33,1},{49,17},{2,34}... | collective-permute-start | bytes 442376 | tf_op jit(solution)/shard_map/ppermute | solution.py:248
  29.0 36.4 %collective-permute-start.2 = (bf16[72,1024]{1,0:T(8,128)(2,1)S(1)}, bf16[72,1024]{1,0:T(8,128)(2,1)S(1)}, u32[]{:S(2)}, u32[]{:S(2)}) collective-permute-start(bf16[72,1024]{1,0:T(8,128)(2,1)S(1)} %pad_maximum_fusion.1.refs_0_), channel_id=1, source_target_pairs={{0,48},{16,32},{32,16},{48,0},{1,49},{17,33},{33,17},{49,1},{2,50}... | collective-permute-start | bytes 442376 | tf_op jit(solution)/shard_map/ppermute | solution.py:248
  31.3 40.5 %collective-permute-start.3 = (s32[16]{0:T(128)S(1)}, s32[16]{0:T(128)S(1)}, u32[]{:S(2)}, u32[]{:S(2)}) collective-permute-start(s32[16]{0:T(128)S(1)} %broadcast_maximum_fusion), channel_id=1, source_target_pairs={{0,8},{8,0},{1,9},{9,1},{2,10},{10,2},{3,11},{11,3},{4,12},{12,4},... | collective-permute-start | bytes 200 | tf_op jit(solution)/shard_map/ppermute | solution.py:227
  39.0 26.5 %copy-start.5 = (bf16[72,1024]{1,0:T(8,128)(2,1)}, bf16[72,1024]{1,0:T(8,128)(2,1)S(1)}, u32[]{:S(2)}) copy-start(bf16[72,1024]{1,0:T(8,128)(2,1)S(1)} %collective-permute-done.refs_1_) | copy-start | bytes 442372
  60.5 5.0 %copy-start.6 = (bf16[72,1024]{1,0:T(8,128)(2,1)}, bf16[72,1024]{1,0:T(8,128)(2,1)S(1)}, u32[]{:S(2)}) copy-start(bf16[72,1024]{1,0:T(8,128)(2,1)S(1)} %collective-permute-done.1.refs_2_) | copy-start | bytes 442372
  65.5 0.7 copy-start.7
  68.2 92.2 %all-gather.5.cloned.1.call-start = ((), (), s32[]{:S(2)}) async-start(), calls=%async_computation.3 | async-start | bytes 1179648 | tf_op jit(solution)/shard_map/all_gather | solution.py:281
  72.6 3.8 %collective-permute-start.4 = (bf16[256,576]{1,0:T(8,128)(2,1)S(1)}, bf16[256,576]{1,0:T(8,128)(2,1)S(1)}, u32[]{:S(2)}, u32[]{:S(2)}) collective-permute-start(bf16[256,576]{1,0:T(8,128)(2,1)S(1)} %bitcast.34), channel_id=1, source_target_pairs={{0,8},{8,0},{1,9},{9,1},{2,10},{10,2},{3,11},{11,3},{4,12},{12,4},... | collective-permute-start | bytes 884744 | tf_op jit(solution)/shard_map/ppermute | solution.py:227
  76.5 6.8 %copy-start.1 = (bf16[512,576]{1,0:T(8,128)(2,1)}, bf16[512,576]{1,0:T(8,128)(2,1)S(1)}, u32[]{:S(2)}) copy-start(bf16[512,576]{1,0:T(8,128)(2,1)S(1)} %pad_maximum_fusion.refs_2_) | copy-start | bytes 1769476
  76.8 17.8 %collective-permute-start.5 = (bf16[512,576]{0,1:T(8,128)(2,1)S(1)}, bf16[512,576]{0,1:T(8,128)(2,1)S(1)}, u32[]{:S(2)}, u32[]{:S(2)}) collective-permute-start(bf16[512,576]{0,1:T(8,128)(2,1)S(1)} %copy.15), channel_id=1, source_target_pairs={{0,2},{2,4},{4,6},{6,0},{1,3},{3,5},{5,7},{7,1},{8,10},{10,12},{12... | collective-permute-start | bytes 1769480 | tf_op jit(solution)/shard_map/ppermute | solution.py:265
  79.9 16.3 %collective-permute-start.6 = (bf16[512,576]{0,1:T(8,128)(2,1)S(1)}, bf16[512,576]{0,1:T(8,128)(2,1)S(1)}, u32[]{:S(2)}, u32[]{:S(2)}) collective-permute-start(bf16[512,576]{0,1:T(8,128)(2,1)S(1)} %copy.15), channel_id=1, source_target_pairs={{0,6},{2,0},{4,2},{6,4},{1,7},{3,1},{5,3},{7,5},{8,14},{10,8},{12,... | collective-permute-start | bytes 1769480 | tf_op jit(solution)/shard_map/ppermute | solution.py:266
  96.5 7.1 %copy-start.2 = (bf16[512,576]{1,0:T(8,128)(2,1)}, bf16[512,576]{1,0:T(8,128)(2,1)S(1)}, u32[]{:S(2)}) copy-start(bf16[512,576]{1,0:T(8,128)(2,1)S(1)} %copy.17.refs_2_) | copy-start | bytes 1769476
  96.8 6.8 %copy-start.3 = (bf16[512,576]{1,0:T(8,128)(2,1)}, bf16[512,576]{1,0:T(8,128)(2,1)S(1)}, u32[]{:S(2)}) copy-start(bf16[512,576]{1,0:T(8,128)(2,1)S(1)} %copy.18.refs_3_) | copy-start | bytes 1769476
  96.9 16.5 %collective-permute-start.7 = (bf16[256,576]{1,0:T(8,128)(2,1)S(1)}, bf16[256,576]{1,0:T(8,128)(2,1)S(1)}, u32[]{:S(2)}, u32[]{:S(2)}) collective-permute-start(bf16[256,576]{1,0:T(8,128)(2,1)S(1)} %slice.30), channel_id=1, source_target_pairs={{0,2},{2,4},{4,6},{6,0},{1,3},{3,5},{5,7},{7,1},{8,10},{10,12},{12... | collective-permute-start | bytes 884744 | tf_op jit(solution)/shard_map/ppermute | solution.py:279
  100.0 13.3 %collective-permute-start.8 = (bf16[256,576]{1,0:T(8,128)(2,1)S(1)}, bf16[256,576]{1,0:T(8,128)(2,1)S(1)}, u32[]{:S(2)}, u32[]{:S(2)}) collective-permute-start(bf16[256,576]{1,0:T(8,128)(2,1)S(1)} %slice.31), channel_id=1, source_target_pairs={{0,6},{2,0},{4,2},{6,4},{1,7},{3,1},{5,3},{7,5},{8,14},{10,8},{12,... | collective-permute-start | bytes 884744 | tf_op jit(solution)/shard_map/ppermute | solution.py:280
  113.3 0.7 copy-start.12
  113.3 0.8 copy-start.13
  120.3 5.1 %collective-permute-start.9 = (bf16[1024,128]{1,0:T(8,128)(2,1)}, bf16[1024,128]{1,0:T(8,128)(2,1)S(1)}, u32[]{:S(2)}, u32[]{:S(2)}) collective-permute-start(bf16[1024,128]{1,0:T(8,128)(2,1)} %attend.5), channel_id=1, source_target_pairs={{0,8},{8,0},{1,9},{9,1},{2,10},{10,2},{3,11},{11,3},{4,12},{12,4},... | collective-permute-start | bytes 786440 | tf_op jit(solution)/shard_map/ppermute | solution.py:227
  160.4 15.7 %collective-permute-start.10 = (bf16[32,128,128]{2,1,0:T(8,128)(2,1)}, bf16[32,128,128]{2,1,0:T(8,128)(2,1)S(1)}, u32[]{:S(2)}, u32[]{:S(2)}) collective-permute-start(bf16[32,128,128]{2,1,0:T(8,128)(2,1)} %all-gather.5.cloned.1.call-done.own_ref), channel_id=1, source_target_pairs={{0,8},{8,0},{1,9},{9,1},{2,10},{10,2},{3,11},{11,3},{4,12},{12,4},... | collective-permute-start | bytes 3145736 | tf_op jit(solution)/shard_map/ppermute | solution.py:227
  167.5 36.8 %all-to-all-start.1 = ((bf16[8,224,256]{2,1,0:T(8,128)(2,1)}), bf16[8,224,256]{2,1,0:T(8,128)(2,1)S(1)}, u32[]{:S(2)}, u32[]{:S(2)}) async-start(bf16[8,224,256]{2,1,0:T(8,128)(2,1)} %bitcast.19), calls=%async_computation.1 | async-start | bytes 1835008 | tf_op jit(solution)/shard_map/all_to_all | solution.py:295
  176.1 1.0 copy-start.11
  204.4 3.6 %collective-permute-start.11 = (bf16[224,128]{1,0:T(8,128)(2,1)S(1)}, bf16[224,128]{1,0:T(8,128)(2,1)S(1)}, u32[]{:S(2)}, u32[]{:S(2)}) collective-permute-start(bf16[224,128]{1,0:T(8,128)(2,1)S(1)} %slice.33), channel_id=1, source_target_pairs={{0,8},{8,0},{1,9},{9,1},{2,10},{10,2},{3,11},{11,3},{4,12},{12,4},... | collective-permute-start | bytes 172040 | tf_op jit(solution)/shard_map/ppermute | solution.py:227
Sparse Core Ops, SparseCore 0:
  68.3 53.9 all-gather.2
  124.3 35.9 all-gather.4

commit v4 on v3

--- a/solution.py
+++ b/solution.py
@@ -18,6 +18,8 @@
 BLOCK = 128
 TOPK = 16
 NBLK = 64
+ROWS = 8
+PACKED = 72
 COLS = 56
 NY, NZ, NC, NX, NW = 8, 4, 2, 4, 2
 
@@ -46,15 +48,15 @@
     keys = jnp.concatenate([ref[...] for ref in kv_refs], axis=0)
     n_keys = keys.shape[0]
     vt_ref[...] = keys[:, :KV_RANK].T
-    row = lax.broadcasted_iota(jnp.int32, (16, BLOCK), 0)
-    query = place_ref[TOPK] + lax.broadcasted_iota(jnp.int32, (16, BLOCK), 1)
-    for group in range(n_keys // 16):
+    row = lax.broadcasted_iota(jnp.int32, (ROWS, BLOCK), 0)
+    query = place_ref[TOPK] + lax.broadcasted_iota(jnp.int32, (ROWS, BLOCK), 1)
+    for group in range(n_keys // ROWS):
         part, slot = divmod(group, TOPK)
         entry = place_ref[slot]
         start = jnp.where(entry < 0, 2 * NBLK, entry) * BLOCK + place_ref[TOPK + 1 + part]
         seen = jnp.where(start + row <= query, 0.0, MASKED)
-        bias_ref[group * 16 : (group + 1) * 16, :BLOCK] = seen
-        bias_ref[group * 16 : (group + 1) * 16, BLOCK:] = seen
+        bias_ref[group * ROWS : (group + 1) * ROWS, :BLOCK] = seen
+        bias_ref[group * ROWS : (group + 1) * ROWS, BLOCK:] = seen
     for pair in range(HEADS_DEV // 2):
         scores = lax.dot_general(
             keys, q_ref[pair], (((1,), (1,)), ((), ())), preferred_element_type=jnp.float32
@@ -115,7 +117,7 @@
         ],
         compiler_params=pltpu.CompilerParams(vmem_limit_bytes=VMEM_LIMIT),
         cost_estimate=pl.CostEstimate(
-            flops=40_000_000_000,
+            flops=20000000000,
             bytes_accessed=4 * rows * KV_RANK * 2,
             transcendentals=rows * n_keys,
         ),
@@ -138,7 +140,14 @@
     lane = lax.broadcasted_iota(jnp.int32, (rows, BLOCK), 1)
 
     def chunk(keys_ref, parity, step):
-        keys = keys_ref[pl.ds(step * 2, 2)].reshape(2 * BLOCK, IDX_DIM)
+        keys = jnp.concatenate(
+            [
+                keys_ref[step * 2 + half, :, at * IDX_DIM : (at + 1) * IDX_DIM]
+                for half in range(2)
+                for at in range(8)
+            ],
+            axis=0,
+        )
         dots = lax.dot_general(
             q_ref[...], keys, (((1,), (1,)), ((), ())), preferred_element_type=jnp.float32
         )
@@ -193,34 +202,51 @@
         out_specs=[vmem] * 2,
         compiler_params=pltpu.CompilerParams(vmem_limit_bytes=VMEM_LIMIT),
         cost_estimate=pl.CostEstimate(
-            flops=20_000_000_000, bytes_accessed=20_000_000, transcendentals=0
+            flops=1000000000, bytes_accessed=4000000, transcendentals=0
         ),
         name="prepare",
     )(latent_query, value_up)
 
 
 def arrange_kernel(z_ref, *refs):
-    near, (w_ref, keys_ref) = refs[:NZ], refs[NZ:]
+    out_ref = refs[NZ]
     for step in range(NZ):
-        at = z_ref[0] ^ step
-        w_ref[at] = near[step][16:, :]
-        for block in range(8):
-            keys_ref[at, block * 16 : (block + 1) * 16, :] = near[step][
-                :16, block * BLOCK : (block + 1) * BLOCK
-            ]
+        out_ref[z_ref[0] ^ step] = refs[step][...]
 
 
 def arrange(z, near):
     vmem = pl.BlockSpec(memory_space=pltpu.VMEM)
-    shapes = [(NZ, COLS, 1024), (NZ, BLOCK, IDX_DIM)]
     return pl.pallas_call(
         arrange_kernel,
-        out_shape=[jax.ShapeDtypeStruct(shape, jnp.bfloat16) for shape in shapes],
+        out_shape=jax.ShapeDtypeStruct((NZ, PACKED, 1024), jnp.bfloat16),
         in_specs=[pl.BlockSpec(memory_space=pltpu.SMEM)] + [vmem] * NZ,
-        out_specs=[vmem] * 2,
+        out_specs=vmem,
         compiler_params=pltpu.CompilerParams(vmem_limit_bytes=VMEM_LIMIT),
         name="arrange",
     )(z, *near)
+
+
+def project_kernel(w_ref, own_ref, other_ref, out_ref):
+    weights = w_ref[...].reshape(NZ * PACKED, 1024)
+    for half, values_ref in enumerate((own_ref, other_ref)):
+        terms = lax.dot_general(
+            weights, values_ref[...], (((1,), (0,)), ((), ())), preferred_element_type=jnp.float32
+        )
+        terms = terms.reshape(NZ, PACKED, BLOCK)[:, 16:, :].reshape(NZ * COLS, BLOCK)
+        out_ref[0, :, half * BLOCK : (half + 1) * BLOCK] = terms.astype(jnp.bfloat16)
+
+
+def project(gathered, own, other):
+    values = pl.BlockSpec((HEADS_DEV * V_DIM, BLOCK), lambda i: (0, 0))
+    return pl.pallas_call(
+        project_kernel,
+        out_shape=jax.ShapeDtypeStruct((NY, NZ * COLS, 2 * BLOCK), jnp.bfloat16),
+        grid=(NY,),
+        in_specs=[pl.BlockSpec((NZ, PACKED, 1024), lambda i: (i, 0, 0)), values, values],
+        out_specs=pl.BlockSpec((1, NZ * COLS, 2 * BLOCK), lambda i: (i, 0, 0)),
+        compiler_params=pltpu.CompilerParams(vmem_limit_bytes=VMEM_LIMIT),
+        name="project",
+    )(gathered, own, other)
 
 
 def swap_core(value):
@@ -239,8 +265,8 @@
     ctx_pos = (y * NZ + z) * NC + core
     head_pos = x * NW + w
 
-    own = lax.dynamic_slice_in_dim(latent, x * 32, 32, 0).reshape(1, NC, 16, LAT)
-    wide = jnp.broadcast_to(own, (NY * NZ, NC, 16, LAT)).reshape(NBLK, 16, LAT)
+    own = lax.dynamic_slice_in_dim(latent, head_pos * 16, 16, 0).reshape(1, NC, ROWS, LAT)
+    wide = jnp.broadcast_to(own, (NY * NZ, NC, ROWS, LAT)).reshape(NBLK, ROWS, LAT)
 
     key_rows = jnp.moveaxis(index_key.reshape(8, 16, IDX_DIM), 0, 1).reshape(16, 1024)
     packed = jnp.concatenate([key_rows, out_weight.T], axis=0)
@@ -252,21 +278,26 @@
     safe = jnp.maximum(listed, 0)
     both = jnp.concatenate([safe, swap_core(safe)])
     queries, up_t = prepare(latent_query, value_up)
-    w_z, keys_z = arrange(z.reshape(1), near)
-    w_all = lax.all_gather(w_z, "y", axis=0, tiled=True).reshape(NY * NZ * COLS, 1024)
-    pool, queries, up_t, both, keys_z = lax.optimization_barrier(
-        (pool, queries, up_t, both, keys_z)
+    near_z = arrange(z.reshape(1), near)
+    pool, queries, up_t, both, near_z = lax.optimization_barrier(
+        (pool, queries, up_t, both, near_z)
     )
-
-    picked = jnp.take(pool, both, axis=0, mode="clip").reshape(2, TOPK * 16, LAT)
+    gathered = lax.all_gather(near_z, "y", axis=0, tiled=True)
+
+    picked = jnp.take(pool, both, axis=0, mode="clip").reshape(2, TOPK * ROWS, LAT)
     mine = jnp.concatenate([picked[0], swap_core(picked[1])], axis=0)
+    mine = jnp.concatenate([mine, lax.ppermute(mine, "w", [(0, 1), (1, 0)])], axis=0)
     up = [(at, (at + 1) % NX) for at in range(NX)]
     down = [(at, (at - 1) % NX) for at in range(NX)]
     left = lax.ppermute(mine, "x", up)
     right = lax.ppermute(mine, "x", down)
 
-    def place(*xs):
-        offsets = [((x + step) % NX) * 32 + 16 * (core ^ half) for step, half in xs]
+    def place(*parts):
+        offsets = [
+            ((x + step) % NX) * 32 + (w ^ far) * 16 + (core ^ half) * ROWS
+            for step, far in parts
+            for half in range(NC)
+        ]
         return jnp.concatenate([listed, jnp.stack([ctx_pos * BLOCK] + offsets)])
 
     places = (
@@ -275,19 +306,17 @@
         place((2, 0), (2, 1)),
     )
     state = attend(places[0], queries, [mine], None, None)
-    left, right, state, keys_z = lax.optimization_barrier((left, right, state, keys_z))
+    left, right, state = lax.optimization_barrier((left, right, state))
     far_a = lax.ppermute(left[:256], "x", up)
     far_b = lax.ppermute(right[256:], "x", down)
-    keys_own = lax.all_gather(keys_z, "y", axis=0, tiled=True)
     state = attend(places[1], queries, [left, right], state, None)
     far_a, far_b, state = lax.optimization_barrier((far_a, far_b, state))
     values = attend(places[2], queries, [far_a, far_b], state, up_t)
 
-    both_values = jnp.concatenate([values, swap_core(values)], axis=1)
-    terms = jnp.dot(w_all, both_values, preferred_element_type=jnp.float32).astype(jnp.bfloat16)
-    terms = terms.reshape(NY, NZ * COLS, 2 * BLOCK)
+    values, gathered = lax.optimization_barrier((values, gathered))
+    terms = project(gathered, values, swap_core(values))
+    keys_own = gathered[:, :16]
     first_row = ctx_pos * TOK_DEV + head_pos * 16
-    terms, keys_own = lax.optimization_barrier((terms, keys_own))
     keys_other = swap_core(keys_own)
     index_scores = index_part(
         jnp.stack([core, first_row]), index_query, index_weight, keys_own, keys_other

time: 216 us -> 184 us (0.85)
  waiting for transfers between devices: 90.7 us -> 50 us
  Pallas kernels: 35 us -> 42.7 us
  matrix products: 4.12 us -> 0 us
  local copies, waits for them, and re-layouts: 7.05 us -> 9.96 us
    all_gather x2 -> x1, waiting for transfers between devices: 30.8 us -> 0.01 us  [body(): gathered = lax.all_gather(near_z, 'y', axis=0, tiled=True)]
    ppermute x3, waiting for transfers between devices: 31.1 us -> 15.1 us  [body(): lax.ppermute(packed, 'z', [(at, at ^ step) for at in range(NZ)])]
    ppermute x0 -> x1, waiting for transfers between devices: none -> 10.2 us  [body(): lax.ppermute(mine, 'w', [(0, 1), (1, 0)])]
    ppermute x0 -> x1, starting transfers between devices: none -> 7.94 us  [body(): lax.ppermute(mine, 'w', [(0, 1), (1, 0)])]
    pallas_call x1 -> x2, Pallas kernels: 1.98 us -> 9.83 us  [the longest x1 7.81 us: project(): pl.pallas_call(project_kernel, out_shape=jax.ShapeDtypeStruct((NY, NZ * C...]
    ppermute x5, starting transfers between devices: 18.7 us -> 13.8 us  [swap_core(): return lax.ppermute(value, 'c', [(0, 1), (1, 0)])]
    all_to_all x1, waiting for transfers between devices: 19.7 us -> 15.4 us  [body(): shares = lax.all_to_all(terms, HEAD, 0, 0)]
    dot_general x1 -> x0, matrix products: 4.12 us -> none  [body(): jnp.dot(w_all, both_values, preferred_element_type=jnp.float32)]
  transfers between devices with their start and end apart: 16 -> 16, of which waited for: 9 -> 9; matrix products, arithmetic and copies ran while one was open for 4% -> 2% of each run, Pallas kernels for 16% -> 23%
where the time goes in v4:
time: 184 us; the launch traced here: 183 us
  starting transfers between devices  64 us (35%)
  waiting for transfers between devices  50 us (27%)
  Pallas kernels  42.7 us (23%)
  between operations  14.5 us (8%)
  local copies, waits for them, and re-layouts  9.96 us (5%)
    pallas_call x3, Pallas kernels, attend(): pl.pallas_call(functools.partial(attend_kernel, len(parts), state is None...  21.9 us
    all_to_all x1, waiting for transfers between devices, body(): shares = lax.all_to_all(terms, HEAD, 0, 0)  15.4 us
    ppermute x3, waiting for transfers between devices, body(): lax.ppermute(packed, 'z', [(at, at ^ step) for at in range(NZ)])  15.1 us
    ppermute x5, starting transfers between devices, swap_core(): return lax.ppermute(value, 'c', [(0, 1), (1, 0)])  13.8 us
    all_to_all x1, starting transfers between devices, body(): pool = lax.all_to_all(wide, CTX, 0, 0)  13 us
    ppermute x1, waiting for transfers between devices, body(): lax.ppermute(mine, 'w', [(0, 1), (1, 0)])  10.2 us
    ppermute x3, starting transfers between devices, body(): lax.ppermute(packed, 'z', [(at, at ^ step) for at in range(NZ)])  8.37 us
    ppermute x1, starting transfers between devices, body(): lax.ppermute(mine, 'w', [(0, 1), (1, 0)])  7.94 us
  transfers between devices with their start and end apart: 16, of which 9 were waited for; matrix products, arithmetic and copies ran while one was open for 2% of the time, Pallas kernels for 23%

profile of v4, /device:TPU:65, one launch (start us, length us, event | category | flops | bytes accessed | tf_op | source)
XLA Modules:
  0.0 182.8 jit_solution(12649808871967177902)
XLA Ops:
  7.2 0.9 copy-done
  8.3 0.9 broadcast_in_dim.12
  9.2 13.0 %all-to-all-start = ((bf16[64,8,576]{2,1,0:T(8,128)(2,1)}), bf16[64,8,576]{2,1,0:T(8,128)(2,1)S(1)}, u32[]{:S(2)}, u32[]{:S(2)}) async-start(bf16[64,8,576]{2,1,0:T(8,128)(2,1)} %bitcast.7), calls=%async_computation | async-start | bytes 1310720 | tf_op jit(solution)/shard_map/all_to_all | solution.py:276
  22.4 2.0 %collective-permute-start.1 = (bf16[72,1024]{1,0:T(8,128)(2,1)S(1)}, bf16[72,1024]{1,0:T(8,128)(2,1)S(1)}, u32[]{:S(2)}, u32[]{:S(2)}) collective-permute-start(bf16[72,1024]{1,0:T(8,128)(2,1)S(1)} %pad_maximum_fusion.2.refs_0_), channel_id=1, source_target_pairs={{0,16},{16,0},{32,48},{48,32},{1,17},{17,1},{33,49},{49,33},{2,18}... | collective-permute-start | bytes 442376 | tf_op jit(solution)/shard_map/ppermute | solution.py:274
  24.4 4.2 %collective-permute-start.2 = (bf16[72,1024]{1,0:T(8,128)(2,1)S(1)}, bf16[72,1024]{1,0:T(8,128)(2,1)S(1)}, u32[]{:S(2)}, u32[]{:S(2)}) collective-permute-start(bf16[72,1024]{1,0:T(8,128)(2,1)S(1)} %pad_maximum_fusion.2.refs_0_), channel_id=1, source_target_pairs={{0,32},{16,48},{32,0},{48,16},{1,33},{17,49},{33,1},{49,17},{2,34}... | collective-permute-start | bytes 442376 | tf_op jit(solution)/shard_map/ppermute | solution.py:274
  28.6 2.2 %collective-permute-start.3 = (bf16[72,1024]{1,0:T(8,128)(2,1)S(1)}, bf16[72,1024]{1,0:T(8,128)(2,1)S(1)}, u32[]{:S(2)}, u32[]{:S(2)}) collective-permute-start(bf16[72,1024]{1,0:T(8,128)(2,1)S(1)} %pad_maximum_fusion.2.refs_0_), channel_id=1, source_target_pairs={{0,48},{16,32},{32,16},{48,0},{1,49},{17,33},{33,17},{49,1},{2,50}... | collective-permute-start | bytes 442376 | tf_op jit(solution)/shard_map/ppermute | solution.py:274
  30.9 3.1 %collective-permute-start = (s32[16]{0:T(128)S(1)}, s32[16]{0:T(128)S(1)}, u32[]{:S(2)}, u32[]{:S(2)}) collective-permute-start(s32[16]{0:T(128)S(1)} %broadcast_maximum_fusion), channel_id=1, source_target_pairs={{0,8},{8,0},{1,9},{9,1},{2,10},{10,2},{3,11},{11,3},{4,12},{12,4},... | collective-permute-start | bytes 200 | tf_op jit(solution)/shard_map/ppermute | solution.py:253
  34.0 3.5 %prepare.1 = (bf16[4,256,576]{2,1,0:T(8,128)(2,1)}, bf16[8,128,512]{2,1,0:T(8,128)(2,1)}) custom-call(bf16[128,4608]{1,0:T(8,128)(2,1)} %lq_ref.1, bf16[8,512,128]{2,1,0:T(8,128)(2,1)} %up_ref.1), custom_call_target="tpu_custom_call" | custom-call | flops 1000000000 | bytes 4000000 | tf_op jit(solution)/shard_map/prepare/pallas_call | solution.py:198
  37.6 8.8 %collective-permute-done.2.refs_2_ = bf16[72,1024]{1,0:T(8,128)(2,1)S(1)} collective-permute-done((bf16[72,1024]{1,0:T(8,128)(2,1)S(1)}, bf16[72,1024]{1,0:T(8,128)(2,1)S(1)}, u32[]{:S(2)}, u32[]{:S(2)}) %collective-permute-start.2) | collective-permute-done | bytes 147488 | tf_op jit(solution)/shard_map/ppermute | solution.py:274
  46.4 6.3 %collective-permute-done.3.refs_3_ = bf16[72,1024]{1,0:T(8,128)(2,1)S(1)} collective-permute-done((bf16[72,1024]{1,0:T(8,128)(2,1)S(1)}, bf16[72,1024]{1,0:T(8,128)(2,1)S(1)}, u32[]{:S(2)}, u32[]{:S(2)}) %collective-permute-start.3) | collective-permute-done | bytes 147488 | tf_op jit(solution)/shard_map/ppermute | solution.py:274
  52.7 0.7 copy-done.10
  53.4 2.0 %arrange.1 = bf16[4,72,1024]{2,1,0:T(8,128)(2,1)} custom-call(s32[1]{0:T(128)} %bitcast.8.z_ref, bf16[72,1024]{1,0:T(8,128)(2,1)} %copy-done.5, bf16[72,1024]{1,0:T(8,128)(2,1)} %copy-done.8, bf16[72,1024]{1,0:T(8,128)(2,1)} %copy-done.9, bf16[72,1024]{1,0:T(8,128)(2,1)} %copy-done.10), custom_call_target="tpu_custom_call" | custom-call | tf_op jit(solution)/shard_map/arrange/pallas_call | solution.py:219
  55.4 0.6 gather_fusion
  56.1 2.3 %collective-permute-start.4 = (bf16[128,576]{1,0:T(8,128)(2,1)S(1)}, bf16[128,576]{1,0:T(8,128)(2,1)S(1)}, u32[]{:S(2)}, u32[]{:S(2)}) collective-permute-start(bf16[128,576]{1,0:T(8,128)(2,1)S(1)} %get-tuple-element.57), channel_id=1, source_target_pairs={{0,8},{8,0},{1,9},{9,1},{2,10},{10,2},{3,11},{11,3},{4,12},{12,4},... | collective-permute-start | bytes 442376 | tf_op jit(solution)/shard_map/ppermute | solution.py:253
  58.4 1.0 collective-permute-done.4
  59.4 7.9 %collective-permute-start.5 = (bf16[256,576]{1,0:T(8,128)(2,1)S(1)}, bf16[256,576]{1,0:T(8,128)(2,1)S(1)}, u32[]{:S(2)}, u32[]{:S(2)}) collective-permute-start(bf16[256,576]{1,0:T(8,128)(2,1)S(1)} %pad_maximum_fusion.1), channel_id=1, source_target_pairs={{0,1},{1,0},{2,3},{3,2},{4,5},{5,4},{6,7},{7,6},{8,9},{9,8},{10,11... | collective-permute-start | bytes 884744 | tf_op jit(solution)/shard_map/ppermute | solution.py:289
  67.5 0.7 concatenate.27.refs_0_
  68.1 0.6 concatenate.22.refs_0_
  68.7 0.6 concatenate.28.refs_0_
  69.3 10.2 %collective-permute-done.5 = bf16[256,576]{1,0:T(8,128)(2,1)S(1)} collective-permute-done((bf16[256,576]{1,0:T(8,128)(2,1)S(1)}, bf16[256,576]{1,0:T(8,128)(2,1)S(1)}, u32[]{:S(2)}, u32[]{:S(2)}) %collective-permute-start.5) | collective-permute-done | bytes 294944 | tf_op jit(solution)/shard_map/ppermute | solution.py:289
  79.6 0.2 copy.15
  79.8 3.1 %collective-permute-start.6 = (bf16[512,576]{0,1:T(8,128)(2,1)S(1)}, bf16[512,576]{0,1:T(8,128)(2,1)S(1)}, u32[]{:S(2)}, u32[]{:S(2)}) collective-permute-start(bf16[512,576]{0,1:T(8,128)(2,1)S(1)} %copy.15), channel_id=1, source_target_pairs={{0,2},{2,4},{4,6},{6,0},{1,3},{3,5},{5,7},{7,1},{8,10},{10,12},{12... | collective-permute-start | bytes 1769480 | tf_op jit(solution)/shard_map/ppermute | solution.py:292
  82.9 3.4 %collective-permute-start.7 = (bf16[512,576]{0,1:T(8,128)(2,1)S(1)}, bf16[512,576]{0,1:T(8,128)(2,1)S(1)}, u32[]{:S(2)}, u32[]{:S(2)}) collective-permute-start(bf16[512,576]{0,1:T(8,128)(2,1)S(1)} %copy.15), channel_id=1, source_target_pairs={{0,6},{2,0},{4,2},{6,4},{1,7},{3,1},{5,3},{7,5},{8,14},{10,8},{12,... | collective-permute-start | bytes 1769480 | tf_op jit(solution)/shard_map/ppermute | solution.py:293
  86.3 6.1 %attend.3 = (f32[4,1,256]{2,1,0:T(1,128)}, f32[4,1,256]{2,1,0:T(1,128)}, f32[4,512,256]{2,1,0:T(8,128)}) custom-call(s32[21]{0:T(128)} %concatenate.27.refs_0_, bf16[4,256,576]{2,1,0:T(8,128)(2,1)} %get-tuple-element.31.refs_1_, bf16[512,576]{1,0:T(8,128)(2,1)} %copy-done.1), custom_call_target="tpu_custom_call" | custom-call | flops 20000000000 | bytes 4194304 | tf_op jit(solution)/shard_map/attend/pallas_call | solution.py:109
  92.5 4.9 %collective-permute-done.6 = bf16[512,576]{0,1:T(8,128)(2,1)S(1)} collective-permute-done((bf16[512,576]{0,1:T(8,128)(2,1)S(1)}, bf16[512,576]{0,1:T(8,128)(2,1)S(1)}, u32[]{:S(2)}, u32[]{:S(2)}) %collective-permute-start.6) | collective-permute-done | bytes 589856 | tf_op jit(solution)/shard_map/ppermute | solution.py:292
  97.4 1.6 collective-permute-done.7
  99.0 0.3 copy.17.refs_2_
  99.3 0.3 copy.18.refs_3_
  99.6 3.1 %collective-permute-start.8 = (bf16[256,576]{1,0:T(8,128)(2,1)S(1)}, bf16[256,576]{1,0:T(8,128)(2,1)S(1)}, u32[]{:S(2)}, u32[]{:S(2)}) collective-permute-start(bf16[256,576]{1,0:T(8,128)(2,1)S(1)} %slice.34), channel_id=1, source_target_pairs={{0,2},{2,4},{4,6},{6,0},{1,3},{3,5},{5,7},{7,1},{8,10},{10,12},{12... | collective-permute-start | bytes 884744 | tf_op jit(solution)/shard_map/ppermute | solution.py:310
  102.8 3.6 %collective-permute-start.9 = (bf16[256,576]{1,0:T(8,128)(2,1)S(1)}, bf16[256,576]{1,0:T(8,128)(2,1)S(1)}, u32[]{:S(2)}, u32[]{:S(2)}) collective-permute-start(bf16[256,576]{1,0:T(8,128)(2,1)S(1)} %slice.35), channel_id=1, source_target_pairs={{0,6},{2,0},{4,2},{6,4},{1,7},{3,1},{5,3},{7,5},{8,14},{10,8},{12,... | collective-permute-start | bytes 884744 | tf_op jit(solution)/shard_map/ppermute | solution.py:311
  106.4 9.7 %attend.4 = (f32[4,1,256]{2,1,0:T(1,128)}, f32[4,1,256]{2,1,0:T(1,128)}, f32[4,512,256]{2,1,0:T(8,128)}) custom-call(s32[25]{0:T(128)} %concatenate.28.refs_0_, bf16[4,256,576]{2,1,0:T(8,128)(2,1)} %get-tuple-element.31.refs_1_, bf16[512,576]{1,0:T(8,128)(2,1)} %copy-done.2, bf16[512,576]{1,0:T(8,128)(2,1)} %copy-done.3, ...), custom_call_target="tpu_custom_call" | custom-call | flops 20000000000 | bytes 4194304 | tf_op jit(solution)/shard_map/attend/pallas_call | solution.py:109
  116.1 0.7 copy-done.15
  116.9 6.0 %attend.5.own_ref = bf16[1024,128]{1,0:T(8,128)(2,1)} custom-call(s32[21]{0:T(128)} %concatenate.22.refs_0_, bf16[4,256,576]{2,1,0:T(8,128)(2,1)} %get-tuple-element.31.refs_1_, bf16[256,576]{1,0:T(8,128)(2,1)} %copy-done.15, bf16[256,576]{1,0:T(8,128)(2,1)} %copy-done.16, f32[4,1,256]{2,1,0:T(1,128)} %get-tuple-element.47.refs_4_, ...), custom_call_target="tpu_custom_call" | custom-call | flops 20000000000 | bytes 4194304 | tf_op jit(solution)/shard_map/attend/pallas_call | solution.py:109
  123.0 1.3 slice.27.own_ref
  124.3 4.1 %collective-permute-start.11 = (bf16[32,16,1024]{2,1,0:T(8,128)(2,1)S(1)}, bf16[32,16,1024]{2,1,0:T(8,128)(2,1)S(1)}, u32[]{:S(2)}, u32[]{:S(2)}) collective-permute-start(bf16[32,16,1024]{2,1,0:T(8,128)(2,1)S(1)} %slice.27.own_ref), channel_id=1, source_target_pairs={{0,8},{8,0},{1,9},{9,1},{2,10},{10,2},{3,11},{11,3},{4,12},{12,4},... | collective-permute-start | bytes 3145736 | tf_op jit(solution)/shard_map/ppermute | solution.py:253
  128.4 1.9 %collective-permute-start.10 = (bf16[1024,128]{1,0:T(8,128)(2,1)S(1)}, bf16[1024,128]{1,0:T(8,128)(2,1)S(1)}, u32[]{:S(2)}, u32[]{:S(2)}) collective-permute-start(bf16[1024,128]{1,0:T(8,128)(2,1)S(1)} %copy-done.6), channel_id=1, source_target_pairs={{0,8},{8,0},{1,9},{9,1},{2,10},{10,2},{3,11},{11,3},{4,12},{12,4},... | collective-permute-start | bytes 786440 | tf_op jit(solution)/shard_map/ppermute | solution.py:253
  130.4 0.6 pad_add_fusion.1.place_ref
  130.9 0.9 collective-permute-done.10.other_ref
  131.9 0.7 copy-done.7
  132.6 7.8 %project.1 = bf16[8,224,256]{2,1,0:T(8,128)(2,1)} custom-call(bf16[32,72,1024]{2,1,0:T(8,128)(2,1)} %all-gather.2.cloned.1.call-done.w_ref, bf16[1024,128]{1,0:T(8,128)(2,1)} %attend.5.own_ref, bf16[1024,128]{1,0:T(8,128)(2,1)} %copy-done.7), custom_call_target="tpu_custom_call" | custom-call | tf_op jit(solution)/shard_map/project/pallas_call | solution.py:241
  140.4 7.6 %all-to-all-start.1 = ((bf16[8,224,256]{2,1,0:T(8,128)(2,1)}), bf16[8,224,256]{2,1,0:T(8,128)(2,1)S(1)}, u32[]{:S(2)}, u32[]{:S(2)}) async-start(bf16[8,224,256]{2,1,0:T(8,128)(2,1)} %project.1), calls=%async_computation.1 | async-start | bytes 1835008 | tf_op jit(solution)/shard_map/all_to_all | solution.py:324
  148.0 1.0 copy-done.14
  149.0 7.5 %index_scores.1 = f32[16,8192]{1,0:T(8,128)} custom-call(s32[2]{0:T(128)} %pad_add_fusion.1.place_ref, bf16[16,4096]{1,0:T(8,128)(2,1)} %query_ref.1, f32[16,32]{1,0:T(8,128)} %w_ref.1, bf16[32,16,1024]{2,1,0:T(8,128)(2,1)} %copy-done.4, bf16[32,16,1024]{2,1,0:T(8,128)(2,1)} %copy-done.14), custom_call_target="tpu_custom_call" | custom-call | flops 40000000000 | bytes 104857600 | tf_op jit(solution)/shard_map/index_scores/pallas_call | solution.py:170
  156.5 15.4 %all-to-all-done.1 = bf16[8,224,256]{2,1,0:T(8,128)(2,1)S(1)} async-done(((bf16[8,224,256]{2,1,0:T(8,128)(2,1)}), bf16[8,224,256]{2,1,0:T(8,128)(2,1)S(1)}, u32[]{:S(2)}, u32[]{:S(2)}) %all-to-all-start.1) | async-done | bytes 917536 | tf_op jit(solution)/shard_map/all_to_all | solution.py:324
  171.8 0.1 reduce_sum.12
  172.0 2.4 %collective-permute-start.12 = (bf16[224,128]{1,0:T(8,128)(2,1)S(1)}, bf16[224,128]{1,0:T(8,128)(2,1)S(1)}, u32[]{:S(2)}, u32[]{:S(2)}) collective-permute-start(bf16[224,128]{1,0:T(8,128)(2,1)S(1)} %slice.37), channel_id=1, source_target_pairs={{0,8},{8,0},{1,9},{9,1},{2,10},{10,2},{3,11},{11,3},{4,12},{12,4},... | collective-permute-start | bytes 172040 | tf_op jit(solution)/shard_map/ppermute | solution.py:253
  174.4 0.9 collective-permute-done.12
  175.3 0.7 pad_maximum_fusion.3
  (53 shorter events, 0.8 us)
Async XLA Ops:
  7.2 0.9 copy-start
  7.2 15.2 %copy-start.12 = (bf16[128,128]{1,0:T(8,128)(2,1)S(1)}, bf16[128,128]{1,0:T(8,128)(2,1)}, u32[]{:S(2)}) copy-start(bf16[128,128]{1,0:T(8,128)(2,1)} %param.10) | copy-start | bytes 98308
  7.2 15.2 %copy-start.11 = (bf16[1024,56]{0,1:T(8,128)(2,1)S(1)}, bf16[1024,56]{0,1:T(8,128)(2,1)}, u32[]{:S(2)}) copy-start(bf16[1024,56]{0,1:T(8,128)(2,1)} %param.15) | copy-start | bytes 344068
  8.2 22.6 %copy-start.13 = (s32[1,16]{1,0:T(1,128)S(1)}, s32[1,16]{1,0:T(1,128)}, u32[]{:S(2)}) copy-start(s32[1,16]{1,0:T(1,128)} %param.13) | copy-start | bytes 196
  9.2 46.1 %all-to-all-start = ((bf16[64,8,576]{2,1,0:T(8,128)(2,1)}), bf16[64,8,576]{2,1,0:T(8,128)(2,1)S(1)}, u32[]{:S(2)}, u32[]{:S(2)}) async-start(bf16[64,8,576]{2,1,0:T(8,128)(2,1)} %bitcast.7), calls=%async_computation | async-start | bytes 1310720 | tf_op jit(solution)/shard_map/all_to_all | solution.py:276
  22.3 100.7 %all-gather.2.cloned.1.call-start = ((), (), s32[]{:S(2)}) async-start(), calls=%async_computation.2 | async-start | bytes 5308416 | tf_op jit(solution)/shard_map/all_gather | solution.py:285
  22.4 15.1 %copy-start.5 = (bf16[72,1024]{1,0:T(8,128)(2,1)}, bf16[72,1024]{1,0:T(8,128)(2,1)S(1)}, u32[]{:S(2)}) copy-start(bf16[72,1024]{1,0:T(8,128)(2,1)S(1)} %pad_maximum_fusion.2.refs_0_) | copy-start | bytes 442372
  22.4 15.1 %collective-permute-start.1 = (bf16[72,1024]{1,0:T(8,128)(2,1)S(1)}, bf16[72,1024]{1,0:T(8,128)(2,1)S(1)}, u32[]{:S(2)}, u32[]{:S(2)}) collective-permute-start(bf16[72,1024]{1,0:T(8,128)(2,1)S(1)} %pad_maximum_fusion.2.refs_0_), channel_id=1, source_target_pairs={{0,16},{16,0},{32,48},{48,32},{1,17},{17,1},{33,49},{49,33},{2,18}... | collective-permute-start | bytes 442376 | tf_op jit(solution)/shard_map/ppermute | solution.py:274
  24.4 22.0 %collective-permute-start.2 = (bf16[72,1024]{1,0:T(8,128)(2,1)S(1)}, bf16[72,1024]{1,0:T(8,128)(2,1)S(1)}, u32[]{:S(2)}, u32[]{:S(2)}) collective-permute-start(bf16[72,1024]{1,0:T(8,128)(2,1)S(1)} %pad_maximum_fusion.2.refs_0_), channel_id=1, source_target_pairs={{0,32},{16,48},{32,0},{48,16},{1,33},{17,49},{33,1},{49,17},{2,34}... | collective-permute-start | bytes 442376 | tf_op jit(solution)/shard_map/ppermute | solution.py:274
  28.6 24.1 %collective-permute-start.3 = (bf16[72,1024]{1,0:T(8,128)(2,1)S(1)}, bf16[72,1024]{1,0:T(8,128)(2,1)S(1)}, u32[]{:S(2)}, u32[]{:S(2)}) collective-permute-start(bf16[72,1024]{1,0:T(8,128)(2,1)S(1)} %pad_maximum_fusion.2.refs_0_), channel_id=1, source_target_pairs={{0,48},{16,32},{32,16},{48,0},{1,49},{17,33},{33,17},{49,1},{2,50}... | collective-permute-start | bytes 442376 | tf_op jit(solution)/shard_map/ppermute | solution.py:274
  30.9 6.6 %collective-permute-start = (s32[16]{0:T(128)S(1)}, s32[16]{0:T(128)S(1)}, u32[]{:S(2)}, u32[]{:S(2)}) collective-permute-start(s32[16]{0:T(128)S(1)} %broadcast_maximum_fusion), channel_id=1, source_target_pairs={{0,8},{8,0},{1,9},{9,1},{2,10},{10,2},{3,11},{11,3},{4,12},{12,4},... | collective-permute-start | bytes 200 | tf_op jit(solution)/shard_map/ppermute | solution.py:253
  37.6 15.1 %copy-start.8 = (bf16[72,1024]{1,0:T(8,128)(2,1)}, bf16[72,1024]{1,0:T(8,128)(2,1)S(1)}, u32[]{:S(2)}) copy-start(bf16[72,1024]{1,0:T(8,128)(2,1)S(1)} %collective-permute-done.1.refs_1_) | copy-start | bytes 442372
  46.4 6.3 %copy-start.9 = (bf16[72,1024]{1,0:T(8,128)(2,1)}, bf16[72,1024]{1,0:T(8,128)(2,1)S(1)}, u32[]{:S(2)}) copy-start(bf16[72,1024]{1,0:T(8,128)(2,1)S(1)} %collective-permute-done.2.refs_2_) | copy-start | bytes 442372
  52.7 0.7 copy-start.10
  56.1 3.3 %collective-permute-start.4 = (bf16[128,576]{1,0:T(8,128)(2,1)S(1)}, bf16[128,576]{1,0:T(8,128)(2,1)S(1)}, u32[]{:S(2)}, u32[]{:S(2)}) collective-permute-start(bf16[128,576]{1,0:T(8,128)(2,1)S(1)} %get-tuple-element.57), channel_id=1, source_target_pairs={{0,8},{8,0},{1,9},{9,1},{2,10},{10,2},{3,11},{11,3},{4,12},{12,4},... | collective-permute-start | bytes 442376 | tf_op jit(solution)/shard_map/ppermute | solution.py:253
  59.4 20.1 %collective-permute-start.5 = (bf16[256,576]{1,0:T(8,128)(2,1)S(1)}, bf16[256,576]{1,0:T(8,128)(2,1)S(1)}, u32[]{:S(2)}, u32[]{:S(2)}) collective-permute-start(bf16[256,576]{1,0:T(8,128)(2,1)S(1)} %pad_maximum_fusion.1), channel_id=1, source_target_pairs={{0,1},{1,0},{2,3},{3,2},{4,5},{5,4},{6,7},{7,6},{8,9},{9,8},{10,11... | collective-permute-start | bytes 884744 | tf_op jit(solution)/shard_map/ppermute | solution.py:289
  79.6 6.8 %copy-start.1 = (bf16[512,576]{1,0:T(8,128)(2,1)}, bf16[512,576]{1,0:T(8,128)(2,1)S(1)}, u32[]{:S(2)}) copy-start(bf16[512,576]{1,0:T(8,128)(2,1)S(1)} %pad_maximum_fusion.refs_2_) | copy-start | bytes 1769476
  79.8 17.5 %collective-permute-start.6 = (bf16[512,576]{0,1:T(8,128)(2,1)S(1)}, bf16[512,576]{0,1:T(8,128)(2,1)S(1)}, u32[]{:S(2)}, u32[]{:S(2)}) collective-permute-start(bf16[512,576]{0,1:T(8,128)(2,1)S(1)} %copy.15), channel_id=1, source_target_pairs={{0,2},{2,4},{4,6},{6,0},{1,3},{3,5},{5,7},{7,1},{8,10},{10,12},{12... | collective-permute-start | bytes 1769480 | tf_op jit(solution)/shard_map/ppermute | solution.py:292
  82.9 16.0 %collective-permute-start.7 = (bf16[512,576]{0,1:T(8,128)(2,1)S(1)}, bf16[512,576]{0,1:T(8,128)(2,1)S(1)}, u32[]{:S(2)}, u32[]{:S(2)}) collective-permute-start(bf16[512,576]{0,1:T(8,128)(2,1)S(1)} %copy.15), channel_id=1, source_target_pairs={{0,6},{2,0},{4,2},{6,4},{1,7},{3,1},{5,3},{7,5},{8,14},{10,8},{12,... | collective-permute-start | bytes 1769480 | tf_op jit(solution)/shard_map/ppermute | solution.py:293
  99.3 7.1 %copy-start.2 = (bf16[512,576]{1,0:T(8,128)(2,1)}, bf16[512,576]{1,0:T(8,128)(2,1)S(1)}, u32[]{:S(2)}) copy-start(bf16[512,576]{1,0:T(8,128)(2,1)S(1)} %copy.17.refs_2_) | copy-start | bytes 1769476
  99.6 6.8 %copy-start.3 = (bf16[512,576]{1,0:T(8,128)(2,1)}, bf16[512,576]{1,0:T(8,128)(2,1)S(1)}, u32[]{:S(2)}) copy-start(bf16[512,576]{1,0:T(8,128)(2,1)S(1)} %copy.18.refs_3_) | copy-start | bytes 1769476
  99.6 16.5 %collective-permute-start.8 = (bf16[256,576]{1,0:T(8,128)(2,1)S(1)}, bf16[256,576]{1,0:T(8,128)(2,1)S(1)}, u32[]{:S(2)}, u32[]{:S(2)}) collective-permute-start(bf16[256,576]{1,0:T(8,128)(2,1)S(1)} %slice.34), channel_id=1, source_target_pairs={{0,2},{2,4},{4,6},{6,0},{1,3},{3,5},{5,7},{7,1},{8,10},{10,12},{12... | collective-permute-start | bytes 884744 | tf_op jit(solution)/shard_map/ppermute | solution.py:310
  102.8 13.3 %collective-permute-start.9 = (bf16[256,576]{1,0:T(8,128)(2,1)S(1)}, bf16[256,576]{1,0:T(8,128)(2,1)S(1)}, u32[]{:S(2)}, u32[]{:S(2)}) collective-permute-start(bf16[256,576]{1,0:T(8,128)(2,1)S(1)} %slice.35), channel_id=1, source_target_pairs={{0,6},{2,0},{4,2},{6,4},{1,7},{3,1},{5,3},{7,5},{8,14},{10,8},{12,... | collective-permute-start | bytes 884744 | tf_op jit(solution)/shard_map/ppermute | solution.py:311
  116.1 0.7 copy-start.15
  116.1 0.8 copy-start.16
  123.0 5.5 %copy-start.6 = (bf16[1024,128]{1,0:T(8,128)(2,1)S(1)}, bf16[1024,128]{1,0:T(8,128)(2,1)}, u32[]{:S(2)}) copy-start(bf16[1024,128]{1,0:T(8,128)(2,1)} %attend.5.own_ref) | copy-start | bytes 786436
  124.3 16.1 %copy-start.4 = (bf16[32,16,1024]{2,1,0:T(8,128)(2,1)}, bf16[32,16,1024]{2,1,0:T(8,128)(2,1)S(1)}, u32[]{:S(2)}) copy-start(bf16[32,16,1024]{2,1,0:T(8,128)(2,1)S(1)} %slice.27.own_ref) | copy-start | bytes 3145732
  124.3 23.7 %collective-permute-start.11 = (bf16[32,16,1024]{2,1,0:T(8,128)(2,1)S(1)}, bf16[32,16,1024]{2,1,0:T(8,128)(2,1)S(1)}, u32[]{:S(2)}, u32[]{:S(2)}) collective-permute-start(bf16[32,16,1024]{2,1,0:T(8,128)(2,1)S(1)} %slice.27.own_ref), channel_id=1, source_target_pairs={{0,8},{8,0},{1,9},{9,1},{2,10},{10,2},{3,11},{11,3},{4,12},{12,4},... | collective-permute-start | bytes 3145736 | tf_op jit(solution)/shard_map/ppermute | solution.py:253
  128.4 3.4 %collective-permute-start.10 = (bf16[1024,128]{1,0:T(8,128)(2,1)S(1)}, bf16[1024,128]{1,0:T(8,128)(2,1)S(1)}, u32[]{:S(2)}, u32[]{:S(2)}) collective-permute-start(bf16[1024,128]{1,0:T(8,128)(2,1)S(1)} %copy-done.6), channel_id=1, source_target_pairs={{0,8},{8,0},{1,9},{9,1},{2,10},{10,2},{3,11},{11,3},{4,12},{12,4},... | collective-permute-start | bytes 786440 | tf_op jit(solution)/shard_map/ppermute | solution.py:253
  131.8 0.7 copy-start.7
  140.4 31.5 %all-to-all-start.1 = ((bf16[8,224,256]{2,1,0:T(8,128)(2,1)}), bf16[8,224,256]{2,1,0:T(8,128)(2,1)S(1)}, u32[]{:S(2)}, u32[]{:S(2)}) async-start(bf16[8,224,256]{2,1,0:T(8,128)(2,1)} %project.1), calls=%async_computation.1 | async-start | bytes 1835008 | tf_op jit(solution)/shard_map/all_to_all | solution.py:324
  148.0 1.0 copy-start.14
  172.0 3.3 %collective-permute-start.12 = (bf16[224,128]{1,0:T(8,128)(2,1)S(1)}, bf16[224,128]{1,0:T(8,128)(2,1)S(1)}, u32[]{:S(2)}, u32[]{:S(2)}) collective-permute-start(bf16[224,128]{1,0:T(8,128)(2,1)S(1)} %slice.37), channel_id=1, source_target_pairs={{0,8},{8,0},{1,9},{9,1},{2,10},{10,2},{3,11},{11,3},{4,12},{12,4},... | collective-permute-start | bytes 172040 | tf_op jit(solution)/shard_map/ppermute | solution.py:253
Sparse Core Ops, SparseCore 0:
  55.5 62.1 all-gather.1

commit v5 on v4

--- a/solution.py
+++ b/solution.py
@@ -31,7 +31,7 @@
 VMEM_LIMIT = 56 * 1024 * 1024
 
 
-def attend_kernel(count, first, last, *refs):
+def attend_kernel(start, count, first, last, *refs):
     place_ref, q_ref = refs[:2]
     kv_refs = refs[2 : 2 + count]
     refs = refs[2 + count :]
@@ -53,8 +53,9 @@
     for group in range(n_keys // ROWS):
         part, slot = divmod(group, TOPK)
         entry = place_ref[slot]
-        start = jnp.where(entry < 0, 2 * NBLK, entry) * BLOCK + place_ref[TOPK + 1 + part]
-        seen = jnp.where(start + row <= query, 0.0, MASKED)
+        first_key = jnp.where(entry < 0, 2 * NBLK, entry) * BLOCK
+        first_key = first_key + place_ref[TOPK + 1 + start + part]
+        seen = jnp.where(first_key + row <= query, 0.0, MASKED)
         bias_ref[group * ROWS : (group + 1) * ROWS, :BLOCK] = seen
         bias_ref[group * ROWS : (group + 1) * ROWS, BLOCK:] = seen
     for pair in range(HEADS_DEV // 2):
@@ -94,7 +95,7 @@
             out_ref[head * V_DIM : (head + 1) * V_DIM, :] = values.astype(jnp.bfloat16)
 
 
-def attend(place, queries, parts, state, up_t):
+def attend(start, place, queries, parts, state, up_t):
     pairs = HEADS_DEV // 2
     n_keys = sum(part.shape[0] for part in parts)
     stat = jax.ShapeDtypeStruct((pairs, 1, 2 * BLOCK), jnp.float32)
@@ -107,7 +108,7 @@
     vmem = pl.BlockSpec(memory_space=pltpu.VMEM)
     rows = HEADS_DEV * BLOCK
     return pl.pallas_call(
-        functools.partial(attend_kernel, len(parts), state is None, last),
+        functools.partial(attend_kernel, start, len(parts), state is None, last),
         out_shape=out,
         in_specs=[pl.BlockSpec(memory_space=pltpu.SMEM)] + [vmem] * (len(operands) - 1),
         out_specs=vmem if last else (vmem,) * 3,
@@ -179,7 +180,7 @@
         ],
         compiler_params=pltpu.CompilerParams(vmem_limit_bytes=VMEM_LIMIT),
         cost_estimate=pl.CostEstimate(
-            flops=40_000_000_000, bytes_accessed=100 << 20, transcendentals=0
+            flops=1_000_000_000, bytes_accessed=4 << 20, transcendentals=0
         ),
         name="index_scores",
     )(place, query, weight, own, other)
@@ -202,7 +203,7 @@
         out_specs=[vmem] * 2,
         compiler_params=pltpu.CompilerParams(vmem_limit_bytes=VMEM_LIMIT),
         cost_estimate=pl.CostEstimate(
-            flops=1000000000, bytes_accessed=4000000, transcendentals=0
+            flops=20000000000, bytes_accessed=20000000, transcendentals=0
         ),
         name="prepare",
     )(latent_query, value_up)
@@ -226,14 +227,20 @@
     )(z, *near)
 
 
-def project_kernel(w_ref, own_ref, other_ref, out_ref):
-    weights = w_ref[...].reshape(NZ * PACKED, 1024)
-    for half, values_ref in enumerate((own_ref, other_ref)):
-        terms = lax.dot_general(
-            weights, values_ref[...], (((1,), (0,)), ((), ())), preferred_element_type=jnp.float32
-        )
-        terms = terms.reshape(NZ, PACKED, BLOCK)[:, 16:, :].reshape(NZ * COLS, BLOCK)
-        out_ref[0, :, half * BLOCK : (half + 1) * BLOCK] = terms.astype(jnp.bfloat16)
+def project_kernel(w_ref, own_ref, other_ref, out_ref, values_ref):
+    @pl.when(pl.program_id(0) == 0)
+    def _():
+        values_ref[:, :BLOCK] = own_ref[...]
+        values_ref[:, BLOCK:] = other_ref[...]
+
+    terms = lax.dot_general(
+        w_ref[...].reshape(NZ * PACKED, 1024),
+        values_ref[...],
+        (((1,), (0,)), ((), ())),
+        preferred_element_type=jnp.float32,
+    )
+    terms = terms.reshape(NZ, PACKED, 2 * BLOCK)[:, 16:, :].reshape(NZ * COLS, 2 * BLOCK)
+    out_ref[0] = terms.astype(jnp.bfloat16)
 
 
 def project(gathered, own, other):
@@ -244,6 +251,7 @@
         grid=(NY,),
         in_specs=[pl.BlockSpec((NZ, PACKED, 1024), lambda i: (i, 0, 0)), values, values],
         out_specs=pl.BlockSpec((1, NZ * COLS, 2 * BLOCK), lambda i: (i, 0, 0)),
+        scratch_shapes=[pltpu.VMEM((HEADS_DEV * V_DIM, 2 * BLOCK), jnp.bfloat16)],
         compiler_params=pltpu.CompilerParams(vmem_limit_bytes=VMEM_LIMIT),
         name="project",
     )(gathered, own, other)
@@ -277,10 +285,16 @@
     listed = block_lists[0]
     safe = jnp.maximum(listed, 0)
     both = jnp.concatenate([safe, swap_core(safe)])
+    offsets = [
+        ((x + step) % NX) * 32 + (w ^ far) * 16 + (core ^ half) * ROWS
+        for step, far in ((0, 0), (0, 1), (3, 0), (3, 1), (1, 0), (1, 1), (2, 0), (2, 1))
+        for half in range(NC)
+    ]
+    place = jnp.concatenate([listed, jnp.stack([ctx_pos * BLOCK] + offsets)])
     queries, up_t = prepare(latent_query, value_up)
     near_z = arrange(z.reshape(1), near)
-    pool, queries, up_t, both, near_z = lax.optimization_barrier(
-        (pool, queries, up_t, both, near_z)
+    pool, queries, up_t, both, place, near_z = lax.optimization_barrier(
+        (pool, queries, up_t, both, place, near_z)
     )
     gathered = lax.all_gather(near_z, "y", axis=0, tiled=True)
 
@@ -292,26 +306,13 @@
     left = lax.ppermute(mine, "x", up)
     right = lax.ppermute(mine, "x", down)
 
-    def place(*parts):
-        offsets = [
-            ((x + step) % NX) * 32 + (w ^ far) * 16 + (core ^ half) * ROWS
-            for step, far in parts
-            for half in range(NC)
-        ]
-        return jnp.concatenate([listed, jnp.stack([ctx_pos * BLOCK] + offsets)])
-
-    places = (
-        place((0, 0), (0, 1)),
-        place((3, 0), (3, 1), (1, 0), (1, 1)),
-        place((2, 0), (2, 1)),
-    )
-    state = attend(places[0], queries, [mine], None, None)
+    state = attend(0, place, queries, [mine], None, None)
     left, right, state = lax.optimization_barrier((left, right, state))
     far_a = lax.ppermute(left[:256], "x", up)
     far_b = lax.ppermute(right[256:], "x", down)
-    state = attend(places[1], queries, [left, right], state, None)
+    state = attend(4, place, queries, [left, right], state, None)
     far_a, far_b, state = lax.optimization_barrier((far_a, far_b, state))
-    values = attend(places[2], queries, [far_a, far_b], state, up_t)
+    values = attend(12, place, queries, [far_a, far_b], state, up_t)
 
     values, gathered = lax.optimization_barrier((values, gathered))
     terms = project(gathered, values, swap_core(values))

time: 184 us -> 182 us (0.989)
  waiting for transfers between devices: 50 us -> 47.2 us
  starting transfers between devices: 64 us -> 66.1 us
    ppermute x3, waiting for transfers between devices: 15.1 us -> 0.01 us  [body(): lax.ppermute(packed, 'z', [(at, at ^ step) for at in range(NZ)])]
    all_to_all x1, waiting for transfers between devices: 0.01 us -> 10.6 us  [body(): pool = lax.all_to_all(wide, CTX, 0, 0)]
    ppermute x1, waiting for transfers between devices: 10.2 us -> 14.8 us  [body(): lax.ppermute(mine, 'w', [(0, 1), (1, 0)])]
    all_to_all x1, waiting for transfers between devices: 15.4 us -> 10.9 us  [body(): shares = lax.all_to_all(terms, HEAD, 0, 0)]
    ppermute x5, waiting for transfers between devices: 2.78 us -> 4.82 us  [swap_core(): return lax.ppermute(value, 'c', [(0, 1), (1, 0)])]
    unnamed x36 -> x30, local copies, waits for them, and re-layouts: 4.18 us -> 3.37 us
  transfers between devices with their start and end apart: 16 -> 16, of which waited for: 9 -> 9; matrix products, arithmetic and copies ran while one was open for 2% -> 3% of each run, Pallas kernels for 23% -> 19%
where the time goes in v5:
time: 182 us; the launch traced here: 181 us
  starting transfers between devices  66.1 us (36%)
  waiting for transfers between devices  47.2 us (26%)
  Pallas kernels  42.3 us (23%)
  between operations  14.4 us (8%)
  local copies, waits for them, and re-layouts  8.73 us (5%)
  other arithmetic  2.56 us (1%)
    pallas_call x3, Pallas kernels, attend(): pl.pallas_call(functools.partial(attend_kernel, start, len(parts), state...  21.9 us
    ppermute x1, waiting for transfers between devices, body(): lax.ppermute(mine, 'w', [(0, 1), (1, 0)])  14.8 us
    ppermute x5, starting transfers between devices, swap_core(): return lax.ppermute(value, 'c', [(0, 1), (1, 0)])  14.3 us
    all_to_all x1, starting transfers between devices, body(): pool = lax.all_to_all(wide, CTX, 0, 0)  13.2 us
    all_to_all x1, waiting for transfers between devices, body(): shares = lax.all_to_all(terms, HEAD, 0, 0)  10.9 us
    all_to_all x1, waiting for transfers between devices, body(): pool = lax.all_to_all(wide, CTX, 0, 0)  10.6 us
    ppermute x3, starting transfers between devices, body(): lax.ppermute(packed, 'z', [(at, at ^ step) for at in range(NZ)])  10.1 us
    ppermute x1, starting transfers between devices, body(): lax.ppermute(mine, 'w', [(0, 1), (1, 0)])  7.94 us
  transfers between devices with their start and end apart: 16, of which 9 were waited for; matrix products, arithmetic and copies ran while one was open for 3% of the time, Pallas kernels for 19%

profile of v5, /device:TPU:65, one launch (start us, length us, event | category | flops | bytes accessed | tf_op | source)
XLA Modules:
  0.0 181.2 jit_solution(11174042252532687475)
XLA Ops:
  7.2 0.8 copy.14
  8.0 0.9 pad_maximum_fusion.2.refs_0_
  8.9 2.1 %collective-permute-start.1 = (bf16[72,1024]{1,0:T(8,128)(2,1)S(1)}, bf16[72,1024]{1,0:T(8,128)(2,1)S(1)}, u32[]{:S(2)}, u32[]{:S(2)}) collective-permute-start(bf16[72,1024]{1,0:T(8,128)(2,1)S(1)} %pad_maximum_fusion.2.refs_0_), channel_id=1, source_target_pairs={{0,16},{16,0},{32,48},{48,32},{1,17},{17,1},{33,49},{49,33},{2,18}... | collective-permute-start | bytes 442376 | tf_op jit(solution)/shard_map/ppermute | solution.py:282
  11.0 5.8 %collective-permute-start.2 = (bf16[72,1024]{1,0:T(8,128)(2,1)S(1)}, bf16[72,1024]{1,0:T(8,128)(2,1)S(1)}, u32[]{:S(2)}, u32[]{:S(2)}) collective-permute-start(bf16[72,1024]{1,0:T(8,128)(2,1)S(1)} %pad_maximum_fusion.2.refs_0_), channel_id=1, source_target_pairs={{0,32},{16,48},{32,0},{48,16},{1,33},{17,49},{33,1},{49,17},{2,34}... | collective-permute-start | bytes 442376 | tf_op jit(solution)/shard_map/ppermute | solution.py:282
  16.8 2.2 %collective-permute-start.3 = (bf16[72,1024]{1,0:T(8,128)(2,1)S(1)}, bf16[72,1024]{1,0:T(8,128)(2,1)S(1)}, u32[]{:S(2)}, u32[]{:S(2)}) collective-permute-start(bf16[72,1024]{1,0:T(8,128)(2,1)S(1)} %pad_maximum_fusion.2.refs_0_), channel_id=1, source_target_pairs={{0,48},{16,32},{32,16},{48,0},{1,49},{17,33},{33,17},{49,1},{2,50}... | collective-permute-start | bytes 442376 | tf_op jit(solution)/shard_map/ppermute | solution.py:282
  19.3 0.9 broadcast_in_dim.12
  20.2 13.2 %all-to-all-start = ((bf16[64,8,576]{2,1,0:T(8,128)(2,1)}), bf16[64,8,576]{2,1,0:T(8,128)(2,1)S(1)}, u32[]{:S(2)}, u32[]{:S(2)}) async-start(bf16[64,8,576]{2,1,0:T(8,128)(2,1)} %bitcast.1), calls=%async_computation | async-start | bytes 1310720 | tf_op jit(solution)/shard_map/all_to_all | solution.py:284
  33.5 2.3 %collective-permute-start = (s32[16]{0:T(128)S(1)}, s32[16]{0:T(128)S(1)}, u32[]{:S(2)}, u32[]{:S(2)}) collective-permute-start(s32[16]{0:T(128)S(1)} %broadcast_maximum_fusion), channel_id=1, source_target_pairs={{0,8},{8,0},{1,9},{9,1},{2,10},{10,2},{3,11},{11,3},{4,12},{12,4},... | collective-permute-start | bytes 200 | tf_op jit(solution)/shard_map/ppermute | solution.py:261
  35.8 3.5 %prepare.1 = (bf16[4,256,576]{2,1,0:T(8,128)(2,1)}, bf16[8,128,512]{2,1,0:T(8,128)(2,1)}) custom-call(bf16[128,4608]{1,0:T(8,128)(2,1)} %lq_ref.1, bf16[8,512,128]{2,1,0:T(8,128)(2,1)} %up_ref.1), custom_call_target="tpu_custom_call" | custom-call | flops 20000000000 | bytes 20000000 | tf_op jit(solution)/shard_map/prepare/pallas_call | solution.py:199
  39.3 0.7 concatenate.17.refs_0_
  40.1 0.6 copy-done.7
  40.8 2.0 %arrange.1 = bf16[4,72,1024]{2,1,0:T(8,128)(2,1)} custom-call(s32[1]{0:T(128)} %bitcast.20.z_ref, bf16[72,1024]{1,0:T(8,128)(2,1)} %copy-done.5, bf16[72,1024]{1,0:T(8,128)(2,1)} %copy-done.7, bf16[72,1024]{1,0:T(8,128)(2,1)} %copy-done.8, bf16[72,1024]{1,0:T(8,128)(2,1)} %copy-done.9), custom_call_target="tpu_custom_call" | custom-call | tf_op jit(solution)/shard_map/arrange/pallas_call | solution.py:220
  42.9 10.6 %all-to-all-done = bf16[64,8,576]{2,1,0:T(8,128)(2,1)S(1)} async-done(((bf16[64,8,576]{2,1,0:T(8,128)(2,1)}), bf16[64,8,576]{2,1,0:T(8,128)(2,1)S(1)}, u32[]{:S(2)}, u32[]{:S(2)}) %all-to-all-start) | async-done | bytes 589856 | tf_op jit(solution)/shard_map/all_to_all | solution.py:284
  53.5 0.6 gather_fusion
  54.2 2.6 %collective-permute-start.4 = (bf16[128,576]{1,0:T(8,128)(2,1)S(1)}, bf16[128,576]{1,0:T(8,128)(2,1)S(1)}, u32[]{:S(2)}, u32[]{:S(2)}) collective-permute-start(bf16[128,576]{1,0:T(8,128)(2,1)S(1)} %get-tuple-element.59), channel_id=1, source_target_pairs={{0,8},{8,0},{1,9},{9,1},{2,10},{10,2},{3,11},{11,3},{4,12},{12,4},... | collective-permute-start | bytes 442376 | tf_op jit(solution)/shard_map/ppermute | solution.py:261
  56.8 1.0 collective-permute-done.4
  57.8 7.9 %collective-permute-start.5 = (bf16[256,576]{1,0:T(8,128)(2,1)S(1)}, bf16[256,576]{1,0:T(8,128)(2,1)S(1)}, u32[]{:S(2)}, u32[]{:S(2)}) collective-permute-start(bf16[256,576]{1,0:T(8,128)(2,1)S(1)} %pad_maximum_fusion.1), channel_id=1, source_target_pairs={{0,1},{1,0},{2,3},{3,2},{4,5},{5,4},{6,7},{7,6},{8,9},{9,8},{10,11... | collective-permute-start | bytes 884744 | tf_op jit(solution)/shard_map/ppermute | solution.py:303
  65.8 14.8 %collective-permute-done.5 = bf16[256,576]{1,0:T(8,128)(2,1)S(1)} collective-permute-done((bf16[256,576]{1,0:T(8,128)(2,1)S(1)}, bf16[256,576]{1,0:T(8,128)(2,1)S(1)}, u32[]{:S(2)}, u32[]{:S(2)}) %collective-permute-start.5) | collective-permute-done | bytes 294944 | tf_op jit(solution)/shard_map/ppermute | solution.py:303
  80.6 0.2 copy.15
  80.9 3.1 %collective-permute-start.6 = (bf16[512,576]{0,1:T(8,128)(2,1)S(1)}, bf16[512,576]{0,1:T(8,128)(2,1)S(1)}, u32[]{:S(2)}, u32[]{:S(2)}) collective-permute-start(bf16[512,576]{0,1:T(8,128)(2,1)S(1)} %copy.15), channel_id=1, source_target_pairs={{0,2},{2,4},{4,6},{6,0},{1,3},{3,5},{5,7},{7,1},{8,10},{10,12},{12... | collective-permute-start | bytes 1769480 | tf_op jit(solution)/shard_map/ppermute | solution.py:306
  84.0 3.4 %collective-permute-start.7 = (bf16[512,576]{0,1:T(8,128)(2,1)S(1)}, bf16[512,576]{0,1:T(8,128)(2,1)S(1)}, u32[]{:S(2)}, u32[]{:S(2)}) collective-permute-start(bf16[512,576]{0,1:T(8,128)(2,1)S(1)} %copy.15), channel_id=1, source_target_pairs={{0,6},{2,0},{4,2},{6,4},{1,7},{3,1},{5,3},{7,5},{8,14},{10,8},{12,... | collective-permute-start | bytes 1769480 | tf_op jit(solution)/shard_map/ppermute | solution.py:307
  87.4 6.1 %attend.3 = (f32[4,1,256]{2,1,0:T(1,128)}, f32[4,1,256]{2,1,0:T(1,128)}, f32[4,512,256]{2,1,0:T(8,128)}) custom-call(s32[33]{0:T(128)} %concatenate.17.refs_0_, bf16[4,256,576]{2,1,0:T(8,128)(2,1)} %get-tuple-element.33.refs_1_, bf16[512,576]{1,0:T(8,128)(2,1)} %copy-done.1), custom_call_target="tpu_custom_call" | custom-call | flops 20000000000 | bytes 4194304 | tf_op jit(solution)/shard_map/attend/pallas_call | solution.py:110
  93.5 4.4 %collective-permute-done.6 = bf16[512,576]{0,1:T(8,128)(2,1)S(1)} collective-permute-done((bf16[512,576]{0,1:T(8,128)(2,1)S(1)}, bf16[512,576]{0,1:T(8,128)(2,1)S(1)}, u32[]{:S(2)}, u32[]{:S(2)}) %collective-permute-start.6) | collective-permute-done | bytes 589856 | tf_op jit(solution)/shard_map/ppermute | solution.py:306
  98.0 1.6 collective-permute-done.7
  99.6 0.3 copy.17.refs_2_
  99.9 0.3 copy.18.refs_3_
  100.3 3.1 %collective-permute-start.8 = (bf16[256,576]{1,0:T(8,128)(2,1)S(1)}, bf16[256,576]{1,0:T(8,128)(2,1)S(1)}, u32[]{:S(2)}, u32[]{:S(2)}) collective-permute-start(bf16[256,576]{1,0:T(8,128)(2,1)S(1)} %slice.34), channel_id=1, source_target_pairs={{0,2},{2,4},{4,6},{6,0},{1,3},{3,5},{5,7},{7,1},{8,10},{10,12},{12... | collective-permute-start | bytes 884744 | tf_op jit(solution)/shard_map/ppermute | solution.py:311
  103.4 3.6 %collective-permute-start.9 = (bf16[256,576]{1,0:T(8,128)(2,1)S(1)}, bf16[256,576]{1,0:T(8,128)(2,1)S(1)}, u32[]{:S(2)}, u32[]{:S(2)}) collective-permute-start(bf16[256,576]{1,0:T(8,128)(2,1)S(1)} %slice.35), channel_id=1, source_target_pairs={{0,6},{2,0},{4,2},{6,4},{1,7},{3,1},{5,3},{7,5},{8,14},{10,8},{12,... | collective-permute-start | bytes 884744 | tf_op jit(solution)/shard_map/ppermute | solution.py:312
  107.0 9.7 %attend.4 = (f32[4,1,256]{2,1,0:T(1,128)}, f32[4,1,256]{2,1,0:T(1,128)}, f32[4,512,256]{2,1,0:T(8,128)}) custom-call(s32[33]{0:T(128)} %concatenate.17.refs_0_, bf16[4,256,576]{2,1,0:T(8,128)(2,1)} %get-tuple-element.33.refs_1_, bf16[512,576]{1,0:T(8,128)(2,1)} %copy-done.2, bf16[512,576]{1,0:T(8,128)(2,1)} %copy-done.3, ...), custom_call_target="tpu_custom_call" | custom-call | flops 20000000000 | bytes 4194304 | tf_op jit(solution)/shard_map/attend/pallas_call | solution.py:110
  116.8 0.7 copy-done.12
  117.5 0.1 copy-done.13
  117.6 6.0 %attend.5.own_ref = bf16[1024,128]{1,0:T(8,128)(2,1)} custom-call(s32[33]{0:T(128)} %concatenate.17.refs_0_, bf16[4,256,576]{2,1,0:T(8,128)(2,1)} %get-tuple-element.33.refs_1_, bf16[256,576]{1,0:T(8,128)(2,1)} %copy-done.12, bf16[256,576]{1,0:T(8,128)(2,1)} %copy-done.13, f32[4,1,256]{2,1,0:T(1,128)} %get-tuple-element.49.refs_4_, ...), custom_call_target="tpu_custom_call" | custom-call | flops 20000000000 | bytes 4194304 | tf_op jit(solution)/shard_map/attend/pallas_call | solution.py:110
  123.6 4.5 %collective-permute-start.10 = (bf16[1024,128]{1,0:T(8,128)(2,1)}, bf16[1024,128]{1,0:T(8,128)(2,1)S(1)}, u32[]{:S(2)}, u32[]{:S(2)}) collective-permute-start(bf16[1024,128]{1,0:T(8,128)(2,1)} %attend.5.own_ref), channel_id=1, source_target_pairs={{0,8},{8,0},{1,9},{9,1},{2,10},{10,2},{3,11},{11,3},{4,12},{12,4},... | collective-permute-start | bytes 786440 | tf_op jit(solution)/shard_map/ppermute | solution.py:261
  128.1 1.4 collective-permute-done.10.other_ref
  129.4 0.7 copy-done.6
  130.1 7.3 %project.1 = bf16[8,224,256]{2,1,0:T(8,128)(2,1)} custom-call(bf16[32,72,1024]{2,1,0:T(8,128)(2,1)} %all-gather.2.cloned.1.call-done.w_ref, bf16[1024,128]{1,0:T(8,128)(2,1)} %attend.5.own_ref, bf16[1024,128]{1,0:T(8,128)(2,1)} %copy-done.6), custom_call_target="tpu_custom_call" | custom-call | tf_op jit(solution)/shard_map/project/pallas_call | solution.py:248
  137.4 7.3 %all-to-all-start.1 = ((bf16[8,224,256]{2,1,0:T(8,128)(2,1)}), bf16[8,224,256]{2,1,0:T(8,128)(2,1)S(1)}, u32[]{:S(2)}, u32[]{:S(2)}) async-start(bf16[8,224,256]{2,1,0:T(8,128)(2,1)} %project.1), calls=%async_computation.1 | async-start | bytes 1835008 | tf_op jit(solution)/shard_map/all_to_all | solution.py:325
  144.8 1.3 slice.27.own_ref
  146.1 2.6 %collective-permute-start.11 = (bf16[32,16,1024]{2,1,0:T(8,128)(2,1)S(1)}, bf16[32,16,1024]{2,1,0:T(8,128)(2,1)S(1)}, u32[]{:S(2)}, u32[]{:S(2)}) collective-permute-start(bf16[32,16,1024]{2,1,0:T(8,128)(2,1)S(1)} %slice.27.own_ref), channel_id=1, source_target_pairs={{0,8},{8,0},{1,9},{9,1},{2,10},{10,2},{3,11},{11,3},{4,12},{12,4},... | collective-permute-start | bytes 3145736 | tf_op jit(solution)/shard_map/ppermute | solution.py:261
  148.7 0.7 pad_add_fusion.1.place_ref
  149.3 1.6 collective-permute-done.11.other_ref
  150.9 1.0 copy-done.11
  151.9 7.5 %index_scores.1 = f32[16,8192]{1,0:T(8,128)} custom-call(s32[2]{0:T(128)} %pad_add_fusion.1.place_ref, bf16[16,4096]{1,0:T(8,128)(2,1)} %query_ref.1, f32[16,32]{1,0:T(8,128)} %w_ref.1, bf16[32,16,1024]{2,1,0:T(8,128)(2,1)} %copy-done.4, bf16[32,16,1024]{2,1,0:T(8,128)(2,1)} %copy-done.11), custom_call_target="tpu_custom_call" | custom-call | flops 1000000000 | bytes 4194304 | tf_op jit(solution)/shard_map/index_scores/pallas_call | solution.py:171
  159.4 10.9 %all-to-all-done.1 = bf16[8,224,256]{2,1,0:T(8,128)(2,1)S(1)} async-done(((bf16[8,224,256]{2,1,0:T(8,128)(2,1)}), bf16[8,224,256]{2,1,0:T(8,128)(2,1)S(1)}, u32[]{:S(2)}, u32[]{:S(2)}) %all-to-all-start.1) | async-done | bytes 917536 | tf_op jit(solution)/shard_map/all_to_all | solution.py:325
  170.3 0.1 reduce_sum.12
  170.4 2.4 %collective-permute-start.12 = (bf16[224,128]{1,0:T(8,128)(2,1)S(1)}, bf16[224,128]{1,0:T(8,128)(2,1)S(1)}, u32[]{:S(2)}, u32[]{:S(2)}) collective-permute-start(bf16[224,128]{1,0:T(8,128)(2,1)S(1)} %slice.37), channel_id=1, source_target_pairs={{0,8},{8,0},{1,9},{9,1},{2,10},{10,2},{3,11},{11,3},{4,12},{12,4},... | collective-permute-start | bytes 172040 | tf_op jit(solution)/shard_map/ppermute | solution.py:261
  172.8 0.9 collective-permute-done.12
  173.7 0.7 pad_maximum_fusion.3
  (45 shorter events, 0.8 us)
Async XLA Ops:
  7.2 11.9 %copy-start = (bf16[128,576]{0,1:T(8,128)(2,1)S(1)}, bf16[128,576]{0,1:T(8,128)(2,1)}, u32[]{:S(2)}) copy-start(bf16[128,576]{0,1:T(8,128)(2,1)} %param.12) | copy-start | bytes 442372
  8.9 30.4 %copy-start.5 = (bf16[72,1024]{1,0:T(8,128)(2,1)}, bf16[72,1024]{1,0:T(8,128)(2,1)S(1)}, u32[]{:S(2)}) copy-start(bf16[72,1024]{1,0:T(8,128)(2,1)S(1)} %pad_maximum_fusion.2.refs_0_) | copy-start | bytes 442372
  8.9 24.6 %copy-start.10 = (s32[1,16]{1,0:T(1,128)S(1)}, s32[1,16]{1,0:T(1,128)}, u32[]{:S(2)}) copy-start(s32[1,16]{1,0:T(1,128)} %param.13) | copy-start | bytes 196
  8.9 31.1 %collective-permute-start.1 = (bf16[72,1024]{1,0:T(8,128)(2,1)S(1)}, bf16[72,1024]{1,0:T(8,128)(2,1)S(1)}, u32[]{:S(2)}, u32[]{:S(2)}) collective-permute-start(bf16[72,1024]{1,0:T(8,128)(2,1)S(1)} %pad_maximum_fusion.2.refs_0_), channel_id=1, source_target_pairs={{0,16},{16,0},{32,48},{48,32},{1,17},{17,1},{33,49},{49,33},{2,18}... | collective-permute-start | bytes 442376 | tf_op jit(solution)/shard_map/ppermute | solution.py:282
  11.0 29.1 %collective-permute-start.2 = (bf16[72,1024]{1,0:T(8,128)(2,1)S(1)}, bf16[72,1024]{1,0:T(8,128)(2,1)S(1)}, u32[]{:S(2)}, u32[]{:S(2)}) collective-permute-start(bf16[72,1024]{1,0:T(8,128)(2,1)S(1)} %pad_maximum_fusion.2.refs_0_), channel_id=1, source_target_pairs={{0,32},{16,48},{32,0},{48,16},{1,33},{17,49},{33,1},{49,17},{2,34}... | collective-permute-start | bytes 442376 | tf_op jit(solution)/shard_map/ppermute | solution.py:282
  16.8 23.3 %collective-permute-start.3 = (bf16[72,1024]{1,0:T(8,128)(2,1)S(1)}, bf16[72,1024]{1,0:T(8,128)(2,1)S(1)}, u32[]{:S(2)}, u32[]{:S(2)}) collective-permute-start(bf16[72,1024]{1,0:T(8,128)(2,1)S(1)} %pad_maximum_fusion.2.refs_0_), channel_id=1, source_target_pairs={{0,48},{16,32},{32,16},{48,0},{1,49},{17,33},{33,17},{49,1},{2,50}... | collective-permute-start | bytes 442376 | tf_op jit(solution)/shard_map/ppermute | solution.py:282
  20.2 33.3 %all-to-all-start = ((bf16[64,8,576]{2,1,0:T(8,128)(2,1)}), bf16[64,8,576]{2,1,0:T(8,128)(2,1)S(1)}, u32[]{:S(2)}, u32[]{:S(2)}) async-start(bf16[64,8,576]{2,1,0:T(8,128)(2,1)} %bitcast.1), calls=%async_computation | async-start | bytes 1310720 | tf_op jit(solution)/shard_map/all_to_all | solution.py:284
  33.4 90.2 %all-gather.2.cloned.1.call-start = ((), (), s32[]{:S(2)}) async-start(), calls=%async_computation.2 | async-start | bytes 5308416 | tf_op jit(solution)/shard_map/all_gather | solution.py:299
  33.5 6.5 %collective-permute-start = (s32[16]{0:T(128)S(1)}, s32[16]{0:T(128)S(1)}, u32[]{:S(2)}, u32[]{:S(2)}) collective-permute-start(s32[16]{0:T(128)S(1)} %broadcast_maximum_fusion), channel_id=1, source_target_pairs={{0,8},{8,0},{1,9},{9,1},{2,10},{10,2},{3,11},{11,3},{4,12},{12,4},... | collective-permute-start | bytes 200 | tf_op jit(solution)/shard_map/ppermute | solution.py:261
  40.1 0.7 copy-start.7
  40.1 0.7 copy-start.8
  40.1 0.7 copy-start.9
  54.2 3.6 %collective-permute-start.4 = (bf16[128,576]{1,0:T(8,128)(2,1)S(1)}, bf16[128,576]{1,0:T(8,128)(2,1)S(1)}, u32[]{:S(2)}, u32[]{:S(2)}) collective-permute-start(bf16[128,576]{1,0:T(8,128)(2,1)S(1)} %get-tuple-element.59), channel_id=1, source_target_pairs={{0,8},{8,0},{1,9},{9,1},{2,10},{10,2},{3,11},{11,3},{4,12},{12,4},... | collective-permute-start | bytes 442376 | tf_op jit(solution)/shard_map/ppermute | solution.py:261
  57.8 22.7 %collective-permute-start.5 = (bf16[256,576]{1,0:T(8,128)(2,1)S(1)}, bf16[256,576]{1,0:T(8,128)(2,1)S(1)}, u32[]{:S(2)}, u32[]{:S(2)}) collective-permute-start(bf16[256,576]{1,0:T(8,128)(2,1)S(1)} %pad_maximum_fusion.1), channel_id=1, source_target_pairs={{0,1},{1,0},{2,3},{3,2},{4,5},{5,4},{6,7},{7,6},{8,9},{9,8},{10,11... | collective-permute-start | bytes 884744 | tf_op jit(solution)/shard_map/ppermute | solution.py:303
  80.6 6.8 %copy-start.1 = (bf16[512,576]{1,0:T(8,128)(2,1)}, bf16[512,576]{1,0:T(8,128)(2,1)S(1)}, u32[]{:S(2)}) copy-start(bf16[512,576]{1,0:T(8,128)(2,1)S(1)} %pad_maximum_fusion.refs_2_) | copy-start | bytes 1769476
  80.9 17.1 %collective-permute-start.6 = (bf16[512,576]{0,1:T(8,128)(2,1)S(1)}, bf16[512,576]{0,1:T(8,128)(2,1)S(1)}, u32[]{:S(2)}, u32[]{:S(2)}) collective-permute-start(bf16[512,576]{0,1:T(8,128)(2,1)S(1)} %copy.15), channel_id=1, source_target_pairs={{0,2},{2,4},{4,6},{6,0},{1,3},{3,5},{5,7},{7,1},{8,10},{10,12},{12... | collective-permute-start | bytes 1769480 | tf_op jit(solution)/shard_map/ppermute | solution.py:306
  84.0 15.6 %collective-permute-start.7 = (bf16[512,576]{0,1:T(8,128)(2,1)S(1)}, bf16[512,576]{0,1:T(8,128)(2,1)S(1)}, u32[]{:S(2)}, u32[]{:S(2)}) collective-permute-start(bf16[512,576]{0,1:T(8,128)(2,1)S(1)} %copy.15), channel_id=1, source_target_pairs={{0,6},{2,0},{4,2},{6,4},{1,7},{3,1},{5,3},{7,5},{8,14},{10,8},{12,... | collective-permute-start | bytes 1769480 | tf_op jit(solution)/shard_map/ppermute | solution.py:307
  99.9 7.1 %copy-start.2 = (bf16[512,576]{1,0:T(8,128)(2,1)}, bf16[512,576]{1,0:T(8,128)(2,1)S(1)}, u32[]{:S(2)}) copy-start(bf16[512,576]{1,0:T(8,128)(2,1)S(1)} %copy.17.refs_2_) | copy-start | bytes 1769476
  100.2 6.8 %copy-start.3 = (bf16[512,576]{1,0:T(8,128)(2,1)}, bf16[512,576]{1,0:T(8,128)(2,1)S(1)}, u32[]{:S(2)}) copy-start(bf16[512,576]{1,0:T(8,128)(2,1)S(1)} %copy.18.refs_3_) | copy-start | bytes 1769476
  100.3 16.5 %collective-permute-start.8 = (bf16[256,576]{1,0:T(8,128)(2,1)S(1)}, bf16[256,576]{1,0:T(8,128)(2,1)S(1)}, u32[]{:S(2)}, u32[]{:S(2)}) collective-permute-start(bf16[256,576]{1,0:T(8,128)(2,1)S(1)} %slice.34), channel_id=1, source_target_pairs={{0,2},{2,4},{4,6},{6,0},{1,3},{3,5},{5,7},{7,1},{8,10},{10,12},{12... | collective-permute-start | bytes 884744 | tf_op jit(solution)/shard_map/ppermute | solution.py:311
  103.4 13.3 %collective-permute-start.9 = (bf16[256,576]{1,0:T(8,128)(2,1)S(1)}, bf16[256,576]{1,0:T(8,128)(2,1)S(1)}, u32[]{:S(2)}, u32[]{:S(2)}) collective-permute-start(bf16[256,576]{1,0:T(8,128)(2,1)S(1)} %slice.35), channel_id=1, source_target_pairs={{0,6},{2,0},{4,2},{6,4},{1,7},{3,1},{5,3},{7,5},{8,14},{10,8},{12,... | collective-permute-start | bytes 884744 | tf_op jit(solution)/shard_map/ppermute | solution.py:312
  116.7 0.7 copy-start.12
  116.7 0.8 copy-start.13
  123.6 5.8 %collective-permute-start.10 = (bf16[1024,128]{1,0:T(8,128)(2,1)}, bf16[1024,128]{1,0:T(8,128)(2,1)S(1)}, u32[]{:S(2)}, u32[]{:S(2)}) collective-permute-start(bf16[1024,128]{1,0:T(8,128)(2,1)} %attend.5.own_ref), channel_id=1, source_target_pairs={{0,8},{8,0},{1,9},{9,1},{2,10},{10,2},{3,11},{11,3},{4,12},{12,4},... | collective-permute-start | bytes 786440 | tf_op jit(solution)/shard_map/ppermute | solution.py:261
  129.4 0.7 copy-start.6
  137.4 32.8 %all-to-all-start.1 = ((bf16[8,224,256]{2,1,0:T(8,128)(2,1)}), bf16[8,224,256]{2,1,0:T(8,128)(2,1)S(1)}, u32[]{:S(2)}, u32[]{:S(2)}) async-start(bf16[8,224,256]{2,1,0:T(8,128)(2,1)} %project.1), calls=%async_computation.1 | async-start | bytes 1835008 | tf_op jit(solution)/shard_map/all_to_all | solution.py:325
  146.1 4.8 %copy-start.4 = (bf16[32,16,1024]{2,1,0:T(8,128)(2,1)}, bf16[32,16,1024]{2,1,0:T(8,128)(2,1)S(1)}, u32[]{:S(2)}) copy-start(bf16[32,16,1024]{2,1,0:T(8,128)(2,1)S(1)} %slice.27.own_ref) | copy-start | bytes 3145732
  146.1 4.8 %collective-permute-start.11 = (bf16[32,16,1024]{2,1,0:T(8,128)(2,1)S(1)}, bf16[32,16,1024]{2,1,0:T(8,128)(2,1)S(1)}, u32[]{:S(2)}, u32[]{:S(2)}) collective-permute-start(bf16[32,16,1024]{2,1,0:T(8,128)(2,1)S(1)} %slice.27.own_ref), channel_id=1, source_target_pairs={{0,8},{8,0},{1,9},{9,1},{2,10},{10,2},{3,11},{11,3},{4,12},{12,4},... | collective-permute-start | bytes 3145736 | tf_op jit(solution)/shard_map/ppermute | solution.py:261
  150.9 1.0 copy-start.11
  170.4 3.3 %collective-permute-start.12 = (bf16[224,128]{1,0:T(8,128)(2,1)S(1)}, bf16[224,128]{1,0:T(8,128)(2,1)S(1)}, u32[]{:S(2)}, u32[]{:S(2)}) collective-permute-start(bf16[224,128]{1,0:T(8,128)(2,1)S(1)} %slice.37), channel_id=1, source_target_pairs={{0,8},{8,0},{1,9},{9,1},{2,10},{10,2},{3,11},{11,3},{4,12},{12,4},... | collective-permute-start | bytes 172040 | tf_op jit(solution)/shard_map/ppermute | solution.py:261
Sparse Core Ops, SparseCore 0:
  53.6 61.0 all-gather.1

commit v6 on v5

--- a/solution.py
+++ b/solution.py
@@ -18,7 +18,7 @@
 BLOCK = 128
 TOPK = 16
 NBLK = 64
-ROWS = 8
+ROWS = 16
 PACKED = 72
 COLS = 56
 NY, NZ, NC, NX, NW = 8, 4, 2, 4, 2
@@ -203,7 +203,7 @@
         out_specs=[vmem] * 2,
         compiler_params=pltpu.CompilerParams(vmem_limit_bytes=VMEM_LIMIT),
         cost_estimate=pl.CostEstimate(
-            flops=20000000000, bytes_accessed=20000000, transcendentals=0
+            flops=80000000000, bytes_accessed=209715200, transcendentals=0
         ),
         name="prepare",
     )(latent_query, value_up)
@@ -273,7 +273,7 @@
     ctx_pos = (y * NZ + z) * NC + core
     head_pos = x * NW + w
 
-    own = lax.dynamic_slice_in_dim(latent, head_pos * 16, 16, 0).reshape(1, NC, ROWS, LAT)
+    own = lax.dynamic_slice_in_dim(latent, x * 32, 32, 0).reshape(1, NC, ROWS, LAT)
     wide = jnp.broadcast_to(own, (NY * NZ, NC, ROWS, LAT)).reshape(NBLK, ROWS, LAT)
 
     key_rows = jnp.moveaxis(index_key.reshape(8, 16, IDX_DIM), 0, 1).reshape(16, 1024)
@@ -286,21 +286,20 @@
     safe = jnp.maximum(listed, 0)
     both = jnp.concatenate([safe, swap_core(safe)])
     offsets = [
-        ((x + step) % NX) * 32 + (w ^ far) * 16 + (core ^ half) * ROWS
-        for step, far in ((0, 0), (0, 1), (3, 0), (3, 1), (1, 0), (1, 1), (2, 0), (2, 1))
+        ((x + step) % NX) * 32 + (core ^ half) * ROWS
+        for step in (0, 3, 1, 2)
         for half in range(NC)
     ]
     place = jnp.concatenate([listed, jnp.stack([ctx_pos * BLOCK] + offsets)])
     queries, up_t = prepare(latent_query, value_up)
     near_z = arrange(z.reshape(1), near)
-    pool, queries, up_t, both, place, near_z = lax.optimization_barrier(
-        (pool, queries, up_t, both, place, near_z)
+    gathered = lax.all_gather(near_z, "y", axis=0, tiled=True)
+    pool, queries, up_t, both, place = lax.optimization_barrier(
+        (pool, queries, up_t, both, place)
     )
-    gathered = lax.all_gather(near_z, "y", axis=0, tiled=True)
 
     picked = jnp.take(pool, both, axis=0, mode="clip").reshape(2, TOPK * ROWS, LAT)
     mine = jnp.concatenate([picked[0], swap_core(picked[1])], axis=0)
-    mine = jnp.concatenate([mine, lax.ppermute(mine, "w", [(0, 1), (1, 0)])], axis=0)
     up = [(at, (at + 1) % NX) for at in range(NX)]
     down = [(at, (at - 1) % NX) for at in range(NX)]
     left = lax.ppermute(mine, "x", up)
@@ -310,9 +309,9 @@
     left, right, state = lax.optimization_barrier((left, right, state))
     far_a = lax.ppermute(left[:256], "x", up)
     far_b = lax.ppermute(right[256:], "x", down)
-    state = attend(4, place, queries, [left, right], state, None)
+    state = attend(2, place, queries, [left, right], state, None)
     far_a, far_b, state = lax.optimization_barrier((far_a, far_b, state))
-    values = attend(12, place, queries, [far_a, far_b], state, up_t)
+    values = attend(6, place, queries, [far_a, far_b], state, up_t)
 
     values, gathered = lax.optimization_barrier((values, gathered))
     terms = project(gathered, values, swap_core(values))

time: 182 us -> 182 us (level)
  the two profiles are of different devices: /device:TPU:65 before, /device:TPU:89 now
where the time goes in v6:
time: 182 us; the launch traced here: 181 us
  starting transfers between devices  60.5 us (33%)
  waiting for transfers between devices  52.1 us (29%)
  Pallas kernels  42.3 us (23%)
  between operations  14.4 us (8%)
  local copies, waits for them, and re-layouts  9.02 us (5%)
  other arithmetic  2.52 us (1%)
    all_to_all x1, waiting for transfers between devices, body(): pool = lax.all_to_all(wide, CTX, 0, 0)  26.5 us
    pallas_call x3, Pallas kernels, attend(): pl.pallas_call(functools.partial(attend_kernel, start, len(parts), state...  21.9 us
    ppermute x5, starting transfers between devices, swap_core(): return lax.ppermute(value, 'c', [(0, 1), (1, 0)])  13.9 us
    all_to_all x1, waiting for transfers between devices, body(): shares = lax.all_to_all(terms, HEAD, 0, 0)  13.8 us
    all_to_all x1, starting transfers between devices, body(): pool = lax.all_to_all(wide, CTX, 0, 0)  13.1 us
    all_to_all x1, starting transfers between devices, body(): shares = lax.all_to_all(terms, HEAD, 0, 0)  10.3 us
    ppermute x3, starting transfers between devices, body(): lax.ppermute(packed, 'z', [(at, at ^ step) for at in range(NZ)])  9.92 us
    pallas_call x1, Pallas kernels, index_part(): pl.pallas_call(index_kernel, out_shape=jax.ShapeDtypeStruct((16, NBLK * B...  7.52 us
  transfers between devices with their start and end apart: 15, of which 8 were waited for; matrix products, arithmetic and copies ran while one was open for 3% of the time, Pallas kernels for 19%

profile of v6, /device:TPU:89, one launch (start us, length us, event | category | flops | bytes accessed | tf_op | source)
XLA Modules:
  0.0 180.8 jit_solution(16351010876837808753)
XLA Ops:
  7.2 0.8 copy.20
  8.0 0.9 pad_maximum_fusion.1.refs_0_
  8.9 1.9 %collective-permute-start.6 = (bf16[72,1024]{1,0:T(8,128)(2,1)S(1)}, bf16[72,1024]{1,0:T(8,128)(2,1)S(1)}, u32[]{:S(2)}, u32[]{:S(2)}) collective-permute-start(bf16[72,1024]{1,0:T(8,128)(2,1)S(1)} %pad_maximum_fusion.1.refs_0_), channel_id=1, source_target_pairs={{0,16},{16,0},{32,48},{48,32},{1,17},{17,1},{33,49},{49,33},{2,18}... | collective-permute-start | bytes 442376 | tf_op jit(solution)/shard_map/ppermute | solution.py:282
  10.9 5.8 %collective-permute-start.7 = (bf16[72,1024]{1,0:T(8,128)(2,1)S(1)}, bf16[72,1024]{1,0:T(8,128)(2,1)S(1)}, u32[]{:S(2)}, u32[]{:S(2)}) collective-permute-start(bf16[72,1024]{1,0:T(8,128)(2,1)S(1)} %pad_maximum_fusion.1.refs_0_), channel_id=1, source_target_pairs={{0,32},{16,48},{32,0},{48,16},{1,33},{17,49},{33,1},{49,17},{2,34}... | collective-permute-start | bytes 442376 | tf_op jit(solution)/shard_map/ppermute | solution.py:282
  16.7 2.2 %collective-permute-start.8 = (bf16[72,1024]{1,0:T(8,128)(2,1)S(1)}, bf16[72,1024]{1,0:T(8,128)(2,1)S(1)}, u32[]{:S(2)}, u32[]{:S(2)}) collective-permute-start(bf16[72,1024]{1,0:T(8,128)(2,1)S(1)} %pad_maximum_fusion.1.refs_0_), channel_id=1, source_target_pairs={{0,48},{16,32},{32,16},{48,0},{1,49},{17,33},{33,17},{49,1},{2,50}... | collective-permute-start | bytes 442376 | tf_op jit(solution)/shard_map/ppermute | solution.py:282
  18.9 0.1 constant_dynamic-slice_fusion
  19.0 0.1 copy.21
  19.1 1.2 broadcast_in_dim.12
  20.4 13.1 %all-to-all-start = ((bf16[64,16,576]{2,1,0:T(8,128)(2,1)}), bf16[64,16,576]{2,1,0:T(8,128)(2,1)S(1)}, u32[]{:S(2)}, u32[]{:S(2)}) async-start(bf16[64,16,576]{2,1,0:T(8,128)(2,1)} %bitcast.1), calls=%async_computation | async-start | bytes 2621440 | tf_op jit(solution)/shard_map/all_to_all | solution.py:284
  33.5 2.3 %collective-permute-start = (s32[16]{0:T(128)S(1)}, s32[16]{0:T(128)S(1)}, u32[]{:S(2)}, u32[]{:S(2)}) collective-permute-start(s32[16]{0:T(128)S(1)} %broadcast_maximum_fusion), channel_id=1, source_target_pairs={{0,8},{8,0},{1,9},{9,1},{2,10},{10,2},{3,11},{11,3},{4,12},{12,4},... | collective-permute-start | bytes 200 | tf_op jit(solution)/shard_map/ppermute | solution.py:261
  35.9 0.6 copy-done.7
  36.6 2.0 %arrange.1 = bf16[4,72,1024]{2,1,0:T(8,128)(2,1)} custom-call(s32[1]{0:T(128)} %bitcast.14.z_ref, bf16[72,1024]{1,0:T(8,128)(2,1)} %copy-done.5, bf16[72,1024]{1,0:T(8,128)(2,1)} %copy-done.7, bf16[72,1024]{1,0:T(8,128)(2,1)} %copy-done.8, bf16[72,1024]{1,0:T(8,128)(2,1)} %copy-done.9), custom_call_target="tpu_custom_call" | custom-call | tf_op jit(solution)/shard_map/arrange/pallas_call | solution.py:220
  38.6 3.5 %prepare.1 = (bf16[4,256,576]{2,1,0:T(8,128)(2,1)}, bf16[8,128,512]{2,1,0:T(8,128)(2,1)}) custom-call(bf16[128,4608]{1,0:T(8,128)(2,1)} %lq_ref.1, bf16[8,512,128]{2,1,0:T(8,128)(2,1)} %up_ref.1), custom_call_target="tpu_custom_call" | custom-call | flops 80000000000 | bytes 209715200 | tf_op jit(solution)/shard_map/prepare/pallas_call | solution.py:199
  42.1 0.6 concatenate.13.refs_0_
  42.8 26.5 %all-to-all-done = bf16[64,16,576]{2,1,0:T(8,128)(2,1)S(1)} async-done(((bf16[64,16,576]{2,1,0:T(8,128)(2,1)}), bf16[64,16,576]{2,1,0:T(8,128)(2,1)S(1)}, u32[]{:S(2)}, u32[]{:S(2)}) %all-to-all-start) | async-done | bytes 1179680 | tf_op jit(solution)/shard_map/all_to_all | solution.py:284
  69.4 0.7 gather_fusion
  70.1 2.8 %collective-permute-start.1 = (bf16[256,576]{1,0:T(8,128)(2,1)S(1)}, bf16[256,576]{1,0:T(8,128)(2,1)S(1)}, u32[]{:S(2)}, u32[]{:S(2)}) collective-permute-start(bf16[256,576]{1,0:T(8,128)(2,1)S(1)} %bitcast.31), channel_id=1, source_target_pairs={{0,8},{8,0},{1,9},{9,1},{2,10},{10,2},{3,11},{11,3},{4,12},{12,4},... | collective-permute-start | bytes 884744 | tf_op jit(solution)/shard_map/ppermute | solution.py:261
  72.9 1.2 collective-permute-done.1
  74.2 0.2 copy.14
  74.4 3.1 %collective-permute-start.2 = (bf16[512,576]{0,1:T(8,128)(2,1)S(1)}, bf16[512,576]{0,1:T(8,128)(2,1)S(1)}, u32[]{:S(2)}, u32[]{:S(2)}) collective-permute-start(bf16[512,576]{0,1:T(8,128)(2,1)S(1)} %copy.14), channel_id=1, source_target_pairs={{0,2},{2,4},{4,6},{6,0},{1,3},{3,5},{5,7},{7,1},{8,10},{10,12},{12... | collective-permute-start | bytes 1769480 | tf_op jit(solution)/shard_map/ppermute | solution.py:305
  77.6 3.4 %collective-permute-start.3 = (bf16[512,576]{0,1:T(8,128)(2,1)S(1)}, bf16[512,576]{0,1:T(8,128)(2,1)S(1)}, u32[]{:S(2)}, u32[]{:S(2)}) collective-permute-start(bf16[512,576]{0,1:T(8,128)(2,1)S(1)} %copy.14), channel_id=1, source_target_pairs={{0,6},{2,0},{4,2},{6,4},{1,7},{3,1},{5,3},{7,5},{8,14},{10,8},{12,... | collective-permute-start | bytes 1769480 | tf_op jit(solution)/shard_map/ppermute | solution.py:306
  81.0 6.1 %attend.3 = (f32[4,1,256]{2,1,0:T(1,128)}, f32[4,1,256]{2,1,0:T(1,128)}, f32[4,512,256]{2,1,0:T(8,128)}) custom-call(s32[25]{0:T(128)} %concatenate.13.refs_0_, bf16[4,256,576]{2,1,0:T(8,128)(2,1)} %get-tuple-element.32.refs_1_, bf16[512,576]{1,0:T(8,128)(2,1)} %copy-done.1), custom_call_target="tpu_custom_call" | custom-call | flops 20000000000 | bytes 4194304 | tf_op jit(solution)/shard_map/attend/pallas_call | solution.py:110
  87.1 5.1 %collective-permute-done.2 = bf16[512,576]{0,1:T(8,128)(2,1)S(1)} collective-permute-done((bf16[512,576]{0,1:T(8,128)(2,1)S(1)}, bf16[512,576]{0,1:T(8,128)(2,1)S(1)}, u32[]{:S(2)}, u32[]{:S(2)}) %collective-permute-start.2) | collective-permute-done | bytes 589856 | tf_op jit(solution)/shard_map/ppermute | solution.py:305
  92.2 1.6 collective-permute-done.3
  93.8 0.3 copy.16.refs_2_
  94.1 0.3 copy.17.refs_3_
  94.5 3.1 %collective-permute-start.4 = (bf16[256,576]{1,0:T(8,128)(2,1)S(1)}, bf16[256,576]{1,0:T(8,128)(2,1)S(1)}, u32[]{:S(2)}, u32[]{:S(2)}) collective-permute-start(bf16[256,576]{1,0:T(8,128)(2,1)S(1)} %slice.34), channel_id=1, source_target_pairs={{0,2},{2,4},{4,6},{6,0},{1,3},{3,5},{5,7},{7,1},{8,10},{10,12},{12... | collective-permute-start | bytes 884744 | tf_op jit(solution)/shard_map/ppermute | solution.py:310
  97.7 3.5 %collective-permute-start.5 = (bf16[256,576]{1,0:T(8,128)(2,1)S(1)}, bf16[256,576]{1,0:T(8,128)(2,1)S(1)}, u32[]{:S(2)}, u32[]{:S(2)}) collective-permute-start(bf16[256,576]{1,0:T(8,128)(2,1)S(1)} %slice.35), channel_id=1, source_target_pairs={{0,6},{2,0},{4,2},{6,4},{1,7},{3,1},{5,3},{7,5},{8,14},{10,8},{12,... | collective-permute-start | bytes 884744 | tf_op jit(solution)/shard_map/ppermute | solution.py:311
  101.2 9.7 %attend.4 = (f32[4,1,256]{2,1,0:T(1,128)}, f32[4,1,256]{2,1,0:T(1,128)}, f32[4,512,256]{2,1,0:T(8,128)}) custom-call(s32[25]{0:T(128)} %concatenate.13.refs_0_, bf16[4,256,576]{2,1,0:T(8,128)(2,1)} %get-tuple-element.32.refs_1_, bf16[512,576]{1,0:T(8,128)(2,1)} %copy-done.2, bf16[512,576]{1,0:T(8,128)(2,1)} %copy-done.3, ...), custom_call_target="tpu_custom_call" | custom-call | flops 20000000000 | bytes 4194304 | tf_op jit(solution)/shard_map/attend/pallas_call | solution.py:110
  111.0 0.7 copy-done.12
  111.7 0.1 copy-done.13
  111.8 6.0 %attend.5.own_ref = bf16[1024,128]{1,0:T(8,128)(2,1)} custom-call(s32[25]{0:T(128)} %concatenate.13.refs_0_, bf16[4,256,576]{2,1,0:T(8,128)(2,1)} %get-tuple-element.32.refs_1_, bf16[256,576]{1,0:T(8,128)(2,1)} %copy-done.12, bf16[256,576]{1,0:T(8,128)(2,1)} %copy-done.13, f32[4,1,256]{2,1,0:T(1,128)} %get-tuple-element.48.refs_4_, ...), custom_call_target="tpu_custom_call" | custom-call | flops 20000000000 | bytes 4194304 | tf_op jit(solution)/shard_map/attend/pallas_call | solution.py:110
  117.8 3.9 %collective-permute-start.9 = (bf16[1024,128]{1,0:T(8,128)(2,1)}, bf16[1024,128]{1,0:T(8,128)(2,1)S(1)}, u32[]{:S(2)}, u32[]{:S(2)}) collective-permute-start(bf16[1024,128]{1,0:T(8,128)(2,1)} %attend.5.own_ref), channel_id=1, source_target_pairs={{0,8},{8,0},{1,9},{9,1},{2,10},{10,2},{3,11},{11,3},{4,12},{12,4},... | collective-permute-start | bytes 786440 | tf_op jit(solution)/shard_map/ppermute | solution.py:261
  121.7 1.4 collective-permute-done.9.other_ref
  123.0 0.7 copy-done.6
  123.7 7.3 %project.1 = bf16[8,224,256]{2,1,0:T(8,128)(2,1)} custom-call(bf16[32,72,1024]{2,1,0:T(8,128)(2,1)} %all-gather.2.cloned.1.call-done.w_ref, bf16[1024,128]{1,0:T(8,128)(2,1)} %attend.5.own_ref, bf16[1024,128]{1,0:T(8,128)(2,1)} %copy-done.6), custom_call_target="tpu_custom_call" | custom-call | tf_op jit(solution)/shard_map/project/pallas_call | solution.py:248
  131.0 10.3 %all-to-all-start.1 = ((bf16[8,224,256]{2,1,0:T(8,128)(2,1)}), bf16[8,224,256]{2,1,0:T(8,128)(2,1)S(1)}, u32[]{:S(2)}, u32[]{:S(2)}) async-start(bf16[8,224,256]{2,1,0:T(8,128)(2,1)} %project.1), calls=%async_computation.1 | async-start | bytes 1835008 | tf_op jit(solution)/shard_map/all_to_all | solution.py:324
  141.4 1.3 slice.27.own_ref
  142.7 2.6 %collective-permute-start.10 = (bf16[32,16,1024]{2,1,0:T(8,128)(2,1)S(1)}, bf16[32,16,1024]{2,1,0:T(8,128)(2,1)S(1)}, u32[]{:S(2)}, u32[]{:S(2)}) collective-permute-start(bf16[32,16,1024]{2,1,0:T(8,128)(2,1)S(1)} %slice.27.own_ref), channel_id=1, source_target_pairs={{0,8},{8,0},{1,9},{9,1},{2,10},{10,2},{3,11},{11,3},{4,12},{12,4},... | collective-permute-start | bytes 3145736 | tf_op jit(solution)/shard_map/ppermute | solution.py:261
  145.3 0.7 pad_add_fusion.1.place_ref
  145.9 1.6 collective-permute-done.10.other_ref
  147.5 1.0 copy-done.11
  148.5 7.5 %index_scores.1 = f32[16,8192]{1,0:T(8,128)} custom-call(s32[2]{0:T(128)} %pad_add_fusion.1.place_ref, bf16[16,4096]{1,0:T(8,128)(2,1)} %query_ref.1, f32[16,32]{1,0:T(8,128)} %w_ref.1, bf16[32,16,1024]{2,1,0:T(8,128)(2,1)} %copy-done.4, bf16[32,16,1024]{2,1,0:T(8,128)(2,1)} %copy-done.11), custom_call_target="tpu_custom_call" | custom-call | flops 1000000000 | bytes 4194304 | tf_op jit(solution)/shard_map/index_scores/pallas_call | solution.py:171
  156.0 13.8 %all-to-all-done.1 = bf16[8,224,256]{2,1,0:T(8,128)(2,1)S(1)} async-done(((bf16[8,224,256]{2,1,0:T(8,128)(2,1)}), bf16[8,224,256]{2,1,0:T(8,128)(2,1)S(1)}, u32[]{:S(2)}, u32[]{:S(2)}) %all-to-all-start.1) | async-done | bytes 917536 | tf_op jit(solution)/shard_map/all_to_all | solution.py:324
  169.8 0.1 reduce_sum.12
  169.9 2.5 %collective-permute-start.11 = (bf16[224,128]{1,0:T(8,128)(2,1)S(1)}, bf16[224,128]{1,0:T(8,128)(2,1)S(1)}, u32[]{:S(2)}, u32[]{:S(2)}) collective-permute-start(bf16[224,128]{1,0:T(8,128)(2,1)S(1)} %slice.37), channel_id=1, source_target_pairs={{0,8},{8,0},{1,9},{9,1},{2,10},{10,2},{3,11},{11,3},{4,12},{12,4},... | collective-permute-start | bytes 172040 | tf_op jit(solution)/shard_map/ppermute | solution.py:261
  172.4 0.9 collective-permute-done.11
  173.3 0.7 pad_maximum_fusion.2
  (42 shorter events, 0.5 us)
Async XLA Ops:
  7.2 11.7 %copy-start = (bf16[128,576]{0,1:T(8,128)(2,1)S(1)}, bf16[128,576]{0,1:T(8,128)(2,1)}, u32[]{:S(2)}) copy-start(bf16[128,576]{0,1:T(8,128)(2,1)} %param.12) | copy-start | bytes 442372
  8.9 11.4 %copy-start.5 = (bf16[72,1024]{1,0:T(8,128)(2,1)}, bf16[72,1024]{1,0:T(8,128)(2,1)S(1)}, u32[]{:S(2)}) copy-start(bf16[72,1024]{1,0:T(8,128)(2,1)S(1)} %pad_maximum_fusion.1.refs_0_) | copy-start | bytes 442372
  8.9 26.9 %collective-permute-start.6 = (bf16[72,1024]{1,0:T(8,128)(2,1)S(1)}, bf16[72,1024]{1,0:T(8,128)(2,1)S(1)}, u32[]{:S(2)}, u32[]{:S(2)}) collective-permute-start(bf16[72,1024]{1,0:T(8,128)(2,1)S(1)} %pad_maximum_fusion.1.refs_0_), channel_id=1, source_target_pairs={{0,16},{16,0},{32,48},{48,32},{1,17},{17,1},{33,49},{49,33},{2,18}... | collective-permute-start | bytes 442376 | tf_op jit(solution)/shard_map/ppermute | solution.py:282
  10.9 25.0 %collective-permute-start.7 = (bf16[72,1024]{1,0:T(8,128)(2,1)S(1)}, bf16[72,1024]{1,0:T(8,128)(2,1)S(1)}, u32[]{:S(2)}, u32[]{:S(2)}) collective-permute-start(bf16[72,1024]{1,0:T(8,128)(2,1)S(1)} %pad_maximum_fusion.1.refs_0_), channel_id=1, source_target_pairs={{0,32},{16,48},{32,0},{48,16},{1,33},{17,49},{33,1},{49,17},{2,34}... | collective-permute-start | bytes 442376 | tf_op jit(solution)/shard_map/ppermute | solution.py:282
  16.7 19.2 %collective-permute-start.8 = (bf16[72,1024]{1,0:T(8,128)(2,1)S(1)}, bf16[72,1024]{1,0:T(8,128)(2,1)S(1)}, u32[]{:S(2)}, u32[]{:S(2)}) collective-permute-start(bf16[72,1024]{1,0:T(8,128)(2,1)S(1)} %pad_maximum_fusion.1.refs_0_), channel_id=1, source_target_pairs={{0,48},{16,32},{32,16},{48,0},{1,49},{17,33},{33,17},{49,1},{2,50}... | collective-permute-start | bytes 442376 | tf_op jit(solution)/shard_map/ppermute | solution.py:282
  20.3 13.2 %copy-start.10 = (s32[1,16]{1,0:T(1,128)S(1)}, s32[1,16]{1,0:T(1,128)}, u32[]{:S(2)}) copy-start(s32[1,16]{1,0:T(1,128)} %param.13) | copy-start | bytes 196
  20.4 49.0 %all-to-all-start = ((bf16[64,16,576]{2,1,0:T(8,128)(2,1)}), bf16[64,16,576]{2,1,0:T(8,128)(2,1)S(1)}, u32[]{:S(2)}, u32[]{:S(2)}) async-start(bf16[64,16,576]{2,1,0:T(8,128)(2,1)} %bitcast.1), calls=%async_computation | async-start | bytes 2621440 | tf_op jit(solution)/shard_map/all_to_all | solution.py:284
  33.5 84.4 %all-gather.2.cloned.1.call-start = ((), (), s32[]{:S(2)}) async-start(), calls=%async_computation.2 | async-start | bytes 5308416 | tf_op jit(solution)/shard_map/all_gather | solution.py:296
  33.5 9.2 %collective-permute-start = (s32[16]{0:T(128)S(1)}, s32[16]{0:T(128)S(1)}, u32[]{:S(2)}, u32[]{:S(2)}) collective-permute-start(s32[16]{0:T(128)S(1)} %broadcast_maximum_fusion), channel_id=1, source_target_pairs={{0,8},{8,0},{1,9},{9,1},{2,10},{10,2},{3,11},{11,3},{4,12},{12,4},... | collective-permute-start | bytes 200 | tf_op jit(solution)/shard_map/ppermute | solution.py:261
  35.8 0.7 copy-start.7
  35.8 0.7 copy-start.8
  35.9 0.7 copy-start.9
  70.1 4.0 %collective-permute-start.1 = (bf16[256,576]{1,0:T(8,128)(2,1)S(1)}, bf16[256,576]{1,0:T(8,128)(2,1)S(1)}, u32[]{:S(2)}, u32[]{:S(2)}) collective-permute-start(bf16[256,576]{1,0:T(8,128)(2,1)S(1)} %bitcast.31), channel_id=1, source_target_pairs={{0,8},{8,0},{1,9},{9,1},{2,10},{10,2},{3,11},{11,3},{4,12},{12,4},... | collective-permute-start | bytes 884744 | tf_op jit(solution)/shard_map/ppermute | solution.py:261
  74.2 6.8 %copy-start.1 = (bf16[512,576]{1,0:T(8,128)(2,1)}, bf16[512,576]{1,0:T(8,128)(2,1)S(1)}, u32[]{:S(2)}) copy-start(bf16[512,576]{1,0:T(8,128)(2,1)S(1)} %pad_maximum_fusion.refs_2_) | copy-start | bytes 1769476
  74.4 17.8 %collective-permute-start.2 = (bf16[512,576]{0,1:T(8,128)(2,1)S(1)}, bf16[512,576]{0,1:T(8,128)(2,1)S(1)}, u32[]{:S(2)}, u32[]{:S(2)}) collective-permute-start(bf16[512,576]{0,1:T(8,128)(2,1)S(1)} %copy.14), channel_id=1, source_target_pairs={{0,2},{2,4},{4,6},{6,0},{1,3},{3,5},{5,7},{7,1},{8,10},{10,12},{12... | collective-permute-start | bytes 1769480 | tf_op jit(solution)/shard_map/ppermute | solution.py:305
  77.6 16.2 %collective-permute-start.3 = (bf16[512,576]{0,1:T(8,128)(2,1)S(1)}, bf16[512,576]{0,1:T(8,128)(2,1)S(1)}, u32[]{:S(2)}, u32[]{:S(2)}) collective-permute-start(bf16[512,576]{0,1:T(8,128)(2,1)S(1)} %copy.14), channel_id=1, source_target_pairs={{0,6},{2,0},{4,2},{6,4},{1,7},{3,1},{5,3},{7,5},{8,14},{10,8},{12,... | collective-permute-start | bytes 1769480 | tf_op jit(solution)/shard_map/ppermute | solution.py:306
  94.1 7.1 %copy-start.2 = (bf16[512,576]{1,0:T(8,128)(2,1)}, bf16[512,576]{1,0:T(8,128)(2,1)S(1)}, u32[]{:S(2)}) copy-start(bf16[512,576]{1,0:T(8,128)(2,1)S(1)} %copy.16.refs_2_) | copy-start | bytes 1769476
  94.4 6.8 %copy-start.3 = (bf16[512,576]{1,0:T(8,128)(2,1)}, bf16[512,576]{1,0:T(8,128)(2,1)S(1)}, u32[]{:S(2)}) copy-start(bf16[512,576]{1,0:T(8,128)(2,1)S(1)} %copy.17.refs_3_) | copy-start | bytes 1769476
  94.5 16.5 %collective-permute-start.4 = (bf16[256,576]{1,0:T(8,128)(2,1)S(1)}, bf16[256,576]{1,0:T(8,128)(2,1)S(1)}, u32[]{:S(2)}, u32[]{:S(2)}) collective-permute-start(bf16[256,576]{1,0:T(8,128)(2,1)S(1)} %slice.34), channel_id=1, source_target_pairs={{0,2},{2,4},{4,6},{6,0},{1,3},{3,5},{5,7},{7,1},{8,10},{10,12},{12... | collective-permute-start | bytes 884744 | tf_op jit(solution)/shard_map/ppermute | solution.py:310
  97.7 13.3 %collective-permute-start.5 = (bf16[256,576]{1,0:T(8,128)(2,1)S(1)}, bf16[256,576]{1,0:T(8,128)(2,1)S(1)}, u32[]{:S(2)}, u32[]{:S(2)}) collective-permute-start(bf16[256,576]{1,0:T(8,128)(2,1)S(1)} %slice.35), channel_id=1, source_target_pairs={{0,6},{2,0},{4,2},{6,4},{1,7},{3,1},{5,3},{7,5},{8,14},{10,8},{12,... | collective-permute-start | bytes 884744 | tf_op jit(solution)/shard_map/ppermute | solution.py:311
  110.9 0.7 copy-start.12
  111.0 0.8 copy-start.13
  117.8 5.2 %collective-permute-start.9 = (bf16[1024,128]{1,0:T(8,128)(2,1)}, bf16[1024,128]{1,0:T(8,128)(2,1)S(1)}, u32[]{:S(2)}, u32[]{:S(2)}) collective-permute-start(bf16[1024,128]{1,0:T(8,128)(2,1)} %attend.5.own_ref), channel_id=1, source_target_pairs={{0,8},{8,0},{1,9},{9,1},{2,10},{10,2},{3,11},{11,3},{4,12},{12,4},... | collective-permute-start | bytes 786440 | tf_op jit(solution)/shard_map/ppermute | solution.py:261
  123.0 0.7 copy-start.6
  131.0 38.8 %all-to-all-start.1 = ((bf16[8,224,256]{2,1,0:T(8,128)(2,1)}), bf16[8,224,256]{2,1,0:T(8,128)(2,1)S(1)}, u32[]{:S(2)}, u32[]{:S(2)}) async-start(bf16[8,224,256]{2,1,0:T(8,128)(2,1)} %project.1), calls=%async_computation.1 | async-start | bytes 1835008 | tf_op jit(solution)/shard_map/all_to_all | solution.py:324
  142.7 4.8 %copy-start.4 = (bf16[32,16,1024]{2,1,0:T(8,128)(2,1)}, bf16[32,16,1024]{2,1,0:T(8,128)(2,1)S(1)}, u32[]{:S(2)}) copy-start(bf16[32,16,1024]{2,1,0:T(8,128)(2,1)S(1)} %slice.27.own_ref) | copy-start | bytes 3145732
  142.7 4.8 %collective-permute-start.10 = (bf16[32,16,1024]{2,1,0:T(8,128)(2,1)S(1)}, bf16[32,16,1024]{2,1,0:T(8,128)(2,1)S(1)}, u32[]{:S(2)}, u32[]{:S(2)}) collective-permute-start(bf16[32,16,1024]{2,1,0:T(8,128)(2,1)S(1)} %slice.27.own_ref), channel_id=1, source_target_pairs={{0,8},{8,0},{1,9},{9,1},{2,10},{10,2},{3,11},{11,3},{4,12},{12,4},... | collective-permute-start | bytes 3145736 | tf_op jit(solution)/shard_map/ppermute | solution.py:261
  147.5 1.0 copy-start.11
  169.9 3.4 %collective-permute-start.11 = (bf16[224,128]{1,0:T(8,128)(2,1)S(1)}, bf16[224,128]{1,0:T(8,128)(2,1)S(1)}, u32[]{:S(2)}, u32[]{:S(2)}) collective-permute-start(bf16[224,128]{1,0:T(8,128)(2,1)S(1)} %slice.37), channel_id=1, source_target_pairs={{0,8},{8,0},{1,9},{9,1},{2,10},{10,2},{3,11},{11,3},{4,12},{12,4},... | collective-permute-start | bytes 172040 | tf_op jit(solution)/shard_map/ppermute | solution.py:261
Sparse Core Ops, SparseCore 0:
  38.7 71.0 all-gather.1

commit v7 on v6

--- a/solution.py
+++ b/solution.py
@@ -180,7 +180,7 @@
         ],
         compiler_params=pltpu.CompilerParams(vmem_limit_bytes=VMEM_LIMIT),
         cost_estimate=pl.CostEstimate(
-            flops=1_000_000_000, bytes_accessed=4 << 20, transcendentals=0
+            flops=100_000_000, bytes_accessed=100_000, transcendentals=0
         ),
         name="index_scores",
     )(place, query, weight, own, other)
@@ -315,15 +315,20 @@
 
     values, gathered = lax.optimization_barrier((values, gathered))
     terms = project(gathered, values, swap_core(values))
+    terms, gathered = lax.optimization_barrier((terms, gathered))
     keys_own = gathered[:, :16]
+    keys_other = swap_core(keys_own)
+    shares = lax.all_to_all(terms.reshape(NX, NW, NZ * COLS, 2 * BLOCK), "x", 0, 0)
     first_row = ctx_pos * TOK_DEV + head_pos * 16
-    keys_other = swap_core(keys_own)
     index_scores = index_part(
         jnp.stack([core, first_row]), index_query, index_weight, keys_own, keys_other
     )
-    shares = lax.all_to_all(terms, HEAD, 0, 0)
     shares, index_scores = lax.optimization_barrier((shares, index_scores))
-    summed = jnp.sum(shares.astype(jnp.float32), axis=0).astype(jnp.bfloat16)
+    summed = jnp.sum(shares.astype(jnp.float32), axis=0)
+    sent = jnp.where(w == 0, summed[1], summed[0]).astype(jnp.bfloat16)
+    kept = jnp.where(w == 0, summed[0], summed[1])
+    came = lax.ppermute(sent, "w", [(0, 1), (1, 0)])
+    summed = (kept + came.astype(jnp.float32)).astype(jnp.bfloat16)
     kept = summed[:, :BLOCK].reshape(NZ, COLS, BLOCK)
     other = swap_core(summed[:, BLOCK:]).reshape(NZ, COLS, BLOCK)
     first = jnp.where(core == 0, kept, other)

time: 182 us -> 181 us (level)
  the two profiles are of different devices: /device:TPU:89 before, /device:TPU:1 now
where the time goes in v7:
time: 181 us; the launch traced here: 180 us
  starting transfers between devices  67.4 us (37%)
  waiting for transfers between devices  44.5 us (25%)
  Pallas kernels  42.3 us (23%)
  between operations  14.5 us (8%)
  local copies, waits for them, and re-layouts  9.12 us (5%)
  other arithmetic  2.59 us (1%)
    all_to_all x1, waiting for transfers between devices, body(): pool = lax.all_to_all(wide, CTX, 0, 0)  27.3 us
    pallas_call x3, Pallas kernels, attend(): pl.pallas_call(functools.partial(attend_kernel, start, len(parts), state...  21.9 us
    ppermute x5, starting transfers between devices, swap_core(): return lax.ppermute(value, 'c', [(0, 1), (1, 0)])  17.8 us
    ppermute x3, starting transfers between devices, body(): lax.ppermute(packed, 'z', [(at, at ^ step) for at in range(NZ)])  12.6 us
    all_to_all x1, starting transfers between devices, body(): pool = lax.all_to_all(wide, CTX, 0, 0)  12.3 us
    ppermute x1, starting transfers between devices, body(): came = lax.ppermute(sent, 'w', [(0, 1), (1, 0)])  7.97 us
    pallas_call x1, Pallas kernels, index_part(): pl.pallas_call(index_kernel, out_shape=jax.ShapeDtypeStruct((16, NBLK * B...  7.52 us
    pallas_call x1, Pallas kernels, project(): pl.pallas_call(project_kernel, out_shape=jax.ShapeDtypeStruct((NY, NZ * C...  7.32 us
  transfers between devices with their start and end apart: 16, of which 8 were waited for; matrix products, arithmetic and copies ran while one was open for 3% of the time, Pallas kernels for 19%

profile of v7, /device:TPU:1, one launch (start us, length us, event | category | flops | bytes accessed | tf_op | source)
XLA Modules:
  0.0 180.4 jit_solution(11136867045980730476)
XLA Ops:
  7.2 0.8 copy.20
  8.0 0.9 pad_maximum_fusion.1.refs_0_
  8.9 4.8 %collective-permute-start.6 = (bf16[72,1024]{1,0:T(8,128)(2,1)S(1)}, bf16[72,1024]{1,0:T(8,128)(2,1)S(1)}, u32[]{:S(2)}, u32[]{:S(2)}) collective-permute-start(bf16[72,1024]{1,0:T(8,128)(2,1)S(1)} %pad_maximum_fusion.1.refs_0_), channel_id=1, source_target_pairs={{0,16},{16,0},{32,48},{48,32},{1,17},{17,1},{33,49},{49,33},{2,18}... | collective-permute-start | bytes 442376 | tf_op jit(solution)/shard_map/ppermute | solution.py:282
  13.8 5.8 %collective-permute-start.7 = (bf16[72,1024]{1,0:T(8,128)(2,1)S(1)}, bf16[72,1024]{1,0:T(8,128)(2,1)S(1)}, u32[]{:S(2)}, u32[]{:S(2)}) collective-permute-start(bf16[72,1024]{1,0:T(8,128)(2,1)S(1)} %pad_maximum_fusion.1.refs_0_), channel_id=1, source_target_pairs={{0,32},{16,48},{32,0},{48,16},{1,33},{17,49},{33,1},{49,17},{2,34}... | collective-permute-start | bytes 442376 | tf_op jit(solution)/shard_map/ppermute | solution.py:282
  19.6 1.9 %collective-permute-start.8 = (bf16[72,1024]{1,0:T(8,128)(2,1)S(1)}, bf16[72,1024]{1,0:T(8,128)(2,1)S(1)}, u32[]{:S(2)}, u32[]{:S(2)}) collective-permute-start(bf16[72,1024]{1,0:T(8,128)(2,1)S(1)} %pad_maximum_fusion.1.refs_0_), channel_id=1, source_target_pairs={{0,48},{16,32},{32,16},{48,0},{1,49},{17,33},{33,17},{49,1},{2,50}... | collective-permute-start | bytes 442376 | tf_op jit(solution)/shard_map/ppermute | solution.py:282
  21.6 0.1 copy.21
  21.8 1.2 broadcast_in_dim.12
  23.0 12.3 %all-to-all-start = ((bf16[64,16,576]{2,1,0:T(8,128)(2,1)}), bf16[64,16,576]{2,1,0:T(8,128)(2,1)S(1)}, u32[]{:S(2)}, u32[]{:S(2)}) async-start(bf16[64,16,576]{2,1,0:T(8,128)(2,1)} %bitcast.1), calls=%async_computation | async-start | bytes 2621440 | tf_op jit(solution)/shard_map/all_to_all | solution.py:284
  35.3 2.4 %collective-permute-start = (s32[16]{0:T(128)S(1)}, s32[16]{0:T(128)S(1)}, u32[]{:S(2)}, u32[]{:S(2)}) collective-permute-start(s32[16]{0:T(128)S(1)} %broadcast_maximum_fusion), channel_id=1, source_target_pairs={{0,8},{8,0},{1,9},{9,1},{2,10},{10,2},{3,11},{11,3},{4,12},{12,4},... | collective-permute-start | bytes 200 | tf_op jit(solution)/shard_map/ppermute | solution.py:261
  37.8 0.6 copy-done.8
  38.5 2.0 %arrange.1 = bf16[4,72,1024]{2,1,0:T(8,128)(2,1)} custom-call(s32[1]{0:T(128)} %bitcast.14.z_ref, bf16[72,1024]{1,0:T(8,128)(2,1)} %copy-done.6, bf16[72,1024]{1,0:T(8,128)(2,1)} %copy-done.8, bf16[72,1024]{1,0:T(8,128)(2,1)} %copy-done.9, bf16[72,1024]{1,0:T(8,128)(2,1)} %copy-done.10), custom_call_target="tpu_custom_call" | custom-call | tf_op jit(solution)/shard_map/arrange/pallas_call | solution.py:220
  40.5 3.5 %prepare.1 = (bf16[4,256,576]{2,1,0:T(8,128)(2,1)}, bf16[8,128,512]{2,1,0:T(8,128)(2,1)}) custom-call(bf16[128,4608]{1,0:T(8,128)(2,1)} %lq_ref.1, bf16[8,512,128]{2,1,0:T(8,128)(2,1)} %up_ref.1), custom_call_target="tpu_custom_call" | custom-call | flops 80000000000 | bytes 209715200 | tf_op jit(solution)/shard_map/prepare/pallas_call | solution.py:199
  44.0 0.7 concatenate.13.refs_0_
  44.8 27.3 %all-to-all-done = bf16[64,16,576]{2,1,0:T(8,128)(2,1)S(1)} async-done(((bf16[64,16,576]{2,1,0:T(8,128)(2,1)}), bf16[64,16,576]{2,1,0:T(8,128)(2,1)S(1)}, u32[]{:S(2)}, u32[]{:S(2)}) %all-to-all-start) | async-done | bytes 1179680 | tf_op jit(solution)/shard_map/all_to_all | solution.py:284
  72.2 0.7 gather_fusion
  72.9 4.0 %collective-permute-start.1 = (bf16[256,576]{1,0:T(8,128)(2,1)S(1)}, bf16[256,576]{1,0:T(8,128)(2,1)S(1)}, u32[]{:S(2)}, u32[]{:S(2)}) collective-permute-start(bf16[256,576]{1,0:T(8,128)(2,1)S(1)} %bitcast.38), channel_id=1, source_target_pairs={{0,8},{8,0},{1,9},{9,1},{2,10},{10,2},{3,11},{11,3},{4,12},{12,4},... | collective-permute-start | bytes 884744 | tf_op jit(solution)/shard_map/ppermute | solution.py:261
  76.9 1.2 collective-permute-done.1
  78.3 0.2 copy.14
  78.5 3.1 %collective-permute-start.2 = (bf16[512,576]{0,1:T(8,128)(2,1)S(1)}, bf16[512,576]{0,1:T(8,128)(2,1)S(1)}, u32[]{:S(2)}, u32[]{:S(2)}) collective-permute-start(bf16[512,576]{0,1:T(8,128)(2,1)S(1)} %copy.14), channel_id=1, source_target_pairs={{0,2},{2,4},{4,6},{6,0},{1,3},{3,5},{5,7},{7,1},{8,10},{10,12},{12... | collective-permute-start | bytes 1769480 | tf_op jit(solution)/shard_map/ppermute | solution.py:305
  81.6 3.4 %collective-permute-start.3 = (bf16[512,576]{0,1:T(8,128)(2,1)S(1)}, bf16[512,576]{0,1:T(8,128)(2,1)S(1)}, u32[]{:S(2)}, u32[]{:S(2)}) collective-permute-start(bf16[512,576]{0,1:T(8,128)(2,1)S(1)} %copy.14), channel_id=1, source_target_pairs={{0,6},{2,0},{4,2},{6,4},{1,7},{3,1},{5,3},{7,5},{8,14},{10,8},{12,... | collective-permute-start | bytes 1769480 | tf_op jit(solution)/shard_map/ppermute | solution.py:306
  85.0 6.2 %attend.3 = (f32[4,1,256]{2,1,0:T(1,128)}, f32[4,1,256]{2,1,0:T(1,128)}, f32[4,512,256]{2,1,0:T(8,128)}) custom-call(s32[25]{0:T(128)} %concatenate.13.refs_0_, bf16[4,256,576]{2,1,0:T(8,128)(2,1)} %get-tuple-element.34.refs_1_, bf16[512,576]{1,0:T(8,128)(2,1)} %copy-done.2), custom_call_target="tpu_custom_call" | custom-call | flops 20000000000 | bytes 4194304 | tf_op jit(solution)/shard_map/attend/pallas_call | solution.py:110
  91.2 5.1 %collective-permute-done.2 = bf16[512,576]{0,1:T(8,128)(2,1)S(1)} collective-permute-done((bf16[512,576]{0,1:T(8,128)(2,1)S(1)}, bf16[512,576]{0,1:T(8,128)(2,1)S(1)}, u32[]{:S(2)}, u32[]{:S(2)}) %collective-permute-start.2) | collective-permute-done | bytes 589856 | tf_op jit(solution)/shard_map/ppermute | solution.py:305
  96.3 1.6 collective-permute-done.3
  97.8 0.3 copy.16.refs_2_
  98.2 0.3 copy.17.refs_3_
  98.5 3.1 %collective-permute-start.4 = (bf16[256,576]{1,0:T(8,128)(2,1)S(1)}, bf16[256,576]{1,0:T(8,128)(2,1)S(1)}, u32[]{:S(2)}, u32[]{:S(2)}) collective-permute-start(bf16[256,576]{1,0:T(8,128)(2,1)S(1)} %slice.44), channel_id=1, source_target_pairs={{0,2},{2,4},{4,6},{6,0},{1,3},{3,5},{5,7},{7,1},{8,10},{10,12},{12... | collective-permute-start | bytes 884744 | tf_op jit(solution)/shard_map/ppermute | solution.py:310
  101.7 3.6 %collective-permute-start.5 = (bf16[256,576]{1,0:T(8,128)(2,1)S(1)}, bf16[256,576]{1,0:T(8,128)(2,1)S(1)}, u32[]{:S(2)}, u32[]{:S(2)}) collective-permute-start(bf16[256,576]{1,0:T(8,128)(2,1)S(1)} %slice.45), channel_id=1, source_target_pairs={{0,6},{2,0},{4,2},{6,4},{1,7},{3,1},{5,3},{7,5},{8,14},{10,8},{12,... | collective-permute-start | bytes 884744 | tf_op jit(solution)/shard_map/ppermute | solution.py:311
  105.3 9.7 %attend.4 = (f32[4,1,256]{2,1,0:T(1,128)}, f32[4,1,256]{2,1,0:T(1,128)}, f32[4,512,256]{2,1,0:T(8,128)}) custom-call(s32[25]{0:T(128)} %concatenate.13.refs_0_, bf16[4,256,576]{2,1,0:T(8,128)(2,1)} %get-tuple-element.34.refs_1_, bf16[512,576]{1,0:T(8,128)(2,1)} %copy-done.3, bf16[512,576]{1,0:T(8,128)(2,1)} %copy-done.4, ...), custom_call_target="tpu_custom_call" | custom-call | flops 20000000000 | bytes 4194304 | tf_op jit(solution)/shard_map/attend/pallas_call | solution.py:110
  115.0 0.7 copy-done.12
  115.7 0.1 copy-done.13
  115.8 6.0 %attend.5.own_ref = bf16[1024,128]{1,0:T(8,128)(2,1)} custom-call(s32[25]{0:T(128)} %concatenate.13.refs_0_, bf16[4,256,576]{2,1,0:T(8,128)(2,1)} %get-tuple-element.34.refs_1_, bf16[256,576]{1,0:T(8,128)(2,1)} %copy-done.12, bf16[256,576]{1,0:T(8,128)(2,1)} %copy-done.13, f32[4,1,256]{2,1,0:T(1,128)} %get-tuple-element.50.refs_4_, ...), custom_call_target="tpu_custom_call" | custom-call | flops 20000000000 | bytes 4194304 | tf_op jit(solution)/shard_map/attend/pallas_call | solution.py:110
  121.9 3.8 %collective-permute-start.9 = (bf16[1024,128]{1,0:T(8,128)(2,1)}, bf16[1024,128]{1,0:T(8,128)(2,1)S(1)}, u32[]{:S(2)}, u32[]{:S(2)}) collective-permute-start(bf16[1024,128]{1,0:T(8,128)(2,1)} %attend.5.own_ref), channel_id=1, source_target_pairs={{0,8},{8,0},{1,9},{9,1},{2,10},{10,2},{3,11},{11,3},{4,12},{12,4},... | collective-permute-start | bytes 786440 | tf_op jit(solution)/shard_map/ppermute | solution.py:261
  125.7 1.4 collective-permute-done.9.other_ref
  127.1 0.7 copy-done.7
  127.8 7.3 %project.1 = bf16[8,224,256]{2,1,0:T(8,128)(2,1)} custom-call(bf16[32,72,1024]{2,1,0:T(8,128)(2,1)} %all-gather.2.cloned.1.call-done.w_ref, bf16[1024,128]{1,0:T(8,128)(2,1)} %attend.5.own_ref, bf16[1024,128]{1,0:T(8,128)(2,1)} %copy-done.7), custom_call_target="tpu_custom_call" | custom-call | tf_op jit(solution)/shard_map/project/pallas_call | solution.py:248
  135.1 1.3 slice.35.own_ref
  136.4 2.3 %collective-permute-start.10 = (bf16[32,16,1024]{2,1,0:T(8,128)(2,1)S(1)}, bf16[32,16,1024]{2,1,0:T(8,128)(2,1)S(1)}, u32[]{:S(2)}, u32[]{:S(2)}) collective-permute-start(bf16[32,16,1024]{2,1,0:T(8,128)(2,1)S(1)} %slice.35.own_ref), channel_id=1, source_target_pairs={{0,8},{8,0},{1,9},{9,1},{2,10},{10,2},{3,11},{11,3},{4,12},{12,4},... | collective-permute-start | bytes 3145736 | tf_op jit(solution)/shard_map/ppermute | solution.py:261
  138.7 3.5 %all-to-all-start.1 = ((bf16[4,2,224,256]{3,2,1,0:T(8,128)(2,1)}), bf16[4,2,224,256]{3,2,1,0:T(8,128)(2,1)S(1)}, u32[]{:S(2)}, u32[]{:S(2)}) async-start(bf16[4,2,224,256]{3,2,1,0:T(8,128)(2,1)} %bitcast.18), calls=%async_computation.1 | async-start | bytes 1835008 | tf_op jit(solution)/shard_map/all_to_all | solution.py:321
  142.2 0.7 pad_add_fusion.1.place_ref
  142.9 1.0 copy-done.5
  143.9 7.5 %index_scores.1 = f32[16,8192]{1,0:T(8,128)} custom-call(s32[2]{0:T(128)} %pad_add_fusion.1.place_ref, bf16[16,4096]{1,0:T(8,128)(2,1)} %query_ref.1, f32[16,32]{1,0:T(8,128)} %w_ref.1, bf16[32,16,1024]{2,1,0:T(8,128)(2,1)} %copy-done.1, bf16[32,16,1024]{2,1,0:T(8,128)(2,1)} %copy-done.5), custom_call_target="tpu_custom_call" | custom-call | flops 100000000 | bytes 100000 | tf_op jit(solution)/shard_map/index_scores/pallas_call | solution.py:171
  151.4 4.5 %all-to-all-done.1 = bf16[4,2,224,256]{3,2,1,0:T(8,128)(2,1)S(1)} async-done(((bf16[4,2,224,256]{3,2,1,0:T(8,128)(2,1)}), bf16[4,2,224,256]{3,2,1,0:T(8,128)(2,1)S(1)}, u32[]{:S(2)}, u32[]{:S(2)}) %all-to-all-start.1) | async-done | bytes 917536 | tf_op jit(solution)/shard_map/all_to_all | solution.py:321
  155.9 0.1 convert_reduce_fusion
  156.0 8.0 %collective-permute-start.11 = (bf16[224,256]{1,0:T(8,128)(2,1)S(1)}, bf16[224,256]{1,0:T(8,128)(2,1)S(1)}, u32[]{:S(2)}, u32[]{:S(2)}) collective-permute-start(bf16[224,256]{1,0:T(8,128)(2,1)S(1)} %fusion.1), channel_id=1, source_target_pairs={{0,1},{1,0},{2,3},{3,2},{4,5},{5,4},{6,7},{7,6},{8,9},{9,8},{10,11... | collective-permute-start | bytes 344072 | tf_op jit(solution)/shard_map/ppermute | solution.py:330
  164.0 2.5 %collective-permute-done.11 = bf16[224,256]{1,0:T(8,128)(2,1)S(1)} collective-permute-done((bf16[224,256]{1,0:T(8,128)(2,1)S(1)}, bf16[224,256]{1,0:T(8,128)(2,1)S(1)}, u32[]{:S(2)}, u32[]{:S(2)}) %collective-permute-start.11) | collective-permute-done | bytes 114720 | tf_op jit(solution)/shard_map/ppermute | solution.py:330
  166.6 5.3 %collective-permute-start.12 = (bf16[224,128]{1,0:T(8,128)(2,1)S(1)}, bf16[224,128]{1,0:T(8,128)(2,1)S(1)}, u32[]{:S(2)}, u32[]{:S(2)}) collective-permute-start(bf16[224,128]{1,0:T(8,128)(2,1)S(1)} %slice.49), channel_id=1, source_target_pairs={{0,8},{8,0},{1,9},{9,1},{2,10},{10,2},{3,11},{11,3},{4,12},{12,4},... | collective-permute-start | bytes 172040 | tf_op jit(solution)/shard_map/ppermute | solution.py:261
  172.0 0.9 collective-permute-done.12
  172.8 0.7 pad_maximum_fusion.2
  (46 shorter events, 0.7 us)
Async XLA Ops:
  7.2 14.4 %copy-start = (bf16[128,576]{0,1:T(8,128)(2,1)S(1)}, bf16[128,576]{0,1:T(8,128)(2,1)}, u32[]{:S(2)}) copy-start(bf16[128,576]{0,1:T(8,128)(2,1)} %param.12) | copy-start | bytes 442372
  8.9 14.1 %copy-start.6 = (bf16[72,1024]{1,0:T(8,128)(2,1)}, bf16[72,1024]{1,0:T(8,128)(2,1)S(1)}, u32[]{:S(2)}) copy-start(bf16[72,1024]{1,0:T(8,128)(2,1)S(1)} %pad_maximum_fusion.1.refs_0_) | copy-start | bytes 442372
  8.9 28.8 %collective-permute-start.6 = (bf16[72,1024]{1,0:T(8,128)(2,1)S(1)}, bf16[72,1024]{1,0:T(8,128)(2,1)S(1)}, u32[]{:S(2)}, u32[]{:S(2)}) collective-permute-start(bf16[72,1024]{1,0:T(8,128)(2,1)S(1)} %pad_maximum_fusion.1.refs_0_), channel_id=1, source_target_pairs={{0,16},{16,0},{32,48},{48,32},{1,17},{17,1},{33,49},{49,33},{2,18}... | collective-permute-start | bytes 442376 | tf_op jit(solution)/shard_map/ppermute | solution.py:282
  13.8 24.0 %collective-permute-start.7 = (bf16[72,1024]{1,0:T(8,128)(2,1)S(1)}, bf16[72,1024]{1,0:T(8,128)(2,1)S(1)}, u32[]{:S(2)}, u32[]{:S(2)}) collective-permute-start(bf16[72,1024]{1,0:T(8,128)(2,1)S(1)} %pad_maximum_fusion.1.refs_0_), channel_id=1, source_target_pairs={{0,32},{16,48},{32,0},{48,16},{1,33},{17,49},{33,1},{49,17},{2,34}... | collective-permute-start | bytes 442376 | tf_op jit(solution)/shard_map/ppermute | solution.py:282
  19.6 18.2 %collective-permute-start.8 = (bf16[72,1024]{1,0:T(8,128)(2,1)S(1)}, bf16[72,1024]{1,0:T(8,128)(2,1)S(1)}, u32[]{:S(2)}, u32[]{:S(2)}) collective-permute-start(bf16[72,1024]{1,0:T(8,128)(2,1)S(1)} %pad_maximum_fusion.1.refs_0_), channel_id=1, source_target_pairs={{0,48},{16,32},{32,16},{48,0},{1,49},{17,33},{33,17},{49,1},{2,50}... | collective-permute-start | bytes 442376 | tf_op jit(solution)/shard_map/ppermute | solution.py:282
  23.0 12.3 %copy-start.11 = (s32[1,16]{1,0:T(1,128)S(1)}, s32[1,16]{1,0:T(1,128)}, u32[]{:S(2)}) copy-start(s32[1,16]{1,0:T(1,128)} %param.13) | copy-start | bytes 196
  23.0 49.2 %all-to-all-start = ((bf16[64,16,576]{2,1,0:T(8,128)(2,1)}), bf16[64,16,576]{2,1,0:T(8,128)(2,1)S(1)}, u32[]{:S(2)}, u32[]{:S(2)}) async-start(bf16[64,16,576]{2,1,0:T(8,128)(2,1)} %bitcast.1), calls=%async_computation | async-start | bytes 2621440 | tf_op jit(solution)/shard_map/all_to_all | solution.py:284
  35.3 86.6 %all-gather.2.cloned.1.call-start = ((), (), s32[]{:S(2)}) async-start(), calls=%async_computation.2 | async-start | bytes 5308416 | tf_op jit(solution)/shard_map/all_gather | solution.py:296
  35.3 9.4 %collective-permute-start = (s32[16]{0:T(128)S(1)}, s32[16]{0:T(128)S(1)}, u32[]{:S(2)}, u32[]{:S(2)}) collective-permute-start(s32[16]{0:T(128)S(1)} %broadcast_maximum_fusion), channel_id=1, source_target_pairs={{0,8},{8,0},{1,9},{9,1},{2,10},{10,2},{3,11},{11,3},{4,12},{12,4},... | collective-permute-start | bytes 200 | tf_op jit(solution)/shard_map/ppermute | solution.py:261
  37.7 0.7 copy-start.8
  37.7 0.7 copy-start.9
  37.8 0.7 copy-start.10
  72.9 5.3 %collective-permute-start.1 = (bf16[256,576]{1,0:T(8,128)(2,1)S(1)}, bf16[256,576]{1,0:T(8,128)(2,1)S(1)}, u32[]{:S(2)}, u32[]{:S(2)}) collective-permute-start(bf16[256,576]{1,0:T(8,128)(2,1)S(1)} %bitcast.38), channel_id=1, source_target_pairs={{0,8},{8,0},{1,9},{9,1},{2,10},{10,2},{3,11},{11,3},{4,12},{12,4},... | collective-permute-start | bytes 884744 | tf_op jit(solution)/shard_map/ppermute | solution.py:261
  78.2 6.8 %copy-start.2 = (bf16[512,576]{1,0:T(8,128)(2,1)}, bf16[512,576]{1,0:T(8,128)(2,1)S(1)}, u32[]{:S(2)}) copy-start(bf16[512,576]{1,0:T(8,128)(2,1)S(1)} %pad_maximum_fusion.refs_2_) | copy-start | bytes 1769476
  78.5 17.8 %collective-permute-start.2 = (bf16[512,576]{0,1:T(8,128)(2,1)S(1)}, bf16[512,576]{0,1:T(8,128)(2,1)S(1)}, u32[]{:S(2)}, u32[]{:S(2)}) collective-permute-start(bf16[512,576]{0,1:T(8,128)(2,1)S(1)} %copy.14), channel_id=1, source_target_pairs={{0,2},{2,4},{4,6},{6,0},{1,3},{3,5},{5,7},{7,1},{8,10},{10,12},{12... | collective-permute-start | bytes 1769480 | tf_op jit(solution)/shard_map/ppermute | solution.py:305
  81.6 16.2 %collective-permute-start.3 = (bf16[512,576]{0,1:T(8,128)(2,1)S(1)}, bf16[512,576]{0,1:T(8,128)(2,1)S(1)}, u32[]{:S(2)}, u32[]{:S(2)}) collective-permute-start(bf16[512,576]{0,1:T(8,128)(2,1)S(1)} %copy.14), channel_id=1, source_target_pairs={{0,6},{2,0},{4,2},{6,4},{1,7},{3,1},{5,3},{7,5},{8,14},{10,8},{12,... | collective-permute-start | bytes 1769480 | tf_op jit(solution)/shard_map/ppermute | solution.py:306
  98.1 7.1 %copy-start.3 = (bf16[512,576]{1,0:T(8,128)(2,1)}, bf16[512,576]{1,0:T(8,128)(2,1)S(1)}, u32[]{:S(2)}) copy-start(bf16[512,576]{1,0:T(8,128)(2,1)S(1)} %copy.16.refs_2_) | copy-start | bytes 1769476
  98.4 6.8 %copy-start.4 = (bf16[512,576]{1,0:T(8,128)(2,1)}, bf16[512,576]{1,0:T(8,128)(2,1)S(1)}, u32[]{:S(2)}) copy-start(bf16[512,576]{1,0:T(8,128)(2,1)S(1)} %copy.17.refs_3_) | copy-start | bytes 1769476
  98.5 16.5 %collective-permute-start.4 = (bf16[256,576]{1,0:T(8,128)(2,1)S(1)}, bf16[256,576]{1,0:T(8,128)(2,1)S(1)}, u32[]{:S(2)}, u32[]{:S(2)}) collective-permute-start(bf16[256,576]{1,0:T(8,128)(2,1)S(1)} %slice.44), channel_id=1, source_target_pairs={{0,2},{2,4},{4,6},{6,0},{1,3},{3,5},{5,7},{7,1},{8,10},{10,12},{12... | collective-permute-start | bytes 884744 | tf_op jit(solution)/shard_map/ppermute | solution.py:310
  101.7 13.3 %collective-permute-start.5 = (bf16[256,576]{1,0:T(8,128)(2,1)S(1)}, bf16[256,576]{1,0:T(8,128)(2,1)S(1)}, u32[]{:S(2)}, u32[]{:S(2)}) collective-permute-start(bf16[256,576]{1,0:T(8,128)(2,1)S(1)} %slice.45), channel_id=1, source_target_pairs={{0,6},{2,0},{4,2},{6,4},{1,7},{3,1},{5,3},{7,5},{8,14},{10,8},{12,... | collective-permute-start | bytes 884744 | tf_op jit(solution)/shard_map/ppermute | solution.py:311
  115.0 0.7 copy-start.12
  115.0 0.8 copy-start.13
  121.9 5.2 %collective-permute-start.9 = (bf16[1024,128]{1,0:T(8,128)(2,1)}, bf16[1024,128]{1,0:T(8,128)(2,1)S(1)}, u32[]{:S(2)}, u32[]{:S(2)}) collective-permute-start(bf16[1024,128]{1,0:T(8,128)(2,1)} %attend.5.own_ref), channel_id=1, source_target_pairs={{0,8},{8,0},{1,9},{9,1},{2,10},{10,2},{3,11},{11,3},{4,12},{12,4},... | collective-permute-start | bytes 786440 | tf_op jit(solution)/shard_map/ppermute | solution.py:261
  127.1 0.7 copy-start.7
  136.4 6.5 %copy-start.1 = (bf16[32,16,1024]{2,1,0:T(8,128)(2,1)}, bf16[32,16,1024]{2,1,0:T(8,128)(2,1)S(1)}, u32[]{:S(2)}) copy-start(bf16[32,16,1024]{2,1,0:T(8,128)(2,1)S(1)} %slice.35.own_ref) | copy-start | bytes 3145732
  136.4 6.5 %collective-permute-start.10 = (bf16[32,16,1024]{2,1,0:T(8,128)(2,1)S(1)}, bf16[32,16,1024]{2,1,0:T(8,128)(2,1)S(1)}, u32[]{:S(2)}, u32[]{:S(2)}) collective-permute-start(bf16[32,16,1024]{2,1,0:T(8,128)(2,1)S(1)} %slice.35.own_ref), channel_id=1, source_target_pairs={{0,8},{8,0},{1,9},{9,1},{2,10},{10,2},{3,11},{11,3},{4,12},{12,4},... | collective-permute-start | bytes 3145736 | tf_op jit(solution)/shard_map/ppermute | solution.py:261
  138.7 17.2 %all-to-all-start.1 = ((bf16[4,2,224,256]{3,2,1,0:T(8,128)(2,1)}), bf16[4,2,224,256]{3,2,1,0:T(8,128)(2,1)S(1)}, u32[]{:S(2)}, u32[]{:S(2)}) async-start(bf16[4,2,224,256]{3,2,1,0:T(8,128)(2,1)} %bitcast.18), calls=%async_computation.1 | async-start | bytes 1835008 | tf_op jit(solution)/shard_map/all_to_all | solution.py:321
  142.9 1.0 copy-start.5
  156.0 10.5 %collective-permute-start.11 = (bf16[224,256]{1,0:T(8,128)(2,1)S(1)}, bf16[224,256]{1,0:T(8,128)(2,1)S(1)}, u32[]{:S(2)}, u32[]{:S(2)}) collective-permute-start(bf16[224,256]{1,0:T(8,128)(2,1)S(1)} %fusion.1), channel_id=1, source_target_pairs={{0,1},{1,0},{2,3},{3,2},{4,5},{5,4},{6,7},{7,6},{8,9},{9,8},{10,11... | collective-permute-start | bytes 344072 | tf_op jit(solution)/shard_map/ppermute | solution.py:330
  166.6 6.2 %collective-permute-start.12 = (bf16[224,128]{1,0:T(8,128)(2,1)S(1)}, bf16[224,128]{1,0:T(8,128)(2,1)S(1)}, u32[]{:S(2)}, u32[]{:S(2)}) collective-permute-start(bf16[224,128]{1,0:T(8,128)(2,1)S(1)} %slice.49), channel_id=1, source_target_pairs={{0,8},{8,0},{1,9},{9,1},{2,10},{10,2},{3,11},{11,3},{4,12},{12,4},... | collective-permute-start | bytes 172040 | tf_op jit(solution)/shard_map/ppermute | solution.py:261
Sparse Core Ops, SparseCore 0:
  40.7 71.4 all-gather.1

commit v8 on v7

--- a/solution.py
+++ b/solution.py
@@ -20,6 +20,8 @@
 NBLK = 64
 ROWS = 16
 PACKED = 72
+SHARED = 8
+STEPS = 2
 COLS = 56
 NY, NZ, NC, NX, NW = 8, 4, 2, 4, 2
 
@@ -56,9 +58,8 @@
         first_key = jnp.where(entry < 0, 2 * NBLK, entry) * BLOCK
         first_key = first_key + place_ref[TOPK + 1 + start + part]
         seen = jnp.where(first_key + row <= query, 0.0, MASKED)
-        bias_ref[group * ROWS : (group + 1) * ROWS, :BLOCK] = seen
-        bias_ref[group * ROWS : (group + 1) * ROWS, BLOCK:] = seen
-    for pair in range(HEADS_DEV // 2):
+        bias_ref[group * ROWS : (group + 1) * ROWS, :] = jnp.concatenate([seen] * SHARED, axis=1)
+    for pair in range(HEADS_DEV // SHARED):
         scores = lax.dot_general(
             keys, q_ref[pair], (((1,), (1,)), ((), ())), preferred_element_type=jnp.float32
         )
@@ -84,8 +85,8 @@
             sum_out[pair] = lat_sum
             continue
         lat_out = (lat_sum / total).astype(jnp.bfloat16)
-        for half in range(2):
-            head = 2 * pair + half
+        for half in range(SHARED):
+            head = SHARED * pair + half
             values = lax.dot_general(
                 up_ref[head],
                 lat_out[:, half * BLOCK : (half + 1) * BLOCK],
@@ -96,10 +97,10 @@
 
 
 def attend(start, place, queries, parts, state, up_t):
-    pairs = HEADS_DEV // 2
+    pairs = HEADS_DEV // SHARED
     n_keys = sum(part.shape[0] for part in parts)
-    stat = jax.ShapeDtypeStruct((pairs, 1, 2 * BLOCK), jnp.float32)
-    out = (stat, stat, jax.ShapeDtypeStruct((pairs, KV_RANK, 2 * BLOCK), jnp.float32))
+    stat = jax.ShapeDtypeStruct((pairs, 1, SHARED * BLOCK), jnp.float32)
+    out = (stat, stat, jax.ShapeDtypeStruct((pairs, KV_RANK, SHARED * BLOCK), jnp.float32))
     last = up_t is not None
     operands = [place, queries, *parts, *(state or ())]
     if last:
@@ -113,7 +114,7 @@
         in_specs=[pl.BlockSpec(memory_space=pltpu.SMEM)] + [vmem] * (len(operands) - 1),
         out_specs=vmem if last else (vmem,) * 3,
         scratch_shapes=[
-            pltpu.VMEM((n_keys, 2 * BLOCK), jnp.float32),
+            pltpu.VMEM((n_keys, SHARED * BLOCK), jnp.float32),
             pltpu.VMEM((KV_RANK, n_keys), jnp.bfloat16),
         ],
         compiler_params=pltpu.CompilerParams(vmem_limit_bytes=VMEM_LIMIT),
@@ -188,14 +189,14 @@
 
 def prepare_kernel(lq_ref, up_ref, q_ref, up_t_ref):
     for head in range(HEADS_DEV):
-        pair, half = divmod(head, 2)
+        pair, half = divmod(head, SHARED)
         q_ref[pair, half * BLOCK : (half + 1) * BLOCK, :] = lq_ref[:, head * LAT : (head + 1) * LAT]
         up_t_ref[head] = up_ref[head].T
 
 
 def prepare(latent_query, value_up):
     vmem = pl.BlockSpec(memory_space=pltpu.VMEM)
-    shapes = [(HEADS_DEV // 2, 2 * BLOCK, LAT), (HEADS_DEV, V_DIM, KV_RANK)]
+    shapes = [(HEADS_DEV // SHARED, SHARED * BLOCK, LAT), (HEADS_DEV, V_DIM, KV_RANK)]
     return pl.pallas_call(
         prepare_kernel,
         out_shape=[jax.ShapeDtypeStruct(shape, jnp.bfloat16) for shape in shapes],
@@ -234,13 +235,13 @@
         values_ref[:, BLOCK:] = other_ref[...]
 
     terms = lax.dot_general(
-        w_ref[...].reshape(NZ * PACKED, 1024),
+        w_ref[...].reshape(NY * NZ * PACKED // STEPS, 1024),
         values_ref[...],
         (((1,), (0,)), ((), ())),
         preferred_element_type=jnp.float32,
     )
-    terms = terms.reshape(NZ, PACKED, 2 * BLOCK)[:, 16:, :].reshape(NZ * COLS, 2 * BLOCK)
-    out_ref[0] = terms.astype(jnp.bfloat16)
+    terms = terms.reshape(NY * NZ // STEPS, PACKED, 2 * BLOCK)[:, 16:, :]
+    out_ref[...] = terms.reshape(NY // STEPS, NZ * COLS, 2 * BLOCK).astype(jnp.bfloat16)
 
 
 def project(gathered, own, other):
@@ -248,9 +249,9 @@
     return pl.pallas_call(
         project_kernel,
         out_shape=jax.ShapeDtypeStruct((NY, NZ * COLS, 2 * BLOCK), jnp.bfloat16),
-        grid=(NY,),
-        in_specs=[pl.BlockSpec((NZ, PACKED, 1024), lambda i: (i, 0, 0)), values, values],
-        out_specs=pl.BlockSpec((1, NZ * COLS, 2 * BLOCK), lambda i: (i, 0, 0)),
+        grid=(STEPS,),
+        in_specs=[pl.BlockSpec((NY * NZ // STEPS, PACKED, 1024), lambda i: (i, 0, 0)), values, values],
+        out_specs=pl.BlockSpec((NY // STEPS, NZ * COLS, 2 * BLOCK), lambda i: (i, 0, 0)),
         scratch_shapes=[pltpu.VMEM((HEADS_DEV * V_DIM, 2 * BLOCK), jnp.bfloat16)],
         compiler_params=pltpu.CompilerParams(vmem_limit_bytes=VMEM_LIMIT),
         name="project",

time: 181 us -> 175 us (0.967)
  Pallas kernels: 42.3 us -> 34.6 us
    pallas_call x3, Pallas kernels: 21.9 us -> 17.4 us  [attend(): pl.pallas_call(functools.partial(attend_kernel, start, len(parts), state...]
    pallas_call x1, Pallas kernels: 7.32 us -> 4.2 us  [project(): pl.pallas_call(project_kernel, out_shape=jax.ShapeDtypeStruct((NY, NZ * C...]
  transfers between devices with their start and end apart: 16 -> 16, of which waited for: 8 -> 8; matrix products, arithmetic and copies ran while one was open for 3% -> 3% of each run, Pallas kernels for 19% -> 18%
where the time goes in v8:
time: 175 us; the launch traced here: 174 us
  starting transfers between devices  67.2 us (38%)
  waiting for transfers between devices  45.9 us (26%)
  Pallas kernels  34.6 us (20%)
  between operations  14.5 us (8%)
  local copies, waits for them, and re-layouts  9.12 us (5%)
  other arithmetic  2.59 us (1%)
    all_to_all x1, waiting for transfers between devices, body(): pool = lax.all_to_all(wide, CTX, 0, 0)  27.3 us
    ppermute x5, starting transfers between devices, swap_core(): return lax.ppermute(value, 'c', [(0, 1), (1, 0)])  17.9 us
    pallas_call x3, Pallas kernels, attend(): pl.pallas_call(functools.partial(attend_kernel, start, len(parts), state...  17.4 us
    ppermute x3, starting transfers between devices, body(): lax.ppermute(packed, 'z', [(at, at ^ step) for at in range(NZ)])  12.6 us
    all_to_all x1, starting transfers between devices, body(): pool = lax.all_to_all(wide, CTX, 0, 0)  12.3 us
    ppermute x1, starting transfers between devices, body(): came = lax.ppermute(sent, 'w', [(0, 1), (1, 0)])  7.95 us
    pallas_call x1, Pallas kernels, index_part(): pl.pallas_call(index_kernel, out_shape=jax.ShapeDtypeStruct((16, NBLK * B...  7.52 us
    ppermute x1, waiting for transfers between devices, body(): left = lax.ppermute(mine, 'x', up)  6.47 us
  transfers between devices with their start and end apart: 16, of which 8 were waited for; matrix products, arithmetic and copies ran while one was open for 3% of the time, Pallas kernels for 18%

profile of v8, /device:TPU:1, one launch (start us, length us, event | category | flops | bytes accessed | tf_op | source)
XLA Modules:
  0.0 173.9 jit_solution(8616831251983053413)
XLA Ops:
  7.2 0.8 copy.20
  8.0 0.9 pad_maximum_fusion.1.refs_0_
  8.9 4.8 %collective-permute-start.6 = (bf16[72,1024]{1,0:T(8,128)(2,1)S(1)}, bf16[72,1024]{1,0:T(8,128)(2,1)S(1)}, u32[]{:S(2)}, u32[]{:S(2)}) collective-permute-start(bf16[72,1024]{1,0:T(8,128)(2,1)S(1)} %pad_maximum_fusion.1.refs_0_), channel_id=1, source_target_pairs={{0,16},{16,0},{32,48},{48,32},{1,17},{17,1},{33,49},{49,33},{2,18}... | collective-permute-start | bytes 442376 | tf_op jit(solution)/shard_map/ppermute | solution.py:283
  13.8 5.8 %collective-permute-start.7 = (bf16[72,1024]{1,0:T(8,128)(2,1)S(1)}, bf16[72,1024]{1,0:T(8,128)(2,1)S(1)}, u32[]{:S(2)}, u32[]{:S(2)}) collective-permute-start(bf16[72,1024]{1,0:T(8,128)(2,1)S(1)} %pad_maximum_fusion.1.refs_0_), channel_id=1, source_target_pairs={{0,32},{16,48},{32,0},{48,16},{1,33},{17,49},{33,1},{49,17},{2,34}... | collective-permute-start | bytes 442376 | tf_op jit(solution)/shard_map/ppermute | solution.py:283
  19.6 1.9 %collective-permute-start.8 = (bf16[72,1024]{1,0:T(8,128)(2,1)S(1)}, bf16[72,1024]{1,0:T(8,128)(2,1)S(1)}, u32[]{:S(2)}, u32[]{:S(2)}) collective-permute-start(bf16[72,1024]{1,0:T(8,128)(2,1)S(1)} %pad_maximum_fusion.1.refs_0_), channel_id=1, source_target_pairs={{0,48},{16,32},{32,16},{48,0},{1,49},{17,33},{33,17},{49,1},{2,50}... | collective-permute-start | bytes 442376 | tf_op jit(solution)/shard_map/ppermute | solution.py:283
  21.6 0.1 copy.21
  21.8 1.2 broadcast_in_dim.12
  23.0 12.3 %all-to-all-start = ((bf16[64,16,576]{2,1,0:T(8,128)(2,1)}), bf16[64,16,576]{2,1,0:T(8,128)(2,1)S(1)}, u32[]{:S(2)}, u32[]{:S(2)}) async-start(bf16[64,16,576]{2,1,0:T(8,128)(2,1)} %bitcast.1), calls=%async_computation | async-start | bytes 2621440 | tf_op jit(solution)/shard_map/all_to_all | solution.py:285
  35.3 2.4 %collective-permute-start = (s32[16]{0:T(128)S(1)}, s32[16]{0:T(128)S(1)}, u32[]{:S(2)}, u32[]{:S(2)}) collective-permute-start(s32[16]{0:T(128)S(1)} %broadcast_maximum_fusion), channel_id=1, source_target_pairs={{0,8},{8,0},{1,9},{9,1},{2,10},{10,2},{3,11},{11,3},{4,12},{12,4},... | collective-permute-start | bytes 200 | tf_op jit(solution)/shard_map/ppermute | solution.py:262
  37.8 0.6 copy-done.8
  38.5 2.0 %arrange.1 = bf16[4,72,1024]{2,1,0:T(8,128)(2,1)} custom-call(s32[1]{0:T(128)} %bitcast.14.z_ref, bf16[72,1024]{1,0:T(8,128)(2,1)} %copy-done.6, bf16[72,1024]{1,0:T(8,128)(2,1)} %copy-done.8, bf16[72,1024]{1,0:T(8,128)(2,1)} %copy-done.9, bf16[72,1024]{1,0:T(8,128)(2,1)} %copy-done.10), custom_call_target="tpu_custom_call" | custom-call | tf_op jit(solution)/shard_map/arrange/pallas_call | solution.py:221
  40.5 3.5 %prepare.1 = (bf16[1,1024,576]{2,1,0:T(8,128)(2,1)}, bf16[8,128,512]{2,1,0:T(8,128)(2,1)}) custom-call(bf16[128,4608]{1,0:T(8,128)(2,1)} %lq_ref.1, bf16[8,512,128]{2,1,0:T(8,128)(2,1)} %up_ref.1), custom_call_target="tpu_custom_call" | custom-call | flops 80000000000 | bytes 209715200 | tf_op jit(solution)/shard_map/prepare/pallas_call | solution.py:200
  44.0 0.7 concatenate.13.refs_0_
  44.8 27.3 %all-to-all-done = bf16[64,16,576]{2,1,0:T(8,128)(2,1)S(1)} async-done(((bf16[64,16,576]{2,1,0:T(8,128)(2,1)}), bf16[64,16,576]{2,1,0:T(8,128)(2,1)S(1)}, u32[]{:S(2)}, u32[]{:S(2)}) %all-to-all-start) | async-done | bytes 1179680 | tf_op jit(solution)/shard_map/all_to_all | solution.py:285
  72.2 0.7 gather_fusion
  72.9 4.0 %collective-permute-start.1 = (bf16[256,576]{1,0:T(8,128)(2,1)S(1)}, bf16[256,576]{1,0:T(8,128)(2,1)S(1)}, u32[]{:S(2)}, u32[]{:S(2)}) collective-permute-start(bf16[256,576]{1,0:T(8,128)(2,1)S(1)} %bitcast.38), channel_id=1, source_target_pairs={{0,8},{8,0},{1,9},{9,1},{2,10},{10,2},{3,11},{11,3},{4,12},{12,4},... | collective-permute-start | bytes 884744 | tf_op jit(solution)/shard_map/ppermute | solution.py:262
  76.9 1.2 collective-permute-done.1
  78.3 0.2 copy.14
  78.5 3.1 %collective-permute-start.2 = (bf16[512,576]{0,1:T(8,128)(2,1)S(1)}, bf16[512,576]{0,1:T(8,128)(2,1)S(1)}, u32[]{:S(2)}, u32[]{:S(2)}) collective-permute-start(bf16[512,576]{0,1:T(8,128)(2,1)S(1)} %copy.14), channel_id=1, source_target_pairs={{0,2},{2,4},{4,6},{6,0},{1,3},{3,5},{5,7},{7,1},{8,10},{10,12},{12... | collective-permute-start | bytes 1769480 | tf_op jit(solution)/shard_map/ppermute | solution.py:306
  81.6 3.4 %collective-permute-start.3 = (bf16[512,576]{0,1:T(8,128)(2,1)S(1)}, bf16[512,576]{0,1:T(8,128)(2,1)S(1)}, u32[]{:S(2)}, u32[]{:S(2)}) collective-permute-start(bf16[512,576]{0,1:T(8,128)(2,1)S(1)} %copy.14), channel_id=1, source_target_pairs={{0,6},{2,0},{4,2},{6,4},{1,7},{3,1},{5,3},{7,5},{8,14},{10,8},{12,... | collective-permute-start | bytes 1769480 | tf_op jit(solution)/shard_map/ppermute | solution.py:307
  85.0 4.8 %attend.3 = (f32[1,1,1024]{2,1,0:T(1,128)}, f32[1,1,1024]{2,1,0:T(1,128)}, f32[1,512,1024]{2,1,0:T(8,128)}) custom-call(s32[25]{0:T(128)} %concatenate.13.refs_0_, bf16[1,1024,576]{2,1,0:T(8,128)(2,1)} %get-tuple-element.34.refs_1_, bf16[512,576]{1,0:T(8,128)(2,1)} %copy-done.2), custom_call_target="tpu_custom_call" | custom-call | flops 20000000000 | bytes 4194304 | tf_op jit(solution)/shard_map/attend/pallas_call | solution.py:111
  89.8 6.5 %collective-permute-done.2 = bf16[512,576]{0,1:T(8,128)(2,1)S(1)} collective-permute-done((bf16[512,576]{0,1:T(8,128)(2,1)S(1)}, bf16[512,576]{0,1:T(8,128)(2,1)S(1)}, u32[]{:S(2)}, u32[]{:S(2)}) %collective-permute-start.2) | collective-permute-done | bytes 589856 | tf_op jit(solution)/shard_map/ppermute | solution.py:306
  96.3 1.6 collective-permute-done.3
  97.8 0.3 copy.16.refs_2_
  98.2 0.3 copy.17.refs_3_
  98.5 3.1 %collective-permute-start.4 = (bf16[256,576]{1,0:T(8,128)(2,1)S(1)}, bf16[256,576]{1,0:T(8,128)(2,1)S(1)}, u32[]{:S(2)}, u32[]{:S(2)}) collective-permute-start(bf16[256,576]{1,0:T(8,128)(2,1)S(1)} %slice.44), channel_id=1, source_target_pairs={{0,2},{2,4},{4,6},{6,0},{1,3},{3,5},{5,7},{7,1},{8,10},{10,12},{12... | collective-permute-start | bytes 884744 | tf_op jit(solution)/shard_map/ppermute | solution.py:311
  101.7 3.4 %collective-permute-start.5 = (bf16[256,576]{1,0:T(8,128)(2,1)S(1)}, bf16[256,576]{1,0:T(8,128)(2,1)S(1)}, u32[]{:S(2)}, u32[]{:S(2)}) collective-permute-start(bf16[256,576]{1,0:T(8,128)(2,1)S(1)} %slice.45), channel_id=1, source_target_pairs={{0,6},{2,0},{4,2},{6,4},{1,7},{3,1},{5,3},{7,5},{8,14},{10,8},{12,... | collective-permute-start | bytes 884744 | tf_op jit(solution)/shard_map/ppermute | solution.py:312
  105.1 7.4 %attend.4 = (f32[1,1,1024]{2,1,0:T(1,128)}, f32[1,1,1024]{2,1,0:T(1,128)}, f32[1,512,1024]{2,1,0:T(8,128)}) custom-call(s32[25]{0:T(128)} %concatenate.13.refs_0_, bf16[1,1024,576]{2,1,0:T(8,128)(2,1)} %get-tuple-element.34.refs_1_, bf16[512,576]{1,0:T(8,128)(2,1)} %copy-done.3, bf16[512,576]{1,0:T(8,128)(2,1)} %copy-done.4, ...), custom_call_target="tpu_custom_call" | custom-call | flops 20000000000 | bytes 4194304 | tf_op jit(solution)/shard_map/attend/pallas_call | solution.py:111
  112.5 0.7 copy-done.12
  113.2 0.1 copy-done.13
  113.3 5.3 %attend.5.own_ref = bf16[1024,128]{1,0:T(8,128)(2,1)} custom-call(s32[25]{0:T(128)} %concatenate.13.refs_0_, bf16[1,1024,576]{2,1,0:T(8,128)(2,1)} %get-tuple-element.34.refs_1_, bf16[256,576]{1,0:T(8,128)(2,1)} %copy-done.12, bf16[256,576]{1,0:T(8,128)(2,1)} %copy-done.13, f32[1,1,1024]{2,1,0:T(1,128)} %get-tuple-element.50.refs_4_, ...), custom_call_target="tpu_custom_call" | custom-call | flops 20000000000 | bytes 4194304 | tf_op jit(solution)/shard_map/attend/pallas_call | solution.py:111
  118.6 3.8 %collective-permute-start.9 = (bf16[1024,128]{1,0:T(8,128)(2,1)}, bf16[1024,128]{1,0:T(8,128)(2,1)S(1)}, u32[]{:S(2)}, u32[]{:S(2)}) collective-permute-start(bf16[1024,128]{1,0:T(8,128)(2,1)} %attend.5.own_ref), channel_id=1, source_target_pairs={{0,8},{8,0},{1,9},{9,1},{2,10},{10,2},{3,11},{11,3},{4,12},{12,4},... | collective-permute-start | bytes 786440 | tf_op jit(solution)/shard_map/ppermute | solution.py:262
  122.4 1.4 collective-permute-done.9.other_ref
  123.8 0.7 copy-done.7
  124.5 4.2 %project.1 = bf16[8,224,256]{2,1,0:T(8,128)(2,1)} custom-call(bf16[32,72,1024]{2,1,0:T(8,128)(2,1)} %all-gather.2.cloned.1.call-done.w_ref, bf16[1024,128]{1,0:T(8,128)(2,1)} %attend.5.own_ref, bf16[1024,128]{1,0:T(8,128)(2,1)} %copy-done.7), custom_call_target="tpu_custom_call" | custom-call | tf_op jit(solution)/shard_map/project/pallas_call | solution.py:249
  128.7 1.3 slice.35.own_ref
  130.0 2.3 %collective-permute-start.10 = (bf16[32,16,1024]{2,1,0:T(8,128)(2,1)S(1)}, bf16[32,16,1024]{2,1,0:T(8,128)(2,1)S(1)}, u32[]{:S(2)}, u32[]{:S(2)}) collective-permute-start(bf16[32,16,1024]{2,1,0:T(8,128)(2,1)S(1)} %slice.35.own_ref), channel_id=1, source_target_pairs={{0,8},{8,0},{1,9},{9,1},{2,10},{10,2},{3,11},{11,3},{4,12},{12,4},... | collective-permute-start | bytes 3145736 | tf_op jit(solution)/shard_map/ppermute | solution.py:262
  132.3 3.5 %all-to-all-start.1 = ((bf16[4,2,224,256]{3,2,1,0:T(8,128)(2,1)}), bf16[4,2,224,256]{3,2,1,0:T(8,128)(2,1)S(1)}, u32[]{:S(2)}, u32[]{:S(2)}) async-start(bf16[4,2,224,256]{3,2,1,0:T(8,128)(2,1)} %bitcast.18), calls=%async_computation.1 | async-start | bytes 1835008 | tf_op jit(solution)/shard_map/all_to_all | solution.py:322
  135.8 0.7 pad_add_fusion.1.place_ref
  136.5 1.0 copy-done.5
  137.5 7.5 %index_scores.1 = f32[16,8192]{1,0:T(8,128)} custom-call(s32[2]{0:T(128)} %pad_add_fusion.1.place_ref, bf16[16,4096]{1,0:T(8,128)(2,1)} %query_ref.1, f32[16,32]{1,0:T(8,128)} %w_ref.1, bf16[32,16,1024]{2,1,0:T(8,128)(2,1)} %copy-done.1, bf16[32,16,1024]{2,1,0:T(8,128)(2,1)} %copy-done.5), custom_call_target="tpu_custom_call" | custom-call | flops 100000000 | bytes 100000 | tf_op jit(solution)/shard_map/index_scores/pallas_call | solution.py:172
  145.0 4.5 %all-to-all-done.1 = bf16[4,2,224,256]{3,2,1,0:T(8,128)(2,1)S(1)} async-done(((bf16[4,2,224,256]{3,2,1,0:T(8,128)(2,1)}), bf16[4,2,224,256]{3,2,1,0:T(8,128)(2,1)S(1)}, u32[]{:S(2)}, u32[]{:S(2)}) %all-to-all-start.1) | async-done | bytes 917536 | tf_op jit(solution)/shard_map/all_to_all | solution.py:322
  149.5 0.1 convert_reduce_fusion
  149.6 8.0 %collective-permute-start.11 = (bf16[224,256]{1,0:T(8,128)(2,1)S(1)}, bf16[224,256]{1,0:T(8,128)(2,1)S(1)}, u32[]{:S(2)}, u32[]{:S(2)}) collective-permute-start(bf16[224,256]{1,0:T(8,128)(2,1)S(1)} %fusion.1), channel_id=1, source_target_pairs={{0,1},{1,0},{2,3},{3,2},{4,5},{5,4},{6,7},{7,6},{8,9},{9,8},{10,11... | collective-permute-start | bytes 344072 | tf_op jit(solution)/shard_map/ppermute | solution.py:331
  157.6 2.5 %collective-permute-done.11 = bf16[224,256]{1,0:T(8,128)(2,1)S(1)} collective-permute-done((bf16[224,256]{1,0:T(8,128)(2,1)S(1)}, bf16[224,256]{1,0:T(8,128)(2,1)S(1)}, u32[]{:S(2)}, u32[]{:S(2)}) %collective-permute-start.11) | collective-permute-done | bytes 114720 | tf_op jit(solution)/shard_map/ppermute | solution.py:331
  160.2 5.3 %collective-permute-start.12 = (bf16[224,128]{1,0:T(8,128)(2,1)S(1)}, bf16[224,128]{1,0:T(8,128)(2,1)S(1)}, u32[]{:S(2)}, u32[]{:S(2)}) collective-permute-start(bf16[224,128]{1,0:T(8,128)(2,1)S(1)} %slice.49), channel_id=1, source_target_pairs={{0,8},{8,0},{1,9},{9,1},{2,10},{10,2},{3,11},{11,3},{4,12},{12,4},... | collective-permute-start | bytes 172040 | tf_op jit(solution)/shard_map/ppermute | solution.py:262
  165.6 0.9 collective-permute-done.12
  166.4 0.7 pad_maximum_fusion.2
  (46 shorter events, 0.7 us)
Async XLA Ops:
  7.2 14.4 %copy-start = (bf16[128,576]{0,1:T(8,128)(2,1)S(1)}, bf16[128,576]{0,1:T(8,128)(2,1)}, u32[]{:S(2)}) copy-start(bf16[128,576]{0,1:T(8,128)(2,1)} %param.12) | copy-start | bytes 442372
  8.9 14.1 %copy-start.6 = (bf16[72,1024]{1,0:T(8,128)(2,1)}, bf16[72,1024]{1,0:T(8,128)(2,1)S(1)}, u32[]{:S(2)}) copy-start(bf16[72,1024]{1,0:T(8,128)(2,1)S(1)} %pad_maximum_fusion.1.refs_0_) | copy-start | bytes 442372
  8.9 28.8 %collective-permute-start.6 = (bf16[72,1024]{1,0:T(8,128)(2,1)S(1)}, bf16[72,1024]{1,0:T(8,128)(2,1)S(1)}, u32[]{:S(2)}, u32[]{:S(2)}) collective-permute-start(bf16[72,1024]{1,0:T(8,128)(2,1)S(1)} %pad_maximum_fusion.1.refs_0_), channel_id=1, source_target_pairs={{0,16},{16,0},{32,48},{48,32},{1,17},{17,1},{33,49},{49,33},{2,18}... | collective-permute-start | bytes 442376 | tf_op jit(solution)/shard_map/ppermute | solution.py:283
  13.8 24.0 %collective-permute-start.7 = (bf16[72,1024]{1,0:T(8,128)(2,1)S(1)}, bf16[72,1024]{1,0:T(8,128)(2,1)S(1)}, u32[]{:S(2)}, u32[]{:S(2)}) collective-permute-start(bf16[72,1024]{1,0:T(8,128)(2,1)S(1)} %pad_maximum_fusion.1.refs_0_), channel_id=1, source_target_pairs={{0,32},{16,48},{32,0},{48,16},{1,33},{17,49},{33,1},{49,17},{2,34}... | collective-permute-start | bytes 442376 | tf_op jit(solution)/shard_map/ppermute | solution.py:283
  19.6 18.2 %collective-permute-start.8 = (bf16[72,1024]{1,0:T(8,128)(2,1)S(1)}, bf16[72,1024]{1,0:T(8,128)(2,1)S(1)}, u32[]{:S(2)}, u32[]{:S(2)}) collective-permute-start(bf16[72,1024]{1,0:T(8,128)(2,1)S(1)} %pad_maximum_fusion.1.refs_0_), channel_id=1, source_target_pairs={{0,48},{16,32},{32,16},{48,0},{1,49},{17,33},{33,17},{49,1},{2,50}... | collective-permute-start | bytes 442376 | tf_op jit(solution)/shard_map/ppermute | solution.py:283
  23.0 12.3 %copy-start.11 = (s32[1,16]{1,0:T(1,128)S(1)}, s32[1,16]{1,0:T(1,128)}, u32[]{:S(2)}) copy-start(s32[1,16]{1,0:T(1,128)} %param.13) | copy-start | bytes 196
  23.0 49.2 %all-to-all-start = ((bf16[64,16,576]{2,1,0:T(8,128)(2,1)}), bf16[64,16,576]{2,1,0:T(8,128)(2,1)S(1)}, u32[]{:S(2)}, u32[]{:S(2)}) async-start(bf16[64,16,576]{2,1,0:T(8,128)(2,1)} %bitcast.1), calls=%async_computation | async-start | bytes 2621440 | tf_op jit(solution)/shard_map/all_to_all | solution.py:285
  35.3 83.3 %all-gather.2.cloned.1.call-start = ((), (), s32[]{:S(2)}) async-start(), calls=%async_computation.2 | async-start | bytes 5308416 | tf_op jit(solution)/shard_map/all_gather | solution.py:297
  35.3 9.4 %collective-permute-start = (s32[16]{0:T(128)S(1)}, s32[16]{0:T(128)S(1)}, u32[]{:S(2)}, u32[]{:S(2)}) collective-permute-start(s32[16]{0:T(128)S(1)} %broadcast_maximum_fusion), channel_id=1, source_target_pairs={{0,8},{8,0},{1,9},{9,1},{2,10},{10,2},{3,11},{11,3},{4,12},{12,4},... | collective-permute-start | bytes 200 | tf_op jit(solution)/shard_map/ppermute | solution.py:262
  37.7 0.7 copy-start.8
  37.7 0.7 copy-start.9
  37.8 0.7 copy-start.10
  72.9 5.3 %collective-permute-start.1 = (bf16[256,576]{1,0:T(8,128)(2,1)S(1)}, bf16[256,576]{1,0:T(8,128)(2,1)S(1)}, u32[]{:S(2)}, u32[]{:S(2)}) collective-permute-start(bf16[256,576]{1,0:T(8,128)(2,1)S(1)} %bitcast.38), channel_id=1, source_target_pairs={{0,8},{8,0},{1,9},{9,1},{2,10},{10,2},{3,11},{11,3},{4,12},{12,4},... | collective-permute-start | bytes 884744 | tf_op jit(solution)/shard_map/ppermute | solution.py:262
  78.2 6.8 %copy-start.2 = (bf16[512,576]{1,0:T(8,128)(2,1)}, bf16[512,576]{1,0:T(8,128)(2,1)S(1)}, u32[]{:S(2)}) copy-start(bf16[512,576]{1,0:T(8,128)(2,1)S(1)} %pad_maximum_fusion.refs_2_) | copy-start | bytes 1769476
  78.5 17.8 %collective-permute-start.2 = (bf16[512,576]{0,1:T(8,128)(2,1)S(1)}, bf16[512,576]{0,1:T(8,128)(2,1)S(1)}, u32[]{:S(2)}, u32[]{:S(2)}) collective-permute-start(bf16[512,576]{0,1:T(8,128)(2,1)S(1)} %copy.14), channel_id=1, source_target_pairs={{0,2},{2,4},{4,6},{6,0},{1,3},{3,5},{5,7},{7,1},{8,10},{10,12},{12... | collective-permute-start | bytes 1769480 | tf_op jit(solution)/shard_map/ppermute | solution.py:306
  81.6 16.2 %collective-permute-start.3 = (bf16[512,576]{0,1:T(8,128)(2,1)S(1)}, bf16[512,576]{0,1:T(8,128)(2,1)S(1)}, u32[]{:S(2)}, u32[]{:S(2)}) collective-permute-start(bf16[512,576]{0,1:T(8,128)(2,1)S(1)} %copy.14), channel_id=1, source_target_pairs={{0,6},{2,0},{4,2},{6,4},{1,7},{3,1},{5,3},{7,5},{8,14},{10,8},{12,... | collective-permute-start | bytes 1769480 | tf_op jit(solution)/shard_map/ppermute | solution.py:307
  98.1 6.9 %copy-start.3 = (bf16[512,576]{1,0:T(8,128)(2,1)}, bf16[512,576]{1,0:T(8,128)(2,1)S(1)}, u32[]{:S(2)}) copy-start(bf16[512,576]{1,0:T(8,128)(2,1)S(1)} %copy.16.refs_2_) | copy-start | bytes 1769476
  98.4 6.6 %copy-start.4 = (bf16[512,576]{1,0:T(8,128)(2,1)}, bf16[512,576]{1,0:T(8,128)(2,1)S(1)}, u32[]{:S(2)}) copy-start(bf16[512,576]{1,0:T(8,128)(2,1)S(1)} %copy.17.refs_3_) | copy-start | bytes 1769476
  98.5 14.0 %collective-permute-start.4 = (bf16[256,576]{1,0:T(8,128)(2,1)S(1)}, bf16[256,576]{1,0:T(8,128)(2,1)S(1)}, u32[]{:S(2)}, u32[]{:S(2)}) collective-permute-start(bf16[256,576]{1,0:T(8,128)(2,1)S(1)} %slice.44), channel_id=1, source_target_pairs={{0,2},{2,4},{4,6},{6,0},{1,3},{3,5},{5,7},{7,1},{8,10},{10,12},{12... | collective-permute-start | bytes 884744 | tf_op jit(solution)/shard_map/ppermute | solution.py:311
  101.7 10.8 %collective-permute-start.5 = (bf16[256,576]{1,0:T(8,128)(2,1)S(1)}, bf16[256,576]{1,0:T(8,128)(2,1)S(1)}, u32[]{:S(2)}, u32[]{:S(2)}) collective-permute-start(bf16[256,576]{1,0:T(8,128)(2,1)S(1)} %slice.45), channel_id=1, source_target_pairs={{0,6},{2,0},{4,2},{6,4},{1,7},{3,1},{5,3},{7,5},{8,14},{10,8},{12,... | collective-permute-start | bytes 884744 | tf_op jit(solution)/shard_map/ppermute | solution.py:312
  112.5 0.7 copy-start.12
  112.5 0.8 copy-start.13
  118.6 5.2 %collective-permute-start.9 = (bf16[1024,128]{1,0:T(8,128)(2,1)}, bf16[1024,128]{1,0:T(8,128)(2,1)S(1)}, u32[]{:S(2)}, u32[]{:S(2)}) collective-permute-start(bf16[1024,128]{1,0:T(8,128)(2,1)} %attend.5.own_ref), channel_id=1, source_target_pairs={{0,8},{8,0},{1,9},{9,1},{2,10},{10,2},{3,11},{11,3},{4,12},{12,4},... | collective-permute-start | bytes 786440 | tf_op jit(solution)/shard_map/ppermute | solution.py:262
  123.7 0.7 copy-start.7
  130.0 6.5 %copy-start.1 = (bf16[32,16,1024]{2,1,0:T(8,128)(2,1)}, bf16[32,16,1024]{2,1,0:T(8,128)(2,1)S(1)}, u32[]{:S(2)}) copy-start(bf16[32,16,1024]{2,1,0:T(8,128)(2,1)S(1)} %slice.35.own_ref) | copy-start | bytes 3145732
  130.0 6.5 %collective-permute-start.10 = (bf16[32,16,1024]{2,1,0:T(8,128)(2,1)S(1)}, bf16[32,16,1024]{2,1,0:T(8,128)(2,1)S(1)}, u32[]{:S(2)}, u32[]{:S(2)}) collective-permute-start(bf16[32,16,1024]{2,1,0:T(8,128)(2,1)S(1)} %slice.35.own_ref), channel_id=1, source_target_pairs={{0,8},{8,0},{1,9},{9,1},{2,10},{10,2},{3,11},{11,3},{4,12},{12,4},... | collective-permute-start | bytes 3145736 | tf_op jit(solution)/shard_map/ppermute | solution.py:262
  132.3 17.2 %all-to-all-start.1 = ((bf16[4,2,224,256]{3,2,1,0:T(8,128)(2,1)}), bf16[4,2,224,256]{3,2,1,0:T(8,128)(2,1)S(1)}, u32[]{:S(2)}, u32[]{:S(2)}) async-start(bf16[4,2,224,256]{3,2,1,0:T(8,128)(2,1)} %bitcast.18), calls=%async_computation.1 | async-start | bytes 1835008 | tf_op jit(solution)/shard_map/all_to_all | solution.py:322
  136.5 1.0 copy-start.5
  149.6 10.5 %collective-permute-start.11 = (bf16[224,256]{1,0:T(8,128)(2,1)S(1)}, bf16[224,256]{1,0:T(8,128)(2,1)S(1)}, u32[]{:S(2)}, u32[]{:S(2)}) collective-permute-start(bf16[224,256]{1,0:T(8,128)(2,1)S(1)} %fusion.1), channel_id=1, source_target_pairs={{0,1},{1,0},{2,3},{3,2},{4,5},{5,4},{6,7},{7,6},{8,9},{9,8},{10,11... | collective-permute-start | bytes 344072 | tf_op jit(solution)/shard_map/ppermute | solution.py:331
  160.2 6.2 %collective-permute-start.12 = (bf16[224,128]{1,0:T(8,128)(2,1)S(1)}, bf16[224,128]{1,0:T(8,128)(2,1)S(1)}, u32[]{:S(2)}, u32[]{:S(2)}) collective-permute-start(bf16[224,128]{1,0:T(8,128)(2,1)S(1)} %slice.49), channel_id=1, source_target_pairs={{0,8},{8,0},{1,9},{9,1},{2,10},{10,2},{3,11},{11,3},{4,12},{12,4},... | collective-permute-start | bytes 172040 | tf_op jit(solution)/shard_map/ppermute | solution.py:262
Sparse Core Ops, SparseCore 0:
  40.7 71.4 all-gather.1

commit v9 on v8

--- a/solution.py
+++ b/solution.py
@@ -204,28 +204,28 @@
         out_specs=[vmem] * 2,
         compiler_params=pltpu.CompilerParams(vmem_limit_bytes=VMEM_LIMIT),
         cost_estimate=pl.CostEstimate(
-            flops=80000000000, bytes_accessed=209715200, transcendentals=0
+            flops=1000000000, bytes_accessed=4000000, transcendentals=0
         ),
         name="prepare",
     )(latent_query, value_up)
 
 
-def arrange_kernel(z_ref, *refs):
-    out_ref = refs[NZ]
-    for step in range(NZ):
-        out_ref[z_ref[0] ^ step] = refs[step][...]
-
-
-def arrange(z, near):
+def arrange_kernel(z_ref, pair_ref, across_ref, out_ref):
+    for step in range(2):
+        out_ref[z_ref[0] ^ step] = pair_ref[step]
+        out_ref[z_ref[0] ^ 2 ^ step] = across_ref[step]
+
+
+def arrange(z, pair, across):
     vmem = pl.BlockSpec(memory_space=pltpu.VMEM)
     return pl.pallas_call(
         arrange_kernel,
         out_shape=jax.ShapeDtypeStruct((NZ, PACKED, 1024), jnp.bfloat16),
-        in_specs=[pl.BlockSpec(memory_space=pltpu.SMEM)] + [vmem] * NZ,
+        in_specs=[pl.BlockSpec(memory_space=pltpu.SMEM)] + [vmem] * 2,
         out_specs=vmem,
         compiler_params=pltpu.CompilerParams(vmem_limit_bytes=VMEM_LIMIT),
         name="arrange",
-    )(z, *near)
+    )(z, pair, across)
 
 
 def project_kernel(w_ref, own_ref, other_ref, out_ref, values_ref):
@@ -279,9 +279,9 @@
 
     key_rows = jnp.moveaxis(index_key.reshape(8, 16, IDX_DIM), 0, 1).reshape(16, 1024)
     packed = jnp.concatenate([key_rows, out_weight.T], axis=0)
-    near = [packed] + [
-        lax.ppermute(packed, "z", [(at, at ^ step) for at in range(NZ)]) for step in range(1, NZ)
-    ]
+    beside = lax.ppermute(packed, "z", [(at, at ^ 1) for at in range(NZ)])
+    pair = jnp.stack([packed, beside])
+    across = lax.ppermute(pair, "z", [(at, at ^ 2) for at in range(NZ)])
     pool = lax.all_to_all(wide, CTX, 0, 0)
     listed = block_lists[0]
     safe = jnp.maximum(listed, 0)
@@ -293,7 +293,7 @@
     ]
     place = jnp.concatenate([listed, jnp.stack([ctx_pos * BLOCK] + offsets)])
     queries, up_t = prepare(latent_query, value_up)
-    near_z = arrange(z.reshape(1), near)
+    near_z = arrange(z.reshape(1), pair, across)
     gathered = lax.all_gather(near_z, "y", axis=0, tiled=True)
     pool, queries, up_t, both, place = lax.optimization_barrier(
         (pool, queries, up_t, both, place)

time: 175 us -> 193 us (1.10)
  waiting for transfers between devices: 45.9 us -> 70 us
  starting transfers between devices: 67.2 us -> 61.2 us
    ppermute x3 -> x2, waiting for transfers between devices: 0.01 us -> 39.3 us  [the longest x1 39.3 us: body(): across = lax.ppermute(pair, 'z', [(at, at ^ 2) for at in range(NZ)])]
    all_to_all x1, waiting for transfers between devices: 27.3 us -> 0.01 us  [body(): pool = lax.all_to_all(wide, CTX, 0, 0)]
    all_gather x1, waiting for transfers between devices: 0.01 us -> 12 us  [body(): gathered = lax.all_gather(near_z, 'y', axis=0, tiled=True)]
    ppermute x3 -> x2, starting transfers between devices: 12.6 us -> 9.02 us  [the longest x1 4.83 us: body(): beside = lax.ppermute(packed, 'z', [(at, at ^ 1) for at in range(NZ)])]
    ppermute x5, starting transfers between devices: 17.9 us -> 15.2 us  [swap_core(): return lax.ppermute(value, 'c', [(0, 1), (1, 0)])]
  transfers between devices with their start and end apart: 16 -> 15, of which waited for: 8 -> 9; matrix products, arithmetic and copies ran while one was open for 3% -> 2% of each run, Pallas kernels for 18% -> 16%
where the time goes in v9:
time: 193 us; the launch traced here: 192 us
  waiting for transfers between devices  70 us (36%)
  starting transfers between devices  61.2 us (32%)
  Pallas kernels  34.6 us (18%)
  between operations  14.5 us (8%)
  local copies, waits for them, and re-layouts  9.06 us (5%)
  other arithmetic  2.61 us (1%)
    ppermute x1, waiting for transfers between devices, body(): across = lax.ppermute(pair, 'z', [(at, at ^ 2) for at in range(NZ)])  39.3 us
    pallas_call x3, Pallas kernels, attend(): pl.pallas_call(functools.partial(attend_kernel, start, len(parts), state...  17.4 us
    ppermute x5, starting transfers between devices, swap_core(): return lax.ppermute(value, 'c', [(0, 1), (1, 0)])  15.2 us
    all_to_all x1, starting transfers between devices, body(): pool = lax.all_to_all(wide, CTX, 0, 0)  12.2 us
    all_gather x1, waiting for transfers between devices, body(): gathered = lax.all_gather(near_z, 'y', axis=0, tiled=True)  12 us
    ppermute x1, starting transfers between devices, body(): came = lax.ppermute(sent, 'w', [(0, 1), (1, 0)])  7.72 us
    pallas_call x1, Pallas kernels, index_part(): pl.pallas_call(index_kernel, out_shape=jax.ShapeDtypeStruct((16, NBLK * B...  7.52 us
    ppermute x1, waiting for transfers between devices, body(): left = lax.ppermute(mine, 'x', up)  6.77 us
  transfers between devices with their start and end apart: 15, of which 9 were waited for; matrix products, arithmetic and copies ran while one was open for 2% of the time, Pallas kernels for 16%

profile of v9, /device:TPU:1, one launch (start us, length us, event | category | flops | bytes accessed | tf_op | source)
XLA Modules:
  0.0 191.9 jit_solution(6045121950276461353)
XLA Ops:
  7.2 0.8 copy.20
  8.0 0.9 fusion.2
  8.9 4.8 %collective-permute-start.6 = (bf16[72,1024]{1,0:T(8,128)(2,1)S(1)}, bf16[72,1024]{1,0:T(8,128)(2,1)S(1)}, u32[]{:S(2)}, u32[]{:S(2)}) collective-permute-start(bf16[72,1024]{1,0:T(8,128)(2,1)S(1)} %get-tuple-element.65), channel_id=1, source_target_pairs={{0,16},{16,0},{32,48},{48,32},{1,17},{17,1},{33,49},{49,33},{2,18}... | collective-permute-start | bytes 442376 | tf_op jit(solution)/shard_map/ppermute | solution.py:282
  13.8 0.1 constant_dynamic-slice_fusion
  13.9 0.1 copy.21
  14.0 1.2 broadcast_in_dim.12
  15.3 12.2 %all-to-all-start = ((bf16[64,16,576]{2,1,0:T(8,128)(2,1)}), bf16[64,16,576]{2,1,0:T(8,128)(2,1)S(1)}, u32[]{:S(2)}, u32[]{:S(2)}) async-start(bf16[64,16,576]{2,1,0:T(8,128)(2,1)} %bitcast.1), calls=%async_computation | async-start | bytes 2621440 | tf_op jit(solution)/shard_map/all_to_all | solution.py:285
  27.6 4.2 %collective-permute-start.7 = (bf16[2,72,1024]{2,1,0:T(8,128)(2,1)S(1)}, bf16[2,72,1024]{2,1,0:T(8,128)(2,1)S(1)}, u32[]{:S(2)}, u32[]{:S(2)}) collective-permute-start(bf16[2,72,1024]{2,1,0:T(8,128)(2,1)S(1)} %pad_maximum_fusion.1.pair_ref), channel_id=1, source_target_pairs={{0,32},{16,48},{32,0},{48,16},{1,33},{17,49},{33,1},{49,17},{2,34}... | collective-permute-start | bytes 884744 | tf_op jit(solution)/shard_map/ppermute | solution.py:284
  31.8 39.3 %collective-permute-done.7.across_ref = bf16[2,72,1024]{2,1,0:T(8,128)(2,1)S(1)} collective-permute-done((bf16[2,72,1024]{2,1,0:T(8,128)(2,1)S(1)}, bf16[2,72,1024]{2,1,0:T(8,128)(2,1)S(1)}, u32[]{:S(2)}, u32[]{:S(2)}) %collective-permute-start.7) | collective-permute-done | bytes 294944 | tf_op jit(solution)/shard_map/ppermute | solution.py:284
  71.1 0.7 copy-done.7
  71.8 1.9 %arrange.1 = bf16[4,72,1024]{2,1,0:T(8,128)(2,1)} custom-call(s32[1]{0:T(128)} %bitcast.14.z_ref, bf16[2,72,1024]{2,1,0:T(8,128)(2,1)} %copy-done.5, bf16[2,72,1024]{2,1,0:T(8,128)(2,1)} %copy-done.7), custom_call_target="tpu_custom_call" | custom-call | tf_op jit(solution)/shard_map/arrange/pallas_call | solution.py:221
  73.8 2.8 %collective-permute-start = (s32[16]{0:T(128)S(1)}, s32[16]{0:T(128)S(1)}, u32[]{:S(2)}, u32[]{:S(2)}) collective-permute-start(s32[16]{0:T(128)S(1)} %broadcast_maximum_fusion), channel_id=1, source_target_pairs={{0,8},{8,0},{1,9},{9,1},{2,10},{10,2},{3,11},{11,3},{4,12},{12,4},... | collective-permute-start | bytes 200 | tf_op jit(solution)/shard_map/ppermute | solution.py:262
  76.7 3.5 %prepare.1 = (bf16[1,1024,576]{2,1,0:T(8,128)(2,1)}, bf16[8,128,512]{2,1,0:T(8,128)(2,1)}) custom-call(bf16[128,4608]{1,0:T(8,128)(2,1)} %lq_ref.1, bf16[8,512,128]{2,1,0:T(8,128)(2,1)} %up_ref.1), custom_call_target="tpu_custom_call" | custom-call | flops 1000000000 | bytes 4000000 | tf_op jit(solution)/shard_map/prepare/pallas_call | solution.py:200
  80.2 0.6 concatenate.13.refs_0_
  80.9 0.7 gather_fusion
  81.7 1.9 %collective-permute-start.1 = (bf16[256,576]{1,0:T(8,128)(2,1)S(1)}, bf16[256,576]{1,0:T(8,128)(2,1)S(1)}, u32[]{:S(2)}, u32[]{:S(2)}) collective-permute-start(bf16[256,576]{1,0:T(8,128)(2,1)S(1)} %bitcast.41), channel_id=1, source_target_pairs={{0,8},{8,0},{1,9},{9,1},{2,10},{10,2},{3,11},{11,3},{4,12},{12,4},... | collective-permute-start | bytes 884744 | tf_op jit(solution)/shard_map/ppermute | solution.py:262
  83.6 1.6 collective-permute-done.1
  85.2 0.2 copy.14
  85.5 3.1 %collective-permute-start.2 = (bf16[512,576]{0,1:T(8,128)(2,1)S(1)}, bf16[512,576]{0,1:T(8,128)(2,1)S(1)}, u32[]{:S(2)}, u32[]{:S(2)}) collective-permute-start(bf16[512,576]{0,1:T(8,128)(2,1)S(1)} %copy.14), channel_id=1, source_target_pairs={{0,2},{2,4},{4,6},{6,0},{1,3},{3,5},{5,7},{7,1},{8,10},{10,12},{12... | collective-permute-start | bytes 1769480 | tf_op jit(solution)/shard_map/ppermute | solution.py:306
  88.6 3.4 %collective-permute-start.3 = (bf16[512,576]{0,1:T(8,128)(2,1)S(1)}, bf16[512,576]{0,1:T(8,128)(2,1)S(1)}, u32[]{:S(2)}, u32[]{:S(2)}) collective-permute-start(bf16[512,576]{0,1:T(8,128)(2,1)S(1)} %copy.14), channel_id=1, source_target_pairs={{0,6},{2,0},{4,2},{6,4},{1,7},{3,1},{5,3},{7,5},{8,14},{10,8},{12,... | collective-permute-start | bytes 1769480 | tf_op jit(solution)/shard_map/ppermute | solution.py:307
  92.0 4.7 %attend.3 = (f32[1,1,1024]{2,1,0:T(1,128)}, f32[1,1,1024]{2,1,0:T(1,128)}, f32[1,512,1024]{2,1,0:T(8,128)}) custom-call(s32[25]{0:T(128)} %concatenate.13.refs_0_, bf16[1,1024,576]{2,1,0:T(8,128)(2,1)} %get-tuple-element.34.refs_1_, bf16[512,576]{1,0:T(8,128)(2,1)} %copy-done.2), custom_call_target="tpu_custom_call" | custom-call | flops 20000000000 | bytes 4194304 | tf_op jit(solution)/shard_map/attend/pallas_call | solution.py:111
  96.7 6.8 %collective-permute-done.2 = bf16[512,576]{0,1:T(8,128)(2,1)S(1)} collective-permute-done((bf16[512,576]{0,1:T(8,128)(2,1)S(1)}, bf16[512,576]{0,1:T(8,128)(2,1)S(1)}, u32[]{:S(2)}, u32[]{:S(2)}) %collective-permute-start.2) | collective-permute-done | bytes 589856 | tf_op jit(solution)/shard_map/ppermute | solution.py:306
  103.5 1.6 collective-permute-done.3
  105.1 0.3 copy.16.refs_2_
  105.4 0.3 copy.17.refs_3_
  105.7 3.1 %collective-permute-start.4 = (bf16[256,576]{1,0:T(8,128)(2,1)S(1)}, bf16[256,576]{1,0:T(8,128)(2,1)S(1)}, u32[]{:S(2)}, u32[]{:S(2)}) collective-permute-start(bf16[256,576]{1,0:T(8,128)(2,1)S(1)} %slice.44), channel_id=1, source_target_pairs={{0,2},{2,4},{4,6},{6,0},{1,3},{3,5},{5,7},{7,1},{8,10},{10,12},{12... | collective-permute-start | bytes 884744 | tf_op jit(solution)/shard_map/ppermute | solution.py:311
  108.9 3.4 %collective-permute-start.5 = (bf16[256,576]{1,0:T(8,128)(2,1)S(1)}, bf16[256,576]{1,0:T(8,128)(2,1)S(1)}, u32[]{:S(2)}, u32[]{:S(2)}) collective-permute-start(bf16[256,576]{1,0:T(8,128)(2,1)S(1)} %slice.45), channel_id=1, source_target_pairs={{0,6},{2,0},{4,2},{6,4},{1,7},{3,1},{5,3},{7,5},{8,14},{10,8},{12,... | collective-permute-start | bytes 884744 | tf_op jit(solution)/shard_map/ppermute | solution.py:312
  112.3 7.4 %attend.4 = (f32[1,1,1024]{2,1,0:T(1,128)}, f32[1,1,1024]{2,1,0:T(1,128)}, f32[1,512,1024]{2,1,0:T(8,128)}) custom-call(s32[25]{0:T(128)} %concatenate.13.refs_0_, bf16[1,1024,576]{2,1,0:T(8,128)(2,1)} %get-tuple-element.34.refs_1_, bf16[512,576]{1,0:T(8,128)(2,1)} %copy-done.3, bf16[512,576]{1,0:T(8,128)(2,1)} %copy-done.4, ...), custom_call_target="tpu_custom_call" | custom-call | flops 20000000000 | bytes 4194304 | tf_op jit(solution)/shard_map/attend/pallas_call | solution.py:111
  119.7 0.7 copy-done.10
  120.5 5.3 %attend.5.own_ref = bf16[1024,128]{1,0:T(8,128)(2,1)} custom-call(s32[25]{0:T(128)} %concatenate.13.refs_0_, bf16[1,1024,576]{2,1,0:T(8,128)(2,1)} %get-tuple-element.34.refs_1_, bf16[256,576]{1,0:T(8,128)(2,1)} %copy-done.10, bf16[256,576]{1,0:T(8,128)(2,1)} %copy-done.11, f32[1,1,1024]{2,1,0:T(1,128)} %get-tuple-element.50.refs_4_, ...), custom_call_target="tpu_custom_call" | custom-call | flops 20000000000 | bytes 4194304 | tf_op jit(solution)/shard_map/attend/pallas_call | solution.py:111
  125.8 12.0 %all-gather.2.cloned.1.call-done.w_ref = bf16[32,72,1024]{2,1,0:T(8,128)(2,1)} async-done(((bf16[4,72,1024]{2,1,0:T(8,128)(2,1)}), bf16[32,72,1024]{2,1,0:T(8,128)(2,1)}) %all-gather.2.cloned.1.call-update) | async-done | bytes 4718608 | tf_op jit(solution)/shard_map/all_gather | solution.py:297
  137.8 2.6 %collective-permute-start.8 = (bf16[1024,128]{1,0:T(8,128)(2,1)}, bf16[1024,128]{1,0:T(8,128)(2,1)S(1)}, u32[]{:S(2)}, u32[]{:S(2)}) collective-permute-start(bf16[1024,128]{1,0:T(8,128)(2,1)} %attend.5.own_ref), channel_id=1, source_target_pairs={{0,8},{8,0},{1,9},{9,1},{2,10},{10,2},{3,11},{11,3},{4,12},{12,4},... | collective-permute-start | bytes 786440 | tf_op jit(solution)/shard_map/ppermute | solution.py:262
  140.4 1.4 collective-permute-done.8.other_ref
  141.7 0.7 copy-done.8
  142.4 4.2 %project.1 = bf16[8,224,256]{2,1,0:T(8,128)(2,1)} custom-call(bf16[32,72,1024]{2,1,0:T(8,128)(2,1)} %all-gather.2.cloned.1.call-done.w_ref, bf16[1024,128]{1,0:T(8,128)(2,1)} %attend.5.own_ref, bf16[1024,128]{1,0:T(8,128)(2,1)} %copy-done.8), custom_call_target="tpu_custom_call" | custom-call | tf_op jit(solution)/shard_map/project/pallas_call | solution.py:249
  146.6 1.3 slice.35.own_ref
  148.0 2.3 %collective-permute-start.9 = (bf16[32,16,1024]{2,1,0:T(8,128)(2,1)S(1)}, bf16[32,16,1024]{2,1,0:T(8,128)(2,1)S(1)}, u32[]{:S(2)}, u32[]{:S(2)}) collective-permute-start(bf16[32,16,1024]{2,1,0:T(8,128)(2,1)S(1)} %slice.35.own_ref), channel_id=1, source_target_pairs={{0,8},{8,0},{1,9},{9,1},{2,10},{10,2},{3,11},{11,3},{4,12},{12,4},... | collective-permute-start | bytes 3145736 | tf_op jit(solution)/shard_map/ppermute | solution.py:262
  150.3 4.0 %all-to-all-start.1 = ((bf16[4,2,224,256]{3,2,1,0:T(8,128)(2,1)}), bf16[4,2,224,256]{3,2,1,0:T(8,128)(2,1)S(1)}, u32[]{:S(2)}, u32[]{:S(2)}) async-start(bf16[4,2,224,256]{3,2,1,0:T(8,128)(2,1)} %bitcast.20), calls=%async_computation.1 | async-start | bytes 1835008 | tf_op jit(solution)/shard_map/all_to_all | solution.py:322
  154.2 0.6 pad_add_fusion.1.place_ref
  154.9 1.0 copy-done.6
  155.9 7.5 %index_scores.1 = f32[16,8192]{1,0:T(8,128)} custom-call(s32[2]{0:T(128)} %pad_add_fusion.1.place_ref, bf16[16,4096]{1,0:T(8,128)(2,1)} %query_ref.1, f32[16,32]{1,0:T(8,128)} %w_ref.1, bf16[32,16,1024]{2,1,0:T(8,128)(2,1)} %copy-done.1, bf16[32,16,1024]{2,1,0:T(8,128)(2,1)} %copy-done.6), custom_call_target="tpu_custom_call" | custom-call | flops 100000000 | bytes 100000 | tf_op jit(solution)/shard_map/index_scores/pallas_call | solution.py:172
  163.4 4.2 %all-to-all-done.1 = bf16[4,2,224,256]{3,2,1,0:T(8,128)(2,1)S(1)} async-done(((bf16[4,2,224,256]{3,2,1,0:T(8,128)(2,1)}), bf16[4,2,224,256]{3,2,1,0:T(8,128)(2,1)S(1)}, u32[]{:S(2)}, u32[]{:S(2)}) %all-to-all-start.1) | async-done | bytes 917536 | tf_op jit(solution)/shard_map/all_to_all | solution.py:322
  167.6 0.1 convert_reduce_fusion
  167.8 7.7 %collective-permute-start.10 = (bf16[224,256]{1,0:T(8,128)(2,1)S(1)}, bf16[224,256]{1,0:T(8,128)(2,1)S(1)}, u32[]{:S(2)}, u32[]{:S(2)}) collective-permute-start(bf16[224,256]{1,0:T(8,128)(2,1)S(1)} %fusion.1), channel_id=1, source_target_pairs={{0,1},{1,0},{2,3},{3,2},{4,5},{5,4},{6,7},{7,6},{8,9},{9,8},{10,11... | collective-permute-start | bytes 344072 | tf_op jit(solution)/shard_map/ppermute | solution.py:331
  175.5 2.3 %collective-permute-done.10 = bf16[224,256]{1,0:T(8,128)(2,1)S(1)} collective-permute-done((bf16[224,256]{1,0:T(8,128)(2,1)S(1)}, bf16[224,256]{1,0:T(8,128)(2,1)S(1)}, u32[]{:S(2)}, u32[]{:S(2)}) %collective-permute-start.10) | collective-permute-done | bytes 114720 | tf_op jit(solution)/shard_map/ppermute | solution.py:331
  177.8 5.7 %collective-permute-start.11 = (bf16[224,128]{1,0:T(8,128)(2,1)S(1)}, bf16[224,128]{1,0:T(8,128)(2,1)S(1)}, u32[]{:S(2)}, u32[]{:S(2)}) collective-permute-start(bf16[224,128]{1,0:T(8,128)(2,1)S(1)} %slice.49), channel_id=1, source_target_pairs={{0,8},{8,0},{1,9},{9,1},{2,10},{10,2},{3,11},{11,3},{4,12},{12,4},... | collective-permute-start | bytes 172040 | tf_op jit(solution)/shard_map/ppermute | solution.py:262
  183.5 0.9 collective-permute-done.11
  184.4 0.7 pad_maximum_fusion.3
  (41 shorter events, 0.6 us)
Async XLA Ops:
  7.2 6.6 %copy-start = (bf16[128,576]{0,1:T(8,128)(2,1)S(1)}, bf16[128,576]{0,1:T(8,128)(2,1)}, u32[]{:S(2)}) copy-start(bf16[128,576]{0,1:T(8,128)(2,1)} %param.12) | copy-start | bytes 442372
  8.9 18.6 %collective-permute-start.6 = (bf16[72,1024]{1,0:T(8,128)(2,1)S(1)}, bf16[72,1024]{1,0:T(8,128)(2,1)S(1)}, u32[]{:S(2)}, u32[]{:S(2)}) collective-permute-start(bf16[72,1024]{1,0:T(8,128)(2,1)S(1)} %get-tuple-element.65), channel_id=1, source_target_pairs={{0,16},{16,0},{32,48},{48,32},{1,17},{17,1},{33,49},{49,33},{2,18}... | collective-permute-start | bytes 442376 | tf_op jit(solution)/shard_map/ppermute | solution.py:282
  15.3 65.6 %all-to-all-start = ((bf16[64,16,576]{2,1,0:T(8,128)(2,1)}), bf16[64,16,576]{2,1,0:T(8,128)(2,1)S(1)}, u32[]{:S(2)}, u32[]{:S(2)}) async-start(bf16[64,16,576]{2,1,0:T(8,128)(2,1)} %bitcast.1), calls=%async_computation | async-start | bytes 2621440 | tf_op jit(solution)/shard_map/all_to_all | solution.py:285
  27.5 46.3 %copy-start.9 = (s32[1,16]{1,0:T(1,128)S(1)}, s32[1,16]{1,0:T(1,128)}, u32[]{:S(2)}) copy-start(s32[1,16]{1,0:T(1,128)} %param.13) | copy-start | bytes 196
  27.5 110.3 %all-gather.2.cloned.1.call-start = ((), (), s32[]{:S(2)}) async-start(), calls=%async_computation.2 | async-start | bytes 5308416 | tf_op jit(solution)/shard_map/all_gather | solution.py:297
  27.6 43.5 %copy-start.5 = (bf16[2,72,1024]{2,1,0:T(8,128)(2,1)}, bf16[2,72,1024]{2,1,0:T(8,128)(2,1)S(1)}, u32[]{:S(2)}) copy-start(bf16[2,72,1024]{2,1,0:T(8,128)(2,1)S(1)} %pad_maximum_fusion.1.pair_ref) | copy-start | bytes 884740
  27.6 43.5 %collective-permute-start.7 = (bf16[2,72,1024]{2,1,0:T(8,128)(2,1)S(1)}, bf16[2,72,1024]{2,1,0:T(8,128)(2,1)S(1)}, u32[]{:S(2)}, u32[]{:S(2)}) collective-permute-start(bf16[2,72,1024]{2,1,0:T(8,128)(2,1)S(1)} %pad_maximum_fusion.1.pair_ref), channel_id=1, source_target_pairs={{0,32},{16,48},{32,0},{48,16},{1,33},{17,49},{33,1},{49,17},{2,34}... | collective-permute-start | bytes 884744 | tf_op jit(solution)/shard_map/ppermute | solution.py:284
  71.1 0.7 copy-start.7
  73.8 7.0 %collective-permute-start = (s32[16]{0:T(128)S(1)}, s32[16]{0:T(128)S(1)}, u32[]{:S(2)}, u32[]{:S(2)}) collective-permute-start(s32[16]{0:T(128)S(1)} %broadcast_maximum_fusion), channel_id=1, source_target_pairs={{0,8},{8,0},{1,9},{9,1},{2,10},{10,2},{3,11},{11,3},{4,12},{12,4},... | collective-permute-start | bytes 200 | tf_op jit(solution)/shard_map/ppermute | solution.py:262
  81.7 3.5 %collective-permute-start.1 = (bf16[256,576]{1,0:T(8,128)(2,1)S(1)}, bf16[256,576]{1,0:T(8,128)(2,1)S(1)}, u32[]{:S(2)}, u32[]{:S(2)}) collective-permute-start(bf16[256,576]{1,0:T(8,128)(2,1)S(1)} %bitcast.41), channel_id=1, source_target_pairs={{0,8},{8,0},{1,9},{9,1},{2,10},{10,2},{3,11},{11,3},{4,12},{12,4},... | collective-permute-start | bytes 884744 | tf_op jit(solution)/shard_map/ppermute | solution.py:262
  85.2 6.8 %copy-start.2 = (bf16[512,576]{1,0:T(8,128)(2,1)}, bf16[512,576]{1,0:T(8,128)(2,1)S(1)}, u32[]{:S(2)}) copy-start(bf16[512,576]{1,0:T(8,128)(2,1)S(1)} %pad_maximum_fusion.refs_2_) | copy-start | bytes 1769476
  85.5 18.0 %collective-permute-start.2 = (bf16[512,576]{0,1:T(8,128)(2,1)S(1)}, bf16[512,576]{0,1:T(8,128)(2,1)S(1)}, u32[]{:S(2)}, u32[]{:S(2)}) collective-permute-start(bf16[512,576]{0,1:T(8,128)(2,1)S(1)} %copy.14), channel_id=1, source_target_pairs={{0,2},{2,4},{4,6},{6,0},{1,3},{3,5},{5,7},{7,1},{8,10},{10,12},{12... | collective-permute-start | bytes 1769480 | tf_op jit(solution)/shard_map/ppermute | solution.py:306
  88.6 16.5 %collective-permute-start.3 = (bf16[512,576]{0,1:T(8,128)(2,1)S(1)}, bf16[512,576]{0,1:T(8,128)(2,1)S(1)}, u32[]{:S(2)}, u32[]{:S(2)}) collective-permute-start(bf16[512,576]{0,1:T(8,128)(2,1)S(1)} %copy.14), channel_id=1, source_target_pairs={{0,6},{2,0},{4,2},{6,4},{1,7},{3,1},{5,3},{7,5},{8,14},{10,8},{12,... | collective-permute-start | bytes 1769480 | tf_op jit(solution)/shard_map/ppermute | solution.py:307
  105.4 6.9 %copy-start.3 = (bf16[512,576]{1,0:T(8,128)(2,1)}, bf16[512,576]{1,0:T(8,128)(2,1)S(1)}, u32[]{:S(2)}) copy-start(bf16[512,576]{1,0:T(8,128)(2,1)S(1)} %copy.16.refs_2_) | copy-start | bytes 1769476
  105.7 6.6 %copy-start.4 = (bf16[512,576]{1,0:T(8,128)(2,1)}, bf16[512,576]{1,0:T(8,128)(2,1)S(1)}, u32[]{:S(2)}) copy-start(bf16[512,576]{1,0:T(8,128)(2,1)S(1)} %copy.17.refs_3_) | copy-start | bytes 1769476
  105.7 13.9 %collective-permute-start.4 = (bf16[256,576]{1,0:T(8,128)(2,1)S(1)}, bf16[256,576]{1,0:T(8,128)(2,1)S(1)}, u32[]{:S(2)}, u32[]{:S(2)}) collective-permute-start(bf16[256,576]{1,0:T(8,128)(2,1)S(1)} %slice.44), channel_id=1, source_target_pairs={{0,2},{2,4},{4,6},{6,0},{1,3},{3,5},{5,7},{7,1},{8,10},{10,12},{12... | collective-permute-start | bytes 884744 | tf_op jit(solution)/shard_map/ppermute | solution.py:311
  108.9 10.8 %collective-permute-start.5 = (bf16[256,576]{1,0:T(8,128)(2,1)S(1)}, bf16[256,576]{1,0:T(8,128)(2,1)S(1)}, u32[]{:S(2)}, u32[]{:S(2)}) collective-permute-start(bf16[256,576]{1,0:T(8,128)(2,1)S(1)} %slice.45), channel_id=1, source_target_pairs={{0,6},{2,0},{4,2},{6,4},{1,7},{3,1},{5,3},{7,5},{8,14},{10,8},{12,... | collective-permute-start | bytes 884744 | tf_op jit(solution)/shard_map/ppermute | solution.py:312
  119.7 0.7 copy-start.10
  119.7 0.8 copy-start.11
  137.8 3.9 %collective-permute-start.8 = (bf16[1024,128]{1,0:T(8,128)(2,1)}, bf16[1024,128]{1,0:T(8,128)(2,1)S(1)}, u32[]{:S(2)}, u32[]{:S(2)}) collective-permute-start(bf16[1024,128]{1,0:T(8,128)(2,1)} %attend.5.own_ref), channel_id=1, source_target_pairs={{0,8},{8,0},{1,9},{9,1},{2,10},{10,2},{3,11},{11,3},{4,12},{12,4},... | collective-permute-start | bytes 786440 | tf_op jit(solution)/shard_map/ppermute | solution.py:262
  141.7 0.7 copy-start.8
  148.0 6.9 %copy-start.1 = (bf16[32,16,1024]{2,1,0:T(8,128)(2,1)}, bf16[32,16,1024]{2,1,0:T(8,128)(2,1)S(1)}, u32[]{:S(2)}) copy-start(bf16[32,16,1024]{2,1,0:T(8,128)(2,1)S(1)} %slice.35.own_ref) | copy-start | bytes 3145732
  148.0 6.9 %collective-permute-start.9 = (bf16[32,16,1024]{2,1,0:T(8,128)(2,1)S(1)}, bf16[32,16,1024]{2,1,0:T(8,128)(2,1)S(1)}, u32[]{:S(2)}, u32[]{:S(2)}) collective-permute-start(bf16[32,16,1024]{2,1,0:T(8,128)(2,1)S(1)} %slice.35.own_ref), channel_id=1, source_target_pairs={{0,8},{8,0},{1,9},{9,1},{2,10},{10,2},{3,11},{11,3},{4,12},{12,4},... | collective-permute-start | bytes 3145736 | tf_op jit(solution)/shard_map/ppermute | solution.py:262
  150.3 17.4 %all-to-all-start.1 = ((bf16[4,2,224,256]{3,2,1,0:T(8,128)(2,1)}), bf16[4,2,224,256]{3,2,1,0:T(8,128)(2,1)S(1)}, u32[]{:S(2)}, u32[]{:S(2)}) async-start(bf16[4,2,224,256]{3,2,1,0:T(8,128)(2,1)} %bitcast.20), calls=%async_computation.1 | async-start | bytes 1835008 | tf_op jit(solution)/shard_map/all_to_all | solution.py:322
  154.9 1.0 copy-start.6
  167.8 10.0 %collective-permute-start.10 = (bf16[224,256]{1,0:T(8,128)(2,1)S(1)}, bf16[224,256]{1,0:T(8,128)(2,1)S(1)}, u32[]{:S(2)}, u32[]{:S(2)}) collective-permute-start(bf16[224,256]{1,0:T(8,128)(2,1)S(1)} %fusion.1), channel_id=1, source_target_pairs={{0,1},{1,0},{2,3},{3,2},{4,5},{5,4},{6,7},{7,6},{8,9},{9,8},{10,11... | collective-permute-start | bytes 344072 | tf_op jit(solution)/shard_map/ppermute | solution.py:331
  177.8 6.5 %collective-permute-start.11 = (bf16[224,128]{1,0:T(8,128)(2,1)S(1)}, bf16[224,128]{1,0:T(8,128)(2,1)S(1)}, u32[]{:S(2)}, u32[]{:S(2)}) collective-permute-start(bf16[224,128]{1,0:T(8,128)(2,1)S(1)} %slice.49), channel_id=1, source_target_pairs={{0,8},{8,0},{1,9},{9,1},{2,10},{10,2},{3,11},{11,3},{4,12},{12,4},... | collective-permute-start | bytes 172040 | tf_op jit(solution)/shard_map/ppermute | solution.py:262
Sparse Core Ops, SparseCore 0:
  73.9 63.8 all-gather.1

commit v10 on v8

--- a/solution.py
+++ b/solution.py
@@ -46,7 +46,18 @@
     else:
         max_out, total_out, sum_out = refs[:3]
         refs = refs[3:]
-    bias_ref, vt_ref = refs
+    bias_ref, vt_ref = refs[:2]
+    waits = []
+    if not first:
+        held, sem = refs[2], refs[-1]
+        waits.append(pltpu.make_async_copy(sum_in, held, sem.at[0]))
+        sum_in = held
+    if last:
+        held_up = refs[3]
+        waits.append(pltpu.make_async_copy(up_ref, held_up, sem.at[1]))
+        up_ref = held_up
+    for copy in waits:
+        copy.start()
     keys = jnp.concatenate([ref[...] for ref in kv_refs], axis=0)
     n_keys = keys.shape[0]
     vt_ref[...] = keys[:, :KV_RANK].T
@@ -76,6 +87,9 @@
             (((1,), (0,)), ((), ())),
             preferred_element_type=jnp.float32,
         )
+        if pair == 0:
+            for copy in waits:
+                copy.wait()
         if not first:
             total = total + total_in[pair] * keep
             lat_sum = lat_sum + sum_in[pair] * keep
@@ -107,16 +121,27 @@
         operands.append(up_t)
         out = jax.ShapeDtypeStruct((HEADS_DEV * V_DIM, BLOCK), jnp.bfloat16)
     vmem = pl.BlockSpec(memory_space=pltpu.VMEM)
+    outside = pl.BlockSpec(memory_space=pl.ANY)
+    specs = [pl.BlockSpec(memory_space=pltpu.SMEM)] + [vmem] * (1 + len(parts))
+    scratch = [
+        pltpu.VMEM((n_keys, SHARED * BLOCK), jnp.float32),
+        pltpu.VMEM((KV_RANK, n_keys), jnp.bfloat16),
+    ]
+    if state is not None:
+        specs += [vmem, vmem, outside]
+        scratch.append(pltpu.VMEM((pairs, KV_RANK, SHARED * BLOCK), jnp.float32))
+    if last:
+        specs.append(outside)
+        scratch.append(pltpu.VMEM(up_t.shape, jnp.bfloat16))
+    if state is not None:
+        scratch.append(pltpu.SemaphoreType.DMA((2,)))
     rows = HEADS_DEV * BLOCK
     return pl.pallas_call(
         functools.partial(attend_kernel, start, len(parts), state is None, last),
         out_shape=out,
-        in_specs=[pl.BlockSpec(memory_space=pltpu.SMEM)] + [vmem] * (len(operands) - 1),
+        in_specs=specs,
         out_specs=vmem if last else (vmem,) * 3,
-        scratch_shapes=[
-            pltpu.VMEM((n_keys, SHARED * BLOCK), jnp.float32),
-            pltpu.VMEM((KV_RANK, n_keys), jnp.bfloat16),
-        ],
+        scratch_shapes=scratch,
         compiler_params=pltpu.CompilerParams(vmem_limit_bytes=VMEM_LIMIT),
         cost_estimate=pl.CostEstimate(
             flops=20000000000,

time: 175 us -> 175 us (level)
  no operation moved by 1% of the time
where the time goes in v10:
time: 175 us; the launch traced here: 174 us
  starting transfers between devices  67.6 us (39%)
  waiting for transfers between devices  45.3 us (26%)
  Pallas kernels  34.6 us (20%)
  between operations  14.5 us (8%)
  local copies, waits for them, and re-layouts  9.11 us (5%)
  other arithmetic  2.59 us (1%)
    all_to_all x1, waiting for transfers between devices, body(): pool = lax.all_to_all(wide, CTX, 0, 0)  27.3 us
    ppermute x5, starting transfers between devices, swap_core(): return lax.ppermute(value, 'c', [(0, 1), (1, 0)])  18.3 us
    pallas_call x3, Pallas kernels, attend(): pl.pallas_call(functools.partial(attend_kernel, start, len(parts), state...  17.4 us
    ppermute x3, starting transfers between devices, body(): lax.ppermute(packed, 'z', [(at, at ^ step) for at in range(NZ)])  12.6 us
    all_to_all x1, starting transfers between devices, body(): pool = lax.all_to_all(wide, CTX, 0, 0)  12.3 us
    ppermute x1, starting transfers between devices, body(): came = lax.ppermute(sent, 'w', [(0, 1), (1, 0)])  7.95 us
    pallas_call x1, Pallas kernels, index_part(): pl.pallas_call(index_kernel, out_shape=jax.ShapeDtypeStruct((16, NBLK * B...  7.52 us
    ppermute x1, waiting for transfers between devices, body(): left = lax.ppermute(mine, 'x', up)  6.47 us
  transfers between devices with their start and end apart: 16, of which 8 were waited for; matrix products, arithmetic and copies ran while one was open for 3% of the time, Pallas kernels for 18%

profile of v10, /device:TPU:1, one launch (start us, length us, event | category | flops | bytes accessed | tf_op | source)
XLA Modules:
  0.0 173.7 jit_solution(6229253357548914447)
XLA Ops:
  7.2 0.8 copy.20
  8.0 0.9 pad_maximum_fusion.1.refs_0_
  8.9 4.8 %collective-permute-start.6 = (bf16[72,1024]{1,0:T(8,128)(2,1)S(1)}, bf16[72,1024]{1,0:T(8,128)(2,1)S(1)}, u32[]{:S(2)}, u32[]{:S(2)}) collective-permute-start(bf16[72,1024]{1,0:T(8,128)(2,1)S(1)} %pad_maximum_fusion.1.refs_0_), channel_id=1, source_target_pairs={{0,16},{16,0},{32,48},{48,32},{1,17},{17,1},{33,49},{49,33},{2,18}... | collective-permute-start | bytes 442376 | tf_op jit(solution)/shard_map/ppermute | solution.py:308
  13.8 5.8 %collective-permute-start.7 = (bf16[72,1024]{1,0:T(8,128)(2,1)S(1)}, bf16[72,1024]{1,0:T(8,128)(2,1)S(1)}, u32[]{:S(2)}, u32[]{:S(2)}) collective-permute-start(bf16[72,1024]{1,0:T(8,128)(2,1)S(1)} %pad_maximum_fusion.1.refs_0_), channel_id=1, source_target_pairs={{0,32},{16,48},{32,0},{48,16},{1,33},{17,49},{33,1},{49,17},{2,34}... | collective-permute-start | bytes 442376 | tf_op jit(solution)/shard_map/ppermute | solution.py:308
  19.6 1.9 %collective-permute-start.8 = (bf16[72,1024]{1,0:T(8,128)(2,1)S(1)}, bf16[72,1024]{1,0:T(8,128)(2,1)S(1)}, u32[]{:S(2)}, u32[]{:S(2)}) collective-permute-start(bf16[72,1024]{1,0:T(8,128)(2,1)S(1)} %pad_maximum_fusion.1.refs_0_), channel_id=1, source_target_pairs={{0,48},{16,32},{32,16},{48,0},{1,49},{17,33},{33,17},{49,1},{2,50}... | collective-permute-start | bytes 442376 | tf_op jit(solution)/shard_map/ppermute | solution.py:308
  21.6 0.1 copy.21
  21.8 1.2 broadcast_in_dim.12
  23.0 12.3 %all-to-all-start = ((bf16[64,16,576]{2,1,0:T(8,128)(2,1)}), bf16[64,16,576]{2,1,0:T(8,128)(2,1)S(1)}, u32[]{:S(2)}, u32[]{:S(2)}) async-start(bf16[64,16,576]{2,1,0:T(8,128)(2,1)} %bitcast.1), calls=%async_computation | async-start | bytes 2621440 | tf_op jit(solution)/shard_map/all_to_all | solution.py:310
  35.3 2.4 %collective-permute-start = (s32[16]{0:T(128)S(1)}, s32[16]{0:T(128)S(1)}, u32[]{:S(2)}, u32[]{:S(2)}) collective-permute-start(s32[16]{0:T(128)S(1)} %broadcast_maximum_fusion), channel_id=1, source_target_pairs={{0,8},{8,0},{1,9},{9,1},{2,10},{10,2},{3,11},{11,3},{4,12},{12,4},... | collective-permute-start | bytes 200 | tf_op jit(solution)/shard_map/ppermute | solution.py:287
  37.8 0.6 copy-done.8
  38.5 2.0 %arrange.1 = bf16[4,72,1024]{2,1,0:T(8,128)(2,1)} custom-call(s32[1]{0:T(128)} %bitcast.14.z_ref, bf16[72,1024]{1,0:T(8,128)(2,1)} %copy-done.6, bf16[72,1024]{1,0:T(8,128)(2,1)} %copy-done.8, bf16[72,1024]{1,0:T(8,128)(2,1)} %copy-done.9, bf16[72,1024]{1,0:T(8,128)(2,1)} %copy-done.10), custom_call_target="tpu_custom_call" | custom-call | tf_op jit(solution)/shard_map/arrange/pallas_call | solution.py:246
  40.5 3.5 %prepare.1 = (bf16[1,1024,576]{2,1,0:T(8,128)(2,1)}, bf16[8,128,512]{2,1,0:T(8,128)(2,1)}) custom-call(bf16[128,4608]{1,0:T(8,128)(2,1)} %lq_ref.1, bf16[8,512,128]{2,1,0:T(8,128)(2,1)} %up_ref.1), custom_call_target="tpu_custom_call" | custom-call | flops 80000000000 | bytes 209715200 | tf_op jit(solution)/shard_map/prepare/pallas_call | solution.py:225
  44.0 0.7 concatenate.13.refs_0_
  44.8 27.3 %all-to-all-done = bf16[64,16,576]{2,1,0:T(8,128)(2,1)S(1)} async-done(((bf16[64,16,576]{2,1,0:T(8,128)(2,1)}), bf16[64,16,576]{2,1,0:T(8,128)(2,1)S(1)}, u32[]{:S(2)}, u32[]{:S(2)}) %all-to-all-start) | async-done | bytes 1179680 | tf_op jit(solution)/shard_map/all_to_all | solution.py:310
  72.2 0.7 gather_fusion
  72.9 4.0 %collective-permute-start.1 = (bf16[256,576]{1,0:T(8,128)(2,1)S(1)}, bf16[256,576]{1,0:T(8,128)(2,1)S(1)}, u32[]{:S(2)}, u32[]{:S(2)}) collective-permute-start(bf16[256,576]{1,0:T(8,128)(2,1)S(1)} %bitcast.38), channel_id=1, source_target_pairs={{0,8},{8,0},{1,9},{9,1},{2,10},{10,2},{3,11},{11,3},{4,12},{12,4},... | collective-permute-start | bytes 884744 | tf_op jit(solution)/shard_map/ppermute | solution.py:287
  76.9 1.2 collective-permute-done.1
  78.3 0.2 copy.14
  78.5 3.1 %collective-permute-start.2 = (bf16[512,576]{0,1:T(8,128)(2,1)S(1)}, bf16[512,576]{0,1:T(8,128)(2,1)S(1)}, u32[]{:S(2)}, u32[]{:S(2)}) collective-permute-start(bf16[512,576]{0,1:T(8,128)(2,1)S(1)} %copy.14), channel_id=1, source_target_pairs={{0,2},{2,4},{4,6},{6,0},{1,3},{3,5},{5,7},{7,1},{8,10},{10,12},{12... | collective-permute-start | bytes 1769480 | tf_op jit(solution)/shard_map/ppermute | solution.py:331
  81.6 3.4 %collective-permute-start.3 = (bf16[512,576]{0,1:T(8,128)(2,1)S(1)}, bf16[512,576]{0,1:T(8,128)(2,1)S(1)}, u32[]{:S(2)}, u32[]{:S(2)}) collective-permute-start(bf16[512,576]{0,1:T(8,128)(2,1)S(1)} %copy.14), channel_id=1, source_target_pairs={{0,6},{2,0},{4,2},{6,4},{1,7},{3,1},{5,3},{7,5},{8,14},{10,8},{12,... | collective-permute-start | bytes 1769480 | tf_op jit(solution)/shard_map/ppermute | solution.py:332
  85.0 4.8 %attend.3 = (f32[1,1,1024]{2,1,0:T(1,128)}, f32[1,1,1024]{2,1,0:T(1,128)}, f32[1,512,1024]{2,1,0:T(8,128)}) custom-call(s32[25]{0:T(128)} %concatenate.13.refs_0_, bf16[1,1024,576]{2,1,0:T(8,128)(2,1)} %get-tuple-element.34.refs_1_, bf16[512,576]{1,0:T(8,128)(2,1)} %copy-done.2), custom_call_target="tpu_custom_call" | custom-call | flops 20000000000 | bytes 4194304 | tf_op jit(solution)/shard_map/attend/pallas_call | solution.py:139
  89.8 6.5 %collective-permute-done.2 = bf16[512,576]{0,1:T(8,128)(2,1)S(1)} collective-permute-done((bf16[512,576]{0,1:T(8,128)(2,1)S(1)}, bf16[512,576]{0,1:T(8,128)(2,1)S(1)}, u32[]{:S(2)}, u32[]{:S(2)}) %collective-permute-start.2) | collective-permute-done | bytes 589856 | tf_op jit(solution)/shard_map/ppermute | solution.py:331
  96.3 1.6 collective-permute-done.3
  97.8 0.3 copy.16.refs_2_
  98.2 0.3 copy.17.refs_3_
  98.5 3.1 %collective-permute-start.4 = (bf16[256,576]{1,0:T(8,128)(2,1)S(1)}, bf16[256,576]{1,0:T(8,128)(2,1)S(1)}, u32[]{:S(2)}, u32[]{:S(2)}) collective-permute-start(bf16[256,576]{1,0:T(8,128)(2,1)S(1)} %slice.44), channel_id=1, source_target_pairs={{0,2},{2,4},{4,6},{6,0},{1,3},{3,5},{5,7},{7,1},{8,10},{10,12},{12... | collective-permute-start | bytes 884744 | tf_op jit(solution)/shard_map/ppermute | solution.py:336
  101.7 3.4 %collective-permute-start.5 = (bf16[256,576]{1,0:T(8,128)(2,1)S(1)}, bf16[256,576]{1,0:T(8,128)(2,1)S(1)}, u32[]{:S(2)}, u32[]{:S(2)}) collective-permute-start(bf16[256,576]{1,0:T(8,128)(2,1)S(1)} %slice.45), channel_id=1, source_target_pairs={{0,6},{2,0},{4,2},{6,4},{1,7},{3,1},{5,3},{7,5},{8,14},{10,8},{12,... | collective-permute-start | bytes 884744 | tf_op jit(solution)/shard_map/ppermute | solution.py:337
  105.1 7.0 %attend.4 = (f32[1,1,1024]{2,1,0:T(1,128)}, f32[1,1,1024]{2,1,0:T(1,128)}, f32[1,512,1024]{2,1,0:T(8,128)}) custom-call(s32[25]{0:T(128)} %concatenate.13.refs_0_, bf16[1,1024,576]{2,1,0:T(8,128)(2,1)} %get-tuple-element.34.refs_1_, bf16[512,576]{1,0:T(8,128)(2,1)} %copy-done.3, bf16[512,576]{1,0:T(8,128)(2,1)} %copy-done.4, ...), custom_call_target="tpu_custom_call" | custom-call | flops 20000000000 | bytes 4194304 | tf_op jit(solution)/shard_map/attend/pallas_call | solution.py:139
  112.1 0.7 copy-done.12
  112.8 0.1 copy-done.13
  112.9 5.6 %attend.5.own_ref = bf16[1024,128]{1,0:T(8,128)(2,1)} custom-call(s32[25]{0:T(128)} %concatenate.13.refs_0_, bf16[1,1024,576]{2,1,0:T(8,128)(2,1)} %get-tuple-element.34.refs_1_, bf16[256,576]{1,0:T(8,128)(2,1)} %copy-done.12, bf16[256,576]{1,0:T(8,128)(2,1)} %copy-done.13, f32[1,1,1024]{2,1,0:T(1,128)} %get-tuple-element.50.refs_4_, ...), custom_call_target="tpu_custom_call" | custom-call | flops 20000000000 | bytes 4194304 | tf_op jit(solution)/shard_map/attend/pallas_call | solution.py:139
  118.6 3.9 %collective-permute-start.9 = (bf16[1024,128]{1,0:T(8,128)(2,1)}, bf16[1024,128]{1,0:T(8,128)(2,1)S(1)}, u32[]{:S(2)}, u32[]{:S(2)}) collective-permute-start(bf16[1024,128]{1,0:T(8,128)(2,1)} %attend.5.own_ref), channel_id=1, source_target_pairs={{0,8},{8,0},{1,9},{9,1},{2,10},{10,2},{3,11},{11,3},{4,12},{12,4},... | collective-permute-start | bytes 786440 | tf_op jit(solution)/shard_map/ppermute | solution.py:287
  122.5 1.4 collective-permute-done.9.other_ref
  123.8 0.7 copy-done.7
  124.5 4.2 %project.1 = bf16[8,224,256]{2,1,0:T(8,128)(2,1)} custom-call(bf16[32,72,1024]{2,1,0:T(8,128)(2,1)} %all-gather.2.cloned.1.call-done.w_ref, bf16[1024,128]{1,0:T(8,128)(2,1)} %attend.5.own_ref, bf16[1024,128]{1,0:T(8,128)(2,1)} %copy-done.7), custom_call_target="tpu_custom_call" | custom-call | tf_op jit(solution)/shard_map/project/pallas_call | solution.py:274
  128.7 1.3 slice.35.own_ref
  130.1 2.3 %collective-permute-start.10 = (bf16[32,16,1024]{2,1,0:T(8,128)(2,1)S(1)}, bf16[32,16,1024]{2,1,0:T(8,128)(2,1)S(1)}, u32[]{:S(2)}, u32[]{:S(2)}) collective-permute-start(bf16[32,16,1024]{2,1,0:T(8,128)(2,1)S(1)} %slice.35.own_ref), channel_id=1, source_target_pairs={{0,8},{8,0},{1,9},{9,1},{2,10},{10,2},{3,11},{11,3},{4,12},{12,4},... | collective-permute-start | bytes 3145736 | tf_op jit(solution)/shard_map/ppermute | solution.py:287
  132.3 3.5 %all-to-all-start.1 = ((bf16[4,2,224,256]{3,2,1,0:T(8,128)(2,1)}), bf16[4,2,224,256]{3,2,1,0:T(8,128)(2,1)S(1)}, u32[]{:S(2)}, u32[]{:S(2)}) async-start(bf16[4,2,224,256]{3,2,1,0:T(8,128)(2,1)} %bitcast.18), calls=%async_computation.1 | async-start | bytes 1835008 | tf_op jit(solution)/shard_map/all_to_all | solution.py:347
  135.9 0.7 pad_add_fusion.1.place_ref
  136.6 1.0 copy-done.5
  137.5 7.5 %index_scores.1 = f32[16,8192]{1,0:T(8,128)} custom-call(s32[2]{0:T(128)} %pad_add_fusion.1.place_ref, bf16[16,4096]{1,0:T(8,128)(2,1)} %query_ref.1, f32[16,32]{1,0:T(8,128)} %w_ref.1, bf16[32,16,1024]{2,1,0:T(8,128)(2,1)} %copy-done.1, bf16[32,16,1024]{2,1,0:T(8,128)(2,1)} %copy-done.5), custom_call_target="tpu_custom_call" | custom-call | flops 100000000 | bytes 100000 | tf_op jit(solution)/shard_map/index_scores/pallas_call | solution.py:197
  145.0 4.2 %all-to-all-done.1 = bf16[4,2,224,256]{3,2,1,0:T(8,128)(2,1)S(1)} async-done(((bf16[4,2,224,256]{3,2,1,0:T(8,128)(2,1)}), bf16[4,2,224,256]{3,2,1,0:T(8,128)(2,1)S(1)}, u32[]{:S(2)}, u32[]{:S(2)}) %all-to-all-start.1) | async-done | bytes 917536 | tf_op jit(solution)/shard_map/all_to_all | solution.py:347
  149.2 0.1 convert_reduce_fusion
  149.4 8.0 %collective-permute-start.11 = (bf16[224,256]{1,0:T(8,128)(2,1)S(1)}, bf16[224,256]{1,0:T(8,128)(2,1)S(1)}, u32[]{:S(2)}, u32[]{:S(2)}) collective-permute-start(bf16[224,256]{1,0:T(8,128)(2,1)S(1)} %fusion.1), channel_id=1, source_target_pairs={{0,1},{1,0},{2,3},{3,2},{4,5},{5,4},{6,7},{7,6},{8,9},{9,8},{10,11... | collective-permute-start | bytes 344072 | tf_op jit(solution)/shard_map/ppermute | solution.py:356
  157.3 2.2 %collective-permute-done.11 = bf16[224,256]{1,0:T(8,128)(2,1)S(1)} collective-permute-done((bf16[224,256]{1,0:T(8,128)(2,1)S(1)}, bf16[224,256]{1,0:T(8,128)(2,1)S(1)}, u32[]{:S(2)}, u32[]{:S(2)}) %collective-permute-start.11) | collective-permute-done | bytes 114720 | tf_op jit(solution)/shard_map/ppermute | solution.py:356
  159.6 5.8 %collective-permute-start.12 = (bf16[224,128]{1,0:T(8,128)(2,1)S(1)}, bf16[224,128]{1,0:T(8,128)(2,1)S(1)}, u32[]{:S(2)}, u32[]{:S(2)}) collective-permute-start(bf16[224,128]{1,0:T(8,128)(2,1)S(1)} %slice.49), channel_id=1, source_target_pairs={{0,8},{8,0},{1,9},{9,1},{2,10},{10,2},{3,11},{11,3},{4,12},{12,4},... | collective-permute-start | bytes 172040 | tf_op jit(solution)/shard_map/ppermute | solution.py:287
  165.3 0.9 collective-permute-done.12
  166.2 0.7 pad_maximum_fusion.2
  (46 shorter events, 0.7 us)
Async XLA Ops:
  7.2 14.4 %copy-start = (bf16[128,576]{0,1:T(8,128)(2,1)S(1)}, bf16[128,576]{0,1:T(8,128)(2,1)}, u32[]{:S(2)}) copy-start(bf16[128,576]{0,1:T(8,128)(2,1)} %param.12) | copy-start | bytes 442372
  8.9 14.1 %copy-start.6 = (bf16[72,1024]{1,0:T(8,128)(2,1)}, bf16[72,1024]{1,0:T(8,128)(2,1)S(1)}, u32[]{:S(2)}) copy-start(bf16[72,1024]{1,0:T(8,128)(2,1)S(1)} %pad_maximum_fusion.1.refs_0_) | copy-start | bytes 442372
  8.9 28.8 %collective-permute-start.6 = (bf16[72,1024]{1,0:T(8,128)(2,1)S(1)}, bf16[72,1024]{1,0:T(8,128)(2,1)S(1)}, u32[]{:S(2)}, u32[]{:S(2)}) collective-permute-start(bf16[72,1024]{1,0:T(8,128)(2,1)S(1)} %pad_maximum_fusion.1.refs_0_), channel_id=1, source_target_pairs={{0,16},{16,0},{32,48},{48,32},{1,17},{17,1},{33,49},{49,33},{2,18}... | collective-permute-start | bytes 442376 | tf_op jit(solution)/shard_map/ppermute | solution.py:308
  13.8 24.0 %collective-permute-start.7 = (bf16[72,1024]{1,0:T(8,128)(2,1)S(1)}, bf16[72,1024]{1,0:T(8,128)(2,1)S(1)}, u32[]{:S(2)}, u32[]{:S(2)}) collective-permute-start(bf16[72,1024]{1,0:T(8,128)(2,1)S(1)} %pad_maximum_fusion.1.refs_0_), channel_id=1, source_target_pairs={{0,32},{16,48},{32,0},{48,16},{1,33},{17,49},{33,1},{49,17},{2,34}... | collective-permute-start | bytes 442376 | tf_op jit(solution)/shard_map/ppermute | solution.py:308
  19.6 18.2 %collective-permute-start.8 = (bf16[72,1024]{1,0:T(8,128)(2,1)S(1)}, bf16[72,1024]{1,0:T(8,128)(2,1)S(1)}, u32[]{:S(2)}, u32[]{:S(2)}) collective-permute-start(bf16[72,1024]{1,0:T(8,128)(2,1)S(1)} %pad_maximum_fusion.1.refs_0_), channel_id=1, source_target_pairs={{0,48},{16,32},{32,16},{48,0},{1,49},{17,33},{33,17},{49,1},{2,50}... | collective-permute-start | bytes 442376 | tf_op jit(solution)/shard_map/ppermute | solution.py:308
  23.0 12.3 %copy-start.11 = (s32[1,16]{1,0:T(1,128)S(1)}, s32[1,16]{1,0:T(1,128)}, u32[]{:S(2)}) copy-start(s32[1,16]{1,0:T(1,128)} %param.13) | copy-start | bytes 196
  23.0 49.2 %all-to-all-start = ((bf16[64,16,576]{2,1,0:T(8,128)(2,1)}), bf16[64,16,576]{2,1,0:T(8,128)(2,1)S(1)}, u32[]{:S(2)}, u32[]{:S(2)}) async-start(bf16[64,16,576]{2,1,0:T(8,128)(2,1)} %bitcast.1), calls=%async_computation | async-start | bytes 2621440 | tf_op jit(solution)/shard_map/all_to_all | solution.py:310
  35.3 83.3 %all-gather.2.cloned.1.call-start = ((), (), s32[]{:S(2)}) async-start(), calls=%async_computation.2 | async-start | bytes 5308416 | tf_op jit(solution)/shard_map/all_gather | solution.py:322
  35.3 9.4 %collective-permute-start = (s32[16]{0:T(128)S(1)}, s32[16]{0:T(128)S(1)}, u32[]{:S(2)}, u32[]{:S(2)}) collective-permute-start(s32[16]{0:T(128)S(1)} %broadcast_maximum_fusion), channel_id=1, source_target_pairs={{0,8},{8,0},{1,9},{9,1},{2,10},{10,2},{3,11},{11,3},{4,12},{12,4},... | collective-permute-start | bytes 200 | tf_op jit(solution)/shard_map/ppermute | solution.py:287
  37.7 0.7 copy-start.8
  37.7 0.7 copy-start.9
  37.8 0.7 copy-start.10
  72.9 5.3 %collective-permute-start.1 = (bf16[256,576]{1,0:T(8,128)(2,1)S(1)}, bf16[256,576]{1,0:T(8,128)(2,1)S(1)}, u32[]{:S(2)}, u32[]{:S(2)}) collective-permute-start(bf16[256,576]{1,0:T(8,128)(2,1)S(1)} %bitcast.38), channel_id=1, source_target_pairs={{0,8},{8,0},{1,9},{9,1},{2,10},{10,2},{3,11},{11,3},{4,12},{12,4},... | collective-permute-start | bytes 884744 | tf_op jit(solution)/shard_map/ppermute | solution.py:287
  78.2 6.8 %copy-start.2 = (bf16[512,576]{1,0:T(8,128)(2,1)}, bf16[512,576]{1,0:T(8,128)(2,1)S(1)}, u32[]{:S(2)}) copy-start(bf16[512,576]{1,0:T(8,128)(2,1)S(1)} %pad_maximum_fusion.refs_2_) | copy-start | bytes 1769476
  78.5 17.8 %collective-permute-start.2 = (bf16[512,576]{0,1:T(8,128)(2,1)S(1)}, bf16[512,576]{0,1:T(8,128)(2,1)S(1)}, u32[]{:S(2)}, u32[]{:S(2)}) collective-permute-start(bf16[512,576]{0,1:T(8,128)(2,1)S(1)} %copy.14), channel_id=1, source_target_pairs={{0,2},{2,4},{4,6},{6,0},{1,3},{3,5},{5,7},{7,1},{8,10},{10,12},{12... | collective-permute-start | bytes 1769480 | tf_op jit(solution)/shard_map/ppermute | solution.py:331
  81.6 16.2 %collective-permute-start.3 = (bf16[512,576]{0,1:T(8,128)(2,1)S(1)}, bf16[512,576]{0,1:T(8,128)(2,1)S(1)}, u32[]{:S(2)}, u32[]{:S(2)}) collective-permute-start(bf16[512,576]{0,1:T(8,128)(2,1)S(1)} %copy.14), channel_id=1, source_target_pairs={{0,6},{2,0},{4,2},{6,4},{1,7},{3,1},{5,3},{7,5},{8,14},{10,8},{12,... | collective-permute-start | bytes 1769480 | tf_op jit(solution)/shard_map/ppermute | solution.py:332
  98.1 6.9 %copy-start.3 = (bf16[512,576]{1,0:T(8,128)(2,1)}, bf16[512,576]{1,0:T(8,128)(2,1)S(1)}, u32[]{:S(2)}) copy-start(bf16[512,576]{1,0:T(8,128)(2,1)S(1)} %copy.16.refs_2_) | copy-start | bytes 1769476
  98.4 6.6 %copy-start.4 = (bf16[512,576]{1,0:T(8,128)(2,1)}, bf16[512,576]{1,0:T(8,128)(2,1)S(1)}, u32[]{:S(2)}) copy-start(bf16[512,576]{1,0:T(8,128)(2,1)S(1)} %copy.17.refs_3_) | copy-start | bytes 1769476
  98.5 13.6 %collective-permute-start.4 = (bf16[256,576]{1,0:T(8,128)(2,1)S(1)}, bf16[256,576]{1,0:T(8,128)(2,1)S(1)}, u32[]{:S(2)}, u32[]{:S(2)}) collective-permute-start(bf16[256,576]{1,0:T(8,128)(2,1)S(1)} %slice.44), channel_id=1, source_target_pairs={{0,2},{2,4},{4,6},{6,0},{1,3},{3,5},{5,7},{7,1},{8,10},{10,12},{12... | collective-permute-start | bytes 884744 | tf_op jit(solution)/shard_map/ppermute | solution.py:336
  101.7 10.4 %collective-permute-start.5 = (bf16[256,576]{1,0:T(8,128)(2,1)S(1)}, bf16[256,576]{1,0:T(8,128)(2,1)S(1)}, u32[]{:S(2)}, u32[]{:S(2)}) collective-permute-start(bf16[256,576]{1,0:T(8,128)(2,1)S(1)} %slice.45), channel_id=1, source_target_pairs={{0,6},{2,0},{4,2},{6,4},{1,7},{3,1},{5,3},{7,5},{8,14},{10,8},{12,... | collective-permute-start | bytes 884744 | tf_op jit(solution)/shard_map/ppermute | solution.py:337
  112.1 0.7 copy-start.12
  112.1 0.8 copy-start.13
  118.6 5.2 %collective-permute-start.9 = (bf16[1024,128]{1,0:T(8,128)(2,1)}, bf16[1024,128]{1,0:T(8,128)(2,1)S(1)}, u32[]{:S(2)}, u32[]{:S(2)}) collective-permute-start(bf16[1024,128]{1,0:T(8,128)(2,1)} %attend.5.own_ref), channel_id=1, source_target_pairs={{0,8},{8,0},{1,9},{9,1},{2,10},{10,2},{3,11},{11,3},{4,12},{12,4},... | collective-permute-start | bytes 786440 | tf_op jit(solution)/shard_map/ppermute | solution.py:287
  123.8 0.7 copy-start.7
  130.0 6.5 %copy-start.1 = (bf16[32,16,1024]{2,1,0:T(8,128)(2,1)}, bf16[32,16,1024]{2,1,0:T(8,128)(2,1)S(1)}, u32[]{:S(2)}) copy-start(bf16[32,16,1024]{2,1,0:T(8,128)(2,1)S(1)} %slice.35.own_ref) | copy-start | bytes 3145732
  130.1 6.5 %collective-permute-start.10 = (bf16[32,16,1024]{2,1,0:T(8,128)(2,1)S(1)}, bf16[32,16,1024]{2,1,0:T(8,128)(2,1)S(1)}, u32[]{:S(2)}, u32[]{:S(2)}) collective-permute-start(bf16[32,16,1024]{2,1,0:T(8,128)(2,1)S(1)} %slice.35.own_ref), channel_id=1, source_target_pairs={{0,8},{8,0},{1,9},{9,1},{2,10},{10,2},{3,11},{11,3},{4,12},{12,4},... | collective-permute-start | bytes 3145736 | tf_op jit(solution)/shard_map/ppermute | solution.py:287
  132.3 16.9 %all-to-all-start.1 = ((bf16[4,2,224,256]{3,2,1,0:T(8,128)(2,1)}), bf16[4,2,224,256]{3,2,1,0:T(8,128)(2,1)S(1)}, u32[]{:S(2)}, u32[]{:S(2)}) async-start(bf16[4,2,224,256]{3,2,1,0:T(8,128)(2,1)} %bitcast.18), calls=%async_computation.1 | async-start | bytes 1835008 | tf_op jit(solution)/shard_map/all_to_all | solution.py:347
  136.6 1.0 copy-start.5
  149.4 10.1 %collective-permute-start.11 = (bf16[224,256]{1,0:T(8,128)(2,1)S(1)}, bf16[224,256]{1,0:T(8,128)(2,1)S(1)}, u32[]{:S(2)}, u32[]{:S(2)}) collective-permute-start(bf16[224,256]{1,0:T(8,128)(2,1)S(1)} %fusion.1), channel_id=1, source_target_pairs={{0,1},{1,0},{2,3},{3,2},{4,5},{5,4},{6,7},{7,6},{8,9},{9,8},{10,11... | collective-permute-start | bytes 344072 | tf_op jit(solution)/shard_map/ppermute | solution.py:356
  159.6 6.6 %collective-permute-start.12 = (bf16[224,128]{1,0:T(8,128)(2,1)S(1)}, bf16[224,128]{1,0:T(8,128)(2,1)S(1)}, u32[]{:S(2)}, u32[]{:S(2)}) collective-permute-start(bf16[224,128]{1,0:T(8,128)(2,1)S(1)} %slice.49), channel_id=1, source_target_pairs={{0,8},{8,0},{1,9},{9,1},{2,10},{10,2},{3,11},{11,3},{4,12},{12,4},... | collective-permute-start | bytes 172040 | tf_op jit(solution)/shard_map/ppermute | solution.py:287
Sparse Core Ops, SparseCore 0:
  40.7 71.4 all-gather.1

commit v11 on v10

--- a/solution.py
+++ b/solution.py
@@ -48,14 +48,10 @@
         refs = refs[3:]
     bias_ref, vt_ref = refs[:2]
     waits = []
-    if not first:
+    if not first and not last:
         held, sem = refs[2], refs[-1]
-        waits.append(pltpu.make_async_copy(sum_in, held, sem.at[0]))
+        waits.append(pltpu.make_async_copy(sum_in, held, sem))
         sum_in = held
-    if last:
-        held_up = refs[3]
-        waits.append(pltpu.make_async_copy(up_ref, held_up, sem.at[1]))
-        up_ref = held_up
     for copy in waits:
         copy.start()
     keys = jnp.concatenate([ref[...] for ref in kv_refs], axis=0)
@@ -128,13 +124,12 @@
         pltpu.VMEM((KV_RANK, n_keys), jnp.bfloat16),
     ]
     if state is not None:
-        specs += [vmem, vmem, outside]
+        specs += [vmem, vmem, vmem if last else outside]
+    if last:
+        specs.append(vmem)
+    elif state is not None:
         scratch.append(pltpu.VMEM((pairs, KV_RANK, SHARED * BLOCK), jnp.float32))
-    if last:
-        specs.append(outside)
-        scratch.append(pltpu.VMEM(up_t.shape, jnp.bfloat16))
-    if state is not None:
-        scratch.append(pltpu.SemaphoreType.DMA((2,)))
+        scratch.append(pltpu.SemaphoreType.DMA)
     rows = HEADS_DEV * BLOCK
     return pl.pallas_call(
         functools.partial(attend_kernel, start, len(parts), state is None, last),

time: 175 us -> 174 us (level)
  transfers between devices with their start and end apart: 16 -> 16, of which waited for: 8 -> 8; matrix products, arithmetic and copies ran while one was open for 3% -> 3% of each run, Pallas kernels for 18% -> 17%
where the time goes in v11:
time: 174 us; the launch traced here: 173 us
  starting transfers between devices  67.6 us (39%)
  waiting for transfers between devices  45.3 us (26%)
  Pallas kernels  34.3 us (20%)
  between operations  14.5 us (8%)
  local copies, waits for them, and re-layouts  9.11 us (5%)
  other arithmetic  2.59 us (1%)
    all_to_all x1, waiting for transfers between devices, body(): pool = lax.all_to_all(wide, CTX, 0, 0)  27.3 us
    ppermute x5, starting transfers between devices, swap_core(): return lax.ppermute(value, 'c', [(0, 1), (1, 0)])  18.3 us
    pallas_call x3, Pallas kernels, attend(): pl.pallas_call(functools.partial(attend_kernel, start, len(parts), state...  17 us
    ppermute x3, starting transfers between devices, body(): lax.ppermute(packed, 'z', [(at, at ^ step) for at in range(NZ)])  12.6 us
    all_to_all x1, starting transfers between devices, body(): pool = lax.all_to_all(wide, CTX, 0, 0)  12.3 us
    ppermute x1, starting transfers between devices, body(): came = lax.ppermute(sent, 'w', [(0, 1), (1, 0)])  7.97 us
    pallas_call x1, Pallas kernels, index_part(): pl.pallas_call(index_kernel, out_shape=jax.ShapeDtypeStruct((16, NBLK * B...  7.52 us
    ppermute x1, waiting for transfers between devices, body(): left = lax.ppermute(mine, 'x', up)  6.47 us
  transfers between devices with their start and end apart: 16, of which 8 were waited for; matrix products, arithmetic and copies ran while one was open for 3% of the time, Pallas kernels for 17%

profile of v11, /device:TPU:1, one launch (start us, length us, event | category | flops | bytes accessed | tf_op | source)
XLA Modules:
  0.0 173.3 jit_solution(13375093159260632551)
XLA Ops:
  7.2 0.8 copy.20
  8.0 0.9 pad_maximum_fusion.1.refs_0_
  8.9 4.8 %collective-permute-start.6 = (bf16[72,1024]{1,0:T(8,128)(2,1)S(1)}, bf16[72,1024]{1,0:T(8,128)(2,1)S(1)}, u32[]{:S(2)}, u32[]{:S(2)}) collective-permute-start(bf16[72,1024]{1,0:T(8,128)(2,1)S(1)} %pad_maximum_fusion.1.refs_0_), channel_id=1, source_target_pairs={{0,16},{16,0},{32,48},{48,32},{1,17},{17,1},{33,49},{49,33},{2,18}... | collective-permute-start | bytes 442376 | tf_op jit(solution)/shard_map/ppermute | solution.py:303
  13.8 5.8 %collective-permute-start.7 = (bf16[72,1024]{1,0:T(8,128)(2,1)S(1)}, bf16[72,1024]{1,0:T(8,128)(2,1)S(1)}, u32[]{:S(2)}, u32[]{:S(2)}) collective-permute-start(bf16[72,1024]{1,0:T(8,128)(2,1)S(1)} %pad_maximum_fusion.1.refs_0_), channel_id=1, source_target_pairs={{0,32},{16,48},{32,0},{48,16},{1,33},{17,49},{33,1},{49,17},{2,34}... | collective-permute-start | bytes 442376 | tf_op jit(solution)/shard_map/ppermute | solution.py:303
  19.6 1.9 %collective-permute-start.8 = (bf16[72,1024]{1,0:T(8,128)(2,1)S(1)}, bf16[72,1024]{1,0:T(8,128)(2,1)S(1)}, u32[]{:S(2)}, u32[]{:S(2)}) collective-permute-start(bf16[72,1024]{1,0:T(8,128)(2,1)S(1)} %pad_maximum_fusion.1.refs_0_), channel_id=1, source_target_pairs={{0,48},{16,32},{32,16},{48,0},{1,49},{17,33},{33,17},{49,1},{2,50}... | collective-permute-start | bytes 442376 | tf_op jit(solution)/shard_map/ppermute | solution.py:303
  21.6 0.1 copy.21
  21.8 1.2 broadcast_in_dim.12
  23.0 12.3 %all-to-all-start = ((bf16[64,16,576]{2,1,0:T(8,128)(2,1)}), bf16[64,16,576]{2,1,0:T(8,128)(2,1)S(1)}, u32[]{:S(2)}, u32[]{:S(2)}) async-start(bf16[64,16,576]{2,1,0:T(8,128)(2,1)} %bitcast.1), calls=%async_computation | async-start | bytes 2621440 | tf_op jit(solution)/shard_map/all_to_all | solution.py:305
  35.3 2.4 %collective-permute-start = (s32[16]{0:T(128)S(1)}, s32[16]{0:T(128)S(1)}, u32[]{:S(2)}, u32[]{:S(2)}) collective-permute-start(s32[16]{0:T(128)S(1)} %broadcast_maximum_fusion), channel_id=1, source_target_pairs={{0,8},{8,0},{1,9},{9,1},{2,10},{10,2},{3,11},{11,3},{4,12},{12,4},... | collective-permute-start | bytes 200 | tf_op jit(solution)/shard_map/ppermute | solution.py:282
  37.8 0.6 copy-done.8
  38.5 2.0 %arrange.1 = bf16[4,72,1024]{2,1,0:T(8,128)(2,1)} custom-call(s32[1]{0:T(128)} %bitcast.14.z_ref, bf16[72,1024]{1,0:T(8,128)(2,1)} %copy-done.6, bf16[72,1024]{1,0:T(8,128)(2,1)} %copy-done.8, bf16[72,1024]{1,0:T(8,128)(2,1)} %copy-done.9, bf16[72,1024]{1,0:T(8,128)(2,1)} %copy-done.10), custom_call_target="tpu_custom_call" | custom-call | tf_op jit(solution)/shard_map/arrange/pallas_call | solution.py:241
  40.5 3.5 %prepare.1 = (bf16[1,1024,576]{2,1,0:T(8,128)(2,1)}, bf16[8,128,512]{2,1,0:T(8,128)(2,1)}) custom-call(bf16[128,4608]{1,0:T(8,128)(2,1)} %lq_ref.1, bf16[8,512,128]{2,1,0:T(8,128)(2,1)} %up_ref.1), custom_call_target="tpu_custom_call" | custom-call | flops 80000000000 | bytes 209715200 | tf_op jit(solution)/shard_map/prepare/pallas_call | solution.py:220
  44.0 0.7 concatenate.13.refs_0_
  44.8 27.3 %all-to-all-done = bf16[64,16,576]{2,1,0:T(8,128)(2,1)S(1)} async-done(((bf16[64,16,576]{2,1,0:T(8,128)(2,1)}), bf16[64,16,576]{2,1,0:T(8,128)(2,1)S(1)}, u32[]{:S(2)}, u32[]{:S(2)}) %all-to-all-start) | async-done | bytes 1179680 | tf_op jit(solution)/shard_map/all_to_all | solution.py:305
  72.2 0.7 gather_fusion
  72.9 4.0 %collective-permute-start.1 = (bf16[256,576]{1,0:T(8,128)(2,1)S(1)}, bf16[256,576]{1,0:T(8,128)(2,1)S(1)}, u32[]{:S(2)}, u32[]{:S(2)}) collective-permute-start(bf16[256,576]{1,0:T(8,128)(2,1)S(1)} %bitcast.38), channel_id=1, source_target_pairs={{0,8},{8,0},{1,9},{9,1},{2,10},{10,2},{3,11},{11,3},{4,12},{12,4},... | collective-permute-start | bytes 884744 | tf_op jit(solution)/shard_map/ppermute | solution.py:282
  76.9 1.2 collective-permute-done.1
  78.3 0.2 copy.14
  78.5 3.1 %collective-permute-start.2 = (bf16[512,576]{0,1:T(8,128)(2,1)S(1)}, bf16[512,576]{0,1:T(8,128)(2,1)S(1)}, u32[]{:S(2)}, u32[]{:S(2)}) collective-permute-start(bf16[512,576]{0,1:T(8,128)(2,1)S(1)} %copy.14), channel_id=1, source_target_pairs={{0,2},{2,4},{4,6},{6,0},{1,3},{3,5},{5,7},{7,1},{8,10},{10,12},{12... | collective-permute-start | bytes 1769480 | tf_op jit(solution)/shard_map/ppermute | solution.py:326
  81.6 3.4 %collective-permute-start.3 = (bf16[512,576]{0,1:T(8,128)(2,1)S(1)}, bf16[512,576]{0,1:T(8,128)(2,1)S(1)}, u32[]{:S(2)}, u32[]{:S(2)}) collective-permute-start(bf16[512,576]{0,1:T(8,128)(2,1)S(1)} %copy.14), channel_id=1, source_target_pairs={{0,6},{2,0},{4,2},{6,4},{1,7},{3,1},{5,3},{7,5},{8,14},{10,8},{12,... | collective-permute-start | bytes 1769480 | tf_op jit(solution)/shard_map/ppermute | solution.py:327
  85.0 4.8 %attend.3 = (f32[1,1,1024]{2,1,0:T(1,128)}, f32[1,1,1024]{2,1,0:T(1,128)}, f32[1,512,1024]{2,1,0:T(8,128)}) custom-call(s32[25]{0:T(128)} %concatenate.13.refs_0_, bf16[1,1024,576]{2,1,0:T(8,128)(2,1)} %get-tuple-element.34.refs_1_, bf16[512,576]{1,0:T(8,128)(2,1)} %copy-done.2), custom_call_target="tpu_custom_call" | custom-call | flops 20000000000 | bytes 4194304 | tf_op jit(solution)/shard_map/attend/pallas_call | solution.py:134
  89.8 6.5 %collective-permute-done.2 = bf16[512,576]{0,1:T(8,128)(2,1)S(1)} collective-permute-done((bf16[512,576]{0,1:T(8,128)(2,1)S(1)}, bf16[512,576]{0,1:T(8,128)(2,1)S(1)}, u32[]{:S(2)}, u32[]{:S(2)}) %collective-permute-start.2) | collective-permute-done | bytes 589856 | tf_op jit(solution)/shard_map/ppermute | solution.py:326
  96.3 1.6 collective-permute-done.3
  97.8 0.3 copy.16.refs_2_
  98.2 0.3 copy.17.refs_3_
  98.5 3.1 %collective-permute-start.4 = (bf16[256,576]{1,0:T(8,128)(2,1)S(1)}, bf16[256,576]{1,0:T(8,128)(2,1)S(1)}, u32[]{:S(2)}, u32[]{:S(2)}) collective-permute-start(bf16[256,576]{1,0:T(8,128)(2,1)S(1)} %slice.44), channel_id=1, source_target_pairs={{0,2},{2,4},{4,6},{6,0},{1,3},{3,5},{5,7},{7,1},{8,10},{10,12},{12... | collective-permute-start | bytes 884744 | tf_op jit(solution)/shard_map/ppermute | solution.py:331
  101.7 3.4 %collective-permute-start.5 = (bf16[256,576]{1,0:T(8,128)(2,1)S(1)}, bf16[256,576]{1,0:T(8,128)(2,1)S(1)}, u32[]{:S(2)}, u32[]{:S(2)}) collective-permute-start(bf16[256,576]{1,0:T(8,128)(2,1)S(1)} %slice.45), channel_id=1, source_target_pairs={{0,6},{2,0},{4,2},{6,4},{1,7},{3,1},{5,3},{7,5},{8,14},{10,8},{12,... | collective-permute-start | bytes 884744 | tf_op jit(solution)/shard_map/ppermute | solution.py:332
  105.1 7.0 %attend.4 = (f32[1,1,1024]{2,1,0:T(1,128)}, f32[1,1,1024]{2,1,0:T(1,128)}, f32[1,512,1024]{2,1,0:T(8,128)}) custom-call(s32[25]{0:T(128)} %concatenate.13.refs_0_, bf16[1,1024,576]{2,1,0:T(8,128)(2,1)} %get-tuple-element.34.refs_1_, bf16[512,576]{1,0:T(8,128)(2,1)} %copy-done.3, bf16[512,576]{1,0:T(8,128)(2,1)} %copy-done.4, ...), custom_call_target="tpu_custom_call" | custom-call | flops 20000000000 | bytes 4194304 | tf_op jit(solution)/shard_map/attend/pallas_call | solution.py:134
  112.1 0.7 copy-done.12
  112.8 0.1 copy-done.13
  112.9 5.3 %attend.5.own_ref = bf16[1024,128]{1,0:T(8,128)(2,1)} custom-call(s32[25]{0:T(128)} %concatenate.13.refs_0_, bf16[1,1024,576]{2,1,0:T(8,128)(2,1)} %get-tuple-element.34.refs_1_, bf16[256,576]{1,0:T(8,128)(2,1)} %copy-done.12, bf16[256,576]{1,0:T(8,128)(2,1)} %copy-done.13, f32[1,1,1024]{2,1,0:T(1,128)} %get-tuple-element.50.refs_4_, ...), custom_call_target="tpu_custom_call" | custom-call | flops 20000000000 | bytes 4194304 | tf_op jit(solution)/shard_map/attend/pallas_call | solution.py:134
  118.2 3.9 %collective-permute-start.9 = (bf16[1024,128]{1,0:T(8,128)(2,1)}, bf16[1024,128]{1,0:T(8,128)(2,1)S(1)}, u32[]{:S(2)}, u32[]{:S(2)}) collective-permute-start(bf16[1024,128]{1,0:T(8,128)(2,1)} %attend.5.own_ref), channel_id=1, source_target_pairs={{0,8},{8,0},{1,9},{9,1},{2,10},{10,2},{3,11},{11,3},{4,12},{12,4},... | collective-permute-start | bytes 786440 | tf_op jit(solution)/shard_map/ppermute | solution.py:282
  122.1 1.4 collective-permute-done.9.other_ref
  123.4 0.7 copy-done.7
  124.1 4.2 %project.1 = bf16[8,224,256]{2,1,0:T(8,128)(2,1)} custom-call(bf16[32,72,1024]{2,1,0:T(8,128)(2,1)} %all-gather.2.cloned.1.call-done.w_ref, bf16[1024,128]{1,0:T(8,128)(2,1)} %attend.5.own_ref, bf16[1024,128]{1,0:T(8,128)(2,1)} %copy-done.7), custom_call_target="tpu_custom_call" | custom-call | tf_op jit(solution)/shard_map/project/pallas_call | solution.py:269
  128.3 1.3 slice.35.own_ref
  129.7 2.3 %collective-permute-start.10 = (bf16[32,16,1024]{2,1,0:T(8,128)(2,1)S(1)}, bf16[32,16,1024]{2,1,0:T(8,128)(2,1)S(1)}, u32[]{:S(2)}, u32[]{:S(2)}) collective-permute-start(bf16[32,16,1024]{2,1,0:T(8,128)(2,1)S(1)} %slice.35.own_ref), channel_id=1, source_target_pairs={{0,8},{8,0},{1,9},{9,1},{2,10},{10,2},{3,11},{11,3},{4,12},{12,4},... | collective-permute-start | bytes 3145736 | tf_op jit(solution)/shard_map/ppermute | solution.py:282
  132.0 3.5 %all-to-all-start.1 = ((bf16[4,2,224,256]{3,2,1,0:T(8,128)(2,1)}), bf16[4,2,224,256]{3,2,1,0:T(8,128)(2,1)S(1)}, u32[]{:S(2)}, u32[]{:S(2)}) async-start(bf16[4,2,224,256]{3,2,1,0:T(8,128)(2,1)} %bitcast.18), calls=%async_computation.1 | async-start | bytes 1835008 | tf_op jit(solution)/shard_map/all_to_all | solution.py:342
  135.5 0.7 pad_add_fusion.1.place_ref
  136.2 1.0 copy-done.5
  137.1 7.5 %index_scores.1 = f32[16,8192]{1,0:T(8,128)} custom-call(s32[2]{0:T(128)} %pad_add_fusion.1.place_ref, bf16[16,4096]{1,0:T(8,128)(2,1)} %query_ref.1, f32[16,32]{1,0:T(8,128)} %w_ref.1, bf16[32,16,1024]{2,1,0:T(8,128)(2,1)} %copy-done.1, bf16[32,16,1024]{2,1,0:T(8,128)(2,1)} %copy-done.5), custom_call_target="tpu_custom_call" | custom-call | flops 100000000 | bytes 100000 | tf_op jit(solution)/shard_map/index_scores/pallas_call | solution.py:192
  144.6 4.2 %all-to-all-done.1 = bf16[4,2,224,256]{3,2,1,0:T(8,128)(2,1)S(1)} async-done(((bf16[4,2,224,256]{3,2,1,0:T(8,128)(2,1)}), bf16[4,2,224,256]{3,2,1,0:T(8,128)(2,1)S(1)}, u32[]{:S(2)}, u32[]{:S(2)}) %all-to-all-start.1) | async-done | bytes 917536 | tf_op jit(solution)/shard_map/all_to_all | solution.py:342
  148.8 0.1 convert_reduce_fusion
  149.0 8.0 %collective-permute-start.11 = (bf16[224,256]{1,0:T(8,128)(2,1)S(1)}, bf16[224,256]{1,0:T(8,128)(2,1)S(1)}, u32[]{:S(2)}, u32[]{:S(2)}) collective-permute-start(bf16[224,256]{1,0:T(8,128)(2,1)S(1)} %fusion.1), channel_id=1, source_target_pairs={{0,1},{1,0},{2,3},{3,2},{4,5},{5,4},{6,7},{7,6},{8,9},{9,8},{10,11... | collective-permute-start | bytes 344072 | tf_op jit(solution)/shard_map/ppermute | solution.py:351
  157.0 2.2 %collective-permute-done.11 = bf16[224,256]{1,0:T(8,128)(2,1)S(1)} collective-permute-done((bf16[224,256]{1,0:T(8,128)(2,1)S(1)}, bf16[224,256]{1,0:T(8,128)(2,1)S(1)}, u32[]{:S(2)}, u32[]{:S(2)}) %collective-permute-start.11) | collective-permute-done | bytes 114720 | tf_op jit(solution)/shard_map/ppermute | solution.py:351
  159.2 5.7 %collective-permute-start.12 = (bf16[224,128]{1,0:T(8,128)(2,1)S(1)}, bf16[224,128]{1,0:T(8,128)(2,1)S(1)}, u32[]{:S(2)}, u32[]{:S(2)}) collective-permute-start(bf16[224,128]{1,0:T(8,128)(2,1)S(1)} %slice.49), channel_id=1, source_target_pairs={{0,8},{8,0},{1,9},{9,1},{2,10},{10,2},{3,11},{11,3},{4,12},{12,4},... | collective-permute-start | bytes 172040 | tf_op jit(solution)/shard_map/ppermute | solution.py:282
  165.0 0.9 collective-permute-done.12
  165.8 0.7 pad_maximum_fusion.2
  (46 shorter events, 0.7 us)
Async XLA Ops:
  7.2 14.4 %copy-start = (bf16[128,576]{0,1:T(8,128)(2,1)S(1)}, bf16[128,576]{0,1:T(8,128)(2,1)}, u32[]{:S(2)}) copy-start(bf16[128,576]{0,1:T(8,128)(2,1)} %param.12) | copy-start | bytes 442372
  8.9 14.1 %copy-start.6 = (bf16[72,1024]{1,0:T(8,128)(2,1)}, bf16[72,1024]{1,0:T(8,128)(2,1)S(1)}, u32[]{:S(2)}) copy-start(bf16[72,1024]{1,0:T(8,128)(2,1)S(1)} %pad_maximum_fusion.1.refs_0_) | copy-start | bytes 442372
  8.9 28.8 %collective-permute-start.6 = (bf16[72,1024]{1,0:T(8,128)(2,1)S(1)}, bf16[72,1024]{1,0:T(8,128)(2,1)S(1)}, u32[]{:S(2)}, u32[]{:S(2)}) collective-permute-start(bf16[72,1024]{1,0:T(8,128)(2,1)S(1)} %pad_maximum_fusion.1.refs_0_), channel_id=1, source_target_pairs={{0,16},{16,0},{32,48},{48,32},{1,17},{17,1},{33,49},{49,33},{2,18}... | collective-permute-start | bytes 442376 | tf_op jit(solution)/shard_map/ppermute | solution.py:303
  13.8 24.0 %collective-permute-start.7 = (bf16[72,1024]{1,0:T(8,128)(2,1)S(1)}, bf16[72,1024]{1,0:T(8,128)(2,1)S(1)}, u32[]{:S(2)}, u32[]{:S(2)}) collective-permute-start(bf16[72,1024]{1,0:T(8,128)(2,1)S(1)} %pad_maximum_fusion.1.refs_0_), channel_id=1, source_target_pairs={{0,32},{16,48},{32,0},{48,16},{1,33},{17,49},{33,1},{49,17},{2,34}... | collective-permute-start | bytes 442376 | tf_op jit(solution)/shard_map/ppermute | solution.py:303
  19.6 18.2 %collective-permute-start.8 = (bf16[72,1024]{1,0:T(8,128)(2,1)S(1)}, bf16[72,1024]{1,0:T(8,128)(2,1)S(1)}, u32[]{:S(2)}, u32[]{:S(2)}) collective-permute-start(bf16[72,1024]{1,0:T(8,128)(2,1)S(1)} %pad_maximum_fusion.1.refs_0_), channel_id=1, source_target_pairs={{0,48},{16,32},{32,16},{48,0},{1,49},{17,33},{33,17},{49,1},{2,50}... | collective-permute-start | bytes 442376 | tf_op jit(solution)/shard_map/ppermute | solution.py:303
  23.0 12.3 %copy-start.11 = (s32[1,16]{1,0:T(1,128)S(1)}, s32[1,16]{1,0:T(1,128)}, u32[]{:S(2)}) copy-start(s32[1,16]{1,0:T(1,128)} %param.13) | copy-start | bytes 196
  23.0 49.2 %all-to-all-start = ((bf16[64,16,576]{2,1,0:T(8,128)(2,1)}), bf16[64,16,576]{2,1,0:T(8,128)(2,1)S(1)}, u32[]{:S(2)}, u32[]{:S(2)}) async-start(bf16[64,16,576]{2,1,0:T(8,128)(2,1)} %bitcast.1), calls=%async_computation | async-start | bytes 2621440 | tf_op jit(solution)/shard_map/all_to_all | solution.py:305
  35.3 82.9 %all-gather.2.cloned.1.call-start = ((), (), s32[]{:S(2)}) async-start(), calls=%async_computation.2 | async-start | bytes 5308416 | tf_op jit(solution)/shard_map/all_gather | solution.py:317
  35.3 9.4 %collective-permute-start = (s32[16]{0:T(128)S(1)}, s32[16]{0:T(128)S(1)}, u32[]{:S(2)}, u32[]{:S(2)}) collective-permute-start(s32[16]{0:T(128)S(1)} %broadcast_maximum_fusion), channel_id=1, source_target_pairs={{0,8},{8,0},{1,9},{9,1},{2,10},{10,2},{3,11},{11,3},{4,12},{12,4},... | collective-permute-start | bytes 200 | tf_op jit(solution)/shard_map/ppermute | solution.py:282
  37.7 0.7 copy-start.8
  37.7 0.7 copy-start.9
  37.8 0.7 copy-start.10
  72.9 5.3 %collective-permute-start.1 = (bf16[256,576]{1,0:T(8,128)(2,1)S(1)}, bf16[256,576]{1,0:T(8,128)(2,1)S(1)}, u32[]{:S(2)}, u32[]{:S(2)}) collective-permute-start(bf16[256,576]{1,0:T(8,128)(2,1)S(1)} %bitcast.38), channel_id=1, source_target_pairs={{0,8},{8,0},{1,9},{9,1},{2,10},{10,2},{3,11},{11,3},{4,12},{12,4},... | collective-permute-start | bytes 884744 | tf_op jit(solution)/shard_map/ppermute | solution.py:282
  78.2 6.8 %copy-start.2 = (bf16[512,576]{1,0:T(8,128)(2,1)}, bf16[512,576]{1,0:T(8,128)(2,1)S(1)}, u32[]{:S(2)}) copy-start(bf16[512,576]{1,0:T(8,128)(2,1)S(1)} %pad_maximum_fusion.refs_2_) | copy-start | bytes 1769476
  78.5 17.8 %collective-permute-start.2 = (bf16[512,576]{0,1:T(8,128)(2,1)S(1)}, bf16[512,576]{0,1:T(8,128)(2,1)S(1)}, u32[]{:S(2)}, u32[]{:S(2)}) collective-permute-start(bf16[512,576]{0,1:T(8,128)(2,1)S(1)} %copy.14), channel_id=1, source_target_pairs={{0,2},{2,4},{4,6},{6,0},{1,3},{3,5},{5,7},{7,1},{8,10},{10,12},{12... | collective-permute-start | bytes 1769480 | tf_op jit(solution)/shard_map/ppermute | solution.py:326
  81.6 16.2 %collective-permute-start.3 = (bf16[512,576]{0,1:T(8,128)(2,1)S(1)}, bf16[512,576]{0,1:T(8,128)(2,1)S(1)}, u32[]{:S(2)}, u32[]{:S(2)}) collective-permute-start(bf16[512,576]{0,1:T(8,128)(2,1)S(1)} %copy.14), channel_id=1, source_target_pairs={{0,6},{2,0},{4,2},{6,4},{1,7},{3,1},{5,3},{7,5},{8,14},{10,8},{12,... | collective-permute-start | bytes 1769480 | tf_op jit(solution)/shard_map/ppermute | solution.py:327
  98.1 6.9 %copy-start.3 = (bf16[512,576]{1,0:T(8,128)(2,1)}, bf16[512,576]{1,0:T(8,128)(2,1)S(1)}, u32[]{:S(2)}) copy-start(bf16[512,576]{1,0:T(8,128)(2,1)S(1)} %copy.16.refs_2_) | copy-start | bytes 1769476
  98.4 6.6 %copy-start.4 = (bf16[512,576]{1,0:T(8,128)(2,1)}, bf16[512,576]{1,0:T(8,128)(2,1)S(1)}, u32[]{:S(2)}) copy-start(bf16[512,576]{1,0:T(8,128)(2,1)S(1)} %copy.17.refs_3_) | copy-start | bytes 1769476
  98.5 13.6 %collective-permute-start.4 = (bf16[256,576]{1,0:T(8,128)(2,1)S(1)}, bf16[256,576]{1,0:T(8,128)(2,1)S(1)}, u32[]{:S(2)}, u32[]{:S(2)}) collective-permute-start(bf16[256,576]{1,0:T(8,128)(2,1)S(1)} %slice.44), channel_id=1, source_target_pairs={{0,2},{2,4},{4,6},{6,0},{1,3},{3,5},{5,7},{7,1},{8,10},{10,12},{12... | collective-permute-start | bytes 884744 | tf_op jit(solution)/shard_map/ppermute | solution.py:331
  101.7 10.4 %collective-permute-start.5 = (bf16[256,576]{1,0:T(8,128)(2,1)S(1)}, bf16[256,576]{1,0:T(8,128)(2,1)S(1)}, u32[]{:S(2)}, u32[]{:S(2)}) collective-permute-start(bf16[256,576]{1,0:T(8,128)(2,1)S(1)} %slice.45), channel_id=1, source_target_pairs={{0,6},{2,0},{4,2},{6,4},{1,7},{3,1},{5,3},{7,5},{8,14},{10,8},{12,... | collective-permute-start | bytes 884744 | tf_op jit(solution)/shard_map/ppermute | solution.py:332
  112.1 0.7 copy-start.12
  112.1 0.8 copy-start.13
  118.2 5.2 %collective-permute-start.9 = (bf16[1024,128]{1,0:T(8,128)(2,1)}, bf16[1024,128]{1,0:T(8,128)(2,1)S(1)}, u32[]{:S(2)}, u32[]{:S(2)}) collective-permute-start(bf16[1024,128]{1,0:T(8,128)(2,1)} %attend.5.own_ref), channel_id=1, source_target_pairs={{0,8},{8,0},{1,9},{9,1},{2,10},{10,2},{3,11},{11,3},{4,12},{12,4},... | collective-permute-start | bytes 786440 | tf_op jit(solution)/shard_map/ppermute | solution.py:282
  123.4 0.7 copy-start.7
  129.6 6.5 %copy-start.1 = (bf16[32,16,1024]{2,1,0:T(8,128)(2,1)}, bf16[32,16,1024]{2,1,0:T(8,128)(2,1)S(1)}, u32[]{:S(2)}) copy-start(bf16[32,16,1024]{2,1,0:T(8,128)(2,1)S(1)} %slice.35.own_ref) | copy-start | bytes 3145732
  129.7 6.5 %collective-permute-start.10 = (bf16[32,16,1024]{2,1,0:T(8,128)(2,1)S(1)}, bf16[32,16,1024]{2,1,0:T(8,128)(2,1)S(1)}, u32[]{:S(2)}, u32[]{:S(2)}) collective-permute-start(bf16[32,16,1024]{2,1,0:T(8,128)(2,1)S(1)} %slice.35.own_ref), channel_id=1, source_target_pairs={{0,8},{8,0},{1,9},{9,1},{2,10},{10,2},{3,11},{11,3},{4,12},{12,4},... | collective-permute-start | bytes 3145736 | tf_op jit(solution)/shard_map/ppermute | solution.py:282
  132.0 16.9 %all-to-all-start.1 = ((bf16[4,2,224,256]{3,2,1,0:T(8,128)(2,1)}), bf16[4,2,224,256]{3,2,1,0:T(8,128)(2,1)S(1)}, u32[]{:S(2)}, u32[]{:S(2)}) async-start(bf16[4,2,224,256]{3,2,1,0:T(8,128)(2,1)} %bitcast.18), calls=%async_computation.1 | async-start | bytes 1835008 | tf_op jit(solution)/shard_map/all_to_all | solution.py:342
  136.2 1.0 copy-start.5
  149.0 10.1 %collective-permute-start.11 = (bf16[224,256]{1,0:T(8,128)(2,1)S(1)}, bf16[224,256]{1,0:T(8,128)(2,1)S(1)}, u32[]{:S(2)}, u32[]{:S(2)}) collective-permute-start(bf16[224,256]{1,0:T(8,128)(2,1)S(1)} %fusion.1), channel_id=1, source_target_pairs={{0,1},{1,0},{2,3},{3,2},{4,5},{5,4},{6,7},{7,6},{8,9},{9,8},{10,11... | collective-permute-start | bytes 344072 | tf_op jit(solution)/shard_map/ppermute | solution.py:351
  159.2 6.6 %collective-permute-start.12 = (bf16[224,128]{1,0:T(8,128)(2,1)S(1)}, bf16[224,128]{1,0:T(8,128)(2,1)S(1)}, u32[]{:S(2)}, u32[]{:S(2)}) collective-permute-start(bf16[224,128]{1,0:T(8,128)(2,1)S(1)} %slice.49), channel_id=1, source_target_pairs={{0,8},{8,0},{1,9},{9,1},{2,10},{10,2},{3,11},{11,3},{4,12},{12,4},... | collective-permute-start | bytes 172040 | tf_op jit(solution)/shard_map/ppermute | solution.py:282
Sparse Core Ops, SparseCore 0:
  40.7 71.4 all-gather.1
